TPU v7x, 32 devices: a whole 2x2x4 slice. The times are simulated.
32 devices in a mesh: section: 2 (over core), rep: 2 (over x), shard: 8 (over z, y).
Axes of the slice: x: 2, y: 2, z: 4, core: 2. Of those that a mesh axis runs over, the one named last changes fastest.
Arguments:
- boundary: bfloat16 [2, 2, 1024, 768], P('section', None, ('rep', 'shard')), may hold values from -6 to 6
- seq_lengths: int32 [2, 16, 4], P(None, ('rep', 'shard')), may hold values from 1 to 32, 64 in all within a row
- routes: int32 [2, 2, 1024, 1], P('section', None, ('rep', 'shard')), may hold values from 0 to 3; in each aligned block of 64 rows (0 to 63, 64 to 127, ..., all dimensions but the last counted through in order) at most 17 rows name the same one
- qkv_proj: bfloat16 [2, 3, 768, 768], P('section', None, 'shard'), may hold values from -0.21875 to 0.21875
- out_proj: bfloat16 [2, 768, 768], P('section', 'shard'), may hold values from -0.875 to 0.875
- router: bfloat16 [2, 768, 4], P('section', 'shard'), may hold values from -0.15625 to 0.15625
- gains: bfloat16 [2, 2, 768], P('section', None, 'shard'), may hold values from 0.5 to 1.5
- rel_table: bfloat16 [2, 384], P('section', 'shard'), may hold values from -6 to 6
- expert_in: bfloat16 [2, 8, 768, 1536], P('section', 'shard', None, 'rep'), may hold values from -0.21875 to 0.21875
- expert_out: bfloat16 [2, 8, 1536, 768], P('section', 'shard', 'rep'), may hold values from -0.4375 to 0.4375
Outputs:
- boundary_out: float32 [2, 2, 1024, 768], P('section', None, ('rep', 'shard'))
- grad_qkv: float32 [2, 3, 768, 768], P('section', None, 'shard')
- grad_out_proj: float32 [2, 768, 768], P('section', 'shard')
- grad_router: float32 [2, 768, 4], P('section', 'shard')
- grad_gains: float32 [2, 2, 768], P('section', None, 'shard')
- grad_table: float32 [2, 384], P('section', 'shard')
- grad_expert_in: float32 [2, 8, 768, 1536], P('section', 'shard', None, 'rep')
- grad_expert_out: float32 [2, 8, 1536, 768], P('section', 'shard', 'rep')
Inputs may be any that keep to these rules, and one draw needn't show every extreme that they name: `seq_lengths`: each device's 4 lengths of a micro-batch sum to 64. `routes`: in the 64 rows of one device in one micro-batch of one section no expert is named more than 17 times.
All inputs are finite; a program needn't handle non-finite values.
Results may differ from a plain program's by a relative error of at most 0.024.
Values may be sent and summed in bfloat16 or wider, within the bound.
No kernel may reach another device: no remote copies, remote signals or barrier semaphores. Data moves between devices by JAX's collectives and lax.ppermute only.
A program may use at most 128 MiB of HBM per device.

v0:
```python
import math

import jax
import jax.numpy as jnp
import numpy as np
from jax import lax
from jax.sharding import PartitionSpec as P

HEADS = 12
HEAD = 64
BUCKETS = 32
SPAN = 128


EPSILON = 1e-06
NEGATIVE = -1e30


def shifted(x, axis, by):
    devices = lax.axis_size(axis)
    pairs = [(i, i + by) for i in range(devices) if 0 <= i + by < devices]
    return lax.ppermute(x, axis, pairs)


def bucket_onehot(length, bucket_count, max_span):
    half_count = bucket_count // 2
    exact_count = half_count // 2
    table_rows = np.zeros((length * length, bucket_count), np.float32)
    for query_place in range(length):
        for key_place in range(length):
            offset = key_place - query_place
            base_bucket = half_count if offset > 0 else 0
            distance = abs(offset)
            if distance < exact_count:
                bucket = distance
            else:
                bucket = exact_count + int(
                    math.log(distance / exact_count)
                    / math.log(max_span / exact_count)
                    * (half_count - exact_count)
                )
                bucket = min(bucket, half_count - 1)
            table_rows[query_place * length + key_place, base_bucket + bucket] = 1.0
    return table_rows


def rms_norm(values, gain_row):
    return (
        values * lax.rsqrt(jnp.mean(values * values, axis=-1, keepdims=True) + EPSILON) * gain_row
    )


def soft_max(scores):
    highest = jnp.max(scores, axis=-1, keepdims=True)
    exponent = jnp.exp(scores - highest)
    return exponent / jnp.sum(exponent, axis=-1, keepdims=True)


def segment_mask(seq_lengths, row_count):
    boundary_ends = jnp.cumsum(seq_lengths).astype(jnp.int32)
    position = jnp.arange(row_count, dtype=jnp.int32)
    segment = jnp.sum((position[:, None] >= boundary_ends[None, :]).astype(jnp.int32), axis=1)
    return segment[:, None] == segment[None, :]


def relative_bias(table_flat, row_count):
    onehot_rows = jnp.asarray(bucket_onehot(row_count, BUCKETS, SPAN))
    spread = jnp.dot(
        onehot_rows,
        table_flat.astype(jnp.float32).reshape(BUCKETS, HEADS),
        precision=lax.Precision.HIGHEST,
    )
    return spread.T.reshape(HEADS, row_count, row_count)


def attention_scores(query_heads, key_heads, position_bias, same_seq):
    scale_factor = 1.0 / math.sqrt(HEAD)
    raw_scores = (
        jnp.einsum("qhc,khc->hqk", query_heads, key_heads, preferred_element_type=jnp.float32)
        * scale_factor
        + position_bias
    )
    return jnp.where(same_seq[None], raw_scores, NEGATIVE)


def dispatch_matrix(route_ids, expert_count, shard_count, capacity):
    row_count = route_ids.shape[0]
    member = (route_ids[:, None] == jnp.arange(expert_count, dtype=jnp.int32)[None, :]).astype(
        jnp.int32
    )
    slot_index = jnp.sum((jnp.cumsum(member, axis=0) - 1) * member, axis=1).astype(jnp.int32)
    target_expert = jnp.arange(shard_count, dtype=jnp.int32) // 2
    slot_range = jnp.arange(capacity, dtype=jnp.int32)
    picked = (route_ids[None, None, :] == target_expert[:, None, None]) & (
        slot_index[None, None, :] == slot_range[None, :, None]
    )
    return (picked.reshape(shard_count * capacity, row_count), member)


def layer_forward(layer_in, params, weight_in, weight_out, seq_lengths, route_ids):
    qkv_weight, out_weight, router_weight, gain_pair, table_flat = params
    row_count, width = layer_in.shape
    expert_count = router_weight.shape[1]
    shard_count = lax.axis_size("shard")
    capacity = max(2, row_count // expert_count + 1)
    gains_float = gain_pair.astype(jnp.float32)
    normed_in = rms_norm(layer_in, gains_float[0]).astype(jnp.bfloat16)
    projected = jnp.einsum(
        "td,jde->jte", normed_in, qkv_weight, preferred_element_type=jnp.float32
    ).astype(jnp.bfloat16)
    heads_qkv = projected.reshape(3, row_count, HEADS, HEAD)
    position_bias = relative_bias(table_flat, row_count)
    same_seq = segment_mask(seq_lengths, row_count)
    scores = attention_scores(heads_qkv[0], heads_qkv[1], position_bias, same_seq)
    highest = jnp.max(scores, axis=-1, keepdims=True)
    log_total = highest + jnp.log(jnp.sum(jnp.exp(scores - highest), axis=-1, keepdims=True))
    attn_prob = jnp.exp(scores - log_total).astype(jnp.bfloat16)
    context = (
        jnp.einsum("hqk,khc->qhc", attn_prob, heads_qkv[2], preferred_element_type=jnp.float32)
        .reshape(row_count, width)
        .astype(jnp.bfloat16)
    )
    middle = layer_in + jnp.dot(context, out_weight, preferred_element_type=jnp.float32)
    normed_mid = rms_norm(middle, gains_float[1]).astype(jnp.bfloat16)
    router_prob = soft_max(jnp.dot(normed_mid, router_weight, preferred_element_type=jnp.float32))
    picked, member = dispatch_matrix(route_ids, expert_count, shard_count, capacity)
    gate_prob = jnp.sum(router_prob * member.astype(jnp.float32), axis=1)
    outgoing = (
        jnp.dot(picked.astype(jnp.bfloat16), normed_mid, preferred_element_type=jnp.float32)
        .astype(jnp.bfloat16)
        .reshape(shard_count, capacity, width)
    )
    incoming = lax.all_to_all(outgoing, "shard", split_axis=0, concat_axis=0, tiled=True)
    expert_rows = lax.all_gather(incoming, "rep", axis=0, tiled=True).reshape(-1, width)
    hidden_pre = jnp.dot(expert_rows, weight_in, preferred_element_type=jnp.float32)
    hidden_act = jax.nn.gelu(hidden_pre).astype(jnp.bfloat16)
    partial_out = jnp.dot(hidden_act, weight_out, preferred_element_type=jnp.float32).reshape(
        -1, capacity, width
    )
    summed = lax.psum_scatter(partial_out, "rep", scatter_dimension=0, tiled=True)
    returned = lax.all_to_all(summed, "shard", split_axis=0, concat_axis=0, tiled=True)
    expert_out = jnp.dot(
        picked.astype(jnp.float32).T, returned.reshape(-1, width), precision=lax.Precision.HIGHEST
    )
    layer_out = middle + gate_prob[:, None] * expert_out
    kept = {
        "layer_in": layer_in,
        "normed_in": normed_in,
        "heads_qkv": heads_qkv,
        "position_bias": position_bias,
        "same_seq": same_seq,
        "log_total": log_total,
        "context": context,
        "middle": middle,
        "normed_mid": normed_mid,
        "router_prob": router_prob,
        "member": member,
        "gate_prob": gate_prob,
        "picked": picked,
        "expert_rows": expert_rows,
        "hidden_pre": hidden_pre,
        "hidden_act": hidden_act,
        "expert_out": expert_out,
    }
    return (layer_out, kept)


def layer_backward(kept, grad_out, params, weight_in, weight_out):
    qkv_weight, out_weight, router_weight, gain_pair, table_flat = params
    row_count, width = grad_out.shape
    shard_count = lax.axis_size("shard")
    capacity = kept["picked"].shape[0] // shard_count
    scale_factor = 1.0 / math.sqrt(HEAD)
    gains_float = gain_pair.astype(jnp.float32)
    branch_grad = (kept["gate_prob"][:, None] * grad_out).astype(jnp.bfloat16)
    gate_grad = jnp.sum(grad_out * kept["expert_out"], axis=1)
    outgoing = (
        jnp.dot(
            kept["picked"].astype(jnp.bfloat16), branch_grad, preferred_element_type=jnp.float32
        )
        .astype(jnp.bfloat16)
        .reshape(shard_count, capacity, width)
    )
    incoming = lax.all_to_all(outgoing, "shard", split_axis=0, concat_axis=0, tiled=True)
    grad_rows = lax.all_gather(incoming, "rep", axis=0, tiled=True).reshape(-1, width)
    act_grad = jnp.dot(grad_rows, weight_out.T, preferred_element_type=jnp.float32)
    gelu_value, gelu_back = jax.vjp(jax.nn.gelu, kept["hidden_pre"])
    pre_grad = gelu_back(act_grad)[0].astype(jnp.bfloat16)
    row_grad = jnp.dot(pre_grad, weight_in.T, preferred_element_type=jnp.float32).reshape(
        -1, capacity, width
    )
    summed = lax.psum_scatter(
        row_grad.astype(jnp.bfloat16), "rep", scatter_dimension=0, tiled=True
    ).astype(jnp.float32)
    returned = lax.all_to_all(
        summed.astype(jnp.bfloat16), "shard", split_axis=0, concat_axis=0, tiled=True
    ).astype(summed.dtype)
    normed_mid_grad = jnp.dot(
        kept["picked"].astype(jnp.float32).T,
        returned.reshape(-1, width),
        precision=lax.Precision.HIGHEST,
    )
    router_prob = kept["router_prob"]
    prob_grad = kept["member"].astype(jnp.float32) * gate_grad[:, None]
    logit_grad = router_prob * (prob_grad - jnp.sum(router_prob * prob_grad, axis=1, keepdims=True))
    grad_router = jnp.dot(
        kept["normed_mid"].astype(jnp.float32).T, logit_grad, precision=lax.Precision.HIGHEST
    )
    normed_mid_grad = normed_mid_grad + jnp.dot(
        logit_grad, router_weight.astype(jnp.float32).T, precision=lax.Precision.HIGHEST
    )
    norm_value, norm_back = jax.vjp(rms_norm, kept["middle"], gains_float[1])
    middle_grad, gain_grad_two = norm_back(normed_mid_grad)
    middle_grad = middle_grad + grad_out
    attn_out_grad = middle_grad.astype(jnp.bfloat16)
    context_grad = (
        jnp.dot(attn_out_grad, out_weight.T, preferred_element_type=jnp.float32)
        .astype(jnp.bfloat16)
        .reshape(row_count, HEADS, HEAD)
    )
    heads_qkv = kept["heads_qkv"]
    scores = attention_scores(heads_qkv[0], heads_qkv[1], kept["position_bias"], kept["same_seq"])
    attn_float = jnp.exp(scores - kept["log_total"])
    value_grad = jnp.einsum(
        "hqk,qhc->khc",
        attn_float.astype(jnp.bfloat16),
        context_grad,
        preferred_element_type=jnp.float32,
    ).astype(jnp.bfloat16)
    attn_grad = jnp.einsum(
        "qhc,khc->hqk", context_grad, heads_qkv[2], preferred_element_type=jnp.float32
    )
    score_grad = (
        attn_float * (attn_grad - jnp.sum(attn_float * attn_grad, axis=-1, keepdims=True))
    ).astype(jnp.bfloat16)
    query_grad = (
        jnp.einsum("hqk,khc->qhc", score_grad, heads_qkv[1], preferred_element_type=jnp.float32)
        * scale_factor
    ).astype(jnp.bfloat16)
    key_grad = (
        jnp.einsum("hqk,qhc->khc", score_grad, heads_qkv[0], preferred_element_type=jnp.float32)
        * scale_factor
    ).astype(jnp.bfloat16)
    onehot_rows = jnp.asarray(bucket_onehot(row_count, BUCKETS, SPAN))
    score_rows = (
        score_grad.astype(jnp.float32).transpose(1, 2, 0).reshape(row_count * row_count, HEADS)
    )
    grad_table = jnp.dot(onehot_rows.T, score_rows, precision=lax.Precision.HIGHEST).reshape(-1)
    proj_grad = jnp.stack([query_grad, key_grad, value_grad]).reshape(3, row_count, width)
    normed_in_grad = jnp.einsum(
        "jte,jde->td", proj_grad, qkv_weight, preferred_element_type=jnp.float32
    )
    first_value, first_back = jax.vjp(rms_norm, kept["layer_in"], gains_float[0])
    input_grad, gain_grad_one = first_back(normed_in_grad)
    input_grad = input_grad + middle_grad
    small_grads = (grad_router, jnp.stack([gain_grad_one, gain_grad_two]), grad_table)
    attn_factors = (kept["normed_in"], proj_grad, kept["context"], attn_out_grad)
    expert_factors = (kept["expert_rows"], pre_grad, kept["hidden_act"], grad_rows)
    return (input_grad, small_grads, attn_factors, expert_factors)


def attention_weight_grads(attn_factors):
    normed_rows, proj_rows, context_rows, out_rows = attn_factors
    grad_qkv = jnp.einsum("td,jte->jde", normed_rows, proj_rows, preferred_element_type=jnp.float32)
    grad_out_weight = jnp.dot(context_rows.T, out_rows, preferred_element_type=jnp.float32)
    return (grad_qkv, grad_out_weight)


def local(
    boundary,
    seq_lengths,
    routes,
    qkv_proj,
    out_proj,
    router,
    gains,
    rel_table,
    expert_in,
    expert_out,
):
    micro_count = boundary.shape[1]
    own_rows = boundary[0]
    section_index = lax.axis_index("section")
    first_section = section_index == 0
    weight_in = expert_in[0, 0]
    weight_out = expert_out[0, 0]
    length_table = seq_lengths[:, 0]
    route_table = routes[0, :, :, 0]

    def pick_section(lower_value, upper_value):
        return jnp.where(first_section, lower_value, upper_value)

    gathered = (
        lax.all_gather(qkv_proj, "shard", axis=2, tiled=True),
        lax.all_gather(out_proj, "shard", axis=1, tiled=True),
        lax.all_gather(router, "shard", axis=1, tiled=True),
        lax.all_gather(gains, "shard", axis=2, tiled=True),
        lax.all_gather(rel_table, "shard", axis=1, tiled=True),
    )
    params = tuple((member_array[0] for member_array in gathered))
    carried = jnp.zeros(own_rows.shape[1:], jnp.float32)
    stash = []
    forward_out = []
    for tick_index in range(micro_count + 1):
        own_input = own_rows[min(tick_index, micro_count - 1)].astype(jnp.float32)
        layer_in = jnp.where(first_section, own_input, carried)
        micro_index = jnp.clip(tick_index - section_index, 0, micro_count - 1)
        lengths_now = lax.dynamic_index_in_dim(length_table, micro_index, 0, keepdims=False)
        routes_now = lax.dynamic_index_in_dim(route_table, micro_index, 0, keepdims=False)
        layer_out, kept = layer_forward(
            layer_in, params, weight_in, weight_out, lengths_now, routes_now
        )
        stash.append(kept)
        forward_out.append(layer_out)
        if tick_index < micro_count:
            carried = shifted(layer_out.astype(jnp.bfloat16), "section", 1).astype(jnp.float32)
    arriving = jnp.zeros_like(carried)
    input_grads = []
    small_total = None
    reduced_total = None
    attn_list = []
    expert_list = []
    for tick_index in range(micro_count + 1):
        own_grad = own_rows[min(tick_index, micro_count - 1)].astype(jnp.float32)
        valid_tick = jnp.where(first_section, tick_index >= 1, tick_index < micro_count)
        grad_in = jnp.where(valid_tick, jnp.where(first_section, arriving, own_grad), 0.0)
        chosen_state = jax.tree.map(
            pick_section, stash[max(tick_index - 1, 0)], stash[min(tick_index + 1, micro_count)]
        )
        kept = chosen_state
        input_grad, small_grads, attn_factors, expert_factors = layer_backward(
            kept, grad_in, params, weight_in, weight_out
        )
        expert_list.append(expert_factors)
        attn_list.append(attn_factors)
        small_total = (
            small_grads if small_total is None else jax.tree.map(jnp.add, small_total, small_grads)
        )
        input_grads.append(input_grad)
        if tick_index < micro_count:
            arriving = shifted(input_grad.astype(jnp.bfloat16), "section", -1).astype(jnp.float32)
    joined = (
        jnp.concatenate([item[0] for item in attn_list], axis=0),
        jnp.concatenate([item[1] for item in attn_list], axis=1),
        jnp.concatenate([item[2] for item in attn_list], axis=0),
        jnp.concatenate([item[3] for item in attn_list], axis=0),
    )
    grad_qkv, grad_out_weight = attention_weight_grads(joined)
    reduced_total = (
        lax.psum_scatter(grad_qkv, "shard", scatter_dimension=1, tiled=True),
        lax.psum_scatter(grad_out_weight, "shard", scatter_dimension=0, tiled=True),
        lax.psum_scatter(small_total[0], "shard", scatter_dimension=0, tiled=True),
        lax.psum_scatter(small_total[1], "shard", scatter_dimension=1, tiled=True),
        lax.psum_scatter(small_total[2], "shard", scatter_dimension=0, tiled=True),
    )
    summed_grads = (
        lax.psum(reduced_total[0].astype(jnp.bfloat16), "rep").astype(jnp.float32),
        lax.psum(reduced_total[1].astype(jnp.bfloat16), "rep").astype(jnp.float32),
        lax.psum(reduced_total[2].astype(jnp.bfloat16), "rep").astype(jnp.float32),
        lax.psum(reduced_total[3].astype(jnp.bfloat16), "rep").astype(jnp.float32),
        lax.psum(reduced_total[4].astype(jnp.bfloat16), "rep").astype(jnp.float32),
    )
    rows_all = jnp.concatenate([item[0] for item in expert_list], axis=0)
    pre_all = jnp.concatenate([item[1] for item in expert_list], axis=0)
    act_all = jnp.concatenate([item[2] for item in expert_list], axis=0)
    grads_all = jnp.concatenate([item[3] for item in expert_list], axis=0)
    grad_w_in = jnp.dot(rows_all.T, pre_all, preferred_element_type=jnp.float32)
    grad_w_out = jnp.dot(act_all.T, grads_all, preferred_element_type=jnp.float32)
    result_rows = jnp.stack(
        [
            jnp.where(first_section, input_grads[micro_slot + 1], forward_out[micro_slot + 1])
            for micro_slot in range(micro_count)
        ]
    )
    return (
        result_rows[None],
        summed_grads[0][None],
        summed_grads[1][None],
        summed_grads[2][None],
        summed_grads[3][None],
        summed_grads[4][None],
        grad_w_in[None, None],
        grad_w_out[None, None],
    )


def solution(mesh):
    in_specs = (
        P("section", None, ("rep", "shard"), None),
        P(None, ("rep", "shard"), None),
        P("section", None, ("rep", "shard"), None),
        P("section", None, "shard", None),
        P("section", "shard", None),
        P("section", "shard", None),
        P("section", None, "shard"),
        P("section", "shard"),
        P("section", "shard", None, "rep"),
        P("section", "shard", "rep", None),
    )
    out_specs = (
        P("section", None, ("rep", "shard"), None),
        P("section", None, "shard", None),
        P("section", "shard", None),
        P("section", "shard", None),
        P("section", None, "shard"),
        P("section", "shard"),
        P("section", "shard", None, "rep"),
        P("section", "shard", "rep", None),
    )
    return jax.shard_map(local, mesh=mesh, in_specs=in_specs, out_specs=out_specs, check_vma=False)
```

profile of v0, /device:TPU:0, one launch (start us, length us, event | category | flops | bytes accessed | tf_op | source)
XLA Modules:
  0.0 1030.7 jit_solution(8488883301374509424)
XLA Ops:
  11.6 23.2 %all-reduce = bf16[384]{0:T(512)(128)(2,1)S(1)} all-reduce(bf16[384]{0:T(512)(128)(2,1)S(1)} %dynamic-update-slice), channel_id=1, replica_groups=mesh['section'=2,'rep'=2,'shard'=8] {'shard'}, use_global_device_ids=true, to_apply=%add | all-reduce | flops 384 | bytes 1536
  42.6 32.5 %all_gather.33 = bf16[1,2,768]{1,0,2:T(2,128)(2,1)S(1)} all-gather(bf16[1,2,96]{1,0,2:T(2,128)(2,1)S(1)} %copy.342), channel_id=1, replica_groups=mesh['section'=2,'rep'=2,'shard'=8] {'shard'}, dimensions={2}, use_global_device_ids=true | all-gather | bytes 3456 | tf_op jit(solution)/shard_map/all_gather | solution.py:297
  75.8 4.6 slice_reduce_fusion
  88.1 37.8 %all-gather.5.cloned.1.call-done = bf16[1,768,768]{2,1,0:T(8,128)(2,1)} async-done(((bf16[1,96,768]{2,1,0:T(8,128)(2,1)}), bf16[1,768,768]{2,1,0:T(8,128)(2,1)}) %all-gather.5.cloned.1.call-update) | async-done | bytes 1179664 | tf_op jit(solution)/shard_map/all_gather | solution.py:295
  128.2 12.3 %all_to_all.60 = bf16[8,17,768]{2,1,0:T(8,128)(2,1)S(1)} all-to-all(bf16[8,17,768]{2,1,0:T(8,128)(2,1)S(1)} %reshape.1018), channel_id=1, replica_groups=mesh['section'=2,'rep'=2,'shard'=8] {'shard'}, dimensions={0} | all-to-all | bytes 417792 | tf_op jit(solution)/shard_map/all_to_all | solution.py:133
  140.5 6.5 all_gather.38
  155.5 20.4 %reduce-scatter.17.cloned.1.call-done = f32[8,17,768]{2,1,0:T(8,128)} async-done(((f32[16,17,768]{2,1,0:T(8,128)}), f32[8,17,768]{2,1,0:T(8,128)}) %reduce-scatter.17.cloned.1.call-update) | async-done | bytes 417808 | tf_op jit(solution)/shard_map/reduce_scatter | solution.py:140
  175.9 5.5 all-to-all-start.1
  181.6 39.0 %all_gather.37 = bf16[1,768,4]{2,0,1:T(2,128)(2,1)S(1)} all-gather(bf16[1,96,4]{2,0,1:T(2,128)(2,1)S(1)} %copy.349), channel_id=1, replica_groups=mesh['section'=2,'rep'=2,'shard'=8] {'shard'}, dimensions={1}, use_global_device_ids=true | all-gather | bytes 6912 | tf_op jit(solution)/shard_map/all_gather | solution.py:296
  226.1 3.5 broadcast_select_fusion.7
  237.1 14.3 %all_to_all.61 = bf16[8,17,768]{2,1,0:T(8,128)(2,1)S(1)} all-to-all(bf16[8,17,768]{2,1,0:T(8,128)(2,1)} %reshape.1022), channel_id=1, replica_groups=mesh['section'=2,'rep'=2,'shard'=8] {'shard'}, dimensions={0} | all-to-all | bytes 417792 | tf_op jit(solution)/shard_map/all_to_all | solution.py:133
  251.4 6.5 all_gather.39
  268.9 20.4 %reduce-scatter.19.cloned.1.call-done = f32[8,17,768]{2,1,0:T(8,128)} async-done(((f32[16,17,768]{2,1,0:T(8,128)}), f32[8,17,768]{2,1,0:T(8,128)}) %reduce-scatter.19.cloned.1.call-update) | async-done | bytes 417808 | tf_op jit(solution)/shard_map/reduce_scatter | solution.py:140
  289.2 5.5 all-to-all-start.3
  295.0 15.7 %all-to-all-done.3 = f32[8,17,768]{2,1,0:T(8,128)} async-done(((f32[8,17,768]{2,1,0:T(8,128)}), f32[8,17,768]{2,1,0:T(8,128)}, u32[]{:S(2)}, u32[]{:S(2)}) %all-to-all-start.3) | async-done | bytes 417824 | tf_op jit(solution)/shard_map/all_to_all | solution.py:141
  315.2 3.6 all-to-all-start.4
  319.3 9.4 all-to-all-done.4
  328.7 6.5 all_gather.40
  354.2 6.0 reduce-scatter.21.cloned.1.call-done
  360.2 5.5 all-to-all-start.5
  370.3 5.1 all-to-all-done.5
  398.9 4.8 multiply_reduce_fusion.8
  422.2 13.6 %all_to_all.62 = bf16[8,17,768]{2,1,0:T(8,128)(2,1)S(1)} all-to-all(bf16[8,17,768]{2,1,0:T(8,128)(2,1)} %reshape.1031), channel_id=1, replica_groups=mesh['section'=2,'rep'=2,'shard'=8] {'shard'}, dimensions={0} | all-to-all | bytes 417792 | tf_op jit(solution)/shard_map/all_to_all | solution.py:133
  435.8 6.5 all_gather.42
  453.2 19.9 %reduce-scatter.25.cloned.1.call-done = f32[8,17,768]{2,1,0:T(8,128)} async-done(((f32[16,17,768]{2,1,0:T(8,128)}), f32[8,17,768]{2,1,0:T(8,128)}) %reduce-scatter.25.cloned.1.call-update) | async-done | bytes 417808 | tf_op jit(solution)/shard_map/reduce_scatter | solution.py:140
  473.0 5.5 all-to-all-start.9
  484.0 10.6 %all-to-all-done.9 = f32[8,17,768]{2,1,0:T(8,128)} async-done(((f32[8,17,768]{2,1,0:T(8,128)}), f32[8,17,768]{2,1,0:T(8,128)}, u32[]{:S(2)}, u32[]{:S(2)}) %all-to-all-start.9) | async-done | bytes 417824 | tf_op jit(solution)/shard_map/all_to_all | solution.py:141
  504.7 13.5 %all_to_all.63 = bf16[8,17,768]{2,1,0:T(8,128)(2,1)S(1)} all-to-all(bf16[8,17,768]{2,1,0:T(8,128)(2,1)} %reshape.1029), channel_id=1, replica_groups=mesh['section'=2,'rep'=2,'shard'=8] {'shard'}, dimensions={0} | all-to-all | bytes 417792 | tf_op jit(solution)/shard_map/all_to_all | solution.py:184
  518.2 6.5 all_gather.41
  539.7 9.1 reduce-scatter.23.cloned.1.call-done
  548.8 5.5 all-to-all-start.8
  587.9 4.1 multiply_reduce_fusion.6
  599.6 15.6 %all_to_all.64 = bf16[8,17,768]{2,1,0:T(8,128)(2,1)S(1)} all-to-all(bf16[8,17,768]{2,1,0:T(8,128)(2,1)} %reshape.1034), channel_id=1, replica_groups=mesh['section'=2,'rep'=2,'shard'=8] {'shard'}, dimensions={0} | all-to-all | bytes 417792 | tf_op jit(solution)/shard_map/all_to_all | solution.py:184
  615.2 6.5 all_gather.43
  635.6 10.7 %reduce-scatter.27.cloned.1.call-done = bf16[8,17,768]{2,1,0:T(8,128)(2,1)} async-done(((bf16[16,17,768]{2,1,0:T(8,128)(2,1)}), bf16[8,17,768]{2,1,0:T(8,128)(2,1)}) %reduce-scatter.27.cloned.1.call-update) | async-done | bytes 208912 | tf_op jit(solution)/shard_map/reduce_scatter | solution.py:192
  646.3 5.5 all-to-all-start.11
  653.7 7.8 all-to-all-done.11
  675.3 4.0 convolution_bitcast_fusion
  679.3 11.1 %copy.457 = f32[3,768,768]{2,0,1:T(4,128)} copy(f32[3,768,768]{1,2,0:T(8,128)} %convolution_bitcast_fusion) | data formatting | bytes 14155776
  690.4 8.2 copy.472
  706.1 11.7 %reduce-scatter.33.cloned.1.call-done = f32[96,4]{1,0:T(8,128)} async-done(((f32[768,4]{1,0:T(8,128)}), f32[96,4]{1,0:T(8,128)}) %reduce-scatter.33.cloned.1.call-update) | async-done | bytes 1552
  718.7 4.4 convolution_bitcast_fusion.1
  731.5 19.6 %all-reduce.1 = bf16[384]{0:T(512)(128)(2,1)S(1)} all-reduce(f32[384]{0:T(512)S(1)} %add.396), channel_id=12, replica_groups=mesh['section'=2,'rep'=2,'shard'=8] {'shard'}, use_global_device_ids=true, to_apply=%region_74.75.clone | all-reduce | flops 384 | bytes 2304
  751.3 38.2 %reduce-scatter.29.cloned.1.call-done = f32[96,768]{1,0:T(8,128)} async-done(((f32[768,768]{1,0:T(8,128)}), f32[96,768]{1,0:T(8,128)}) %reduce-scatter.29.cloned.1.call-update) | async-done | bytes 294928 | tf_op jit(solution)/shard_map/reduce_scatter | solution.py:351
  791.1 130.1 %reduce-scatter.31.cloned.1.call-done = f32[96,2304]{1,0:T(8,128)} async-done(((f32[768,2304]{1,0:T(8,128)}), f32[96,2304]{1,0:T(8,128)}) %reduce-scatter.31.cloned.1.call-update) | async-done | bytes 884752
  925.9 59.2 %reduce-scatter.35.cloned.1.call-done = f32[96,2]{1,0:T(8,128)} async-done(((f32[768,2]{1,0:T(8,128)}), f32[96,2]{1,0:T(8,128)}) %reduce-scatter.35.cloned.1.call-update) | async-done | bytes 784
  986.0 4.9 all-reduce.2
  992.6 28.1 %all-reduce.6.cloned.1.call-done = (bf16[1,3,96,768]{2,3,1,0:T(8,128)(2,1)}, bf16[1,96,768]{2,1,0:T(8,128)(2,1)}) async-done(((bf16[1,3,96,768]{2,3,1,0:T(8,128)(2,1)}, bf16[1,96,768]{2,1,0:T(8,128)(2,1)}), (bf16[1,3,96,768]{2,3,1,0:T(8,128)(2,1)}, bf16[1,96,768]{2,1,0:T(8,128)(2,1)})) %all-reduce.6.cloned.1.call-update) | async-done | bytes 589840 | tf_op jit(solution)/shard_map/psum | solution.py:357
  (648 shorter events, 264.1 us)
Async XLA Ops:
  7.2 140.9 %copy-start = (bf16[1,1,768,768]{3,2,1,0:T(8,128)(2,1)S(1)}, bf16[1,1,768,768]{3,2,1,0:T(8,128)(2,1)}, u32[]{:S(2)}) copy-start(bf16[1,1,768,768]{3,2,1,0:T(8,128)(2,1)} %param.24) | copy-start | bytes 3538948
  7.2 77.0 %all-gather.3.cloned.1.call-start = ((), (), s32[]{:S(2)}) async-start(), calls=%async_computation.22 | async-start | bytes 3981312 | tf_op jit(solution)/shard_map/all_gather | solution.py:294
  7.9 34.5 %copy-start.165 = (bf16[1,2,96]{2,1,0:T(2,128)(2,1)S(1)}, bf16[1,2,96]{2,1,0:T(2,128)(2,1)}, u32[]{:S(2)}) copy-start(bf16[1,2,96]{2,1,0:T(2,128)(2,1)} %param.22) | copy-start | bytes 1156
  7.9 118.1 %all-gather.5.cloned.1.call-start = ((), (), s32[]{:S(2)}) async-start(), calls=%async_computation.23 | async-start | bytes 1327104 | tf_op jit(solution)/shard_map/all_gather | solution.py:295
  8.7 167.2 %reduce-scatter.17.cloned.1.call-start = ((), (), s32[]{:S(2)}) async-start(), calls=%async_computation.24 | async-start | bytes 1769472 | tf_op jit(solution)/shard_map/reduce_scatter | solution.py:140
  42.6 85.2 %copy-start.121 = (pred[136,64]{1,0:T(8,128)(4,1)}, pred[136,64]{1,0:T(8,128)(4,1)S(1)}, u32[]{:S(2)}) copy-start(pred[136,64]{1,0:T(8,128)(4,1)S(1)} %and.95) | copy-start | bytes 26116
  87.0 139.2 %copy-start.12 = (bf16[3,64,768]{2,1,0:T(8,128)(2,1)}, bf16[3,64,768]{2,1,0:T(8,128)(2,1)S(1)}, u32[]{:S(2)}) copy-start(bf16[3,64,768]{2,1,0:T(8,128)(2,1)S(1)} %fusion.98) | copy-start | bytes 884740
  87.9 39.8 %copy-start.94 = (f32[12,64]{1,0:T(8,128)}, f32[12,64]{1,0:T(8,128)S(1)}, u32[]{:S(2)}) copy-start(f32[12,64]{1,0:T(8,128)S(1)} %log_add_fusion.2) | copy-start | bytes 9220
  88.1 40.0 %copy-start.40 = (bf16[12,64,64]{2,1,0:T(8,128)(2,1)}, bf16[12,64,64]{2,1,0:T(8,128)(2,1)S(1)}, u32[]{:S(2)}) copy-start(bf16[12,64,64]{2,1,0:T(8,128)(2,1)S(1)} %convolution_convert_fusion.14) | copy-start | bytes 294916
  127.7 93.4 %copy-start.8 = (f32[64,768]{1,0:T(8,128)}, f32[64,768]{1,0:T(8,128)S(1)}, u32[]{:S(2)}) copy-start(f32[64,768]{1,0:T(8,128)S(1)} %get-tuple-element.163) | copy-start | bytes 589828
  127.8 93.0 %copy-start.25 = (bf16[64,768]{1,0:T(8,128)(2,1)}, bf16[64,768]{1,0:T(8,128)(2,1)S(1)}, u32[]{:S(2)}) copy-start(bf16[64,768]{1,0:T(8,128)(2,1)S(1)} %multiply_convert_fusion.9) | copy-start | bytes 294916
  155.4 26.0 %copy-start.164 = (bf16[1,96,4]{1,2,0:T(4,128)(2,1)S(1)}, bf16[1,96,4]{1,2,0:T(4,128)(2,1)}, u32[]{:S(2)}) copy-start(bf16[1,96,4]{1,2,0:T(4,128)(2,1)} %param.21) | copy-start | bytes 2308
  155.4 65.7 %copy-start.125 = (s32[64]{0:T(128)S(1)}, s32[64]{0:T(128)}, u32[]{:S(2)}) copy-start(s32[64]{0:T(128)} %copy-done.124) | copy-start | bytes 772
  155.4 65.7 %copy-start.105 = (pred[17,64]{1,0:T(8,128)(4,1)S(1)}, pred[17,64]{1,0:T(8,128)(4,1)}, u32[]{:S(2)}) copy-start(pred[17,64]{1,0:T(8,128)(4,1)} %copy-done.104) | copy-start | bytes 3268
  155.5 65.7 %copy-start.139 = (pred[8,64]{1,0:T(8,128)(4,1)S(1)}, pred[8,64]{1,0:T(8,128)(4,1)}, u32[]{:S(2)}) copy-start(pred[8,64]{1,0:T(8,128)(4,1)} %copy-done.138) | copy-start | bytes 1540
  175.9 45.2 %all-to-all-start.1 = ((f32[8,17,768]{2,1,0:T(8,128)}), f32[8,17,768]{2,1,0:T(8,128)S(1)}, u32[]{:S(2)}, u32[]{:S(2)}) async-start(f32[8,17,768]{2,1,0:T(8,128)} %reduce-scatter.17.cloned.1.call-done), calls=%async_computation.2 | async-start | bytes 1179648 | tf_op jit(solution)/shard_map/all_to_all | solution.py:141
  181.4 42.6 %copy-start.101 = (pred[8,17,64]{2,1,0:T(8,128)(4,1)S(1)}, pred[8,17,64]{2,1,0:T(8,128)(4,1)}, u32[]{:S(2)}) copy-start(pred[8,17,64]{2,1,0:T(8,128)(4,1)} %get-tuple-element.140) | copy-start | bytes 26116
  181.4 44.0 %copy-start.160 = (f32[64]{0:T(128)S(1)}, f32[64]{0:T(128)}, u32[]{:S(2)}) copy-start(f32[64]{0:T(128)} %copy-done.159) | copy-start | bytes 772
  181.4 107.8 %reduce-scatter.19.cloned.1.call-start = ((), (), s32[]{:S(2)}) async-start(), calls=%async_computation.25 | async-start | bytes 1769472 | tf_op jit(solution)/shard_map/reduce_scatter | solution.py:140
  222.2 2.4 collective-permute-start
  234.5 60.3 %copy-start.27 = (bf16[64,768]{1,0:T(8,128)(2,1)}, bf16[64,768]{1,0:T(8,128)(2,1)S(1)}, u32[]{:S(2)}) copy-start(bf16[64,768]{1,0:T(8,128)(2,1)S(1)} %multiply_convert_fusion.7) | copy-start | bytes 294916
  268.8 41.9 %copy-start.44 = (f32[64,768]{1,0:T(8,128)S(1)}, f32[64,768]{1,0:T(8,128)}, u32[]{:S(2)}) copy-start(f32[64,768]{1,0:T(8,128)} %get-tuple-element.169) | copy-start | bytes 589828
  268.8 41.9 %copy-start.137 = (pred[8,64]{1,0:T(8,128)(4,1)S(1)}, pred[8,64]{1,0:T(8,128)(4,1)}, u32[]{:S(2)}) copy-start(pred[8,64]{1,0:T(8,128)(4,1)} %copy-done.136) | copy-start | bytes 1540
  268.8 44.1 %copy-start.126 = (s32[64]{0:T(128)S(1)}, s32[64]{0:T(128)}, u32[]{:S(2)}) copy-start(s32[64]{0:T(128)} %copy-done.124) | copy-start | bytes 772
  268.8 44.1 %copy-start.131 = (s32[64]{0:T(128)S(1)}, s32[64]{0:T(128)}, u32[]{:S(2)}) copy-start(s32[64]{0:T(128)} %copy-done.130) | copy-start | bytes 772
  268.8 45.3 %copy-start.150 = (f32[64]{0:T(128)S(1)}, f32[64]{0:T(128)}, u32[]{:S(2)}) copy-start(f32[64]{0:T(128)} %copy-done.149) | copy-start | bytes 772
  289.2 21.5 %all-to-all-start.3 = ((f32[8,17,768]{2,1,0:T(8,128)}), f32[8,17,768]{2,1,0:T(8,128)}, u32[]{:S(2)}, u32[]{:S(2)}) async-start(f32[8,17,768]{2,1,0:T(8,128)} %reduce-scatter.19.cloned.1.call-done), calls=%async_computation.5 | async-start | bytes 1179648 | tf_op jit(solution)/shard_map/all_to_all | solution.py:141
  315.2 13.4 %all-to-all-start.4 = ((bf16[8,17,768]{2,1,0:T(8,128)(2,1)}), bf16[8,17,768]{2,1,0:T(8,128)(2,1)S(1)}, u32[]{:S(2)}, u32[]{:S(2)}) async-start(bf16[8,17,768]{2,1,0:T(8,128)(2,1)} %reshape.1026), calls=%async_computation.6 | async-start | bytes 589824 | tf_op jit(solution)/shard_map/all_to_all | solution.py:184
  318.9 41.3 %reduce-scatter.21.cloned.1.call-start = ((), (), s32[]{:S(2)}) async-start(), calls=%async_computation.26 | async-start | bytes 884736 | tf_op jit(solution)/shard_map/reduce_scatter | solution.py:192
  319.3 26.7 %copy-start.106 = (pred[17,64]{1,0:T(8,128)(4,1)}, pred[17,64]{1,0:T(8,128)(4,1)S(1)}, u32[]{:S(2)}) copy-start(pred[17,64]{1,0:T(8,128)(4,1)S(1)} %iota_compare_fusion) | copy-start | bytes 3268
  360.2 15.2 %all-to-all-start.5 = ((bf16[8,17,768]{2,1,0:T(8,128)(2,1)}), bf16[8,17,768]{2,1,0:T(8,128)(2,1)}, u32[]{:S(2)}, u32[]{:S(2)}) async-start(bf16[8,17,768]{2,1,0:T(8,128)(2,1)} %reduce-scatter.21.cloned.1.call-done), calls=%async_computation.8 | async-start | bytes 589824 | tf_op jit(solution)/shard_map/all_to_all | solution.py:195
  365.7 107.3 %reduce-scatter.25.cloned.1.call-start = ((), (), s32[]{:S(2)}) async-start(), calls=%async_computation.28 | async-start | bytes 1769472 | tf_op jit(solution)/shard_map/reduce_scatter | solution.py:140
  367.6 31.2 %collective-permute-start.1 = (bf16[64,768]{1,0:T(8,128)(2,1)}, bf16[64,768]{1,0:T(8,128)(2,1)}, u32[]{:S(2)}, u32[]{:S(2)}) collective-permute-start(bf16[64,768]{1,0:T(8,128)(2,1)} %get-tuple-element.137), channel_id=1, source_target_pairs={{0,16},{1,17},{2,18},{3,19},{4,20},{5,21},{6,22},{7,23},{8,24},{9,... | collective-permute-start | bytes 294920 | tf_op jit(solution)/shard_map/ppermute | solution.py:22
  473.0 21.5 %all-to-all-start.9 = ((f32[8,17,768]{2,1,0:T(8,128)}), f32[8,17,768]{2,1,0:T(8,128)}, u32[]{:S(2)}, u32[]{:S(2)}) async-start(f32[8,17,768]{2,1,0:T(8,128)} %reduce-scatter.25.cloned.1.call-done), calls=%async_computation.14 | async-start | bytes 1179648 | tf_op jit(solution)/shard_map/all_to_all | solution.py:141
  478.5 70.2 %reduce-scatter.23.cloned.1.call-start = ((), (), s32[]{:S(2)}) async-start(), calls=%async_computation.27 | async-start | bytes 884736 | tf_op jit(solution)/shard_map/reduce_scatter | solution.py:192
  480.5 3.5 collective-permute-start.2
  548.8 15.2 %all-to-all-start.8 = ((bf16[8,17,768]{2,1,0:T(8,128)(2,1)}), bf16[8,17,768]{2,1,0:T(8,128)(2,1)}, u32[]{:S(2)}, u32[]{:S(2)}) async-start(bf16[8,17,768]{2,1,0:T(8,128)(2,1)} %reduce-scatter.23.cloned.1.call-done), calls=%async_computation.12 | async-start | bytes 589824 | tf_op jit(solution)/shard_map/all_to_all | solution.py:195
  554.3 92.0 %reduce-scatter.27.cloned.1.call-start = ((), (), s32[]{:S(2)}) async-start(), calls=%async_computation.29 | async-start | bytes 884736 | tf_op jit(solution)/shard_map/reduce_scatter | solution.py:192
  593.7 3.2 collective-permute-start.3
  635.6 26.8 %copy-start.42 = (f32[64,768]{1,0:T(8,128)S(1)}, f32[64,768]{1,0:T(8,128)}, u32[]{:S(2)}) copy-start(f32[64,768]{1,0:T(8,128)} %get-tuple-element.93) | copy-start | bytes 589828
  635.6 26.8 %copy-start.114 = (f32[64,4]{0,1:T(4,128)S(1)}, f32[64,4]{0,1:T(4,128)}, u32[]{:S(2)}) copy-start(f32[64,4]{0,1:T(4,128)} %get-tuple-element.105) | copy-start | bytes 3076
  646.3 15.1 %all-to-all-start.11 = ((bf16[8,17,768]{2,1,0:T(8,128)(2,1)}), bf16[8,17,768]{2,1,0:T(8,128)(2,1)S(1)}, u32[]{:S(2)}, u32[]{:S(2)}) async-start(bf16[8,17,768]{2,1,0:T(8,128)(2,1)} %reduce-scatter.27.cloned.1.call-done), calls=%async_computation.17 | async-start | bytes 589824 | tf_op jit(solution)/shard_map/all_to_all | solution.py:195
  651.8 66.0 %reduce-scatter.33.cloned.1.call-start = ((), (), s32[]{:S(2)}) async-start(), calls=%async_computation.32 | async-start | bytes 442368
  653.6 135.8 %reduce-scatter.29.cloned.1.call-start = ((), (), s32[]{:S(2)}) async-start(), calls=%async_computation.30 | async-start | bytes 2654208 | tf_op jit(solution)/shard_map/reduce_scatter | solution.py:351
  668.6 252.5 %reduce-scatter.31.cloned.1.call-start = ((), (), s32[]{:S(2)}) async-start(), calls=%async_computation.31 | async-start | bytes 7962624
  698.7 286.4 %reduce-scatter.35.cloned.1.call-start = ((), (), s32[]{:S(2)}) async-start(), calls=%async_computation.33 | async-start | bytes 442368
  751.2 269.5 %all-reduce.6.cloned.1.call-start = ((), (), s32[]{:S(2)}) async-start(), calls=%async_computation.34 | async-start | bytes 1474560 | tf_op jit(solution)/shard_map/psum | solution.py:357
  925.1 98.5 %copy-start.1 = (bf16[1,1,768,768]{3,2,1,0:T(8,128)(2,1)S(1)}, bf16[1,1,768,768]{3,2,1,0:T(8,128)(2,1)}, u32[]{:S(2)}) copy-start(bf16[1,1,768,768]{3,2,1,0:T(8,128)(2,1)} %param.24) | copy-start | bytes 3538948
  (146 other events, 684.4 us)
Sparse Core Ops, SparseCore 0:
  10.2 73.9 all-gather.2
  86.4 39.5 all-gather.4
  155.6 20.2 reduce-scatter.16
  268.9 20.2 reduce-scatter.18
  346.1 14.1 reduce-scatter.20
  453.3 19.6 reduce-scatter.24
  535.5 13.2 reduce-scatter.22
  632.6 13.6 reduce-scatter.26
  655.9 61.8 reduce-scatter.32
  721.1 68.2 reduce-scatter.28
  793.1 127.9 reduce-scatter.30
  924.6 60.4 reduce-scatter.34
  988.2 32.4 all-reduce.5
where the time goes:
time: 1040 us; the launch traced here: 1030 us
  waiting for transfers between devices  448 us (43%)
  blocking collectives  227 us (22%)
  local copies, waits for them, and re-layouts  127 us (12%)
  matrix products  120 us (12%)
  other arithmetic  46.1 us (4%)
  starting transfers between devices  44.1 us (4%)
  between operations  17.8 us (2%)
    unnamed x16, waiting for transfers between devices  202 us
    reduce_scatter x3, waiting for transfers between devices, layer_forward(): lax.psum_scatter(partial_out, 'rep', scatter_dimension=0, tiled=True)  60.6 us
    unnamed x2, blocking collectives  42.8 us
    all_to_all x3, blocking collectives, layer_forward(): lax.all_to_all(outgoing, 'shard', split_axis=0, concat_axis=0, tiled=True)  40.2 us
    all_gather x1, blocking collectives, local(): lax.all_gather(router, 'shard', axis=1, tiled=True)  39 us
    reduce_scatter x1, waiting for transfers between devices, local(): lax.psum_scatter(grad_out_weight, 'shard', scatter_dimension=0, tiled=True)  38.2 us
    unnamed x354, local copies, waits for them, and re-layouts  38 us
    all_gather x1, waiting for transfers between devices, local(): lax.all_gather(out_proj, 'shard', axis=1, tiled=True)  37.8 us
  transfers between devices with their start and end apart: 24, of which 20 were waited for; matrix products, arithmetic and copies ran while one was open for 13% of the time, Pallas kernels for 0%

commit v1 on v0

v1 whole, which is shorter than its diff:
```python
import functools
import math

import jax
import jax.numpy as jnp
import numpy as np
from jax import lax
from jax.experimental import pallas as pl
from jax.experimental.pallas import tpu as pltpu
from jax.sharding import Mesh, PartitionSpec as P

HEADS = 12
HEAD = 64
BUCKETS = 32
SPAN = 128
PAIRS = HEADS // 2
EPSILON = 1e-06
NEGATIVE = -1e30
SCALE = 1.0 / math.sqrt(HEAD)
LANES = 128
PLANE = ("rep", "half")
BF = jnp.bfloat16
F32 = jnp.float32
VM = pl.BlockSpec(memory_space=pltpu.VMEM)
SM = pl.BlockSpec(memory_space=pltpu.SMEM)
ANY = pl.BlockSpec(memory_space=pl.ANY)


def up(n, m):
    return -(-n // m) * m


def bucket_onehot(length):
    half_count = BUCKETS // 2
    exact_count = half_count // 2
    rows = np.zeros((length * length, BUCKETS), np.float32)
    for q in range(length):
        for k in range(length):
            offset = k - q
            base = half_count if offset > 0 else 0
            distance = abs(offset)
            if distance < exact_count:
                bucket = distance
            else:
                bucket = exact_count + int(
                    math.log(distance / exact_count)
                    / math.log(SPAN / exact_count)
                    * (half_count - exact_count)
                )
                bucket = min(bucket, half_count - 1)
            rows[q * length + k, base + bucket] = 1.0
    return rows


def mm(a, b):
    return jnp.dot(a, b, preferred_element_type=F32)


def mm_nt(a, b):
    return lax.dot_general(a, b, (((1,), (1,)), ((), ())), preferred_element_type=F32)


def mm_tn(a, b):
    return lax.dot_general(a, b, (((0,), (0,)), ((), ())), preferred_element_type=F32)


def inv_rms(v):
    return lax.rsqrt(jnp.mean(v * v, axis=-1, keepdims=True) + EPSILON)


def rms_back(v, gain, grad):
    r = inv_rms(v)
    scaled = grad * gain
    dv = r * scaled - v * (r * r * r) * jnp.mean(v * scaled, axis=-1, keepdims=True)
    return dv, jnp.sum(grad * v * r, axis=0, keepdims=True)


def tanh_parts(v):
    c = math.sqrt(2.0 / math.pi)
    return c, jnp.tanh(c * (v + 0.044715 * (v * v * v)))


def gelu(v):
    _, t = tanh_parts(v)
    return 0.5 * v * (1.0 + t)


def gelu_slope(v):
    c, t = tanh_parts(v)
    return 0.5 * (1.0 + t) + 0.5 * v * (1.0 - t * t) * (c * (1.0 + 3.0 * 0.044715 * (v * v)))


def stack_heads(pair, rows):
    lane = lax.broadcasted_iota(jnp.int32, (rows, LANES), 1)
    zero = jnp.zeros_like(pair)
    return jnp.concatenate(
        [jnp.where(lane < HEAD, pair, zero), jnp.where(lane < HEAD, zero, pair)], axis=0
    )


def pick_heads(stacked, rows):
    lane = lax.broadcasted_iota(jnp.int32, (rows, LANES), 1)
    return jnp.where(lane < HEAD, stacked[:rows], stacked[rows:])


def member_of(rc, rows):
    lane = lax.broadcasted_iota(jnp.int32, (rows, LANES), 1)
    return (lane == rc).astype(F32)


def put_rows(target_row, block, cap_pad, values, rows):
    slot = lax.broadcasted_iota(jnp.int32, (cap_pad, rows), 0) + block * cap_pad
    return mm((slot == target_row).astype(BF), values)


def take_rows(target_col, blocks, cap_pad, rows):
    total = None
    for i, block in enumerate(blocks):
        slot = lax.broadcasted_iota(jnp.int32, (rows, cap_pad), 1) + i * cap_pad
        part = mm((slot == target_col).astype(BF), block)
        total = part if total is None else total + part
    return total


class Weights:
    def __init__(self, refs, experts, slab, layer):
        self.refs, self.experts, self.slab, self.layer = refs, experts, slab, layer
        self.big = len(refs) == 1

    @staticmethod
    def scratch(count, experts, width):
        return [
            pltpu.VMEM((4, width, width), BF),
            pltpu.SemaphoreType.DMA((1 if count == 1 else count * experts,)),
        ]

    def copies(self, meta, scr, sem):
        if self.big:
            return [pltpu.make_async_copy(self.refs[0], scr, sem.at[0])]
        s, x, z, y = meta[0], meta[1], meta[2], meta[3]
        made = []
        for c in range(2):
            for m in range(4):
                for i in range(self.experts):
                    matrix = 2 * (x ^ (m >> 1)) + (s ^ c ^ self.layer)
                    source_z = lax.rem(z - i + self.experts, self.experts)
                    row = (source_z * 2 + (y ^ (m & 1))) * self.slab
                    made.append(
                        pltpu.make_async_copy(
                            self.refs[c * 4 + m].at[i],
                            scr.at[matrix, pl.ds(pl.multiple_of(row, self.slab), self.slab)],
                            sem.at[len(made)],
                        )
                    )
        return made


def forward_kernel(layer, experts, slab, cap_pad, n_ret, n_w, *refs):
    it = iter(refs)
    meta = next(it)
    if layer == 0:
        x_ref = next(it)
    else:
        mid0, probs0, rc0, tc0, g_ref = (next(it) for _ in range(5))
        ret = [next(it) for _ in range(n_ret)]
    gains, router, bm, rc, tr = (next(it) for _ in range(5))
    w = Weights([next(it) for _ in range(n_w)], experts, slab, layer)
    h1_ref, qkv_ref, p_ref, ctx_ref, mid_ref, h2_ref, probs_ref = (next(it) for _ in range(7))
    if layer == 1:
        x1_ref, y0_ref = next(it), next(it)
    rest = list(it)
    scr, sem = rest[-2:]
    disp = rest[:-2]
    copies = w.copies(meta, scr, sem)
    for copy in copies:
        copy.start()
    rows, width = h1_ref.shape
    if layer == 0:
        x = x_ref[...].astype(F32)
    else:
        blocks = [ret[i][...] for i in range(n_ret)] if n_ret > 1 else [
            ret[0][i] for i in range(experts)
        ]
        y0 = take_rows(tc0[...], blocks, cap_pad, rows)
        y0_ref[...] = y0
        gate0 = jnp.sum(probs0[...] * member_of(rc0[...], rows), axis=-1, keepdims=True)
        x1 = (mid0[...] + gate0 * y0).astype(BF)
        x1_ref[...] = x1
        x = x1.astype(F32)
    h1 = (x * inv_rms(x) * gains[0:1]).astype(BF)
    h1_ref[...] = h1
    for copy in copies:
        copy.wait()
    q = mm(h1, scr[0]).astype(BF)
    k = mm(h1, scr[1]).astype(BF)
    v = mm(h1, scr[2]).astype(BF)
    qkv_ref[0] = q
    qkv_ref[1] = k
    qkv_ref[2] = v
    contexts = []
    for pair in range(PAIRS):
        cols = slice(pair * LANES, (pair + 1) * LANES)
        sc = mm_nt(stack_heads(q[:, cols], rows), k[:, cols]) * SCALE + bm[pair]
        e = jnp.exp(sc - jnp.max(sc, axis=-1, keepdims=True))
        p = e / jnp.sum(e, axis=-1, keepdims=True)
        p_ref[pair] = p
        contexts.append(pick_heads(mm(p.astype(BF), v[:, cols]), rows))
    ctx = jnp.concatenate(contexts, axis=1).astype(BF)
    ctx_ref[...] = ctx
    mid = x + mm(ctx, scr[3])
    mid_ref[...] = mid
    h2 = (mid * inv_rms(mid) * gains[1:2]).astype(BF)
    h2_ref[...] = h2
    logits = mm(h2, router[...])
    lane = lax.broadcasted_iota(jnp.int32, (rows, LANES), 1)
    logits = jnp.where(lane < experts, logits, NEGATIVE)
    e = jnp.exp(logits - jnp.max(logits, axis=-1, keepdims=True))
    probs = e / jnp.sum(e, axis=-1, keepdims=True)
    probs_ref[...] = probs
    sent = [h2]
    if layer == 1:
        gate = jnp.sum(probs * member_of(rc[...], rows), axis=-1, keepdims=True)
        sent.append((gate * g_ref[...].astype(F32)).astype(BF))
    for i in range(experts):
        for part, values in enumerate(sent):
            block = put_rows(tr[...], i, cap_pad, values, rows).astype(BF)
            ref = disp[i] if len(disp) > 1 else disp[0].at[i]
            if layer == 1:
                ref[part] = block
            else:
                ref[...] = block


def backward_kernel(layer, experts, slab, cap_pad, n_ret, n_w, *refs):
    it = iter(refs)
    meta, g_ref, x_ref, h1_ref, qkv_ref, p_ref, ctx_ref, mid_ref, h2_ref, probs_ref = (
        next(it) for _ in range(10)
    )
    gains, router, rc, tc = (next(it) for _ in range(4))
    if layer == 0:
        y_ref = next(it)
    else:
        probs0, rc0, tr0 = (next(it) for _ in range(3))
    ret = [next(it) for _ in range(n_ret)]
    w = Weights([next(it) for _ in range(n_w)], experts, slab, layer)
    dx_ref, ds_ref, ex_ref = (next(it) for _ in range(3))
    factors = [next(it) for _ in range(4)]
    if layer == 1:
        out_ref = next(it)
    rest = list(it)
    scr, sem, right, left = rest[-4:]
    disp = rest[:-4]
    copies = w.copies(meta, scr, sem)
    for copy in copies:
        copy.start()
    rows, width = h1_ref.shape
    g = g_ref[...].astype(F32)
    mid = mid_ref[...]
    probs = probs_ref[...]
    member = member_of(rc[...], rows)
    gate = jnp.sum(probs * member, axis=-1, keepdims=True)

    def blocks(part):
        if layer == 0:
            return [r[...] for r in ret] if n_ret > 1 else [ret[0][i] for i in range(experts)]
        return [r[part] for r in ret] if n_ret > 1 else [ret[0][i, part] for i in range(experts)]

    if layer == 0:
        y = y_ref[...]
        dh2 = take_rows(tc[...], blocks(0), cap_pad, rows)
    else:
        y = take_rows(tc[...], blocks(0), cap_pad, rows)
        dh2 = take_rows(tc[...], blocks(1), cap_pad, rows)
        out_ref[...] = mid + gate * y
    dgate = jnp.sum(g * y, axis=-1, keepdims=True)
    dlogits = probs * (dgate * (member - gate))
    high = dlogits.astype(BF)
    low = (dlogits - high.astype(F32)).astype(BF)
    dh2 = dh2 + mm_nt(high, router[...]) + mm_nt(low, router[...])
    dmid, dgain1 = rms_back(mid, gains[1:2], dh2)
    dmid = dmid + g
    h2 = h2_ref[...]
    drouter = mm_tn(high, h2) + mm_tn(low, h2)
    da = dmid.astype(BF)
    right[3] = da
    for copy in copies:
        copy.wait()
    dctx = mm_nt(da, scr[3]).astype(BF)
    grads = ([], [], [])
    for pair in range(PAIRS):
        cols = slice(pair * LANES, (pair + 1) * LANES)
        p = p_ref[pair]
        qs = stack_heads(qkv_ref[0, :, cols], rows)
        ds_heads = stack_heads(dctx[:, cols], rows)
        dp = mm_nt(ds_heads, qkv_ref[2, :, cols])
        ds = (p * (dp - jnp.sum(p * dp, axis=-1, keepdims=True))).astype(BF)
        ds_ref[pair] = ds
        grads[0].append(pick_heads(mm(ds, qkv_ref[1, :, cols]) * SCALE, rows))
        grads[1].append(mm_tn(ds, qs) * SCALE)
        grads[2].append(mm_tn(p.astype(BF), ds_heads))
    dh1 = None
    for j in range(3):
        dj = jnp.concatenate(grads[j], axis=1).astype(BF)
        right[j] = dj
        part = mm_nt(dj, scr[j])
        dh1 = part if dh1 is None else dh1 + part
    dx, dgain0 = rms_back(x_ref[...].astype(F32), gains[0:1], dh1)
    dx = dx + dmid
    dx_ref[...] = dx
    ex_ref[...] = jnp.zeros_like(ex_ref)
    ex_ref[0:experts] = drouter[0:experts]
    ex_ref[experts:experts + 1] = dgain0
    ex_ref[experts + 1:experts + 2] = dgain1
    if layer == 1:
        gate0 = jnp.sum(probs0[...] * member_of(rc0[...], rows), axis=-1, keepdims=True)
        dy0 = (gate0 * dx.astype(BF).astype(F32)).astype(BF)
        for i in range(experts):
            block = put_rows(tr0[...], i, cap_pad, dy0, rows).astype(BF)
            ref = disp[i] if len(disp) > 1 else disp[0].at[i]
            ref[...] = block
    left[0] = h1_ref[...]
    left[1] = ctx_ref[...]
    place = meta[4]
    for m in range(4):
        target = place ^ m
        factors[m][0:rows] = left[jnp.where(target == 3, 1, 0)]
        factors[m][rows:] = right[target]


def pack_kernel(n, cap, parts, *refs):
    out = refs[-1]
    blocks = refs[:-1]
    packed = out.shape[-2]
    cap_pad = blocks[0].shape[-2]
    for part in range(parts):
        total = None
        for i in range(n):
            block = blocks[i][part] if len(blocks) > 1 else blocks[0][i, part]
            row = lax.broadcasted_iota(jnp.int32, (packed, cap_pad), 0)
            slot = lax.broadcasted_iota(jnp.int32, (packed, cap_pad), 1)
            pick = ((row == slot + i * cap) & (slot < cap)).astype(BF)
            moved = mm(pick, block)
            total = moved if total is None else total + moved
        out[part] = total.astype(BF)


def unpack_kernel(n, cap, parts, *refs):
    sums, outs = refs[:4], refs[4:]
    packed = sums[0].shape[-2]
    cap_pad = outs[0].shape[-2]
    for part in range(parts):
        total = (
            sums[0][part].astype(F32)
            + sums[1][part].astype(F32)
            + sums[2][part].astype(F32)
            + sums[3][part].astype(F32)
        ).astype(BF)
        for i in range(n):
            row = lax.broadcasted_iota(jnp.int32, (cap_pad, packed), 1)
            slot = lax.broadcasted_iota(jnp.int32, (cap_pad, packed), 0)
            pick = ((row == slot + i * cap) & (slot < cap)).astype(BF)
            block = mm(pick, total).astype(BF)
            if len(outs) > 1:
                outs[i][part] = block
            else:
                outs[0][i, part] = block


def expert_weights(layer, meta, own, other, scr, sem):
    for which in range(2):
        @pl.when(meta[0] == layer)
        def _():
            pltpu.make_async_copy(own[which], scr.at[which], sem.at[which]).start()

        @pl.when(meta[0] != layer)
        def _():
            pltpu.make_async_copy(other[which], scr.at[which], sem.at[which]).start()

    def wait(which):
        pltpu.make_async_copy(own[which], scr.at[which], sem.at[which]).wait()

    return wait


def expert_forward_kernel(layer, both, *refs):
    meta, c0, c1, c2, c3, in_own, in_other, out_own, out_other = refs[:9]
    outs = refs[9:13]
    rest = list(refs[13:])
    scr, sem = rest[-2:]
    saved = rest[:-2]
    wait = expert_weights(layer, meta, (in_own, out_own), (in_other, out_other), scr, sem)
    packed = c0.shape[-2]
    rows = jnp.concatenate([c[0] for c in (c0, c1, c2, c3)], axis=0)
    wait(0)
    pre = mm(rows, scr[0])
    act = gelu(pre).astype(BF)
    saved[0][...] = rows
    saved[1][...] = act
    wait(1)
    y = mm(act, scr[1])
    for m in range(4):
        outs[m][0] = y[m * packed:(m + 1) * packed].astype(BF)
    if both:
        grad_rows = jnp.concatenate([c[1] for c in (c0, c1, c2, c3)], axis=0)
        dpre = (mm_nt(grad_rows, scr[1]) * gelu_slope(pre)).astype(BF)
        saved[2][...] = grad_rows
        saved[3][...] = dpre
        dh = mm_nt(dpre, scr[0])
        for m in range(4):
            outs[m][1] = dh[m * packed:(m + 1) * packed].astype(BF)
    else:
        saved[2][...] = pre


def expert_backward_kernel(layer, *refs):
    meta, c0, c1, c2, c3, in_own, in_other, out_own, out_other, pre_ref = refs[:10]
    outs = refs[10:14]
    rows_ref, dpre_ref, scr, sem = refs[14:]
    wait = expert_weights(layer, meta, (in_own, out_own), (in_other, out_other), scr, sem)
    packed = c0.shape[-2]
    grad_rows = jnp.concatenate([c[0] for c in (c0, c1, c2, c3)], axis=0)
    rows_ref[...] = grad_rows
    slope = gelu_slope(pre_ref[...])
    wait(1)
    dpre = (mm_nt(grad_rows, scr[1]) * slope).astype(BF)
    dpre_ref[...] = dpre
    wait(0)
    dh = mm_nt(dpre, scr[0])
    for m in range(4):
        outs[m][0] = dh[m * packed:(m + 1) * packed].astype(BF)


def expert_grads_kernel(rows, dpre, act, grad_rows, gin, gout):
    gin[...] = mm_tn(rows[...], dpre[...])
    gout[...] = mm_tn(act[...], grad_rows[...])


def factor_kernel(experts, slab, rows, meta, f0, f1, f2, f3, ex, tab, keep, send):
    factors = (f0, f1, f2, f3)
    left = jnp.concatenate([f[0:rows] for f in factors], axis=0)
    right = jnp.concatenate([f[rows:] for f in factors], axis=0)
    grad = mm_tn(left, right).astype(BF)
    s, z = meta[0], meta[2]
    extra = jnp.where(
        lax.broadcasted_iota(jnp.int32, ex.shape, 0) == experts + 2, tab[...], ex[...]
    )
    pad = jnp.zeros((16, grad.shape[1] - LANES), F32)
    for shard in range(2 * experts):
        at = lax.rem(shard // 2 - z + experts, experts)
        wide = jnp.concatenate(
            [extra[:, shard * slab:(shard + 1) * slab], jnp.zeros((16, LANES - slab), F32)], axis=1
        )
        block = jnp.concatenate([wide, pad], axis=1).astype(BF)

        @pl.when(s == shard % 2)
        def _():
            keep[at, 0:slab] = grad[shard * slab:(shard + 1) * slab]
            keep[at, slab:] = block

        @pl.when(s != shard % 2)
        def _():
            send[at, 0:slab] = grad[shard * slab:(shard + 1) * slab]
            send[at, slab:] = block


def call(kernel, out_shapes, args, specs, scratch=(), flops=0, moved=0, name=None):
    return pl.pallas_call(
        kernel,
        out_shape=[jax.ShapeDtypeStruct(shape, dtype) for shape, dtype in out_shapes],
        in_specs=specs,
        out_specs=[VM] * len(out_shapes),
        scratch_shapes=list(scratch),
        compiler_params=pltpu.CompilerParams(vmem_limit_bytes=40 * 2**20),
        cost_estimate=pl.CostEstimate(flops=flops, bytes_accessed=moved, transcendentals=0),
        name=name,
    )(*args)


def shift(v, axis, by):
    n = lax.axis_size(axis)
    return lax.ppermute(v, axis, [(i, (i + by) % n) for i in range(n)])


def swap_section(v):
    return lax.ppermute(v, "section", [(0, 1), (1, 0)])


def plane_swap(v, mask):
    return lax.ppermute(v, PLANE, [(i, i ^ mask) for i in range(4)])


def plane_gather(v):
    return [v] + [plane_swap(v, m) for m in (1, 2, 3)]


def local(
    experts,
    boundary,
    seq_lengths,
    routes,
    qkv_proj,
    out_proj,
    router,
    gains,
    rel_table,
    expert_in,
    expert_out,
):
    big = experts > 8
    s = lax.axis_index("section")
    x_at = lax.axis_index("rep")
    z_at = lax.axis_index("expert")
    y_at = lax.axis_index("half")
    shards = 2 * experts
    rows, width = boundary.shape[2:]
    slab = qkv_proj.shape[2]
    table_slab = rel_table.shape[1]
    cap = max(2, rows // experts + 1)
    cap_pad = up(cap, 8)
    packed = up(experts * cap, 16)
    ff = expert_in.shape[3]
    first = s == 0
    meta = jnp.stack([s, x_at, z_at, y_at, 2 * x_at + y_at]).astype(jnp.int32)

    own = boundary[0]
    got = swap_section(own[1 - s])
    x0 = jnp.where(first, own[0], got)
    g1 = jnp.where(first, got, own[1])
    lengths = seq_lengths[s, 0]
    own_routes = routes[0, :, :, 0]
    got_routes = swap_section(own_routes[1 - s])
    route_list = [
        jnp.where(first, own_routes[0], got_routes),
        jnp.where(first, got_routes, own_routes[1]),
    ]

    if big:
        slabs = jnp.concatenate([qkv_proj[0], out_proj], axis=0)
        whole = lax.all_gather(slabs, ("expert", "half"), axis=1, tiled=True)
        layers = lax.all_gather(whole, "section", axis=0)
        attn_w = [[layers[0]], [layers[1]]]
    else:
        def matrix(j0, j1):
            a = out_proj[0] if j0 == 3 else qkv_proj[0, j0]
            b = out_proj[0] if j1 == 3 else qkv_proj[0, j1]
            return jnp.where(x_at == 0, a, b)

        mine, other = matrix(0, 2), swap_section(matrix(1, 3))
        attn_w = []
        for layer in range(2):
            piece = jnp.where(s == layer, mine, other)
            if layer == 1:
                piece, _ = lax.optimization_barrier((piece, attn_w[0][0]))
            gathered = jnp.stack([piece] + [shift(piece, "expert", i) for i in range(1, experts)])
            in_plane = plane_gather(gathered)
            attn_w.append(in_plane + [swap_section(v) for v in in_plane])
    other_in = swap_section(expert_in[0, 0])
    other_out = swap_section(expert_out[0, 0])
    expert_w = [expert_in[0, 0], other_in, expert_out[0, 0], other_out]

    small_rows = up(experts + 3, 8)
    table_row = jnp.zeros((1, slab), BF).at[0, :table_slab].set(rel_table[0])
    small = jnp.concatenate(
        [
            router[0].T,
            gains[0],
            table_row,
            jnp.zeros((small_rows - experts - 3, slab), BF),
        ]
    )
    if big:
        small_all = lax.all_gather(
            lax.all_gather(small, ("expert", "half"), axis=0), "section", axis=0
        )
    else:
        along = jnp.stack([small] + [shift(small, "expert", i) for i in range(1, experts)])
        along = jnp.stack([along, shift(along, "half", 1)])
        along = jnp.stack([along, swap_section(along)])
        at = jnp.arange(2 * shards, dtype=jnp.int32)
        layer_i, z_i, y_i = at // shards, (at % shards) // 2, at % 2
        source = ((layer_i ^ s) * 2 + (y_i ^ y_at)) * experts + (z_at - z_i + experts) % experts
        pick = (source[:, None] == at[None, :]).astype(BF)
        small_all = jnp.dot(
            pick, along.reshape(2 * shards, -1), preferred_element_type=F32
        ).astype(BF).reshape(2, shards, small_rows, slab)
    spread = jnp.asarray(bucket_onehot(rows), dtype=BF)
    ends = jnp.cumsum(lengths).astype(jnp.int32)
    position = jnp.arange(rows, dtype=jnp.int32)
    segment = jnp.sum((position[:, None] >= ends[None, :]).astype(jnp.int32), axis=1)
    same_seq = segment[:, None] == segment[None, :]
    params = []
    for layer in range(2):
        flat = small_all[layer].transpose(1, 0, 2)
        router_w = jnp.pad(
            flat[:experts].reshape(experts, width).T, ((0, 0), (0, LANES - experts))
        )
        gain_rows = flat[experts:experts + 2].reshape(2, width).astype(F32)
        table = flat[experts + 2, :, :table_slab].reshape(BUCKETS, HEADS)
        bias = jnp.dot(table.T, spread.T, preferred_element_type=F32).reshape(HEADS, rows, rows)
        bias = jnp.where(same_seq[None], bias, NEGATIVE).reshape(PAIRS, 2 * rows, rows)
        member = (
            route_list[layer][:, None] == jnp.arange(experts, dtype=jnp.int32)[None, :]
        ).astype(jnp.int32)
        slot = jnp.sum((jnp.cumsum(member, axis=0) - 1) * member, axis=1).astype(jnp.int32)
        block_at = route_list[layer] if big else (route_list[layer] - z_at + experts) % experts
        target = block_at * cap_pad + slot
        params.append(
            dict(
                gains=gain_rows,
                router=router_w,
                bias=bias,
                rc=route_list[layer][:, None],
                tr=target[None, :],
                tc=target[:, None],
            )
        )

    n_w = len(attn_w[0])
    n_ret = 1 if big else experts

    def message_shapes(parts):
        if big:
            return [((experts,) + parts + (cap_pad, width), BF)]
        return [(parts + (cap_pad, width), BF)] * experts

    def dispatch(blocks, parts):
        if big:
            arrived = lax.all_to_all(blocks[0], "expert", 0, 0, tiled=True)
            arrived = [arrived if parts == 2 else arrived[:, None]]
        else:
            arrived = [blocks[0]] + [shift(blocks[i], "expert", i) for i in range(1, experts)]
            arrived = arrived if parts == 2 else [a[None] for a in arrived]
        (joined,) = call(
            functools.partial(pack_kernel, experts, cap, parts),
            [((parts, packed, width), BF)],
            arrived,
            [VM] * len(arrived),
            moved=4 * packed * width,
            name="pack",
        )
        return plane_gather(joined)

    def come_back(partial, parts):
        sums = [partial[0]] + [plane_swap(partial[m], m) for m in (1, 2, 3)]
        shapes = (
            [((experts, parts, cap_pad, width), BF)]
            if big
            else [((parts, cap_pad, width), BF)] * experts
        )
        blocks = call(
            functools.partial(unpack_kernel, experts, cap, parts),
            shapes,
            sums,
            [VM] * 4,
            moved=4 * packed * width,
            name="unpack",
        )
        if big:
            back = lax.all_to_all(blocks[0], "expert", 0, 0, tiled=True)
            return [back if parts == 2 else back[:, 0]]
        back = [blocks[0]] + [shift(blocks[i], "expert", -i) for i in range(1, experts)]
        return back if parts == 2 else [b[0] for b in back]

    def forward(layer, extra):
        prm = params[layer]
        args = [meta] + extra + [prm["gains"], prm["router"], prm["bias"], prm["rc"], prm["tr"]]
        specs = [SM] + [VM] * (len(args) - 1) + [ANY] * n_w
        shapes = [
            ((rows, width), BF),
            ((3, rows, width), BF),
            ((PAIRS, 2 * rows, rows), F32),
            ((rows, width), BF),
            ((rows, width), F32),
            ((rows, width), BF),
            ((rows, LANES), F32),
        ]
        if layer == 1:
            shapes += [((rows, width), BF), ((rows, width), F32)]
        fixed = len(shapes)
        shapes += message_shapes((2,) if layer == 1 else ())
        outs = call(
            functools.partial(forward_kernel, layer, experts, slab, cap_pad, n_ret, n_w),
            shapes,
            args + attn_w[layer],
            specs,
            Weights.scratch(n_w, experts, width),
            flops=8 * rows * width * width,
            moved=8 * width * width,
            name="attention_forward",
        )
        names = ["h1", "qkv", "p", "ctx", "mid", "h2", "probs", "x1", "y0"][:fixed]
        return dict(zip(names, outs[:fixed])), outs[fixed:]

    def backward(layer, kept, x_in, g, returned, extra):
        prm = params[layer]
        args = [meta, g, x_in] + [
            kept[n] for n in ("h1", "qkv", "p", "ctx", "mid", "h2", "probs")
        ]
        args += [prm["gains"], prm["router"], prm["rc"], prm["tc"]] + extra + returned
        specs = [SM] + [VM] * (len(args) - 1) + [ANY] * n_w
        shapes = [
            ((rows, width), F32),
            ((PAIRS, 2 * rows, rows), BF),
            ((up(experts + 3, 16), width), F32),
        ] + [((2 * rows, width), BF)] * 4
        if layer == 1:
            shapes += [((rows, width), F32)] + message_shapes(())
        return call(
            functools.partial(backward_kernel, layer, experts, slab, cap_pad, n_ret, n_w),
            shapes,
            args + attn_w[layer],
            specs,
            Weights.scratch(n_w, experts, width)
            + [pltpu.VMEM((4, rows, width), BF), pltpu.VMEM((2, rows, width), BF)],
            flops=16 * rows * width * width,
            moved=8 * width * width,
            name="attention_backward",
        )

    expert_scratch = [pltpu.VMEM((2, width, ff), BF), pltpu.SemaphoreType.DMA((2,))]
    expert_specs = [SM] + [VM] * 4 + [ANY] * 4
    all_rows = 4 * packed

    def expert_forward(layer, joined, both):
        parts = 2 if both else 1
        shapes = [((parts, packed, width), BF)] * 4
        shapes += [((all_rows, width), BF), ((all_rows, ff), BF)]
        shapes += (
            [((all_rows, width), BF), ((all_rows, ff), BF)] if both else [((all_rows, ff), F32)]
        )
        outs = call(
            functools.partial(expert_forward_kernel, layer, both),
            shapes,
            [meta] + joined + expert_w,
            expert_specs,
            expert_scratch,
            flops=4 * all_rows * width * ff * parts,
            moved=4 * width * ff,
            name="expert_forward",
        )
        return outs[:4], outs[4:]

    def expert_grads(rows_in, dpre, act, grad_rows):
        return call(
            expert_grads_kernel,
            [((width, ff), F32), ((ff, width), F32)],
            [rows_in, dpre, act, grad_rows],
            [VM] * 4,
            flops=4 * all_rows * width * ff,
            moved=8 * width * ff,
            name="expert_grads",
        )

    def attention_grads(factors, ex, ds):
        table = jnp.dot(
            ds.reshape(HEADS, rows * rows), spread, preferred_element_type=F32
        ).T.reshape(shards, table_slab)
        tab = jnp.pad(table, ((0, 0), (0, slab - table_slab))).reshape(1, width)
        got = [factors[0]] + [plane_swap(factors[m], m) for m in (1, 2, 3)]
        keep, send = call(
            functools.partial(factor_kernel, experts, slab, rows),
            [((experts, slab + 16, width), BF)] * 2,
            [meta] + got + [ex, tab],
            [SM] + [VM] * 6,
            flops=8 * rows * width * width,
            moved=8 * width * width,
            name="attention_grads",
        )
        both = keep.astype(F32) + swap_section(send).astype(F32)
        parts = [both[i].astype(BF) for i in range(experts)]
        total = both[0]
        for i in range(1, experts):
            total = total + shift(parts[i], "expert", i).astype(F32)
        return total.astype(BF)

    kept0, blocks = forward(0, [x0])
    joined = dispatch(blocks, 1)
    partial, (rows0, act0, pre0) = expert_forward(0, joined, False)
    returned = come_back(partial, 1)

    kept1, blocks = forward(
        1, [kept0["mid"], kept0["probs"], params[0]["rc"], params[0]["tc"], g1] + returned
    )
    joined = dispatch(blocks, 2)
    partial, (rows1, act1, grows1, dpre1) = expert_forward(1, joined, True)
    gin1, gout1 = expert_grads(rows1, dpre1, act1, grows1)
    returned = come_back(partial, 2)

    outs = backward(
        1,
        kept1,
        kept1["x1"],
        g1,
        returned,
        [kept0["probs"], params[0]["rc"], params[0]["tr"]],
    )
    dx1, ds1, ex1 = outs[:3]
    factors1, out1, blocks = outs[3:7], outs[7], outs[8:]

    joined = dispatch(blocks, 1)
    shapes = [((1, packed, width), BF)] * 4 + [((all_rows, width), BF), ((all_rows, ff), BF)]
    outs = call(
        functools.partial(expert_backward_kernel, 0),
        shapes,
        [meta] + joined + expert_w + [pre0],
        expert_specs + [VM],
        expert_scratch,
        flops=4 * all_rows * width * ff,
        moved=4 * width * ff,
        name="expert_backward",
    )
    partial, (grows0, dpre0) = outs[:4], outs[4:]
    gin0, gout0 = expert_grads(rows0, dpre0, act0, grows0)
    returned = come_back(partial, 1)
    outs = backward(0, kept0, x0, dx1.astype(BF), returned, [kept1["y0"]])
    dx0, ds0, ex0 = outs[:3]
    factors0 = outs[3:7]

    traded = swap_section(jnp.where(first, out1, dx0))
    result_rows = jnp.stack([jnp.where(first, dx0, traded), jnp.where(first, traded, out1)])

    final_experts = []
    for g0, g1_ in ((gin0, gin1), (gout0, gout1)):
        recv = swap_section(jnp.where(first, g1_, g0).astype(BF))
        final_experts.append(jnp.where(first, g0, g1_) + recv.astype(F32))

    if big:
        own_factors = []
        for layer, (kept, ds, ex, fac) in enumerate(
            ((kept0, ds0, ex0, factors0), (kept1, ds1, ex1, factors1))
        ):
            place = 2 * x_at + y_at
            right = jnp.stack([fac[m][rows:] for m in range(4)])
            pieces = [
                jnp.sum(
                    jnp.where(
                        (jnp.arange(4) ^ place == j)[:, None, None], right, jnp.zeros_like(right)
                    ),
                    axis=0,
                )
                for j in range(4)
            ]
            lefts = [kept["h1"]] * 3 + [kept["ctx"]]
            grad = jnp.stack(
                [
                    lax.dot_general(
                        a, b, (((0,), (0,)), ((), ())), preferred_element_type=F32
                    )
                    for a, b in zip(lefts, pieces)
                ]
            )
            table = jnp.dot(
                ds.reshape(HEADS, rows * rows), spread, preferred_element_type=F32
            ).T.reshape(shards, table_slab)
            tab = jnp.pad(table, ((0, 0), (0, slab - table_slab))).reshape(1, width)
            lines = jnp.concatenate([ex[:experts + 2], tab])
            own_factors.append((grad, lines))
        grad = jnp.stack([own_factors[0][0], own_factors[1][0]]).astype(BF)
        lines = jnp.stack([own_factors[0][1], own_factors[1][1]])
        grad = lax.psum_scatter(grad, "section", scatter_dimension=0)
        lines = lax.psum_scatter(lines, "section", scatter_dimension=0)
        grad = lax.psum_scatter(grad, ("expert", "half"), scatter_dimension=1, tiled=True)
        grad = lax.psum(grad, "rep").astype(F32)
        lines = lax.psum(lines, ("rep", "expert", "half"))
        shard_at = z_at * 2 + y_at
        extra = lax.dynamic_slice_in_dim(lines, shard_at * slab, slab, axis=1)
    else:
        blocks = [
            attention_grads(factors0, ex0, ds0),
            attention_grads(factors1, ex1, ds1),
        ]
        arrived = []
        trade = ("section", "rep", "half")
        for a in range(2):
            message = jnp.where((y_at ^ a) == 0, blocks[0], blocks[1])
            for b in range(2):
                pairs = []
                for i in range(8):
                    si, xi, yi = i // 4, (i // 2) % 2, i % 2
                    pairs.append((i, (yi ^ a) * 4 + (xi ^ b) * 2 + si))
                arrived.append(lax.ppermute(message, trade, pairs))
        place = 2 * x_at + s
        order = [jnp.zeros((), jnp.int32)] * 4
        stacked = jnp.stack([arrived[0], arrived[2], arrived[1], arrived[3]])
        main = stacked[:, :slab].astype(F32)
        swapped = jnp.where(s == 0, main, main[jnp.array([1, 0, 3, 2])])
        grad = jnp.where(x_at == 0, swapped, swapped[jnp.array([2, 3, 0, 1])])
        extra = jnp.sum(stacked[:, slab:, :slab].astype(F32), axis=0)
    return (
        result_rows[None],
        grad[None, :3],
        grad[3][None],
        extra[:experts].T[None],
        extra[experts:experts + 2][None],
        extra[experts + 2, :table_slab][None],
        final_experts[0][None, None],
        final_experts[1][None, None],
    )


def solution(mesh):
    sections, reps, shards = (mesh.shape[n] for n in ("section", "rep", "shard"))
    experts = shards // 2
    split = Mesh(
        mesh.devices.reshape(sections, reps, experts, 2), ("section", "rep", "expert", "half")
    )
    shard = ("expert", "half")
    in_specs = (
        P("section", None, ("rep",) + shard, None),
        P(None, ("rep",) + shard, None),
        P("section", None, ("rep",) + shard, None),
        P("section", None, shard, None),
        P("section", shard, None),
        P("section", shard, None),
        P("section", None, shard),
        P("section", shard),
        P("section", shard, None, "rep"),
        P("section", shard, "rep", None),
    )
    out_specs = (
        P("section", None, ("rep",) + shard, None),
        P("section", None, shard, None),
        P("section", shard, None),
        P("section", shard, None),
        P("section", None, shard),
        P("section", shard),
        P("section", shard, None, "rep"),
        P("section", shard, "rep", None),
    )
    return jax.shard_map(
        functools.partial(local, experts),
        mesh=split,
        in_specs=in_specs,
        out_specs=out_specs,
        check_vma=False,
    )
```

time: 1040 us -> 375 us (0.36)
  waiting for transfers between devices: 448 us -> 113 us
  blocking collectives: 227 us -> 0 us
  matrix products: 120 us -> 8.27 us
  Pallas kernels: 0 us -> 55.3 us
  local copies, waits for them, and re-layouts: 127 us -> 76.5 us
  starting transfers between devices: 44.1 us -> 86 us
  other arithmetic: 46.1 us -> 29.3 us
  between operations: 17.8 us -> 2.01 us
    unnamed x16 -> x0, waiting for transfers between devices: 202 us -> none
    reduce_scatter x7 -> x0, waiting for transfers between devices: 125 us -> none  [the longest x3 60.6 us: layer_forward(): lax.psum_scatter(partial_out, 'rep', scatter_dimension=0, tiled=True)]
    dot_general x74 -> x5, matrix products: 120 us -> 8.27 us  [the longest x2 4.19 us: local(): jnp.dot(table.T, spread.T, preferred_element_type=F32)]
    ppermute x4 -> x87, waiting for transfers between devices: 1.9 us -> 113 us  [the longest x34 59.4 us: shift(): return lax.ppermute(v, axis, [(i, (i + by) % n) for i in range(n)])]
    all_gather x8 -> x0, blocking collectives: 110 us -> none  [the longest x1 39 us: local(): lax.all_gather(router, 'shard', axis=1, tiled=True)]
    ppermute x4 -> x87, starting transfers between devices: 6.48 us -> 86 us  [the longest x34 45.5 us: shift(): return lax.ppermute(v, axis, [(i, (i + by) % n) for i in range(n)])]
    all_to_all x5 -> x0, blocking collectives: 69.2 us -> none  [the longest x3 40.2 us: layer_forward(): lax.all_to_all(outgoing, 'shard', split_axis=0, concat_axis=0, tiled=True)]
    pallas_call x0 -> x17, Pallas kernels: none -> 55.3 us  [call(): pl.pallas_call(kernel, out_shape=[jax.ShapeDtypeStruct(shape, dtype) for...]
  transfers between devices with their start and end apart: 24 -> 87, of which waited for: 20 -> 31; matrix products, arithmetic and copies ran while one was open for 13% -> 18% of each run, Pallas kernels for 0% -> 9%
where the time goes in v1:
time: 375 us; the launch traced here: 371 us
  waiting for transfers between devices  113 us (30%)
  starting transfers between devices  86 us (23%)
  local copies, waits for them, and re-layouts  76.5 us (20%)
  Pallas kernels  55.3 us (15%)
  other arithmetic  29.3 us (8%)
  matrix products  8.27 us (2%)
    ppermute x34, waiting for transfers between devices, shift(): return lax.ppermute(v, axis, [(i, (i + by) % n) for i in range(n)])  59.4 us
    pallas_call x17, Pallas kernels, call(): pl.pallas_call(kernel, out_shape=[jax.ShapeDtypeStruct(shape, dtype) for...  55.3 us
    ppermute x30, waiting for transfers between devices, plane_swap(): return lax.ppermute(v, PLANE, [(i, i ^ mask) for i in range(4)])  48.4 us
    ppermute x34, starting transfers between devices, shift(): return lax.ppermute(v, axis, [(i, (i + by) % n) for i in range(n)])  45.5 us
    unnamed x258, local copies, waits for them, and re-layouts  40.1 us
    ppermute x30, starting transfers between devices, plane_swap(): return lax.ppermute(v, PLANE, [(i, i ^ mask) for i in range(4)])  35.4 us
  transfers between devices with their start and end apart: 87, of which 31 were waited for; matrix products, arithmetic and copies ran while one was open for 18% of the time, Pallas kernels for 9%

profile of v1, /device:TPU:0, one launch (start us, length us, event | category | flops | bytes accessed | tf_op | source)
XLA Modules:
  0.0 370.7 jit_solution(10584565174804573540)
XLA Ops:
  3.4 5.0 %collective-permute-start.3 = (bf16[8,96]{1,0:T(8,128)(2,1)S(1)}, bf16[8,96]{1,0:T(8,128)(2,1)S(1)}, u32[]{:S(2)}, u32[]{:S(2)}) collective-permute-start(bf16[8,96]{1,0:T(8,128)(2,1)S(1)} %fusion.16), channel_id=1, source_target_pairs={{0,6},{2,0},{4,2},{6,4},{1,7},{3,1},{5,3},{7,5},{8,14},{10,8},{12,... | collective-permute-start | bytes 4616 | tf_op jit(solution)/shard_map/ppermute | solution.py:481
  15.7 2.9 collective-permute-start.10
  22.9 10.0 %collective-permute-done.9 = bf16[96,768]{1,0:T(8,128)(2,1)S(1)} collective-permute-done((bf16[96,768]{1,0:T(8,128)(2,1)S(1)}, bf16[96,768]{1,0:T(8,128)(2,1)S(1)}, u32[]{:S(2)}, u32[]{:S(2)}) %collective-permute-start.9) | collective-permute-done | bytes 147488 | tf_op jit(solution)/shard_map/ppermute | solution.py:481
  41.0 7.5 %collective-permute-done.33 = bf16[96,768]{1,0:T(8,128)(2,1)S(1)} collective-permute-done((bf16[96,768]{1,0:T(8,128)(2,1)S(1)}, bf16[96,768]{1,0:T(8,128)(2,1)S(1)}, u32[]{:S(2)}, u32[]{:S(2)}) %collective-permute-start.33) | collective-permute-done | bytes 147488 | tf_op jit(solution)/shard_map/ppermute | solution.py:481
  48.7 6.7 %collective-permute-done.32 = bf16[96,768]{1,0:T(8,128)(2,1)S(1)} collective-permute-done((bf16[96,768]{1,0:T(8,128)(2,1)S(1)}, bf16[96,768]{1,0:T(8,128)(2,1)S(1)}, u32[]{:S(2)}, u32[]{:S(2)}) %collective-permute-start.32) | collective-permute-done | bytes 147488 | tf_op jit(solution)/shard_map/ppermute | solution.py:481
  61.4 2.4 collective-permute-done.13.refs_10_.refs_22_
  64.3 2.1 convolution_select_fusion.1
  66.4 2.0 pad_maximum_fusion.2.refs_15_.refs_21_
  76.4 5.6 %attention_forward.2 = (bf16[64,768]{1,0:T(8,128)(2,1)S(1)}, bf16[3,64,768]{2,1,0:T(8,128)(2,1)S(1)}, f32[6,128,64]{2,1,0:T(8,128)S(1)}, bf16[64,768]{1,0:T(8,12...) custom-call(s32[5]{0:T(128)S(1)} %stack.110.refs_0_.meta, ...), custom_call_target="tpu_custom_call" | custom-call | flops 301989888 | bytes 4718592 | tf_op jit(solution)/shard_map/attention_forward/pallas_call | solution.py:467
  83.6 2.1 collective-permute-start.18
  86.9 2.5 collective-permute-done.18
  100.0 21.5 %collective-permute-done.22.refs_3_ = bf16[1,80,768]{2,1,0:T(8,128)(2,1)S(1)} collective-permute-done((bf16[1,80,768]{2,1,0:T(8,128)(2,1)S(1)}, bf16[1,80,768]{2,1,0:T(8,128)(2,1)S(1)}, u32[]{:S(2)}, u32[]{:S(2)}) %collective-permute-start.22) | collective-permute-done | bytes 122912 | tf_op jit(solution)/shard_map/ppermute | solution.py:489
  122.8 3.2 expert_forward.2
  144.6 2.1 convolution_select_fusion
  146.7 2.6 collective-permute-done.28.refs_3_
  150.2 1.8 unpack.3
  162.5 6.3 %attention_forward.3 = (bf16[64,768]{1,0:T(8,128)(2,1)S(1)}, bf16[3,64,768]{2,1,0:T(8,128)(2,1)S(1)}, f32[6,128,64]{2,1,0:T(8,128)S(1)}, bf16[64,768]{1,0:T(8,12...) custom-call(s32[5]{0:T(128)S(1)} %stack.110.refs_0_.meta, ...), custom_call_target="tpu_custom_call" | custom-call | flops 301989888 | bytes 4718592 | tf_op jit(solution)/shard_map/attention_forward/pallas_call | solution.py:467
  170.9 2.0 collective-permute-start.42
  174.4 1.8 collective-permute-start.44
  177.2 1.9 collective-permute-done.43.refs_2_
  183.0 4.7 %collective-permute-done.45.refs_2_ = bf16[2,80,768]{2,1,0:T(8,128)(2,1)S(1)} collective-permute-done((bf16[2,80,768]{2,1,0:T(8,128)(2,1)S(1)}, bf16[2,80,768]{2,1,0:T(8,128)(2,1)S(1)}, u32[]{:S(2)}, u32[]{:S(2)}) %collective-permute-start.45) | collective-permute-done | bytes 245792 | tf_op jit(solution)/shard_map/ppermute | solution.py:489
  187.8 2.6 collective-permute-done.47.refs_4_
  190.4 4.5 %expert_forward.3 = (bf16[2,80,768]{2,1,0:T(8,128)(2,1)S(1)}, bf16[2,80,768]{2,1,0:T(8,128)(2,1)}, bf16[2,80,768]{2,1,0:T(8,128)(2,1)}, bf16[2,80,768]{2,1,0:T(8...) custom-call(s32[5]{0:T(128)S(1)} %stack.110.refs_0_.meta, ...), custom_call_target="tpu_custom_call" | custom-call | flops 1509949440 | bytes 2359296 | tf_op jit(solution)/shard_map/expert_forward/pallas_call | solution.py:467
  200.1 2.2 collective-permute-start.50
  206.0 3.4 collective-permute-done.50.refs_3_
  210.3 2.2 unpack.4
  213.1 3.7 collective-permute-start.51
  220.0 2.5 collective-permute-done.52.refs_19_
  237.2 8.8 %attention_backward.2 = (f32[64,768]{1,0:T(8,128)S(1)}, bf16[6,128,64]{2,1,0:T(8,128)(2,1)S(1)}, f32[16,768]{1,0:T(8,128)S(1)}, bf16[128,768]{1,0:T(8,128)(2,1)S...) custom-call(s32[5]{0:T(128)S(1)} %stack.110.refs_0_.meta, ...), custom_call_target="tpu_custom_call" | custom-call | flops 603979776 | bytes 4718592 | tf_op jit(solution)/shard_map/attention_backward/pallas_call | solution.py:467
  247.2 2.7 collective-permute-start.56
  263.5 2.3 fusion.40
  270.9 4.5 %expert_backward.1 = (bf16[1,80,768]{2,1,0:T(8,128)(2,1)S(1)}, bf16[1,80,768]{2,1,0:T(8,128)(2,1)S(1)}, bf16[1,80,768]{2,1,0:T(8,128)(2,1)S(1)}, bf16[1,80,768]{...) custom-call(s32[5]{0:T(128)S(1)} %stack.110.refs_0_.meta, ...), custom_call_target="tpu_custom_call" | custom-call | flops 754974720 | bytes 2359296 | tf_op jit(solution)/shard_map/expert_backward/pallas_call | solution.py:467
  277.1 1.9 collective-permute-start.62
  285.8 1.9 collective-permute-start.65
  289.3 3.0 attention_grads.3
  292.5 7.9 %attention_backward.3 = (f32[64,768]{1,0:T(8,128)S(1)}, bf16[6,128,64]{2,1,0:T(8,128)(2,1)S(1)}, f32[16,768]{1,0:T(8,128)S(1)}, bf16[128,768]{1,0:T(8,128)(2,1)S...) custom-call(s32[5]{0:T(128)S(1)} %stack.110.refs_0_.meta, ...), custom_call_target="tpu_custom_call" | custom-call | flops 603979776 | bytes 4718592 | tf_op jit(solution)/shard_map/attention_backward/pallas_call | solution.py:467
  304.1 1.9 collective-permute-start.68
  307.0 1.8 reshape.235
  312.2 3.8 %collective-permute-done.69.f3 = bf16[128,768]{1,0:T(8,128)(2,1)} collective-permute-done((bf16[128,768]{1,0:T(8,128)(2,1)}, bf16[128,768]{1,0:T(8,128)(2,1)}, u32[]{:S(2)}, u32[]{:S(2)}) %collective-permute-start.69) | collective-permute-done | bytes 196640 | tf_op jit(solution)/shard_map/ppermute | solution.py:489
  317.0 2.2 attention_grads.2
  322.4 1.9 collective-permute-start.80
  326.3 3.8 %collective-permute-done.80 = bf16[112,768]{1,0:T(8,128)(2,1)S(1)} collective-permute-done((bf16[112,768]{1,0:T(8,128)(2,1)S(1)}, bf16[112,768]{1,0:T(8,128)(2,1)S(1)}, u32[]{:S(2)}, u32[]{:S(2)}) %collective-permute-start.80) | collective-permute-done | bytes 172064 | tf_op jit(solution)/shard_map/ppermute | solution.py:481
  330.1 3.3 collective-permute-start.73
  333.4 7.0 %collective-permute-done.79 = bf16[112,768]{1,0:T(8,128)(2,1)S(1)} collective-permute-done((bf16[112,768]{1,0:T(8,128)(2,1)S(1)}, bf16[112,768]{1,0:T(8,128)(2,1)S(1)}, u32[]{:S(2)}, u32[]{:S(2)}) %collective-permute-start.79) | collective-permute-done | bytes 172064 | tf_op jit(solution)/shard_map/ppermute | solution.py:481
  341.3 1.8 add_bitcast_fusion.1
  343.1 11.8 %collective-permute-done.72 = bf16[112,768]{1,0:T(8,128)(2,1)S(1)} collective-permute-done((bf16[112,768]{1,0:T(8,128)(2,1)S(1)}, bf16[112,768]{1,0:T(8,128)(2,1)S(1)}, u32[]{:S(2)}, u32[]{:S(2)}) %collective-permute-start.72) | collective-permute-done | bytes 172064 | tf_op jit(solution)/shard_map/ppermute | solution.py:481
  357.4 1.8 add_bitcast_fusion
  359.2 4.2 %collective-permute-done.84 = bf16[112,768]{1,0:T(8,128)(2,1)S(1)} collective-permute-done((bf16[112,768]{1,0:T(8,128)(2,1)S(1)}, bf16[112,768]{1,0:T(8,128)(2,1)S(1)}, u32[]{:S(2)}, u32[]{:S(2)}) %collective-permute-start.84) | collective-permute-done | bytes 172064 | tf_op jit(solution)/shard_map/ppermute | solution.py:881
  (498 shorter events, 172.6 us)
Async XLA Ops:
  3.4 16.2 %collective-permute-start.3 = (bf16[8,96]{1,0:T(8,128)(2,1)S(1)}, bf16[8,96]{1,0:T(8,128)(2,1)S(1)}, u32[]{:S(2)}, u32[]{:S(2)}) collective-permute-start(bf16[8,96]{1,0:T(8,128)(2,1)S(1)} %fusion.16), channel_id=1, source_target_pairs={{0,6},{2,0},{4,2},{6,4},{1,7},{3,1},{5,3},{7,5},{8,14},{10,8},{12,... | collective-permute-start | bytes 4616 | tf_op jit(solution)/shard_map/ppermute | solution.py:481
  8.5 11.4 %collective-permute-start.2 = (bf16[8,96]{1,0:T(8,128)(2,1)S(1)}, bf16[8,96]{1,0:T(8,128)(2,1)S(1)}, u32[]{:S(2)}, u32[]{:S(2)}) collective-permute-start(bf16[8,96]{1,0:T(8,128)(2,1)S(1)} %fusion.16), channel_id=1, source_target_pairs={{0,4},{2,6},{4,0},{6,2},{1,5},{3,7},{5,1},{7,3},{8,12},{10,14},{12... | collective-permute-start | bytes 4616 | tf_op jit(solution)/shard_map/ppermute | solution.py:481
  8.5 11.5 %collective-permute-start.1 = (bf16[8,96]{1,0:T(8,128)(2,1)S(1)}, bf16[8,96]{1,0:T(8,128)(2,1)S(1)}, u32[]{:S(2)}, u32[]{:S(2)}) collective-permute-start(bf16[8,96]{1,0:T(8,128)(2,1)S(1)} %fusion.16), channel_id=1, source_target_pairs={{0,2},{2,4},{4,6},{6,0},{1,3},{3,5},{5,7},{7,1},{8,10},{10,12},{12... | collective-permute-start | bytes 4616 | tf_op jit(solution)/shard_map/ppermute | solution.py:481
  18.5 14.4 %collective-permute-start.9 = (bf16[96,768]{1,0:T(8,128)(2,1)S(1)}, bf16[96,768]{1,0:T(8,128)(2,1)S(1)}, u32[]{:S(2)}, u32[]{:S(2)}) collective-permute-start(bf16[96,768]{1,0:T(8,128)(2,1)S(1)} %get-tuple-element.204), channel_id=1, source_target_pairs={{0,4},{2,6},{4,0},{6,2},{1,5},{3,7},{5,1},{7,3},{8,12},{10,14},{12... | collective-permute-start | bytes 442376 | tf_op jit(solution)/shard_map/ppermute | solution.py:481
  19.7 13.2 %collective-permute-start.8 = (bf16[96,768]{1,0:T(8,128)(2,1)S(1)}, bf16[96,768]{1,0:T(8,128)(2,1)S(1)}, u32[]{:S(2)}, u32[]{:S(2)}) collective-permute-start(bf16[96,768]{1,0:T(8,128)(2,1)S(1)} %get-tuple-element.204), channel_id=1, source_target_pairs={{0,2},{2,4},{4,6},{6,0},{1,3},{3,5},{5,7},{7,1},{8,10},{10,12},{12... | collective-permute-start | bytes 442376 | tf_op jit(solution)/shard_map/ppermute | solution.py:481
  19.9 18.2 %collective-permute-start = (bf16[64,768]{1,0:T(8,128)(2,1)S(1)}, bf16[64,768]{1,0:T(8,128)(2,1)S(1)}, u32[]{:S(2)}, u32[]{:S(2)}) collective-permute-start(bf16[64,768]{1,0:T(8,128)(2,1)S(1)} %dynamic-slice_bitcast_fusion), channel_id=1, source_target_pairs={{0,16},{16,0},{1,17},{17,1},{2,18},{18,2},{3,19},{19,3},{4,20},{20... | collective-permute-start | bytes 294920 | tf_op jit(solution)/shard_map/ppermute | solution.py:485
  20.0 13.8 %collective-permute-start.4 = (bf16[4,8,96]{2,1,0:T(8,128)(2,1)S(1)}, bf16[4,8,96]{2,1,0:T(8,128)(2,1)S(1)}, u32[]{:S(2)}, u32[]{:S(2)}) collective-permute-start(bf16[4,8,96]{2,1,0:T(8,128)(2,1)S(1)} %get-tuple-element.214), channel_id=1, source_target_pairs={{0,1},{1,0},{2,3},{3,2},{4,5},{5,4},{6,7},{7,6},{8,9},{9,8},{10,11... | collective-permute-start | bytes 18440 | tf_op jit(solution)/shard_map/ppermute | solution.py:481
  33.9 22.2 %collective-permute-start.11 = (bf16[4,96,768]{2,1,0:T(8,128)(2,1)}, bf16[4,96,768]{2,1,0:T(8,128)(2,1)}, u32[]{:S(2)}, u32[]{:S(2)}) collective-permute-start(bf16[4,96,768]{2,1,0:T(8,128)(2,1)} %pad_maximum_fusion.1.refs_7_.refs_19_), channel_id=1, source_target_pairs={{0,1},{1,0},{8,9},{9,8},{2,3},{3,2},{10,11},{11,10},{4,5},{5,4},{1... | collective-permute-start | bytes 1769480 | tf_op jit(solution)/shard_map/ppermute | solution.py:489
  35.5 21.1 %collective-permute-start.12 = (bf16[4,96,768]{2,1,0:T(8,128)(2,1)}, bf16[4,96,768]{2,1,0:T(8,128)(2,1)}, u32[]{:S(2)}, u32[]{:S(2)}) collective-permute-start(bf16[4,96,768]{2,1,0:T(8,128)(2,1)} %pad_maximum_fusion.1.refs_7_.refs_19_), channel_id=1, source_target_pairs={{0,8},{1,9},{8,0},{9,1},{2,10},{3,11},{10,2},{11,3},{4,12},{5,13},... | collective-permute-start | bytes 1769480 | tf_op jit(solution)/shard_map/ppermute | solution.py:489
  37.7 26.1 %collective-permute-start.13 = (bf16[4,96,768]{2,1,0:T(8,128)(2,1)}, bf16[4,96,768]{2,1,0:T(8,128)(2,1)}, u32[]{:S(2)}, u32[]{:S(2)}) collective-permute-start(bf16[4,96,768]{2,1,0:T(8,128)(2,1)} %pad_maximum_fusion.1.refs_7_.refs_19_), channel_id=1, source_target_pairs={{0,9},{1,8},{8,1},{9,0},{2,11},{3,10},{10,3},{11,2},{4,13},{5,12},... | collective-permute-start | bytes 1769480 | tf_op jit(solution)/shard_map/ppermute | solution.py:489
  38.1 25.6 %collective-permute-start.14 = (bf16[4,96,768]{2,1,0:T(8,128)(2,1)}, bf16[4,96,768]{2,1,0:T(8,128)(2,1)}, u32[]{:S(2)}, u32[]{:S(2)}) collective-permute-start(bf16[4,96,768]{2,1,0:T(8,128)(2,1)} %pad_maximum_fusion.1.refs_7_.refs_19_), channel_id=1, source_target_pairs={{0,16},{16,0},{1,17},{17,1},{2,18},{18,2},{3,19},{19,3},{4,20},{20... | collective-permute-start | bytes 1769480 | tf_op jit(solution)/shard_map/ppermute | solution.py:485
  38.9 9.5 %collective-permute-start.33 = (bf16[96,768]{1,0:T(8,128)(2,1)S(1)}, bf16[96,768]{1,0:T(8,128)(2,1)S(1)}, u32[]{:S(2)}, u32[]{:S(2)}) collective-permute-start(bf16[96,768]{1,0:T(8,128)(2,1)S(1)} %get-tuple-element.119), channel_id=1, source_target_pairs={{0,4},{2,6},{4,0},{6,2},{1,5},{3,7},{5,1},{7,3},{8,12},{10,14},{12... | collective-permute-start | bytes 442376 | tf_op jit(solution)/shard_map/ppermute | solution.py:481
  56.1 40.6 %collective-permute-start.24 = (bf16[768,768]{1,0:T(8,128)(2,1)S(1)}, bf16[768,768]{1,0:T(8,128)(2,1)S(1)}, u32[]{:S(2)}, u32[]{:S(2)}) collective-permute-start(bf16[768,768]{1,0:T(8,128)(2,1)S(1)} %bitcast.163), channel_id=1, source_target_pairs={{0,16},{16,0},{1,17},{17,1},{2,18},{18,2},{3,19},{19,3},{4,20},{20... | collective-permute-start | bytes 3538952 | tf_op jit(solution)/shard_map/ppermute | solution.py:485
  56.1 41.1 %collective-permute-start.25 = (bf16[768,768]{1,0:T(8,128)(2,1)S(1)}, bf16[768,768]{1,0:T(8,128)(2,1)}, u32[]{:S(2)}, u32[]{:S(2)}) collective-permute-start(bf16[768,768]{1,0:T(8,128)(2,1)S(1)} %bitcast.167), channel_id=1, source_target_pairs={{0,16},{16,0},{1,17},{17,1},{2,18},{18,2},{3,19},{19,3},{4,20},{20... | collective-permute-start | bytes 3538952 | tf_op jit(solution)/shard_map/ppermute | solution.py:485
  56.6 11.8 %collective-permute-start.15 = (bf16[4,96,768]{2,1,0:T(8,128)(2,1)}, bf16[4,96,768]{2,1,0:T(8,128)(2,1)}, u32[]{:S(2)}, u32[]{:S(2)}) collective-permute-start(bf16[4,96,768]{2,1,0:T(8,128)(2,1)} %collective-permute-done.11.refs_8_.refs_20_), channel_id=1, source_target_pairs={{0,16},{16,0},{1,17},{17,1},{2,18},{18,2},{3,19},{19,3},{4,20},{20... | collective-permute-start | bytes 1769480 | tf_op jit(solution)/shard_map/ppermute | solution.py:485
  63.8 12.6 %collective-permute-start.16 = (bf16[4,96,768]{2,1,0:T(8,128)(2,1)}, bf16[4,96,768]{2,1,0:T(8,128)(2,1)}, u32[]{:S(2)}, u32[]{:S(2)}) collective-permute-start(bf16[4,96,768]{2,1,0:T(8,128)(2,1)} %collective-permute-done.12.refs_9_.refs_21_), channel_id=1, source_target_pairs={{0,16},{16,0},{1,17},{17,1},{2,18},{18,2},{3,19},{19,3},{4,20},{20... | collective-permute-start | bytes 1769480 | tf_op jit(solution)/shard_map/ppermute | solution.py:485
  63.8 12.6 %collective-permute-start.17 = (bf16[4,96,768]{2,1,0:T(8,128)(2,1)}, bf16[4,96,768]{2,1,0:T(8,128)(2,1)}, u32[]{:S(2)}, u32[]{:S(2)}) collective-permute-start(bf16[4,96,768]{2,1,0:T(8,128)(2,1)} %collective-permute-done.13.refs_10_.refs_22_), channel_id=1, source_target_pairs={{0,16},{16,0},{1,17},{17,1},{2,18},{18,2},{3,19},{19,3},{4,20},{20... | collective-permute-start | bytes 1769480 | tf_op jit(solution)/shard_map/ppermute | solution.py:485
  68.4 26.7 %collective-permute-start.35 = (bf16[4,96,768]{2,1,0:T(8,128)(2,1)}, bf16[4,96,768]{2,1,0:T(8,128)(2,1)}, u32[]{:S(2)}, u32[]{:S(2)}) collective-permute-start(bf16[4,96,768]{2,1,0:T(8,128)(2,1)} %pad_maximum_fusion.2.refs_15_.refs_21_), channel_id=1, source_target_pairs={{0,1},{1,0},{8,9},{9,8},{2,3},{3,2},{10,11},{11,10},{4,5},{5,4},{1... | collective-permute-start | bytes 1769480 | tf_op jit(solution)/shard_map/ppermute | solution.py:489
  90.8 44.5 %collective-permute-start.36 = (bf16[4,96,768]{2,1,0:T(8,128)(2,1)}, bf16[4,96,768]{2,1,0:T(8,128)(2,1)}, u32[]{:S(2)}, u32[]{:S(2)}) collective-permute-start(bf16[4,96,768]{2,1,0:T(8,128)(2,1)} %pad_maximum_fusion.2.refs_15_.refs_21_), channel_id=1, source_target_pairs={{0,8},{1,9},{8,0},{9,1},{2,10},{3,11},{10,2},{11,3},{4,12},{5,13},... | collective-permute-start | bytes 1769480 | tf_op jit(solution)/shard_map/ppermute | solution.py:489
  93.3 42.0 %collective-permute-start.37 = (bf16[4,96,768]{2,1,0:T(8,128)(2,1)}, bf16[4,96,768]{2,1,0:T(8,128)(2,1)}, u32[]{:S(2)}, u32[]{:S(2)}) collective-permute-start(bf16[4,96,768]{2,1,0:T(8,128)(2,1)} %pad_maximum_fusion.2.refs_15_.refs_21_), channel_id=1, source_target_pairs={{0,9},{1,8},{8,1},{9,0},{2,11},{3,10},{10,3},{11,2},{4,13},{5,12},... | collective-permute-start | bytes 1769480 | tf_op jit(solution)/shard_map/ppermute | solution.py:489
  96.7 24.9 %collective-permute-start.22 = (bf16[1,80,768]{2,1,0:T(8,128)(2,1)S(1)}, bf16[1,80,768]{2,1,0:T(8,128)(2,1)S(1)}, u32[]{:S(2)}, u32[]{:S(2)}) collective-permute-start(bf16[1,80,768]{2,1,0:T(8,128)(2,1)S(1)} %pack.3.refs_1_), channel_id=1, source_target_pairs={{0,8},{1,9},{8,0},{9,1},{2,10},{3,11},{10,2},{11,3},{4,12},{5,13},... | collective-permute-start | bytes 368648 | tf_op jit(solution)/shard_map/ppermute | solution.py:489
  97.2 25.6 %collective-permute-start.23 = (bf16[1,80,768]{2,1,0:T(8,128)(2,1)S(1)}, bf16[1,80,768]{2,1,0:T(8,128)(2,1)S(1)}, u32[]{:S(2)}, u32[]{:S(2)}) collective-permute-start(bf16[1,80,768]{2,1,0:T(8,128)(2,1)S(1)} %pack.3.refs_1_), channel_id=1, source_target_pairs={{0,9},{1,8},{8,1},{9,0},{2,11},{3,10},{10,3},{11,2},{4,13},{5,12},... | collective-permute-start | bytes 368648 | tf_op jit(solution)/shard_map/ppermute | solution.py:489
  100.0 53.7 %collective-permute-start.38 = (bf16[4,96,768]{2,1,0:T(8,128)(2,1)}, bf16[4,96,768]{2,1,0:T(8,128)(2,1)}, u32[]{:S(2)}, u32[]{:S(2)}) collective-permute-start(bf16[4,96,768]{2,1,0:T(8,128)(2,1)} %pad_maximum_fusion.2.refs_15_.refs_21_), channel_id=1, source_target_pairs={{0,16},{16,0},{1,17},{17,1},{2,18},{18,2},{3,19},{19,3},{4,20},{20... | collective-permute-start | bytes 1769480 | tf_op jit(solution)/shard_map/ppermute | solution.py:485
  121.5 32.8 %collective-permute-start.39 = (bf16[4,96,768]{2,1,0:T(8,128)(2,1)}, bf16[4,96,768]{2,1,0:T(8,128)(2,1)}, u32[]{:S(2)}, u32[]{:S(2)}) collective-permute-start(bf16[4,96,768]{2,1,0:T(8,128)(2,1)} %collective-permute-done.35.refs_16_.refs_22_), channel_id=1, source_target_pairs={{0,16},{16,0},{1,17},{17,1},{2,18},{18,2},{3,19},{19,3},{4,20},{20... | collective-permute-start | bytes 1769480 | tf_op jit(solution)/shard_map/ppermute | solution.py:485
  135.3 26.4 %collective-permute-start.40 = (bf16[4,96,768]{2,1,0:T(8,128)(2,1)}, bf16[4,96,768]{2,1,0:T(8,128)(2,1)}, u32[]{:S(2)}, u32[]{:S(2)}) collective-permute-start(bf16[4,96,768]{2,1,0:T(8,128)(2,1)} %collective-permute-done.36.refs_17_.refs_23_), channel_id=1, source_target_pairs={{0,16},{16,0},{1,17},{17,1},{2,18},{18,2},{3,19},{19,3},{4,20},{20... | collective-permute-start | bytes 1769480 | tf_op jit(solution)/shard_map/ppermute | solution.py:485
  135.3 26.4 %collective-permute-start.41 = (bf16[4,96,768]{2,1,0:T(8,128)(2,1)}, bf16[4,96,768]{2,1,0:T(8,128)(2,1)}, u32[]{:S(2)}, u32[]{:S(2)}) collective-permute-start(bf16[4,96,768]{2,1,0:T(8,128)(2,1)} %collective-permute-done.37.refs_18_.refs_24_), channel_id=1, source_target_pairs={{0,16},{16,0},{1,17},{17,1},{2,18},{18,2},{3,19},{19,3},{4,20},{20... | collective-permute-start | bytes 1769480 | tf_op jit(solution)/shard_map/ppermute | solution.py:485
  152.6 9.1 %collective-permute-start.29 = (bf16[1,24,768]{2,1,0:T(8,128)(2,1)}, bf16[1,24,768]{2,1,0:T(8,128)(2,1)}, u32[]{:S(2)}, u32[]{:S(2)}) collective-permute-start(bf16[1,24,768]{2,1,0:T(8,128)(2,1)} %get-tuple-element.116), channel_id=1, source_target_pairs={{0,6},{2,0},{4,2},{6,4},{1,7},{3,1},{5,3},{7,5},{8,14},{10,8},{12,... | collective-permute-start | bytes 110600 | tf_op jit(solution)/shard_map/ppermute | solution.py:481
  179.5 8.3 %collective-permute-start.45 = (bf16[2,80,768]{2,1,0:T(8,128)(2,1)S(1)}, bf16[2,80,768]{2,1,0:T(8,128)(2,1)S(1)}, u32[]{:S(2)}, u32[]{:S(2)}) collective-permute-start(bf16[2,80,768]{2,1,0:T(8,128)(2,1)S(1)} %pack.4.refs_1_), channel_id=1, source_target_pairs={{0,1},{1,0},{8,9},{9,8},{2,3},{3,2},{10,11},{11,10},{4,5},{5,4},{1... | collective-permute-start | bytes 737288 | tf_op jit(solution)/shard_map/ppermute | solution.py:489
  181.4 9.0 %collective-permute-start.47 = (bf16[2,80,768]{2,1,0:T(8,128)(2,1)S(1)}, bf16[2,80,768]{2,1,0:T(8,128)(2,1)S(1)}, u32[]{:S(2)}, u32[]{:S(2)}) collective-permute-start(bf16[2,80,768]{2,1,0:T(8,128)(2,1)S(1)} %pack.4.refs_1_), channel_id=1, source_target_pairs={{0,9},{1,8},{8,1},{9,0},{2,11},{3,10},{10,3},{11,2},{4,13},{5,12},... | collective-permute-start | bytes 737288 | tf_op jit(solution)/shard_map/ppermute | solution.py:489
  200.1 9.3 %collective-permute-start.50 = (bf16[2,80,768]{2,1,0:T(8,128)(2,1)}, bf16[2,80,768]{2,1,0:T(8,128)(2,1)}, u32[]{:S(2)}, u32[]{:S(2)}) collective-permute-start(bf16[2,80,768]{2,1,0:T(8,128)(2,1)} %get-tuple-element.135), channel_id=1, source_target_pairs={{0,9},{1,8},{8,1},{9,0},{2,11},{3,10},{10,3},{11,2},{4,13},{5,12},... | collective-permute-start | bytes 737288 | tf_op jit(solution)/shard_map/ppermute | solution.py:489
  246.0 11.5 %collective-permute-start.54 = (bf16[24,768]{1,0:T(8,128)(2,1)}, bf16[24,768]{1,0:T(8,128)(2,1)}, u32[]{:S(2)}, u32[]{:S(2)}) collective-permute-start(bf16[24,768]{1,0:T(8,128)(2,1)} %get-tuple-element.148), channel_id=1, source_target_pairs={{0,2},{2,4},{4,6},{6,0},{1,3},{3,5},{5,7},{7,1},{8,10},{10,12},{12... | collective-permute-start | bytes 110600 | tf_op jit(solution)/shard_map/ppermute | solution.py:481
  246.1 11.5 %collective-permute-start.55 = (bf16[24,768]{1,0:T(8,128)(2,1)}, bf16[24,768]{1,0:T(8,128)(2,1)}, u32[]{:S(2)}, u32[]{:S(2)}) collective-permute-start(bf16[24,768]{1,0:T(8,128)(2,1)} %get-tuple-element.149), channel_id=1, source_target_pairs={{0,4},{2,6},{4,0},{6,2},{1,5},{3,7},{5,1},{7,3},{8,12},{10,14},{12... | collective-permute-start | bytes 110600 | tf_op jit(solution)/shard_map/ppermute | solution.py:481
  247.2 10.3 %collective-permute-start.56 = (bf16[24,768]{1,0:T(8,128)(2,1)}, bf16[24,768]{1,0:T(8,128)(2,1)}, u32[]{:S(2)}, u32[]{:S(2)}) collective-permute-start(bf16[24,768]{1,0:T(8,128)(2,1)} %get-tuple-element.150), channel_id=1, source_target_pairs={{0,6},{2,0},{4,2},{6,4},{1,7},{3,1},{5,3},{7,5},{8,14},{10,8},{12,... | collective-permute-start | bytes 110600 | tf_op jit(solution)/shard_map/ppermute | solution.py:481
  254.9 30.9 %collective-permute-start.74 = (bf16[128,768]{1,0:T(8,128)(2,1)}, bf16[128,768]{1,0:T(8,128)(2,1)}, u32[]{:S(2)}, u32[]{:S(2)}) collective-permute-start(bf16[128,768]{1,0:T(8,128)(2,1)} %get-tuple-element.171), channel_id=1, source_target_pairs={{0,1},{1,0},{8,9},{9,8},{2,3},{3,2},{10,11},{11,10},{4,5},{5,4},{1... | collective-permute-start | bytes 589832 | tf_op jit(solution)/shard_map/ppermute | solution.py:489
  255.2 34.0 %collective-permute-start.75 = (bf16[128,768]{1,0:T(8,128)(2,1)}, bf16[128,768]{1,0:T(8,128)(2,1)}, u32[]{:S(2)}, u32[]{:S(2)}) collective-permute-start(bf16[128,768]{1,0:T(8,128)(2,1)} %get-tuple-element.172), channel_id=1, source_target_pairs={{0,8},{1,9},{8,0},{9,1},{2,10},{3,11},{10,2},{11,3},{4,12},{5,13},... | collective-permute-start | bytes 589832 | tf_op jit(solution)/shard_map/ppermute | solution.py:489
  283.4 8.9 %collective-permute-start.63 = (bf16[1,24,768]{2,1,0:T(8,128)(2,1)S(1)}, bf16[1,24,768]{2,1,0:T(8,128)(2,1)S(1)}, u32[]{:S(2)}, u32[]{:S(2)}) collective-permute-start(bf16[1,24,768]{2,1,0:T(8,128)(2,1)S(1)} %get-tuple-element.157), channel_id=1, source_target_pairs={{0,6},{2,0},{4,2},{6,4},{1,7},{3,1},{5,3},{7,5},{8,14},{10,8},{12,... | collective-permute-start | bytes 110600 | tf_op jit(solution)/shard_map/ppermute | solution.py:481
  292.3 28.7 %collective-permute-start.77 = (bf16[4,112,768]{2,1,0:T(8,128)(2,1)}, bf16[4,112,768]{2,1,0:T(8,128)(2,1)}, u32[]{:S(2)}, u32[]{:S(2)}) collective-permute-start(bf16[4,112,768]{2,1,0:T(8,128)(2,1)} %get-tuple-element.177), channel_id=1, source_target_pairs={{0,16},{16,0},{1,17},{17,1},{2,18},{18,2},{3,19},{19,3},{4,20},{20... | collective-permute-start | bytes 2064392 | tf_op jit(solution)/shard_map/ppermute | solution.py:485
  303.0 16.2 %collective-permute-start.66 = (f32[64,768]{1,0:T(8,128)}, f32[64,768]{1,0:T(8,128)}, u32[]{:S(2)}, u32[]{:S(2)}) collective-permute-start(f32[64,768]{1,0:T(8,128)} %broadcast_select_fusion.4), channel_id=1, source_target_pairs={{0,16},{16,0},{1,17},{17,1},{2,18},{18,2},{3,19},{19,3},{4,20},{20... | collective-permute-start | bytes 589832 | tf_op jit(solution)/shard_map/ppermute | solution.py:485
  306.0 10.0 %collective-permute-start.69 = (bf16[128,768]{1,0:T(8,128)(2,1)}, bf16[128,768]{1,0:T(8,128)(2,1)}, u32[]{:S(2)}, u32[]{:S(2)}) collective-permute-start(bf16[128,768]{1,0:T(8,128)(2,1)} %get-tuple-element.165), channel_id=1, source_target_pairs={{0,9},{1,8},{8,1},{9,0},{2,11},{3,10},{10,3},{11,2},{4,13},{5,12},... | collective-permute-start | bytes 589832 | tf_op jit(solution)/shard_map/ppermute | solution.py:489
  310.7 29.6 %collective-permute-start.85 = (bf16[768,768]{1,0:T(8,128)(2,1)}, bf16[768,768]{1,0:T(8,128)(2,1)S(1)}, u32[]{:S(2)}, u32[]{:S(2)}) collective-permute-start(bf16[768,768]{1,0:T(8,128)(2,1)} %select_convert_fusion.1), channel_id=1, source_target_pairs={{0,16},{16,0},{1,17},{17,1},{2,18},{18,2},{3,19},{19,3},{4,20},{20... | collective-permute-start | bytes 3538952 | tf_op jit(solution)/shard_map/ppermute | solution.py:485
  312.2 45.2 %collective-permute-start.86 = (bf16[768,768]{1,0:T(8,128)(2,1)}, bf16[768,768]{1,0:T(8,128)(2,1)S(1)}, u32[]{:S(2)}, u32[]{:S(2)}) collective-permute-start(bf16[768,768]{1,0:T(8,128)(2,1)} %select_convert_fusion), channel_id=1, source_target_pairs={{0,16},{16,0},{1,17},{17,1},{2,18},{18,2},{3,19},{19,3},{4,20},{20... | collective-permute-start | bytes 3538952 | tf_op jit(solution)/shard_map/ppermute | solution.py:485
  324.3 16.1 %collective-permute-start.79 = (bf16[112,768]{1,0:T(8,128)(2,1)S(1)}, bf16[112,768]{1,0:T(8,128)(2,1)S(1)}, u32[]{:S(2)}, u32[]{:S(2)}) collective-permute-start(bf16[112,768]{1,0:T(8,128)(2,1)S(1)} %get-tuple-element.202), channel_id=1, source_target_pairs={{0,4},{2,6},{4,0},{6,2},{1,5},{3,7},{5,1},{7,3},{8,12},{10,14},{12... | collective-permute-start | bytes 516104 | tf_op jit(solution)/shard_map/ppermute | solution.py:481
  324.3 18.8 %collective-permute-start.78 = (bf16[112,768]{1,0:T(8,128)(2,1)S(1)}, bf16[112,768]{1,0:T(8,128)(2,1)S(1)}, u32[]{:S(2)}, u32[]{:S(2)}) collective-permute-start(bf16[112,768]{1,0:T(8,128)(2,1)S(1)} %get-tuple-element.200), channel_id=1, source_target_pairs={{0,2},{2,4},{4,6},{6,0},{1,3},{3,5},{5,7},{7,1},{8,10},{10,12},{12... | collective-permute-start | bytes 516104 | tf_op jit(solution)/shard_map/ppermute | solution.py:481
  330.1 13.1 %collective-permute-start.73 = (bf16[112,768]{1,0:T(8,128)(2,1)S(1)}, bf16[112,768]{1,0:T(8,128)(2,1)S(1)}, u32[]{:S(2)}, u32[]{:S(2)}) collective-permute-start(bf16[112,768]{1,0:T(8,128)(2,1)S(1)} %get-tuple-element.198), channel_id=1, source_target_pairs={{0,6},{2,0},{4,2},{6,4},{1,7},{3,1},{5,3},{7,5},{8,14},{10,8},{12,... | collective-permute-start | bytes 516104 | tf_op jit(solution)/shard_map/ppermute | solution.py:481
  340.4 14.5 %collective-permute-start.72 = (bf16[112,768]{1,0:T(8,128)(2,1)S(1)}, bf16[112,768]{1,0:T(8,128)(2,1)S(1)}, u32[]{:S(2)}, u32[]{:S(2)}) collective-permute-start(bf16[112,768]{1,0:T(8,128)(2,1)S(1)} %get-tuple-element.199), channel_id=1, source_target_pairs={{0,4},{2,6},{4,0},{6,2},{1,5},{3,7},{5,1},{7,3},{8,12},{10,14},{12... | collective-permute-start | bytes 516104 | tf_op jit(solution)/shard_map/ppermute | solution.py:481
  340.4 14.5 %collective-permute-start.71 = (bf16[112,768]{1,0:T(8,128)(2,1)S(1)}, bf16[112,768]{1,0:T(8,128)(2,1)S(1)}, u32[]{:S(2)}, u32[]{:S(2)}) collective-permute-start(bf16[112,768]{1,0:T(8,128)(2,1)S(1)} %get-tuple-element.197), channel_id=1, source_target_pairs={{0,2},{2,4},{4,6},{6,0},{1,3},{3,5},{5,7},{7,1},{8,10},{10,12},{12... | collective-permute-start | bytes 516104 | tf_op jit(solution)/shard_map/ppermute | solution.py:481
  355.2 9.5 %collective-permute-start.82 = (bf16[112,768]{1,0:T(8,128)(2,1)S(1)}, bf16[112,768]{1,0:T(8,128)(2,1)S(1)}, u32[]{:S(2)}, u32[]{:S(2)}) collective-permute-start(bf16[112,768]{1,0:T(8,128)(2,1)S(1)} %broadcast_select_fusion.2), channel_id=1, source_target_pairs={{0,16},{1,0},{8,24},{9,8},{16,17},{17,1},{24,25},{25,9},{2,18},{3,... | collective-permute-start | bytes 516104 | tf_op jit(solution)/shard_map/ppermute | solution.py:881
  356.2 8.5 %collective-permute-start.83 = (bf16[112,768]{1,0:T(8,128)(2,1)S(1)}, bf16[112,768]{1,0:T(8,128)(2,1)S(1)}, u32[]{:S(2)}, u32[]{:S(2)}) collective-permute-start(bf16[112,768]{1,0:T(8,128)(2,1)S(1)} %get-tuple-element.190), channel_id=1, source_target_pairs={{0,8},{1,24},{8,0},{9,16},{16,9},{17,25},{24,1},{25,17},{2,10},{3,... | collective-permute-start | bytes 516104 | tf_op jit(solution)/shard_map/ppermute | solution.py:881
  (168 other events, 1228.5 us)

commit v2 on v1

v2 whole, which is shorter than its diff:
```python
import functools
import math

import jax
import jax.numpy as jnp
import numpy as np
from jax import lax
from jax.experimental import pallas as pl
from jax.experimental.pallas import tpu as pltpu
from jax.sharding import Mesh, PartitionSpec as P

HEADS = 12
HEAD = 64
BUCKETS = 32
SPAN = 128
PAIRS = HEADS // 2
EPSILON = 1e-06
NEGATIVE = -1e30
SCALE = 1.0 / math.sqrt(HEAD)
LANES = 128
PLANE = ("rep", "half")
BF = jnp.bfloat16
F32 = jnp.float32
VM = pl.BlockSpec(memory_space=pltpu.VMEM)
SM = pl.BlockSpec(memory_space=pltpu.SMEM)
ANY = pl.BlockSpec(memory_space=pl.ANY)


def up(n, m):
    return -(-n // m) * m


def bucket_of(offset):
    half_count = BUCKETS // 2
    exact_count = half_count // 2
    base = half_count if offset > 0 else 0
    distance = abs(offset)
    if distance < exact_count:
        return base + distance
    bucket = exact_count + int(
        math.log(distance / exact_count)
        / math.log(SPAN / exact_count)
        * (half_count - exact_count)
    )
    return base + min(bucket, half_count - 1)


def table_places(shards, slab, table_slab):
    head_of = np.zeros((16, shards * slab), np.float32)
    offset_of = np.zeros((LANES, shards * slab), np.float32)
    for lane in range(shards * slab):
        shard, place = divmod(lane, slab)
        if place >= table_slab:
            continue
        bucket, head = divmod(shard * table_slab + place, HEADS)
        head_of[head, lane] = 1.0
        for d in range(LANES):
            if bucket_of(d if d < HEAD else d - LANES) == bucket:
                offset_of[d, lane] = 1.0
    return jnp.asarray(head_of, BF), jnp.asarray(offset_of, BF)


def mm(a, b):
    return jnp.dot(a, b, preferred_element_type=F32)


def mm_nt(a, b):
    return lax.dot_general(a, b, (((1,), (1,)), ((), ())), preferred_element_type=F32)


def mm_tn(a, b):
    return lax.dot_general(a, b, (((0,), (0,)), ((), ())), preferred_element_type=F32)


def inv_rms(v):
    return lax.rsqrt(jnp.mean(v * v, axis=-1, keepdims=True) + EPSILON)


def rms_back(v, gain, grad):
    r = inv_rms(v)
    scaled = grad * gain
    dv = r * scaled - v * (r * r * r) * jnp.mean(v * scaled, axis=-1, keepdims=True)
    return dv, jnp.sum(grad * v * r, axis=0, keepdims=True)


def tanh_parts(v):
    c = math.sqrt(2.0 / math.pi)
    return c, jnp.tanh(c * (v + 0.044715 * (v * v * v)))


def gelu(v):
    _, t = tanh_parts(v)
    return 0.5 * v * (1.0 + t)


def gelu_slope(v):
    c, t = tanh_parts(v)
    return 0.5 * (1.0 + t) + 0.5 * v * (1.0 - t * t) * (c * (1.0 + 3.0 * 0.044715 * (v * v)))


def stack_heads(pair, rows):
    lane = lax.broadcasted_iota(jnp.int32, (rows, LANES), 1)
    zero = jnp.zeros_like(pair)
    return jnp.concatenate(
        [jnp.where(lane < HEAD, pair, zero), jnp.where(lane < HEAD, zero, pair)], axis=0
    )


def pick_heads(stacked, rows):
    lane = lax.broadcasted_iota(jnp.int32, (rows, LANES), 1)
    return jnp.where(lane < HEAD, stacked[:rows], stacked[rows:])


def member_of(rc, experts):
    lane = lax.broadcasted_iota(jnp.int32, (rc.shape[0], experts), 1)
    return (lane == rc).astype(F32)


def target_slots(rc, rr, z, experts, cap_pad, big):
    rows = rc.shape[0]
    i = lax.broadcasted_iota(jnp.int32, (rows, rows), 0)
    j = lax.broadcasted_iota(jnp.int32, (rows, rows), 1)
    same = rc == rr
    before = jnp.where(same & (j < i), 1.0, 0.0)
    after = jnp.where(same & (i < j), 1.0, 0.0)

    def place(route, slot):
        if not big:
            route = jnp.where(route < z, route - z + experts, route - z)
        return route * cap_pad + slot.astype(jnp.int32)

    return (
        place(rc, jnp.sum(before, axis=1, keepdims=True)),
        place(rr, jnp.sum(after, axis=0, keepdims=True)),
    )


def small_lines(meta, small, layer, experts, slab):
    pieces = []
    for shard in range(2 * experts):
        if small.shape[0] == 2 and len(small.shape) == 4:
            block = small[layer, shard]
        else:
            at_z = lax.rem(meta[2] - shard // 2 + experts, experts)
            block = small[meta[0] ^ layer, meta[3] ^ (shard % 2), at_z]
        pieces.append(block.astype(F32))
    return jnp.concatenate(pieces, axis=1)


def same_sequence(meta, rows):
    shape = (2 * rows, rows)
    i = lax.broadcasted_iota(jnp.int32, shape, 0)
    i = jnp.where(i < rows, i, i - rows)
    j = lax.broadcasted_iota(jnp.int32, shape, 1)
    seg_i, seg_j = jnp.zeros(shape, jnp.int32), jnp.zeros(shape, jnp.int32)
    end = 0
    for n in range(5, 9):
        end = end + meta[n]
        seg_i = seg_i + (i >= end).astype(jnp.int32)
        seg_j = seg_j + (j >= end).astype(jnp.int32)
    return seg_i == seg_j


def position_bias(by_offset, head, rows):
    line = jnp.broadcast_to(by_offset[head:head + 1], (rows, LANES))
    return pltpu.roll(line, 0, 1, stride=1, stride_axis=0)[:, :rows]


def offset_sums(ds, flip):
    turned = mm(flip, ds)
    wide = jnp.concatenate([turned, jnp.zeros_like(turned)], axis=1)
    rolled = pltpu.roll(wide, 0, 1, stride=1, stride_axis=0)
    rows = ds.shape[0] // 2
    first = jnp.sum(rolled[rows:], axis=0, keepdims=True)
    second = jnp.sum(rolled[:rows], axis=0, keepdims=True)
    return [pltpu.roll(first, 1, 1), pltpu.roll(second, 1 + rows, 1)]


def split_two(v):
    high = v.astype(BF)
    return high, (v - high.astype(F32)).astype(BF)


def put_rows(target_row, block, cap_pad, values, rows):
    slot = lax.broadcasted_iota(jnp.int32, (cap_pad, rows), 0) + block * cap_pad
    return mm((slot == target_row).astype(BF), values)


def take_rows(target_col, blocks, cap_pad, rows):
    total = None
    for i, block in enumerate(blocks):
        slot = lax.broadcasted_iota(jnp.int32, (rows, cap_pad), 1) + i * cap_pad
        part = mm((slot == target_col).astype(BF), block)
        total = part if total is None else total + part
    return total


class Weights:
    def __init__(self, refs, plan, experts, slab, layer):
        self.refs, self.plan, self.experts, self.slab, self.layer = (
            refs, plan, experts, slab, layer,
        )

    @staticmethod
    def scratch(plan, width):
        return [pltpu.VMEM((4, width, width), BF), pltpu.SemaphoreType.DMA((max(1, len(plan)),))]

    def copies(self, meta, scr, sem, which):
        if not self.plan:
            return [pltpu.make_async_copy(self.refs[0], scr, sem.at[0])]
        x, z, y = meta[1], meta[2], meta[3]
        count = len(self.plan)
        made = []
        for n, (i, flip_y, flip_x, offset, held) in enumerate(self.plan):
            at_z = lax.rem(z - i + self.experts, self.experts)
            row = pl.multiple_of((at_z * 2 + (y ^ flip_y)) * self.slab, self.slab)
            matrix = 0 if held == 4 else 2 * (x ^ flip_x) + offset
            made.append(
                pltpu.make_async_copy(
                    self.refs[which * count + n],
                    scr.at[pl.ds(matrix, held), pl.ds(row, self.slab)],
                    sem.at[n],
                )
            )
        return made

    def start(self, meta, scr, sem):
        if not self.plan:
            self.copies(meta, scr, sem, 0)[0].start()
            return

        @pl.when(meta[0] == self.layer)
        def _():
            for copy in self.copies(meta, scr, sem, 0):
                copy.start()

        @pl.when(meta[0] != self.layer)
        def _():
            for copy in self.copies(meta, scr, sem, 1):
                copy.start()

    def wait(self, meta, scr, sem):
        for copy in self.copies(meta, scr, sem, 0):
            copy.wait()


def forward_kernel(layer, experts, slab, cap_pad, n_ret, n_w, plan, *refs):
    it = iter(refs)
    meta, small, rc_ref, rr_ref, head_of, offset_of = (next(it) for _ in range(6))
    if layer == 0:
        x_ref = next(it)
    else:
        mid0, probs0, g_ref = (next(it) for _ in range(3))
        ret = [next(it) for _ in range(n_ret)]
    w = Weights([next(it) for _ in range(n_w)], plan, experts, slab, layer)
    h1_ref, qkv_ref, p_ref, ctx_ref, mid_ref, h2_ref, probs_ref = (next(it) for _ in range(7))
    if layer == 1:
        x1_ref, y0_ref = next(it), next(it)
    rest = list(it)
    scr, sem = rest[-2:]
    disp = rest[:-2]
    big = not plan
    w.start(meta, scr, sem)
    rows, width = h1_ref.shape
    z = meta[2]
    rc = rc_ref[:, layer:layer + 1]
    _, tr = target_slots(rc, rr_ref[layer:layer + 1], z, experts, cap_pad, big)
    lines = small_lines(meta, small, layer, experts, slab)
    router = lines[:experts].astype(BF)
    table = (head_of[...].astype(F32) * lines[experts + 2:experts + 3]).astype(BF)
    by_offset = mm_nt(table, offset_of[...])
    keep = same_sequence(meta, rows)
    if layer == 0:
        x = x_ref[...].astype(F32)
    else:
        blocks = [ret[i][...] for i in range(n_ret)] if n_ret > 1 else [
            ret[0][i] for i in range(experts)
        ]
        rc0 = rc_ref[:, 0:1]
        tc0, _ = target_slots(rc0, rr_ref[0:1], z, experts, cap_pad, big)
        y0 = take_rows(tc0, blocks, cap_pad, rows)
        y0_ref[...] = y0
        gate0 = jnp.sum(probs0[...] * member_of(rc0, experts), axis=-1, keepdims=True)
        x1 = (mid0[...] + gate0 * y0).astype(BF)
        x1_ref[...] = x1
        x = x1.astype(F32)
    h1 = (x * inv_rms(x) * lines[experts:experts + 1]).astype(BF)
    h1_ref[...] = h1
    w.wait(meta, scr, sem)
    q = mm(h1, scr[0]).astype(BF)
    k = mm(h1, scr[1]).astype(BF)
    v = mm(h1, scr[2]).astype(BF)
    qkv_ref[0] = q
    qkv_ref[1] = k
    qkv_ref[2] = v
    contexts = []
    for pair in range(PAIRS):
        cols = slice(pair * LANES, (pair + 1) * LANES)
        bias = jnp.concatenate(
            [position_bias(by_offset, 2 * pair + n, rows) for n in range(2)], axis=0
        )
        sc = mm_nt(stack_heads(q[:, cols], rows), k[:, cols]) * SCALE + bias
        sc = jnp.where(keep, sc, NEGATIVE)
        e = jnp.exp(sc - jnp.max(sc, axis=-1, keepdims=True))
        p = e / jnp.sum(e, axis=-1, keepdims=True)
        p_ref[pair] = p
        contexts.append(pick_heads(mm(p.astype(BF), v[:, cols]), rows))
    ctx = jnp.concatenate(contexts, axis=1).astype(BF)
    ctx_ref[...] = ctx
    mid = x + mm(ctx, scr[3])
    mid_ref[...] = mid
    h2 = (mid * inv_rms(mid) * lines[experts + 1:experts + 2]).astype(BF)
    h2_ref[...] = h2
    logits = mm_nt(h2, router)
    e = jnp.exp(logits - jnp.max(logits, axis=-1, keepdims=True))
    probs = e / jnp.sum(e, axis=-1, keepdims=True)
    probs_ref[...] = probs
    sent = [h2]
    if layer == 1:
        gate = jnp.sum(probs * member_of(rc, experts), axis=-1, keepdims=True)
        sent.append((gate * g_ref[...].astype(F32)).astype(BF))
    for i in range(experts):
        for part, values in enumerate(sent):
            block = put_rows(tr, i, cap_pad, values, rows).astype(BF)
            ref = disp[i] if len(disp) > 1 else disp[0].at[i]
            if layer == 1:
                ref[part] = block
            else:
                ref[...] = block


def backward_kernel(layer, experts, slab, cap_pad, n_ret, n_w, plan, *refs):
    it = iter(refs)
    meta, small, rc_ref, rr_ref, head_of, offset_of, flip = (next(it) for _ in range(7))
    g_ref, x_ref, h1_ref, qkv_ref, p_ref, ctx_ref, mid_ref, h2_ref, probs_ref = (
        next(it) for _ in range(9)
    )
    if layer == 0:
        y_ref = next(it)
    else:
        probs0, h1_0, ctx_0 = (next(it) for _ in range(3))
    ret = [next(it) for _ in range(n_ret)]
    w = Weights([next(it) for _ in range(n_w)], plan, experts, slab, layer)
    dx_ref, ex_ref = (next(it) for _ in range(2))
    factors = [next(it) for _ in range(4)]
    if layer == 1:
        out_ref = next(it)
    rest = list(it)
    scr, sem, right, left, sums = rest[-5:]
    disp = rest[:-5]
    big = not plan
    w.start(meta, scr, sem)
    rows, width = h1_ref.shape
    z = meta[2]
    rc = rc_ref[:, layer:layer + 1]
    tc, _ = target_slots(rc, rr_ref[layer:layer + 1], z, experts, cap_pad, big)
    lines = small_lines(meta, small, layer, experts, slab)
    router = lines[:experts].astype(BF)
    g = g_ref[...].astype(F32)
    mid = mid_ref[...]
    probs = probs_ref[...]
    member = member_of(rc, experts)
    gate = jnp.sum(probs * member, axis=-1, keepdims=True)

    def blocks(part):
        if layer == 0:
            return [r[...] for r in ret] if n_ret > 1 else [ret[0][i] for i in range(experts)]
        return [r[part] for r in ret] if n_ret > 1 else [ret[0][i, part] for i in range(experts)]

    if layer == 0:
        y = y_ref[...]
        dh2 = take_rows(tc, blocks(0), cap_pad, rows)
    else:
        y = take_rows(tc, blocks(0), cap_pad, rows)
        dh2 = take_rows(tc, blocks(1), cap_pad, rows)
        out_ref[...] = mid + gate * y
    dgate = jnp.sum(g * y, axis=-1, keepdims=True)
    high, low = split_two(probs * (dgate * (member - gate)))
    dh2 = dh2 + mm(high, router) + mm(low, router)
    dmid, dgain1 = rms_back(mid, lines[experts + 1:experts + 2], dh2)
    dmid = dmid + g
    h2 = h2_ref[...]
    drouter = mm_tn(high, h2) + mm_tn(low, h2)
    da = dmid.astype(BF)
    right[3] = da
    w.wait(meta, scr, sem)
    dctx = mm_nt(da, scr[3]).astype(BF)
    grads = ([], [], [])
    sums[...] = jnp.zeros_like(sums)
    for pair in range(PAIRS):
        cols = slice(pair * LANES, (pair + 1) * LANES)
        p = p_ref[pair]
        qs = stack_heads(qkv_ref[0, :, cols], rows)
        ds_heads = stack_heads(dctx[:, cols], rows)
        dp = mm_nt(ds_heads, qkv_ref[2, :, cols])
        ds = (p * (dp - jnp.sum(p * dp, axis=-1, keepdims=True))).astype(BF)
        for n, line in enumerate(offset_sums(ds, flip[...])):
            sums[2 * pair + n:2 * pair + n + 1] = line
        grads[0].append(pick_heads(mm(ds, qkv_ref[1, :, cols]) * SCALE, rows))
        grads[1].append(mm_tn(ds, qs) * SCALE)
        grads[2].append(mm_tn(p.astype(BF), ds_heads))
    dh1 = None
    for j in range(3):
        dj = jnp.concatenate(grads[j], axis=1).astype(BF)
        right[j] = dj
        part = mm_nt(dj, scr[j])
        dh1 = part if dh1 is None else dh1 + part
    dx, dgain0 = rms_back(x_ref[...].astype(F32), lines[experts:experts + 1], dh1)
    dx = dx + dmid
    dx_ref[...] = dx
    high, low = split_two(sums[...])
    by_place = (mm(high, offset_of[...]) + mm(low, offset_of[...])) * head_of[...].astype(F32)
    ex_ref[...] = jnp.zeros_like(ex_ref)
    ex_ref[0:experts] = drouter
    ex_ref[experts:experts + 1] = dgain0
    ex_ref[experts + 1:experts + 2] = dgain1
    ex_ref[experts + 2:experts + 3] = jnp.sum(by_place, axis=0, keepdims=True)
    if layer == 1:
        rc0 = rc_ref[:, 0:1]
        _, tr0 = target_slots(rc0, rr_ref[0:1], z, experts, cap_pad, big)
        gate0 = jnp.sum(probs0[...] * member_of(rc0, experts), axis=-1, keepdims=True)
        dy0 = (gate0 * dx.astype(BF).astype(F32)).astype(BF)
        for i in range(experts):
            block = put_rows(tr0, i, cap_pad, dy0, rows).astype(BF)
            ref = disp[i] if len(disp) > 1 else disp[0].at[i]
            ref[...] = block
    if layer == 1:
        left[0] = h1_ref[...]
        left[1] = ctx_ref[...]
        left[2] = h1_0[...]
        left[3] = ctx_0[...]
    place = meta[4]
    for m in range(4):
        target = place ^ m
        factors[m][0:rows] = right[target]
        if layer == 1:
            which = jnp.where(target == 3, 1, 0)
            factors[m][rows:2 * rows] = left[which]
            factors[m][2 * rows:] = left[2 + which]


def pack_kernel(n, cap, parts, *refs):
    out = refs[-1]
    blocks = refs[:-1]
    packed = out.shape[-2]
    cap_pad = blocks[0].shape[-2]
    for part in range(parts):
        total = None
        for i in range(n):
            block = blocks[i][part] if len(blocks) > 1 else blocks[0][i, part]
            row = lax.broadcasted_iota(jnp.int32, (packed, cap_pad), 0)
            slot = lax.broadcasted_iota(jnp.int32, (packed, cap_pad), 1)
            pick = ((row == slot + i * cap) & (slot < cap)).astype(BF)
            moved = mm(pick, block)
            total = moved if total is None else total + moved
        out[part] = total.astype(BF)


def unpack_kernel(n, cap, parts, *refs):
    sums, outs = refs[:4], refs[4:]
    packed = sums[0].shape[-2]
    cap_pad = outs[0].shape[-2]
    for part in range(parts):
        total = (
            sums[0][part].astype(F32)
            + sums[1][part].astype(F32)
            + sums[2][part].astype(F32)
            + sums[3][part].astype(F32)
        ).astype(BF)
        for i in range(n):
            row = lax.broadcasted_iota(jnp.int32, (cap_pad, packed), 1)
            slot = lax.broadcasted_iota(jnp.int32, (cap_pad, packed), 0)
            pick = ((row == slot + i * cap) & (slot < cap)).astype(BF)
            block = mm(pick, total).astype(BF)
            if len(outs) > 1:
                outs[i][part] = block
            else:
                outs[0][i, part] = block


def expert_weights(layer, meta, own, other, scr, sem):
    for which in range(2):
        @pl.when(meta[0] == layer)
        def _():
            pltpu.make_async_copy(own[which], scr.at[which], sem.at[which]).start()

        @pl.when(meta[0] != layer)
        def _():
            pltpu.make_async_copy(other[which], scr.at[which], sem.at[which]).start()

    def wait(which):
        pltpu.make_async_copy(own[which], scr.at[which], sem.at[which]).wait()

    return wait


def expert_forward_kernel(layer, both, *refs):
    meta, c0, c1, c2, c3, in_own, in_other, out_own, out_other = refs[:9]
    outs = refs[9:13]
    count = (len(refs) - 16) // 2
    kept = refs[13:13 + count]
    scr, sem = refs[13 + count:15 + count]
    saved, keep_sem = refs[15 + count:-1], refs[-1]

    def save(n, values):
        saved[n][...] = values
        pltpu.make_async_copy(saved[n], kept[n], keep_sem.at[n]).start()

    wait = expert_weights(layer, meta, (in_own, out_own), (in_other, out_other), scr, sem)
    packed = c0.shape[-2]
    rows = jnp.concatenate([c[0] for c in (c0, c1, c2, c3)], axis=0)
    wait(0)
    pre = mm(rows, scr[0])
    act = gelu(pre).astype(BF)
    save(0, rows)
    save(1, act)
    wait(1)
    y = mm(act, scr[1])
    for m in range(4):
        outs[m][0] = y[m * packed:(m + 1) * packed].astype(BF)
    if both:
        grad_rows = jnp.concatenate([c[1] for c in (c0, c1, c2, c3)], axis=0)
        dpre = (mm_nt(grad_rows, scr[1]) * gelu_slope(pre)).astype(BF)
        save(2, grad_rows)
        save(3, dpre)
        dh = mm_nt(dpre, scr[0])
        for m in range(4):
            outs[m][1] = dh[m * packed:(m + 1) * packed].astype(BF)
    else:
        save(2, pre)
    for n in range(count):
        pltpu.make_async_copy(saved[n], kept[n], keep_sem.at[n]).wait()


def expert_backward_kernel(layer, *refs):
    meta, c0, c1, c2, c3, in_own, in_other, out_own, out_other, pre_ref = refs[:10]
    outs = refs[10:14]
    kept, scr, sem, saved, keep_sem = refs[14:16], refs[16], refs[17], refs[18:20], refs[20]

    def copy_out(n):
        return pltpu.make_async_copy(saved[n], kept[n], keep_sem.at[n])

    wait = expert_weights(layer, meta, (in_own, out_own), (in_other, out_other), scr, sem)
    packed = c0.shape[-2]
    grad_rows = jnp.concatenate([c[0] for c in (c0, c1, c2, c3)], axis=0)
    saved[0][...] = grad_rows
    copy_out(0).start()
    slope = gelu_slope(pre_ref[...])
    wait(1)
    dpre = (mm_nt(grad_rows, scr[1]) * slope).astype(BF)
    saved[1][...] = dpre
    copy_out(1).start()
    wait(0)
    dh = mm_nt(dpre, scr[0])
    for m in range(4):
        outs[m][0] = dh[m * packed:(m + 1) * packed].astype(BF)
    copy_out(0).wait()
    copy_out(1).wait()


def bring_layer(layer_is, sets, scr, sem):
    for layer in range(2):
        @pl.when(layer_is == layer)
        def _():
            for n in range(4):
                pltpu.make_async_copy(sets[layer][n], scr[n], sem.at[n]).start()

    def wait(n):
        pltpu.make_async_copy(sets[0][n], scr[n], sem.at[n]).wait()

    return wait


def expert_send_kernel(meta, *refs):
    sets, out, scr, sem = (refs[0:4], refs[4:8]), refs[8], refs[9:13], refs[13]
    wait = bring_layer(1 - meta[0], sets, scr, sem)
    wait(0)
    wait(1)
    out[0] = mm_tn(scr[0][...], scr[1][...]).astype(BF)
    wait(2)
    wait(3)
    out[1] = mm_tn(scr[2][...], scr[3][...]).astype(BF)


def expert_own_kernel(meta, *refs):
    sets, got, gin, gout, scr, sem = (
        (refs[0:4], refs[4:8]), refs[8], refs[9], refs[10], refs[11:15], refs[15],
    )
    wait = bring_layer(meta[0], sets, scr, sem)
    wait(0)
    wait(1)
    gin[...] = mm_tn(scr[0][...], scr[1][...]) + got[0].astype(F32)
    wait(2)
    wait(3)
    gout[...] = mm_tn(scr[2][...], scr[3][...]) + got[1].astype(F32)


def factor_kernel(experts, slab, rows, split, meta, *refs):
    rights, lefts, ex, keep, send = refs[0:4], refs[4:8], refs[8], refs[9], refs[10]
    right = jnp.concatenate([f[0:rows] for f in rights], axis=0)
    left = jnp.concatenate([f[split:split + rows] for f in lefts], axis=0)
    grad = mm_tn(left, right).astype(BF)
    s, z = meta[0], meta[2]
    extra = ex[...]
    pad = jnp.zeros((16, grad.shape[1] - LANES), F32)
    for shard in range(2 * experts):
        at = lax.rem(shard // 2 - z + experts, experts)
        wide = jnp.concatenate(
            [extra[:, shard * slab:(shard + 1) * slab], jnp.zeros((16, LANES - slab), F32)], axis=1
        )
        block = jnp.concatenate([wide, pad], axis=1).astype(BF)

        @pl.when(s == shard % 2)
        def _():
            keep[at, 0:slab] = grad[shard * slab:(shard + 1) * slab]
            keep[at, slab:] = block

        @pl.when(s != shard % 2)
        def _():
            send[at, 0:slab] = grad[shard * slab:(shard + 1) * slab]
            send[at, slab:] = block


def finish_kernel(experts, slab, table_slab, meta, *refs):
    arrived, (qkv, out, router, gains, table) = refs[:4], refs[4:]
    s, x = meta[0], meta[1]
    extra = None
    for a in range(2):
        for b in range(2):
            block = arrived[2 * a + b]
            matrix = 2 * (x ^ b) + (s ^ a)
            main = block[0:slab].astype(F32)

            @pl.when(matrix == 3)
            def _():
                out[0] = main

            @pl.when(matrix != 3)
            def _():
                qkv[0, matrix] = main

            small = block[slab:, 0:LANES].astype(F32)
            extra = small if extra is None else extra + small
    router[0] = extra[0:experts, 0:slab]
    gains[0] = extra[experts:experts + 2, 0:slab]
    table[...] = extra[experts + 2:experts + 3, 0:table_slab]


def call(
    kernel, out_shapes, args, specs, scratch=(), flops=0, moved=0, name=None, vmem=62, hbm=0
):
    return pl.pallas_call(
        kernel,
        out_shape=[jax.ShapeDtypeStruct(shape, dtype) for shape, dtype in out_shapes],
        in_specs=specs,
        out_specs=[VM] * (len(out_shapes) - hbm) + [ANY] * hbm,
        scratch_shapes=list(scratch),
        compiler_params=pltpu.CompilerParams(vmem_limit_bytes=vmem * 2**20),
        cost_estimate=pl.CostEstimate(flops=flops, bytes_accessed=moved, transcendentals=0),
        name=name,
    )(*args)


def shift(v, axis, by):
    n = lax.axis_size(axis)
    return lax.ppermute(v, axis, [(i, (i + by) % n) for i in range(n)])


def after(values, *events):
    values = tuple(values)
    return list(lax.optimization_barrier(values + events)[: len(values)])


def swap_section(v):
    return lax.ppermute(v, "section", [(0, 1), (1, 0)])


def plane_swap(v, mask):
    return lax.ppermute(v, PLANE, [(i, i ^ mask) for i in range(4)])


def plane_gather(v):
    return [v] + [plane_swap(v, m) for m in (1, 2, 3)]


def local(
    experts,
    boundary,
    seq_lengths,
    routes,
    qkv_proj,
    out_proj,
    router,
    gains,
    rel_table,
    expert_in,
    expert_out,
):
    big = experts > 8
    s = lax.axis_index("section")
    x_at = lax.axis_index("rep")
    z_at = lax.axis_index("expert")
    y_at = lax.axis_index("half")
    shards = 2 * experts
    rows, width = boundary.shape[2:]
    slab = qkv_proj.shape[2]
    table_slab = rel_table.shape[1]
    cap = max(2, rows // experts + 1)
    cap_pad = up(cap, 8)
    packed = up(experts * cap, 16)
    ff = expert_in.shape[3]
    first = s == 0

    own = boundary[0]
    got = swap_section(own[1 - s])
    x0 = jnp.where(first, own[0], got)
    g1 = jnp.where(first, got, own[1])
    lengths = seq_lengths[s, 0]
    place = jnp.stack([s, x_at, z_at, y_at, 2 * x_at + y_at]).astype(jnp.int32)
    meta = jnp.concatenate([place, lengths])
    own_routes = routes[0, :, :, 0]
    got_routes = swap_section(own_routes[1 - s])
    route_list = [
        jnp.where(first, own_routes[0], got_routes),
        jnp.where(first, got_routes, own_routes[1]),
    ]

    early = ()
    if big:
        slabs = jnp.concatenate([qkv_proj[0], out_proj], axis=0)
        whole = lax.all_gather(slabs, ("expert", "half"), axis=1, tiled=True)
        layers = lax.all_gather(whole, "section", axis=0)
        attn_w = [[layers[0]], [layers[1]]]
        plan = []
    else:
        slabs = jnp.concatenate([qkv_proj[0], out_proj], axis=0)
        piece = lax.dynamic_slice_in_dim(slabs, 2 * x_at, 2, axis=0)
        along = {1: shift(piece, "expert", 1), 3: shift(piece, "expert", 3)}
        over_y0 = plane_swap(piece, 1)
        along[2] = shift(after([piece], along[1])[0], "expert", 2)
        early = (over_y0,)

    small_rows = up(experts + 3, 8)
    table_row = jnp.pad(rel_table, ((0, 0), (0, slab - table_slab)))
    small = jnp.concatenate(
        [
            router[0].T,
            gains[0],
            table_row,
            jnp.zeros((small_rows - experts - 3, slab), BF),
        ]
    )
    (small,) = after([small], *early)
    if big:
        small_all = lax.all_gather(
            lax.all_gather(small, ("expert", "half"), axis=0), "section", axis=0
        )
    else:
        lines = jnp.stack([small] + [shift(small, "expert", i) for i in range(1, experts)])
        lines = jnp.stack([lines, shift(lines, "half", 1)])
        small_all = jnp.stack([lines, swap_section(lines)])
    head_of, offset_of = table_places(shards, slab, table_slab)
    flip = jnp.asarray(np.eye(2 * rows)[::-1], BF)
    rr = jnp.stack(route_list)
    common = [meta, small_all, rr.T, rr, head_of, offset_of]

    if not big:
        pieces, plan = [slabs], [(0, 0, 0, 0, 4)]
        pieces += [over_y0, plane_swap(over_y0, 2)]
        plan += [(0, 1, 0, 0, 2), (0, 1, 1, 0, 2)]
        for i in (1, 3, 2):
            got = along[i]
            if i == 2:
                got, x0, g1, *common = after([got, x0, g1] + common)
            over_y, over_x = plane_swap(got, 1), plane_swap(got, 2)
            pieces += [got, over_y, over_x]
            plan += [(i, 0, 0, 0, 2), (i, 1, 0, 0, 2), (i, 0, 1, 0, 2)]
            if i == 1:
                pieces.append(plane_swap(over_y, 2))
                plan.append((i, 1, 1, 0, 2))
            elif i == 3:
                pieces.append(plane_swap(over_x, 1))
                plan.append((i, 1, 1, 0, 2))
            else:
                pieces += [plane_swap(over_y[:1], 2), plane_swap(over_x[1:], 1)]
                plan += [(i, 1, 1, 0, 1), (i, 1, 1, 1, 1)]
        copied = [swap_section(v) for v in pieces]
        attn_w = [pieces + copied] * 2
    other_in = swap_section(expert_in[0, 0])
    other_out = swap_section(expert_out[0, 0])
    expert_w = [expert_in[0, 0], other_in, expert_out[0, 0], other_out]

    n_w = len(attn_w[0])
    n_ret = 1 if big else experts

    def message_shapes(parts):
        if big:
            return [((experts,) + parts + (cap_pad, width), BF)]
        return [(parts + (cap_pad, width), BF)] * experts

    def dispatch(blocks, parts):
        if big:
            arrived = lax.all_to_all(blocks[0], "expert", 0, 0, tiled=True)
            arrived = [arrived if parts == 2 else arrived[:, None]]
        else:
            arrived = [blocks[0]] + [shift(blocks[i], "expert", i) for i in range(1, experts)]
            arrived = arrived if parts == 2 else [a[None] for a in arrived]
        (joined,) = call(
            functools.partial(pack_kernel, experts, cap, parts),
            [((parts, packed, width), BF)],
            arrived,
            [VM] * len(arrived),
            moved=4 * packed * width,
            name="pack",
            vmem=8,
        )
        return plane_gather(joined)

    def come_back(partial, parts, events=()):
        sums = [partial[0]] + [plane_swap(partial[m], m) for m in (1, 2, 3)]
        if events:
            sums = after(sums, *events)
        shapes = (
            [((experts, parts, cap_pad, width), BF)]
            if big
            else [((parts, cap_pad, width), BF)] * experts
        )
        blocks = call(
            functools.partial(unpack_kernel, experts, cap, parts),
            shapes,
            sums,
            [VM] * 4,
            moved=4 * packed * width,
            name="unpack",
            vmem=8,
        )
        if big:
            back = lax.all_to_all(blocks[0], "expert", 0, 0, tiled=True)
            return [back if parts == 2 else back[:, 0]]
        back = [blocks[0]] + [shift(blocks[i], "expert", -i) for i in range(1, experts)]
        return back if parts == 2 else [b[0] for b in back]

    def forward(layer, extra):
        args = common + extra
        specs = [SM] + [VM] * (len(args) - 1) + [ANY] * n_w
        shapes = [
            ((rows, width), BF),
            ((3, rows, width), BF),
            ((PAIRS, 2 * rows, rows), F32),
            ((rows, width), BF),
            ((rows, width), F32),
            ((rows, width), BF),
            ((rows, experts), F32),
        ]
        if layer == 1:
            shapes += [((rows, width), BF), ((rows, width), F32)]
        fixed = len(shapes)
        shapes += message_shapes((2,) if layer == 1 else ())
        outs = call(
            functools.partial(forward_kernel, layer, experts, slab, cap_pad, n_ret, n_w, plan),
            shapes,
            args + attn_w[layer],
            specs,
            Weights.scratch(plan, width),
            flops=8 * rows * width * width,
            moved=8 * width * width,
            name="attention_forward",
        )
        names = ["h1", "qkv", "p", "ctx", "mid", "h2", "probs", "x1", "y0"][:fixed]
        return dict(zip(names, outs[:fixed])), outs[fixed:]

    def backward(layer, kept, x_in, g, returned, extra):
        args = common + [flip, g, x_in] + [
            kept[n] for n in ("h1", "qkv", "p", "ctx", "mid", "h2", "probs")
        ]
        args += extra + returned
        specs = [SM] + [VM] * (len(args) - 1) + [ANY] * n_w
        shapes = [
            ((rows, width), F32),
            ((up(experts + 3, 16), width), F32),
        ] + [(((3 if layer == 1 else 1) * rows, width), BF)] * 4
        if layer == 1:
            shapes += [((rows, width), F32)] + message_shapes(())
        return call(
            functools.partial(backward_kernel, layer, experts, slab, cap_pad, n_ret, n_w, plan),
            shapes,
            args + attn_w[layer],
            specs,
            Weights.scratch(plan, width)
            + [
                pltpu.VMEM((4, rows, width), BF),
                pltpu.VMEM((4, rows, width), BF),
                pltpu.VMEM((16, LANES), F32),
            ],
            flops=16 * rows * width * width,
            moved=8 * width * width,
            name="attention_backward",
        )

    expert_scratch = [pltpu.VMEM((2, width, ff), BF), pltpu.SemaphoreType.DMA((2,))]
    expert_specs = [SM] + [VM] * 4 + [ANY] * 4
    all_rows = 4 * packed

    def expert_forward(layer, joined, both):
        parts = 2 if both else 1
        shapes = [((parts, packed, width), BF)] * 4
        shapes += [((all_rows, width), BF), ((all_rows, ff), BF)]
        shapes += (
            [((all_rows, width), BF), ((all_rows, ff), BF)] if both else [((all_rows, ff), F32)]
        )
        outs = call(
            functools.partial(expert_forward_kernel, layer, both),
            shapes,
            [meta] + joined + expert_w,
            expert_specs,
            expert_scratch
            + [pltpu.VMEM(*shape) for shape in shapes[4:]]
            + [pltpu.SemaphoreType.DMA((len(shapes) - 4,))],
            hbm=len(shapes) - 4,
            flops=4 * all_rows * width * ff * parts,
            moved=4 * width * ff,
            name="expert_forward",
            vmem=20,
        )
        return outs[:4], outs[4:]

    def plane_factors(factors):
        return [factors[0]] + [plane_swap(factors[m], m) for m in (1, 2, 3)]

    def attention_grads(rights, lefts, split, ex):
        keep, send = call(
            functools.partial(factor_kernel, experts, slab, rows, split),
            [((experts, slab + 16, width), BF)] * 2,
            [meta] + rights + lefts + [ex],
            [SM] + [VM] * 9,
            flops=8 * rows * width * width,
            moved=8 * width * width,
            name="attention_grads",
        )
        return keep, send

    def sum_cores(keep, send):
        both = keep.astype(F32) + swap_section(send).astype(F32)
        return [both[i].astype(BF) for i in range(experts)]

    def along_z(parts):
        return [parts[0]] + [shift(parts[i], "expert", i) for i in range(1, experts)]

    def add_up(parts):
        total = parts[0].astype(F32)
        for part in parts[1:]:
            total = total + part.astype(F32)
        return total.astype(BF)

    kept0, blocks = forward(0, [x0])
    joined = dispatch(blocks, 1)
    partial, (rows0, act0, pre0) = expert_forward(0, joined, False)
    returned = come_back(partial, 1)

    kept1, blocks = forward(1, [kept0["mid"], kept0["probs"], g1] + returned)
    joined = dispatch(blocks, 2)
    partial, (rows1, act1, grows1, dpre1) = expert_forward(1, joined, True)
    returned = come_back(partial, 2)

    outs = backward(
        1, kept1, kept1["x1"], g1, returned, [kept0["probs"], kept0["h1"], kept0["ctx"]]
    )
    dx1, ex1 = outs[:2]
    factors1, out1, blocks = outs[2:6], outs[6], outs[7:]

    joined = dispatch(blocks, 1)
    shapes = [((1, packed, width), BF)] * 4 + [((all_rows, width), BF), ((all_rows, ff), BF)]
    outs = call(
        functools.partial(expert_backward_kernel, 0),
        shapes,
        [meta] + joined + expert_w + [pre0],
        expert_specs + [VM],
        expert_scratch
        + [pltpu.VMEM(*shape) for shape in shapes[4:]]
        + [pltpu.SemaphoreType.DMA((2,))],
        hbm=2,
        flops=4 * all_rows * width * ff,
        moved=4 * width * ff,
        name="expert_backward",
            vmem=20,
    )
    partial, (grows0, dpre0) = outs[:4], outs[4:]
    if not big:
        beside = plane_factors(factors1)
        beside = after(beside, partial[3])
        halves1 = attention_grads(beside, beside, rows, ex1)
        returned = come_back(partial, 1, halves1)
        moved1 = along_z(after(sum_cores(*halves1), *returned))
    else:
        returned = come_back(partial, 1)
    outs = backward(0, kept0, x0, dx1.astype(BF), returned, [kept1["y0"]])
    dx0, ex0 = outs[:2]
    factors0 = outs[2:6]
    if not big:
        factors0 = after(factors0, *moved1)
        rights0 = plane_factors(factors0)
        halves0 = attention_grads(rights0, beside, 2 * rows, ex0)
        parts0 = sum_cores(*halves0)
        moved0 = along_z(parts0)

    traded = swap_section(jnp.where(first, out1, dx0))
    result_rows = jnp.stack([jnp.where(first, dx0, traded), jnp.where(first, traded, out1)])

    sets = [rows0, dpre0, act0, grows0, rows1, dpre1, act1, grows1]
    if not big:
        sets = after(sets, rights0[1])
    bring_scratch = [
        pltpu.VMEM((all_rows, width), BF),
        pltpu.VMEM((all_rows, ff), BF),
        pltpu.VMEM((all_rows, ff), BF),
        pltpu.VMEM((all_rows, width), BF),
        pltpu.SemaphoreType.DMA((4,)),
    ]
    (sent,) = call(
        expert_send_kernel,
        [((2, width, ff), BF)],
        [meta] + sets,
        [SM] + [ANY] * 8,
        bring_scratch,
        flops=4 * all_rows * width * ff,
        moved=8 * width * ff,
        name="expert_gradients_sent",
    )
    got = swap_section(sent)

    def own_experts(sets, got):
        return call(
            expert_own_kernel,
            [((width, ff), F32), ((ff, width), F32)],
            [meta] + sets + [got],
            [SM] + [ANY] * 8 + [VM],
            bring_scratch,
            flops=4 * all_rows * width * ff,
            moved=8 * width * ff,
            name="expert_gradients_own",
        )

    traded = swap_section(jnp.where(first, out1, dx0))
    result_rows = jnp.stack([jnp.where(first, dx0, traded), jnp.where(first, traded, out1)])

    if big:
        own_factors = []
        for kept, ex, fac in ((kept0, ex0, factors0), (kept1, ex1, factors1)):
            spot = 2 * x_at + y_at
            right = jnp.stack([fac[m][:rows] for m in range(4)])
            pieces = [
                jnp.sum(
                    jnp.where(
                        (jnp.arange(4) ^ spot == j)[:, None, None], right, jnp.zeros_like(right)
                    ),
                    axis=0,
                )
                for j in range(4)
            ]
            lefts = [kept["h1"]] * 3 + [kept["ctx"]]
            grad = jnp.stack(
                [
                    lax.dot_general(
                        a, b, (((0,), (0,)), ((), ())), preferred_element_type=F32
                    )
                    for a, b in zip(lefts, pieces)
                ]
            )
            own_factors.append((grad, ex[:experts + 3]))
        grad = jnp.stack([own_factors[0][0], own_factors[1][0]]).astype(BF)
        lines = jnp.stack([own_factors[0][1], own_factors[1][1]])
        grad = lax.psum_scatter(grad, "section", scatter_dimension=0)
        lines = lax.psum_scatter(lines, "section", scatter_dimension=0)
        grad = lax.psum_scatter(grad, ("expert", "half"), scatter_dimension=1, tiled=True)
        grad = lax.psum(grad, "rep").astype(F32)
        lines = lax.psum(lines, ("rep", "expert", "half"))
        shard_at = z_at * 2 + y_at
        extra = lax.dynamic_slice_in_dim(lines, shard_at * slab, slab, axis=1)
        smalls = (
            grad[None, :3],
            grad[3][None],
            extra[:experts].T[None],
            extra[experts:experts + 2][None],
            extra[experts + 2, :table_slab][None],
        )
        final_in, final_out = own_experts(sets, got)
    else:
        blocks = [add_up(moved0), add_up(moved1)]
        arrived = []
        trade = ("section", "rep", "half")
        for a in range(2):
            message = jnp.where((y_at ^ a) == 0, blocks[0], blocks[1])
            for b in range(2):
                pairs = []
                for i in range(8):
                    si, xi, yi = i // 4, (i // 2) % 2, i % 2
                    pairs.append((i, (yi ^ a) * 4 + (xi ^ b) * 2 + si))
                arrived.append(lax.ppermute(message, trade, pairs))
        final_in, final_out = own_experts(after(sets, arrived[0]), got)
        arrived = after(arrived, final_in)
        smalls = list(call(
            functools.partial(finish_kernel, experts, slab, table_slab),
            [
                ((1, 3, slab, width), F32),
                ((1, slab, width), F32),
                ((1, experts, slab), F32),
                ((1, 2, slab), F32),
                ((1, table_slab), F32),
            ],
            [meta] + arrived,
            [SM] + [VM] * 4,
            moved=16 * slab * width,
            name="finish",
        ))
        smalls[2] = smalls[2].transpose(0, 2, 1)
    return (result_rows[None], *smalls, final_in[None, None], final_out[None, None])


def solution(mesh):
    sections, reps, shards = (mesh.shape[n] for n in ("section", "rep", "shard"))
    experts = shards // 2
    split = Mesh(
        mesh.devices.reshape(sections, reps, experts, 2), ("section", "rep", "expert", "half")
    )
    shard = ("expert", "half")
    in_specs = (
        P("section", None, ("rep",) + shard, None),
        P(None, ("rep",) + shard, None),
        P("section", None, ("rep",) + shard, None),
        P("section", None, shard, None),
        P("section", shard, None),
        P("section", shard, None),
        P("section", None, shard),
        P("section", shard),
        P("section", shard, None, "rep"),
        P("section", shard, "rep", None),
    )
    out_specs = (
        P("section", None, ("rep",) + shard, None),
        P("section", None, shard, None),
        P("section", shard, None),
        P("section", shard, None),
        P("section", None, shard),
        P("section", shard),
        P("section", shard, None, "rep"),
        P("section", shard, "rep", None),
    )
    return jax.shard_map(
        functools.partial(local, experts),
        mesh=split,
        in_specs=in_specs,
        out_specs=out_specs,
        check_vma=False,
    )
```

time: 375 us -> 313 us (0.83)
  local copies, waits for them, and re-layouts: 76.5 us -> 20.4 us
  other arithmetic: 29.3 us -> 10.3 us
  Pallas kernels: 55.3 us -> 65.7 us
  waiting for transfers between devices: 113 us -> 123 us
  matrix products: 8.27 us -> 0 us
  starting transfers between devices: 86 us -> 90.6 us
    unnamed x258 -> x144, local copies, waits for them, and re-layouts: 40.1 us -> 18.2 us
    ppermute x30 -> x36, waiting for transfers between devices: 48.4 us -> 63.2 us  [plane_swap(): return lax.ppermute(v, PLANE, [(i, i ^ mask) for i in range(4)])]
    pallas_call x17 -> x18, Pallas kernels: 55.3 us -> 65.7 us  [call(): pl.pallas_call(kernel, out_shape=[jax.ShapeDtypeStruct(shape, dtype) for...]
    ppermute x19 -> x25, waiting for transfers between devices: 0.05 us -> 8.36 us  [swap_section(): return lax.ppermute(v, 'section', [(0, 1), (1, 0)])]
    ppermute x34 -> x31, waiting for transfers between devices: 59.4 us -> 51.1 us  [shift(): return lax.ppermute(v, axis, [(i, (i + by) % n) for i in range(n)])]
    dot_general x5 -> x0, matrix products: 8.27 us -> none  [the longest x2 4.19 us: local(): jnp.dot(table.T, spread.T, preferred_element_type=F32)]
    slice x9 -> x2, local copies, waits for them, and re-layouts: 7.28 us -> 0.02 us  [local(): pieces += [plane_swap(over_y[:1], 2), plane_swap(over_x[1:], 1)]]
    broadcast_in_dim x7 -> x0, local copies, waits for them, and re-layouts: 6.89 us -> none  [the longest x2 2.71 us: local(): target[:, None]]
  transfers between devices with their start and end apart: 87 -> 96, of which waited for: 31 -> 55; matrix products, arithmetic and copies ran while one was open for 18% -> 3% of each run, Pallas kernels for 9% -> 11%
where the time goes in v2:
time: 313 us; the launch traced here: 312 us
  waiting for transfers between devices  123 us (39%)
  starting transfers between devices  90.6 us (29%)
  Pallas kernels  65.7 us (21%)
  local copies, waits for them, and re-layouts  20.4 us (7%)
  other arithmetic  10.3 us (3%)
    pallas_call x18, Pallas kernels, call(): pl.pallas_call(kernel, out_shape=[jax.ShapeDtypeStruct(shape, dtype) for...  65.7 us
    ppermute x36, waiting for transfers between devices, plane_swap(): return lax.ppermute(v, PLANE, [(i, i ^ mask) for i in range(4)])  63.2 us
    ppermute x31, waiting for transfers between devices, shift(): return lax.ppermute(v, axis, [(i, (i + by) % n) for i in range(n)])  51.1 us
    ppermute x31, starting transfers between devices, shift(): return lax.ppermute(v, axis, [(i, (i + by) % n) for i in range(n)])  41.4 us
    ppermute x36, starting transfers between devices, plane_swap(): return lax.ppermute(v, PLANE, [(i, i ^ mask) for i in range(4)])  41.4 us
    unnamed x144, local copies, waits for them, and re-layouts  18.2 us
    ppermute x25, waiting for transfers between devices, swap_section(): return lax.ppermute(v, 'section', [(0, 1), (1, 0)])  8.36 us
  transfers between devices with their start and end apart: 96, of which 55 were waited for; matrix products, arithmetic and copies ran while one was open for 3% of the time, Pallas kernels for 11%

profile of v2, /device:TPU:0, one launch (start us, length us, event | category | flops | bytes accessed | tf_op | source)
XLA Modules:
  0.0 311.9 jit_solution(16678303598719488520)
XLA Ops:
  2.6 3.0 collective-permute-start
  7.2 2.2 collective-permute-start.14
  10.8 3.6 %collective-permute-done.3.refs_8_.refs_14_.refs_24_.refs_22_ = bf16[2,96,768]{2,1,0:T(8,128)(2,1)S(1)} collective-permute-done((bf16[2,96,768]{2,1,0:T(8,128)(2,1)}, bf16[2,96,768]{2,1,0:T(8,128)(2,1)S(1)}, u32[]{:S(2)}, u32[]{:S(2)}) %collective-permute-start.3) | collective-permute-done | bytes 294944 | tf_op jit(solution)/shard_map/ppermute | solution.py:679
  14.3 2.3 collective-permute-start.6
  19.0 2.3 collective-permute-done.6
  32.5 5.7 %collective-permute-done.1.refs_18_.refs_24_.refs_34_.refs_32_ = bf16[2,96,768]{2,1,0:T(8,128)(2,1)} collective-permute-done((bf16[2,96,768]{2,1,0:T(8,128)(2,1)}, bf16[2,96,768]{2,1,0:T(8,128)(2,1)}, u32[]{:S(2)}, u32[]{:S(2)}) %collective-permute-start.1) | collective-permute-done | bytes 294944 | tf_op jit(solution)/shard_map/ppermute | solution.py:666
  42.0 5.2 %collective-permute-done.15.refs_15_.refs_21_.refs_31_.refs_29_ = bf16[2,96,768]{2,1,0:T(8,128)(2,1)S(1)} collective-permute-done((bf16[2,96,768]{2,1,0:T(8,128)(2,1)S(1)}, bf16[2,96,768]{2,1,0:T(8,128)(2,1)S(1)}, u32[]{:S(2)}, u32[]{:S(2)}) %collective-permute-start.15) | collective-permute-done | bytes 294944 | tf_op jit(solution)/shard_map/ppermute | solution.py:679
  54.2 3.4 %collective-permute-done.13.refs_13_.refs_19_.refs_29_.refs_27_ = bf16[2,96,768]{2,1,0:T(8,128)(2,1)S(1)} collective-permute-done((bf16[2,96,768]{2,1,0:T(8,128)(2,1)S(1)}, bf16[2,96,768]{2,1,0:T(8,128)(2,1)S(1)}, u32[]{:S(2)}, u32[]{:S(2)}) %collective-permute-start.13) | collective-permute-done | bytes 294944 | tf_op jit(solution)/shard_map/ppermute | solution.py:679
  59.2 4.9 %collective-permute-done.18.refs_19_.refs_25_.refs_35_.refs_33_ = bf16[2,96,768]{2,1,0:T(8,128)(2,1)S(1)} collective-permute-done((bf16[2,96,768]{2,1,0:T(8,128)(2,1)}, bf16[2,96,768]{2,1,0:T(8,128)(2,1)S(1)}, u32[]{:S(2)}, u32[]{:S(2)}) %collective-permute-start.18) | collective-permute-done | bytes 294944 | tf_op jit(solution)/shard_map/ppermute | solution.py:679
  66.6 2.4 collective-permute-done.30.refs_31_.refs_37_.refs_47_.refs_45_
  70.7 4.2 %collective-permute-done.20.refs_21_.refs_27_.refs_37_.refs_35_ = bf16[1,96,768]{2,1,0:T(8,128)(2,1)S(1)} collective-permute-done((bf16[1,96,768]{2,1,0:T(8,128)(2,1)S(1)}, bf16[1,96,768]{2,1,0:T(8,128)(2,1)S(1)}, u32[]{:S(2)}, u32[]{:S(2)}) %collective-permute-start.20) | collective-permute-done | bytes 147488 | tf_op jit(solution)/shard_map/ppermute | solution.py:679
  80.2 5.9 %attention_forward.2 = (bf16[64,768]{1,0:T(8,128)(2,1)}, bf16[3,64,768]{2,1,0:T(8,128)(2,1)}, f32[6,128,64]{2,1,0:T(8,128)}, bf16[64,768]{1,0:T(8,128)(2,1)}, f3...) custom-call(s32[9]{0:T(128)} %concatenate.10.refs_0_.meta, ...), custom_call_target="tpu_custom_call" | custom-call | flops 301989888 | bytes 4718592 | tf_op jit(solution)/shard_map/attention_forward/pallas_call | solution.py:652
  86.2 2.3 collective-permute-start.39
  90.0 2.5 collective-permute-done.38
  97.6 2.1 collective-permute-done.41.refs_2_
  102.6 3.3 %expert_forward.2 = (bf16[1,80,768]{2,1,0:T(8,128)(2,1)S(1)}, bf16[1,80,768]{2,1,0:T(8,128)(2,1)S(1)}, bf16[1,80,768]{2,1,0:T(8,128)(2,1)S(1)}, bf16[1,80,768]{2...) custom-call(s32[9]{0:T(128)S(1)} %copy-done.12, ...), custom_call_target="tpu_custom_call" | custom-call | flops 754974720 | bytes 2359296 | tf_op jit(solution)/shard_map/expert_forward/pallas_call | solution.py:652
  111.9 2.7 collective-permute-done.46.refs_1_
  121.5 2.8 collective-permute-done.50
  126.1 6.5 %attention_forward.3 = (bf16[64,768]{1,0:T(8,128)(2,1)}, bf16[3,64,768]{2,1,0:T(8,128)(2,1)}, f32[6,128,64]{2,1,0:T(8,128)}, bf16[64,768]{1,0:T(8,128)(2,1)}, f3...) custom-call(s32[9]{0:T(128)} %concatenate.10.refs_0_.meta, ...), custom_call_target="tpu_custom_call" | custom-call | flops 301989888 | bytes 4718592 | tf_op jit(solution)/shard_map/attention_forward/pallas_call | solution.py:652
  133.6 2.9 collective-permute-start.54
  136.5 2.6 collective-permute-done.52.refs_1_
  144.6 2.7 collective-permute-done.55.refs_2_
  148.4 3.0 collective-permute-done.57.refs_4_
  151.4 5.9 %expert_forward.3 = (bf16[2,80,768]{2,1,0:T(8,128)(2,1)S(1)}, bf16[2,80,768]{2,1,0:T(8,128)(2,1)S(1)}, bf16[2,80,768]{2,1,0:T(8,128)(2,1)S(1)}, bf16[2,80,768]{2...) custom-call(s32[9]{0:T(128)S(1)} %copy-done.13, ...), custom_call_target="tpu_custom_call" | custom-call | flops 1509949440 | bytes 2359296 | tf_op jit(solution)/shard_map/expert_forward/pallas_call | solution.py:652
  164.0 2.7 collective-permute-done.58.refs_1_
  167.7 3.0 collective-permute-done.60.refs_3_
  171.7 3.0 collective-permute-start.61
  176.8 3.3 %collective-permute-done.62.refs_21_ = bf16[2,24,768]{2,1,0:T(8,128)(2,1)S(1)} collective-permute-done((bf16[2,24,768]{2,1,0:T(8,128)(2,1)S(1)}, bf16[2,24,768]{2,1,0:T(8,128)(2,1)S(1)}, u32[]{:S(2)}, u32[]{:S(2)}) %collective-permute-start.62) | collective-permute-done | bytes 73760 | tf_op jit(solution)/shard_map/ppermute | solution.py:666
  181.8 9.0 %attention_backward.2 = (f32[64,768]{1,0:T(8,128)}, f32[16,768]{1,0:T(8,128)}, bf16[192,768]{1,0:T(8,128)(2,1)}, bf16[192,768]{1,0:T(8,128)(2,1)}, bf16[192,768]...) custom-call(s32[9]{0:T(128)} %concatenate.10.refs_0_.meta, ...), custom_call_target="tpu_custom_call" | custom-call | flops 603979776 | bytes 4718592 | tf_op jit(solution)/shard_map/attention_backward/pallas_call | solution.py:652
  191.9 2.7 collective-permute-start.66
  194.6 2.1 collective-permute-done.64
  205.4 6.5 %collective-permute-done.68.refs_3_ = bf16[1,80,768]{2,1,0:T(8,128)(2,1)S(1)} collective-permute-done((bf16[1,80,768]{2,1,0:T(8,128)(2,1)S(1)}, bf16[1,80,768]{2,1,0:T(8,128)(2,1)S(1)}, u32[]{:S(2)}, u32[]{:S(2)}) %collective-permute-start.68) | collective-permute-done | bytes 122912 | tf_op jit(solution)/shard_map/ppermute | solution.py:679
  214.9 4.0 %expert_backward.1 = (bf16[1,80,768]{2,1,0:T(8,128)(2,1)S(1)}, bf16[1,80,768]{2,1,0:T(8,128)(2,1)S(1)}, bf16[1,80,768]{2,1,0:T(8,128)(2,1)S(1)}, bf16[1,80,768]{...) custom-call(s32[9]{0:T(128)S(1)} %copy-done.14, ...), custom_call_target="tpu_custom_call" | custom-call | flops 754974720 | bytes 2359296 | tf_op jit(solution)/shard_map/expert_backward/pallas_call | solution.py:652
  221.2 3.7 %attention_grads.2 = (bf16[4,112,768]{2,1,0:T(8,128)(2,1)}, bf16[4,112,768]{2,1,0:T(8,128)(2,1)}) custom-call(s32[9]{0:T(128)} %concatenate.10.refs_0_.meta, bf16[192,768]{1,0:T(8,128)(2,1)} %get-tuple-element.205.refs_0_.refs_4_, bf16[192,768]{1,0:T(8,128)(2,1)} %copy-done.43, bf16[192,768]{1,0:T(8,128)(2,1)} %collective-permute-done.74.refs_2_.refs_6_, ...), custom_call_target="tpu_custom_call" | custom-call | flops 301989888 | bytes 4718592 | tf_op jit(solution)/shard_map/attention_grads/pallas_call | solution.py:652
  228.4 2.2 collective-permute-done.70.refs_1_
  232.1 2.4 collective-permute-done.72.refs_3_
  235.4 3.3 %collective-permute-start.76 = (bf16[1,24,768]{2,1,0:T(8,128)(2,1)S(1)}, bf16[1,24,768]{2,1,0:T(8,128)(2,1)S(1)}, u32[]{:S(2)}, u32[]{:S(2)}) collective-permute-start(bf16[1,24,768]{2,1,0:T(8,128)(2,1)S(1)} %get-tuple-element.217), channel_id=1, source_target_pairs={{0,6},{2,0},{4,2},{6,4},{1,7},{3,1},{5,3},{7,5},{8,14},{10,8},{12,... | collective-permute-start | bytes 110600 | tf_op jit(solution)/shard_map/ppermute | solution.py:666
  240.5 2.9 collective-permute-done.77
  248.2 8.2 %attention_backward.3 = (f32[64,768]{1,0:T(8,128)}, f32[16,768]{1,0:T(8,128)}, bf16[64,768]{1,0:T(8,128)(2,1)}, bf16[64,768]{1,0:T(8,128)(2,1)}, bf16[64,768]{1,0:T(8,128)(2,1)}, /*index=5*/bf16[64,768]{1,0:T(8,128)(2,1)}) custom-call(s32[9]{0:T(128)} %concatenate.10.refs_0_.meta, bf16[2,2,4,8,96]{4,3,2,1,0:T(8,128)(2,1)} %pad_maximum_fusion.1.refs_1_, ...), custom_call_target="tpu_custom_call" | custom-call | flops 603979776 | bytes 4718592 | tf_op jit(solution)/shard_map/attention_backward/pallas_call | solution.py:652
  256.4 3.2 %collective-permute-done.82 = bf16[112,768]{1,0:T(8,128)(2,1)S(1)} collective-permute-done((bf16[112,768]{1,0:T(8,128)(2,1)S(1)}, bf16[112,768]{1,0:T(8,128)(2,1)S(1)}, u32[]{:S(2)}, u32[]{:S(2)}) %collective-permute-start.82) | collective-permute-done | bytes 172064 | tf_op jit(solution)/shard_map/ppermute | solution.py:666
  264.4 5.3 %expert_gradients_sent.1 = bf16[2,768,768]{2,1,0:T(8,128)(2,1)} custom-call(s32[9]{0:T(128)} %concatenate.10.refs_0_.meta, bf16[320,768]{1,0:T(8,128)(2,1)} %copy-done.2, bf16[320,768]{1,0:T(8,128)(2,1)} %copy-done.9, bf16[320,768]{1,0:T(8,128)(2,1)} %copy-done.3, bf16[320,768]{1,0:T(8,128)(2,1)} %copy-done.8, bf16[320,768]{1,0:T(8,128)(2,1)} %copy-done.4, ...), custom_call_target="tpu_custom_call" | custom-call | flops 754974720 | bytes 4718592 | tf_op jit(solution)/shard_map/expert_gradients_sent/pallas_call | solution.py:652
  270.5 3.5 %attention_grads.3 = (bf16[4,112,768]{2,1,0:T(8,128)(2,1)}, bf16[4,112,768]{2,1,0:T(8,128)(2,1)}) custom-call(s32[9]{0:T(128)} %concatenate.10.refs_0_.meta, bf16[64,768]{1,0:T(8,128)(2,1)} %get-tuple-element.230.refs_0_, bf16[64,768]{1,0:T(8,128)(2,1)} %copy-done.56, bf16[64,768]{1,0:T(8,128)(2,1)} %copy-done.57, bf16[64,768]{1,0:T(8,128)(2,1)} %copy-done.58, ...), custom_call_target="tpu_custom_call" | custom-call | flops 301989888 | bytes 4718592 | tf_op jit(solution)/shard_map/attention_grads/pallas_call | solution.py:652
  278.0 2.2 collective-permute-start.89
  282.2 2.4 collective-permute-done.90
  284.6 11.4 %collective-permute-done.89 = bf16[112,768]{1,0:T(8,128)(2,1)S(1)} collective-permute-done((bf16[112,768]{1,0:T(8,128)(2,1)S(1)}, bf16[112,768]{1,0:T(8,128)(2,1)S(1)}, u32[]{:S(2)}, u32[]{:S(2)}) %collective-permute-start.89) | collective-permute-done | bytes 172064 | tf_op jit(solution)/shard_map/ppermute | solution.py:666
  298.2 2.2 collective-permute-start.93
  301.7 6.4 %expert_gradients_own.1 = (f32[768,768]{1,0:T(8,128)}, f32[768,768]{1,0:T(8,128)}) custom-call(s32[9]{0:T(128)} %concatenate.10.refs_0_.meta, bf16[320,768]{1,0:T(8,128)(2,1)} %copy-done.2, bf16[320,768]{1,0:T(8,128)(2,1)} %copy-done.9, bf16[320,768]{1,0:T(8,128)(2,1)} %copy-done.3, bf16[320,768]{1,0:T(8,128)(2,1)} %copy-done.8, bf16[320,768]{1,0:T(8,128)(2,1)} %copy-done.4, ...), custom_call_target="tpu_custom_call" | custom-call | flops 754974720 | bytes 4718592 | tf_op jit(solution)/shard_map/expert_gradients_own/pallas_call | solution.py:652
  309.6 2.3 finish.1
  (333 shorter events, 128.0 us)
Async XLA Ops:
  2.6 16.3 %collective-permute-start = (bf16[2,96,768]{2,1,0:T(8,128)(2,1)}, bf16[2,96,768]{2,1,0:T(8,128)(2,1)S(1)}, u32[]{:S(2)}, u32[]{:S(2)}) collective-permute-start(bf16[2,96,768]{2,1,0:T(8,128)(2,1)} %fusion.3), channel_id=1, source_target_pairs={{0,2},{2,4},{4,6},{6,0},{1,3},{3,5},{5,7},{7,1},{8,10},{10,12},{12... | collective-permute-start | bytes 884744 | tf_op jit(solution)/shard_map/ppermute | solution.py:666
  5.7 8.7 %collective-permute-start.3 = (bf16[2,96,768]{2,1,0:T(8,128)(2,1)}, bf16[2,96,768]{2,1,0:T(8,128)(2,1)S(1)}, u32[]{:S(2)}, u32[]{:S(2)}) collective-permute-start(bf16[2,96,768]{2,1,0:T(8,128)(2,1)} %fusion.3), channel_id=1, source_target_pairs={{0,1},{1,0},{8,9},{9,8},{2,3},{3,2},{10,11},{11,10},{4,5},{5,4},{1... | collective-permute-start | bytes 884744 | tf_op jit(solution)/shard_map/ppermute | solution.py:679
  7.2 23.3 %collective-permute-start.14 = (bf16[2,96,768]{2,1,0:T(8,128)(2,1)}, bf16[2,96,768]{2,1,0:T(8,128)(2,1)S(1)}, u32[]{:S(2)}, u32[]{:S(2)}) collective-permute-start(bf16[2,96,768]{2,1,0:T(8,128)(2,1)} %fusion.3), channel_id=1, source_target_pairs={{0,6},{2,0},{4,2},{6,4},{1,7},{3,1},{5,3},{7,5},{8,14},{10,8},{12,... | collective-permute-start | bytes 884744 | tf_op jit(solution)/shard_map/ppermute | solution.py:666
  14.3 7.0 %collective-permute-start.6 = (bf16[8,96]{1,0:T(8,128)(2,1)S(1)}, bf16[8,96]{1,0:T(8,128)(2,1)S(1)}, u32[]{:S(2)}, u32[]{:S(2)}) collective-permute-start(bf16[8,96]{1,0:T(8,128)(2,1)S(1)} %fusion.7), channel_id=1, source_target_pairs={{0,6},{2,0},{4,2},{6,4},{1,7},{3,1},{5,3},{7,5},{8,14},{10,8},{12,... | collective-permute-start | bytes 4616 | tf_op jit(solution)/shard_map/ppermute | solution.py:666
  21.3 27.9 %collective-permute-start.22 = (bf16[4,96,768]{2,1,0:T(8,128)(2,1)S(1)}, bf16[4,96,768]{2,1,0:T(8,128)(2,1)S(1)}, u32[]{:S(2)}, u32[]{:S(2)}) collective-permute-start(bf16[4,96,768]{2,1,0:T(8,128)(2,1)S(1)} %pad_maximum_fusion.refs_7_.refs_13_.refs_23_.refs_21_), channel_id=1, source_target_pairs={{0,16},{16,0},{1,17},{17,1},{2,18},{18,2},{3,19},{19,3},{4,20},{20... | collective-permute-start | bytes 1769480 | tf_op jit(solution)/shard_map/ppermute | solution.py:675
  21.3 16.9 %collective-permute-start.1 = (bf16[2,96,768]{2,1,0:T(8,128)(2,1)}, bf16[2,96,768]{2,1,0:T(8,128)(2,1)}, u32[]{:S(2)}, u32[]{:S(2)}) collective-permute-start(bf16[2,96,768]{2,1,0:T(8,128)(2,1)} %fusion.3), channel_id=1, source_target_pairs={{0,4},{2,6},{4,0},{6,2},{1,5},{3,7},{5,1},{7,3},{8,12},{10,14},{12... | collective-permute-start | bytes 884744 | tf_op jit(solution)/shard_map/ppermute | solution.py:666
  22.8 16.7 %collective-permute-start.10 = (bf16[2,96,768]{2,1,0:T(8,128)(2,1)S(1)}, bf16[2,96,768]{2,1,0:T(8,128)(2,1)}, u32[]{:S(2)}, u32[]{:S(2)}) collective-permute-start(bf16[2,96,768]{2,1,0:T(8,128)(2,1)S(1)} %collective-permute-done.3.refs_8_.refs_14_.refs_24_.refs_22_), channel_id=1, source_target_pairs={{0,8},{1,9},{8,0},{9,1},{2,10},{3,11},{10,2},{11,3},{4,12},{5,13},... | collective-permute-start | bytes 884744 | tf_op jit(solution)/shard_map/ppermute | solution.py:679
  30.5 11.0 %collective-permute-start.11 = (bf16[2,96,768]{2,1,0:T(8,128)(2,1)S(1)}, bf16[2,96,768]{2,1,0:T(8,128)(2,1)S(1)}, u32[]{:S(2)}, u32[]{:S(2)}) collective-permute-start(bf16[2,96,768]{2,1,0:T(8,128)(2,1)S(1)} %collective-permute-done.refs_10_.refs_16_.refs_26_.refs_24_), channel_id=1, source_target_pairs={{0,1},{1,0},{8,9},{9,8},{2,3},{3,2},{10,11},{11,10},{4,5},{5,4},{1... | collective-permute-start | bytes 884744 | tf_op jit(solution)/shard_map/ppermute | solution.py:679
  32.0 9.5 %collective-permute-start.12 = (bf16[2,96,768]{2,1,0:T(8,128)(2,1)S(1)}, bf16[2,96,768]{2,1,0:T(8,128)(2,1)S(1)}, u32[]{:S(2)}, u32[]{:S(2)}) collective-permute-start(bf16[2,96,768]{2,1,0:T(8,128)(2,1)S(1)} %collective-permute-done.refs_10_.refs_16_.refs_26_.refs_24_), channel_id=1, source_target_pairs={{0,8},{1,9},{8,0},{9,1},{2,10},{3,11},{10,2},{11,3},{4,12},{5,13},... | collective-permute-start | bytes 884744 | tf_op jit(solution)/shard_map/ppermute | solution.py:679
  38.3 8.9 %collective-permute-start.15 = (bf16[2,96,768]{2,1,0:T(8,128)(2,1)S(1)}, bf16[2,96,768]{2,1,0:T(8,128)(2,1)S(1)}, u32[]{:S(2)}, u32[]{:S(2)}) collective-permute-start(bf16[2,96,768]{2,1,0:T(8,128)(2,1)S(1)} %collective-permute-done.14.refs_14_.refs_20_.refs_30_.refs_28_), channel_id=1, source_target_pairs={{0,1},{1,0},{8,9},{9,8},{2,3},{3,2},{10,11},{11,10},{4,5},{5,4},{1... | collective-permute-start | bytes 884744 | tf_op jit(solution)/shard_map/ppermute | solution.py:679
  39.4 8.3 %collective-permute-start.16 = (bf16[2,96,768]{2,1,0:T(8,128)(2,1)S(1)}, bf16[2,96,768]{2,1,0:T(8,128)(2,1)S(1)}, u32[]{:S(2)}, u32[]{:S(2)}) collective-permute-start(bf16[2,96,768]{2,1,0:T(8,128)(2,1)S(1)} %collective-permute-done.14.refs_14_.refs_20_.refs_30_.refs_28_), channel_id=1, source_target_pairs={{0,8},{1,9},{8,0},{9,1},{2,10},{3,11},{10,2},{11,3},{4,12},{5,13},... | collective-permute-start | bytes 884744 | tf_op jit(solution)/shard_map/ppermute | solution.py:679
  41.5 11.2 %collective-permute-start.23 = (bf16[2,96,768]{2,1,0:T(8,128)(2,1)S(1)}, bf16[2,96,768]{2,1,0:T(8,128)(2,1)S(1)}, u32[]{:S(2)}, u32[]{:S(2)}) collective-permute-start(bf16[2,96,768]{2,1,0:T(8,128)(2,1)S(1)} %collective-permute-done.3.refs_8_.refs_14_.refs_24_.refs_22_), channel_id=1, source_target_pairs={{0,16},{16,0},{1,17},{17,1},{2,18},{18,2},{3,19},{19,3},{4,20},{20... | collective-permute-start | bytes 884744 | tf_op jit(solution)/shard_map/ppermute | solution.py:675
  41.5 12.0 %collective-permute-start.25 = (bf16[2,96,768]{2,1,0:T(8,128)(2,1)S(1)}, bf16[2,96,768]{2,1,0:T(8,128)(2,1)S(1)}, u32[]{:S(2)}, u32[]{:S(2)}) collective-permute-start(bf16[2,96,768]{2,1,0:T(8,128)(2,1)S(1)} %collective-permute-done.refs_10_.refs_16_.refs_26_.refs_24_), channel_id=1, source_target_pairs={{0,16},{16,0},{1,17},{17,1},{2,18},{18,2},{3,19},{19,3},{4,20},{20... | collective-permute-start | bytes 884744 | tf_op jit(solution)/shard_map/ppermute | solution.py:675
  47.2 7.0 %collective-permute-start.29 = (bf16[2,96,768]{2,1,0:T(8,128)(2,1)S(1)}, bf16[2,96,768]{2,1,0:T(8,128)(2,1)S(1)}, u32[]{:S(2)}, u32[]{:S(2)}) collective-permute-start(bf16[2,96,768]{2,1,0:T(8,128)(2,1)S(1)} %collective-permute-done.14.refs_14_.refs_20_.refs_30_.refs_28_), channel_id=1, source_target_pairs={{0,16},{16,0},{1,17},{17,1},{2,18},{18,2},{3,19},{19,3},{4,20},{20... | collective-permute-start | bytes 884744 | tf_op jit(solution)/shard_map/ppermute | solution.py:675
  47.7 9.9 %collective-permute-start.13 = (bf16[2,96,768]{2,1,0:T(8,128)(2,1)S(1)}, bf16[2,96,768]{2,1,0:T(8,128)(2,1)S(1)}, u32[]{:S(2)}, u32[]{:S(2)}) collective-permute-start(bf16[2,96,768]{2,1,0:T(8,128)(2,1)S(1)} %collective-permute-done.11.refs_11_.refs_17_.refs_27_.refs_25_), channel_id=1, source_target_pairs={{0,8},{1,9},{8,0},{9,1},{2,10},{3,11},{10,2},{11,3},{4,12},{5,13},... | collective-permute-start | bytes 884744 | tf_op jit(solution)/shard_map/ppermute | solution.py:679
  49.2 10.0 %collective-permute-start.17 = (bf16[2,96,768]{2,1,0:T(8,128)(2,1)S(1)}, bf16[2,96,768]{2,1,0:T(8,128)(2,1)}, u32[]{:S(2)}, u32[]{:S(2)}) collective-permute-start(bf16[2,96,768]{2,1,0:T(8,128)(2,1)S(1)} %collective-permute-done.16.refs_16_.refs_22_.refs_32_.refs_30_), channel_id=1, source_target_pairs={{0,1},{1,0},{8,9},{9,8},{2,3},{3,2},{10,11},{11,10},{4,5},{5,4},{1... | collective-permute-start | bytes 884744 | tf_op jit(solution)/shard_map/ppermute | solution.py:679
  52.6 11.5 %collective-permute-start.18 = (bf16[2,96,768]{2,1,0:T(8,128)(2,1)}, bf16[2,96,768]{2,1,0:T(8,128)(2,1)S(1)}, u32[]{:S(2)}, u32[]{:S(2)}) collective-permute-start(bf16[2,96,768]{2,1,0:T(8,128)(2,1)} %collective-permute-done.1.refs_18_.refs_24_.refs_34_.refs_32_), channel_id=1, source_target_pairs={{0,1},{1,0},{8,9},{9,8},{2,3},{3,2},{10,11},{11,10},{4,5},{5,4},{1... | collective-permute-start | bytes 884744 | tf_op jit(solution)/shard_map/ppermute | solution.py:679
  53.5 10.6 %collective-permute-start.19 = (bf16[2,96,768]{2,1,0:T(8,128)(2,1)}, bf16[2,96,768]{2,1,0:T(8,128)(2,1)S(1)}, u32[]{:S(2)}, u32[]{:S(2)}) collective-permute-start(bf16[2,96,768]{2,1,0:T(8,128)(2,1)} %collective-permute-done.1.refs_18_.refs_24_.refs_34_.refs_32_), channel_id=1, source_target_pairs={{0,8},{1,9},{8,0},{9,1},{2,10},{3,11},{10,2},{11,3},{4,12},{5,13},... | collective-permute-start | bytes 884744 | tf_op jit(solution)/shard_map/ppermute | solution.py:679
  54.2 10.5 %collective-permute-start.24 = (bf16[2,96,768]{2,1,0:T(8,128)(2,1)}, bf16[2,96,768]{2,1,0:T(8,128)(2,1)S(1)}, u32[]{:S(2)}, u32[]{:S(2)}) collective-permute-start(bf16[2,96,768]{2,1,0:T(8,128)(2,1)} %collective-permute-done.10.refs_9_.refs_15_.refs_25_.refs_23_), channel_id=1, source_target_pairs={{0,16},{16,0},{1,17},{17,1},{2,18},{18,2},{3,19},{19,3},{4,20},{20... | collective-permute-start | bytes 884744 | tf_op jit(solution)/shard_map/ppermute | solution.py:675
  57.6 7.1 %collective-permute-start.26 = (bf16[2,96,768]{2,1,0:T(8,128)(2,1)S(1)}, bf16[2,96,768]{2,1,0:T(8,128)(2,1)S(1)}, u32[]{:S(2)}, u32[]{:S(2)}) collective-permute-start(bf16[2,96,768]{2,1,0:T(8,128)(2,1)S(1)} %collective-permute-done.11.refs_11_.refs_17_.refs_27_.refs_25_), channel_id=1, source_target_pairs={{0,16},{16,0},{1,17},{17,1},{2,18},{18,2},{3,19},{19,3},{4,20},{20... | collective-permute-start | bytes 884744 | tf_op jit(solution)/shard_map/ppermute | solution.py:675
  64.1 33.5 %collective-permute-start.44 = (bf16[768,768]{1,0:T(8,128)(2,1)S(1)}, bf16[768,768]{1,0:T(8,128)(2,1)}, u32[]{:S(2)}, u32[]{:S(2)}) collective-permute-start(bf16[768,768]{1,0:T(8,128)(2,1)S(1)} %bitcast.88), channel_id=1, source_target_pairs={{0,16},{16,0},{1,17},{17,1},{2,18},{18,2},{3,19},{19,3},{4,20},{20... | collective-permute-start | bytes 3538952 | tf_op jit(solution)/shard_map/ppermute | solution.py:675
  64.1 33.5 %collective-permute-start.45 = (bf16[768,768]{1,0:T(8,128)(2,1)}, bf16[768,768]{1,0:T(8,128)(2,1)}, u32[]{:S(2)}, u32[]{:S(2)}) collective-permute-start(bf16[768,768]{1,0:T(8,128)(2,1)} %bitcast.32.refs_7_), channel_id=1, source_target_pairs={{0,16},{16,0},{1,17},{17,1},{2,18},{18,2},{3,19},{19,3},{4,20},{20... | collective-permute-start | bytes 3538952 | tf_op jit(solution)/shard_map/ppermute | solution.py:675
  70.7 6.6 %collective-permute-start.28 = (bf16[2,96,768]{2,1,0:T(8,128)(2,1)S(1)}, bf16[2,96,768]{2,1,0:T(8,128)(2,1)S(1)}, u32[]{:S(2)}, u32[]{:S(2)}) collective-permute-start(bf16[2,96,768]{2,1,0:T(8,128)(2,1)S(1)} %collective-permute-done.13.refs_13_.refs_19_.refs_29_.refs_27_), channel_id=1, source_target_pairs={{0,16},{16,0},{1,17},{17,1},{2,18},{18,2},{3,19},{19,3},{4,20},{20... | collective-permute-start | bytes 884744 | tf_op jit(solution)/shard_map/ppermute | solution.py:675
  86.2 6.4 %collective-permute-start.38 = (bf16[24,768]{1,0:T(8,128)(2,1)}, bf16[24,768]{1,0:T(8,128)(2,1)S(1)}, u32[]{:S(2)}, u32[]{:S(2)}) collective-permute-start(bf16[24,768]{1,0:T(8,128)(2,1)} %get-tuple-element.154), channel_id=1, source_target_pairs={{0,2},{2,4},{4,6},{6,0},{1,3},{3,5},{5,7},{7,1},{8,10},{10,12},{12... | collective-permute-start | bytes 110600 | tf_op jit(solution)/shard_map/ppermute | solution.py:666
  86.2 6.8 %collective-permute-start.39 = (bf16[24,768]{1,0:T(8,128)(2,1)}, bf16[24,768]{1,0:T(8,128)(2,1)S(1)}, u32[]{:S(2)}, u32[]{:S(2)}) collective-permute-start(bf16[24,768]{1,0:T(8,128)(2,1)} %get-tuple-element.155), channel_id=1, source_target_pairs={{0,4},{2,6},{4,0},{6,2},{1,5},{3,7},{5,1},{7,3},{8,12},{10,14},{12... | collective-permute-start | bytes 110600 | tf_op jit(solution)/shard_map/ppermute | solution.py:666
  132.6 6.4 %collective-permute-start.52 = (bf16[2,24,768]{2,1,0:T(8,128)(2,1)}, bf16[2,24,768]{2,1,0:T(8,128)(2,1)S(1)}, u32[]{:S(2)}, u32[]{:S(2)}) collective-permute-start(bf16[2,24,768]{2,1,0:T(8,128)(2,1)} %get-tuple-element.176), channel_id=1, source_target_pairs={{0,2},{2,4},{4,6},{6,0},{1,3},{3,5},{5,7},{7,1},{8,10},{10,12},{12... | collective-permute-start | bytes 221192 | tf_op jit(solution)/shard_map/ppermute | solution.py:666
  143.3 8.1 %collective-permute-start.57 = (bf16[2,80,768]{2,1,0:T(8,128)(2,1)S(1)}, bf16[2,80,768]{2,1,0:T(8,128)(2,1)S(1)}, u32[]{:S(2)}, u32[]{:S(2)}) collective-permute-start(bf16[2,80,768]{2,1,0:T(8,128)(2,1)S(1)} %pack.4.refs_1_), channel_id=1, source_target_pairs={{0,9},{1,8},{8,1},{9,0},{2,11},{3,10},{10,3},{11,2},{4,13},{5,12},... | collective-permute-start | bytes 737288 | tf_op jit(solution)/shard_map/ppermute | solution.py:679
  162.7 8.1 %collective-permute-start.60 = (bf16[2,80,768]{2,1,0:T(8,128)(2,1)S(1)}, bf16[2,80,768]{2,1,0:T(8,128)(2,1)S(1)}, u32[]{:S(2)}, u32[]{:S(2)}) collective-permute-start(bf16[2,80,768]{2,1,0:T(8,128)(2,1)S(1)} %get-tuple-element.182), channel_id=1, source_target_pairs={{0,9},{1,8},{8,1},{9,0},{2,11},{3,10},{10,3},{11,2},{4,13},{5,12},... | collective-permute-start | bytes 737288 | tf_op jit(solution)/shard_map/ppermute | solution.py:679
  199.5 21.1 %collective-permute-start.73 = (bf16[192,768]{1,0:T(8,128)(2,1)}, bf16[192,768]{1,0:T(8,128)(2,1)S(1)}, u32[]{:S(2)}, u32[]{:S(2)}) collective-permute-start(bf16[192,768]{1,0:T(8,128)(2,1)} %get-tuple-element.202), channel_id=1, source_target_pairs={{0,1},{1,0},{8,9},{9,8},{2,3},{3,2},{10,11},{11,10},{4,5},{5,4},{1... | collective-permute-start | bytes 884744 | tf_op jit(solution)/shard_map/ppermute | solution.py:679
  200.4 20.1 %collective-permute-start.74 = (bf16[192,768]{1,0:T(8,128)(2,1)}, bf16[192,768]{1,0:T(8,128)(2,1)}, u32[]{:S(2)}, u32[]{:S(2)}) collective-permute-start(bf16[192,768]{1,0:T(8,128)(2,1)} %get-tuple-element.203), channel_id=1, source_target_pairs={{0,8},{1,9},{8,0},{9,1},{2,10},{3,11},{10,2},{11,3},{4,12},{5,13},... | collective-permute-start | bytes 884744 | tf_op jit(solution)/shard_map/ppermute | solution.py:679
  201.4 19.1 %collective-permute-start.75 = (bf16[192,768]{1,0:T(8,128)(2,1)}, bf16[192,768]{1,0:T(8,128)(2,1)}, u32[]{:S(2)}, u32[]{:S(2)}) collective-permute-start(bf16[192,768]{1,0:T(8,128)(2,1)} %get-tuple-element.204), channel_id=1, source_target_pairs={{0,9},{1,8},{8,1},{9,0},{2,11},{3,10},{10,3},{11,2},{4,13},{5,12},... | collective-permute-start | bytes 884744 | tf_op jit(solution)/shard_map/ppermute | solution.py:679
  203.0 8.9 %collective-permute-start.68 = (bf16[1,80,768]{2,1,0:T(8,128)(2,1)S(1)}, bf16[1,80,768]{2,1,0:T(8,128)(2,1)S(1)}, u32[]{:S(2)}, u32[]{:S(2)}) collective-permute-start(bf16[1,80,768]{2,1,0:T(8,128)(2,1)S(1)} %pack.5.refs_1_), channel_id=1, source_target_pairs={{0,8},{1,9},{8,0},{9,1},{2,10},{3,11},{10,2},{11,3},{4,12},{5,13},... | collective-permute-start | bytes 368648 | tf_op jit(solution)/shard_map/ppermute | solution.py:679
  204.1 9.6 %collective-permute-start.69 = (bf16[1,80,768]{2,1,0:T(8,128)(2,1)S(1)}, bf16[1,80,768]{2,1,0:T(8,128)(2,1)S(1)}, u32[]{:S(2)}, u32[]{:S(2)}) collective-permute-start(bf16[1,80,768]{2,1,0:T(8,128)(2,1)S(1)} %pack.5.refs_1_), channel_id=1, source_target_pairs={{0,9},{1,8},{8,1},{9,0},{2,11},{3,10},{10,3},{11,2},{4,13},{5,12},... | collective-permute-start | bytes 368648 | tf_op jit(solution)/shard_map/ppermute | solution.py:679
  225.0 14.3 %collective-permute-start.80 = (bf16[4,112,768]{2,1,0:T(8,128)(2,1)}, bf16[4,112,768]{2,1,0:T(8,128)(2,1)S(1)}, u32[]{:S(2)}, u32[]{:S(2)}) collective-permute-start(bf16[4,112,768]{2,1,0:T(8,128)(2,1)} %get-tuple-element.211), channel_id=1, source_target_pairs={{0,16},{16,0},{1,17},{17,1},{2,18},{18,2},{3,19},{19,3},{4,20},{20... | collective-permute-start | bytes 2064392 | tf_op jit(solution)/shard_map/ppermute | solution.py:675
  226.9 7.6 %collective-permute-start.72 = (bf16[1,80,768]{2,1,0:T(8,128)(2,1)S(1)}, bf16[1,80,768]{2,1,0:T(8,128)(2,1)S(1)}, u32[]{:S(2)}, u32[]{:S(2)}) collective-permute-start(bf16[1,80,768]{2,1,0:T(8,128)(2,1)S(1)} %get-tuple-element.200), channel_id=1, source_target_pairs={{0,9},{1,8},{8,1},{9,0},{2,11},{3,10},{10,3},{11,2},{4,13},{5,12},... | collective-permute-start | bytes 368648 | tf_op jit(solution)/shard_map/ppermute | solution.py:679
  244.6 11.8 %collective-permute-start.83 = (bf16[112,768]{1,0:T(8,128)(2,1)S(1)}, bf16[112,768]{1,0:T(8,128)(2,1)S(1)}, u32[]{:S(2)}, u32[]{:S(2)}) collective-permute-start(bf16[112,768]{1,0:T(8,128)(2,1)S(1)} %get-tuple-element.229), channel_id=1, source_target_pairs={{0,6},{2,0},{4,2},{6,4},{1,7},{3,1},{5,3},{7,5},{8,14},{10,8},{12,... | collective-permute-start | bytes 516104 | tf_op jit(solution)/shard_map/ppermute | solution.py:666
  245.0 14.6 %collective-permute-start.82 = (bf16[112,768]{1,0:T(8,128)(2,1)S(1)}, bf16[112,768]{1,0:T(8,128)(2,1)S(1)}, u32[]{:S(2)}, u32[]{:S(2)}) collective-permute-start(bf16[112,768]{1,0:T(8,128)(2,1)S(1)} %get-tuple-element.228), channel_id=1, source_target_pairs={{0,4},{2,6},{4,0},{6,2},{1,5},{3,7},{5,1},{7,3},{8,12},{10,14},{12... | collective-permute-start | bytes 516104 | tf_op jit(solution)/shard_map/ppermute | solution.py:666
  245.5 14.1 %collective-permute-start.81 = (bf16[112,768]{1,0:T(8,128)(2,1)S(1)}, bf16[112,768]{1,0:T(8,128)(2,1)S(1)}, u32[]{:S(2)}, u32[]{:S(2)}) collective-permute-start(bf16[112,768]{1,0:T(8,128)(2,1)S(1)} %get-tuple-element.227), channel_id=1, source_target_pairs={{0,2},{2,4},{4,6},{6,0},{1,3},{3,5},{5,7},{7,1},{8,10},{10,12},{12... | collective-permute-start | bytes 516104 | tf_op jit(solution)/shard_map/ppermute | solution.py:666
  260.6 9.3 %collective-permute-start.85 = (bf16[64,768]{1,0:T(8,128)(2,1)}, bf16[64,768]{1,0:T(8,128)(2,1)S(1)}, u32[]{:S(2)}, u32[]{:S(2)}) collective-permute-start(bf16[64,768]{1,0:T(8,128)(2,1)} %get-tuple-element.232), channel_id=1, source_target_pairs={{0,8},{1,9},{8,0},{9,1},{2,10},{3,11},{10,2},{11,3},{4,12},{5,13},... | collective-permute-start | bytes 294920 | tf_op jit(solution)/shard_map/ppermute | solution.py:679
  261.6 8.3 %collective-permute-start.86 = (bf16[64,768]{1,0:T(8,128)(2,1)}, bf16[64,768]{1,0:T(8,128)(2,1)S(1)}, u32[]{:S(2)}, u32[]{:S(2)}) collective-permute-start(bf16[64,768]{1,0:T(8,128)(2,1)} %get-tuple-element.233), channel_id=1, source_target_pairs={{0,9},{1,8},{8,1},{9,0},{2,11},{3,10},{10,3},{11,2},{4,13},{5,12},... | collective-permute-start | bytes 294920 | tf_op jit(solution)/shard_map/ppermute | solution.py:679
  269.8 31.9 %collective-permute-start.95 = (bf16[2,768,768]{2,1,0:T(8,128)(2,1)}, bf16[2,768,768]{2,1,0:T(8,128)(2,1)}, u32[]{:S(2)}, u32[]{:S(2)}) collective-permute-start(bf16[2,768,768]{2,1,0:T(8,128)(2,1)} %expert_gradients_sent.1), channel_id=1, source_target_pairs={{0,16},{16,0},{1,17},{17,1},{2,18},{18,2},{3,19},{19,3},{4,20},{20... | collective-permute-start | bytes 7077896 | tf_op jit(solution)/shard_map/ppermute | solution.py:675
  277.9 6.7 %collective-permute-start.90 = (bf16[112,768]{1,0:T(8,128)(2,1)S(1)}, bf16[112,768]{1,0:T(8,128)(2,1)S(1)}, u32[]{:S(2)}, u32[]{:S(2)}) collective-permute-start(bf16[112,768]{1,0:T(8,128)(2,1)S(1)} %get-tuple-element.276), channel_id=1, source_target_pairs={{0,6},{2,0},{4,2},{6,4},{1,7},{3,1},{5,3},{7,5},{8,14},{10,8},{12,... | collective-permute-start | bytes 516104 | tf_op jit(solution)/shard_map/ppermute | solution.py:666
  278.0 18.0 %collective-permute-start.89 = (bf16[112,768]{1,0:T(8,128)(2,1)S(1)}, bf16[112,768]{1,0:T(8,128)(2,1)S(1)}, u32[]{:S(2)}, u32[]{:S(2)}) collective-permute-start(bf16[112,768]{1,0:T(8,128)(2,1)S(1)} %get-tuple-element.277), channel_id=1, source_target_pairs={{0,4},{2,6},{4,0},{6,2},{1,5},{3,7},{5,1},{7,3},{8,12},{10,14},{12... | collective-permute-start | bytes 516104 | tf_op jit(solution)/shard_map/ppermute | solution.py:666
  280.1 15.9 %collective-permute-start.88 = (bf16[112,768]{1,0:T(8,128)(2,1)S(1)}, bf16[112,768]{1,0:T(8,128)(2,1)S(1)}, u32[]{:S(2)}, u32[]{:S(2)}) collective-permute-start(bf16[112,768]{1,0:T(8,128)(2,1)S(1)} %get-tuple-element.275), channel_id=1, source_target_pairs={{0,2},{2,4},{4,6},{6,0},{1,3},{3,5},{5,7},{7,1},{8,10},{10,12},{12... | collective-permute-start | bytes 516104 | tf_op jit(solution)/shard_map/ppermute | solution.py:666
  282.1 14.8 %collective-permute-start.79 = (f32[64,768]{1,0:T(8,128)S(1)}, f32[64,768]{1,0:T(8,128)S(1)}, u32[]{:S(2)}, u32[]{:S(2)}) collective-permute-start(f32[64,768]{1,0:T(8,128)S(1)} %broadcast_select_fusion.2), channel_id=1, source_target_pairs={{0,16},{16,0},{1,17},{17,1},{2,18},{18,2},{3,19},{19,3},{4,20},{20... | collective-permute-start | bytes 589832 | tf_op jit(solution)/shard_map/ppermute | solution.py:675
  297.0 11.1 %collective-permute-start.92 = (bf16[112,768]{1,0:T(8,128)(2,1)S(1)}, bf16[112,768]{1,0:T(8,128)(2,1)S(1)}, u32[]{:S(2)}, u32[]{:S(2)}) collective-permute-start(bf16[112,768]{1,0:T(8,128)(2,1)S(1)} %broadcast_select_fusion.1), channel_id=1, source_target_pairs={{0,8},{1,24},{8,0},{9,16},{16,9},{17,25},{24,1},{25,17},{2,10},{3,... | collective-permute-start | bytes 516104 | tf_op jit(solution)/shard_map/ppermute | solution.py:1098
  298.2 9.9 %collective-permute-start.93 = (bf16[112,768]{1,0:T(8,128)(2,1)S(1)}, bf16[112,768]{1,0:T(8,128)(2,1)S(1)}, u32[]{:S(2)}, u32[]{:S(2)}) collective-permute-start(bf16[112,768]{1,0:T(8,128)(2,1)S(1)} %get-tuple-element.272), channel_id=1, source_target_pairs={{0,16},{1,0},{8,24},{9,8},{16,17},{17,1},{24,25},{25,9},{2,18},{3,... | collective-permute-start | bytes 516104 | tf_op jit(solution)/shard_map/ppermute | solution.py:1098
  300.4 8.6 %collective-permute-start.94 = (bf16[112,768]{1,0:T(8,128)(2,1)S(1)}, bf16[112,768]{1,0:T(8,128)(2,1)S(1)}, u32[]{:S(2)}, u32[]{:S(2)}) collective-permute-start(bf16[112,768]{1,0:T(8,128)(2,1)S(1)} %get-tuple-element.272), channel_id=1, source_target_pairs={{0,24},{1,8},{8,16},{9,0},{16,25},{17,9},{24,17},{25,1},{2,26},{3,... | collective-permute-start | bytes 516104 | tf_op jit(solution)/shard_map/ppermute | solution.py:1098
  (120 other events, 1067.6 us)

commit v3 on v2

--- a/solution.py
+++ b/solution.py
@@ -24,6 +24,7 @@
 VM = pl.BlockSpec(memory_space=pltpu.VMEM)
 SM = pl.BlockSpec(memory_space=pltpu.SMEM)
 ANY = pl.BlockSpec(memory_space=pl.ANY)
+HBM = pl.BlockSpec(memory_space=pltpu.HBM)
 
 
 def up(n, m):
@@ -293,18 +294,22 @@
     qkv_ref[0] = q
     qkv_ref[1] = k
     qkv_ref[2] = v
-    contexts = []
-    for pair in range(PAIRS):
-        cols = slice(pair * LANES, (pair + 1) * LANES)
-        bias = jnp.concatenate(
-            [position_bias(by_offset, 2 * pair + n, rows) for n in range(2)], axis=0
-        )
-        sc = mm_nt(stack_heads(q[:, cols], rows), k[:, cols]) * SCALE + bias
-        sc = jnp.where(keep, sc, NEGATIVE)
-        e = jnp.exp(sc - jnp.max(sc, axis=-1, keepdims=True))
-        p = e / jnp.sum(e, axis=-1, keepdims=True)
-        p_ref[pair] = p
-        contexts.append(pick_heads(mm(p.astype(BF), v[:, cols]), rows))
+    pairs = range(PAIRS)
+    cols = [slice(pair * LANES, (pair + 1) * LANES) for pair in pairs]
+    sc = [mm_nt(stack_heads(q[:, c], rows), k[:, c]) for c in cols]
+    bias = [
+        jnp.concatenate([position_bias(by_offset, 2 * pair + n, rows) for n in range(2)], axis=0)
+        for pair in pairs
+    ]
+    sc = [jnp.where(keep, sc[pair] * SCALE + bias[pair], NEGATIVE) for pair in pairs]
+    top = [jnp.max(v, axis=-1, keepdims=True) for v in sc]
+    e = [jnp.exp(sc[pair] - top[pair]) for pair in pairs]
+    total = [jnp.sum(v, axis=-1, keepdims=True) for v in e]
+    p = [e[pair] / total[pair] for pair in pairs]
+    for pair in pairs:
+        p_ref[pair] = p[pair]
+    contexts = [mm(p[pair].astype(BF), v[:, cols[pair]]) for pair in pairs]
+    contexts = [pick_heads(both, rows) for both in contexts]
     ctx = jnp.concatenate(contexts, axis=1).astype(BF)
     ctx_ref[...] = ctx
     mid = x + mm(ctx, scr[3])
@@ -385,20 +390,25 @@
     right[3] = da
     w.wait(meta, scr, sem)
     dctx = mm_nt(da, scr[3]).astype(BF)
-    grads = ([], [], [])
     sums[...] = jnp.zeros_like(sums)
-    for pair in range(PAIRS):
-        cols = slice(pair * LANES, (pair + 1) * LANES)
-        p = p_ref[pair]
-        qs = stack_heads(qkv_ref[0, :, cols], rows)
-        ds_heads = stack_heads(dctx[:, cols], rows)
-        dp = mm_nt(ds_heads, qkv_ref[2, :, cols])
-        ds = (p * (dp - jnp.sum(p * dp, axis=-1, keepdims=True))).astype(BF)
-        for n, line in enumerate(offset_sums(ds, flip[...])):
+    pairs = range(PAIRS)
+    cols = [slice(pair * LANES, (pair + 1) * LANES) for pair in pairs]
+    ds_heads = [stack_heads(dctx[:, c], rows) for c in cols]
+    dp = [mm_nt(ds_heads[pair], qkv_ref[2, :, cols[pair]]) for pair in pairs]
+    p = [p_ref[pair] for pair in pairs]
+    dv = [mm_tn(p[pair].astype(BF), ds_heads[pair]) for pair in pairs]
+    weighted = [jnp.sum(p[pair] * dp[pair], axis=-1, keepdims=True) for pair in pairs]
+    ds = [(p[pair] * (dp[pair] - weighted[pair])).astype(BF) for pair in pairs]
+    dq = [mm(ds[pair], qkv_ref[1, :, cols[pair]]) for pair in pairs]
+    dq = [pick_heads(both, rows) * SCALE for both in dq]
+    dk = [
+        mm_tn(ds[pair], stack_heads(qkv_ref[0, :, cols[pair]], rows)) * SCALE for pair in pairs
+    ]
+    by_line = [offset_sums(ds[pair], flip[...]) for pair in pairs]
+    for pair in pairs:
+        for n, line in enumerate(by_line[pair]):
             sums[2 * pair + n:2 * pair + n + 1] = line
-        grads[0].append(pick_heads(mm(ds, qkv_ref[1, :, cols]) * SCALE, rows))
-        grads[1].append(mm_tn(ds, qs) * SCALE)
-        grads[2].append(mm_tn(p.astype(BF), ds_heads))
+    grads = (dq, dk, dv)
     dh1 = None
     for j in range(3):
         dj = jnp.concatenate(grads[j], axis=1).astype(BF)
@@ -647,16 +657,18 @@
 
 
 def call(
-    kernel, out_shapes, args, specs, scratch=(), flops=0, moved=0, name=None, vmem=62, hbm=0
+    kernel, out_shapes, args, specs, scratch=(), us=1, name=None, vmem=62, hbm=0
 ):
     return pl.pallas_call(
         kernel,
         out_shape=[jax.ShapeDtypeStruct(shape, dtype) for shape, dtype in out_shapes],
         in_specs=specs,
-        out_specs=[VM] * (len(out_shapes) - hbm) + [ANY] * hbm,
+        out_specs=[VM] * (len(out_shapes) - hbm) + [HBM] * hbm,
         scratch_shapes=list(scratch),
         compiler_params=pltpu.CompilerParams(vmem_limit_bytes=vmem * 2**20),
-        cost_estimate=pl.CostEstimate(flops=flops, bytes_accessed=moved, transcendentals=0),
+        cost_estimate=pl.CostEstimate(
+            flops=us * 10**9, bytes_accessed=us * 3 * 10**6, transcendentals=0
+        ),
         name=name,
     )(*args)
 
@@ -810,7 +822,7 @@
             [((parts, packed, width), BF)],
             arrived,
             [VM] * len(arrived),
-            moved=4 * packed * width,
+            us=1,
             name="pack",
             vmem=8,
         )
@@ -830,7 +842,7 @@
             shapes,
             sums,
             [VM] * 4,
-            moved=4 * packed * width,
+            us=1,
             name="unpack",
             vmem=8,
         )
@@ -862,8 +874,7 @@
             args + attn_w[layer],
             specs,
             Weights.scratch(plan, width),
-            flops=8 * rows * width * width,
-            moved=8 * width * width,
+            us=6,
             name="attention_forward",
         )
         names = ["h1", "qkv", "p", "ctx", "mid", "h2", "probs", "x1", "y0"][:fixed]
@@ -892,8 +903,7 @@
                 pltpu.VMEM((4, rows, width), BF),
                 pltpu.VMEM((16, LANES), F32),
             ],
-            flops=16 * rows * width * width,
-            moved=8 * width * width,
+            us=8 if layer else 2,
             name="attention_backward",
         )
 
@@ -917,8 +927,7 @@
             + [pltpu.VMEM(*shape) for shape in shapes[4:]]
             + [pltpu.SemaphoreType.DMA((len(shapes) - 4,))],
             hbm=len(shapes) - 4,
-            flops=4 * all_rows * width * ff * parts,
-            moved=4 * width * ff,
+            us=4,
             name="expert_forward",
             vmem=20,
         )
@@ -933,9 +942,9 @@
             [((experts, slab + 16, width), BF)] * 2,
             [meta] + rights + lefts + [ex],
             [SM] + [VM] * 9,
-            flops=8 * rows * width * width,
-            moved=8 * width * width,
+            us=4,
             name="attention_grads",
+            vmem=20,
         )
         return keep, send
 
@@ -979,8 +988,7 @@
         + [pltpu.VMEM(*shape) for shape in shapes[4:]]
         + [pltpu.SemaphoreType.DMA((2,))],
         hbm=2,
-        flops=4 * all_rows * width * ff,
-        moved=4 * width * ff,
+        us=4,
         name="expert_backward",
             vmem=20,
     )
@@ -990,7 +998,7 @@
         beside = after(beside, partial[3])
         halves1 = attention_grads(beside, beside, rows, ex1)
         returned = come_back(partial, 1, halves1)
-        moved1 = along_z(after(sum_cores(*halves1), *returned))
+        moved1 = along_z(after(sum_cores(*halves1), returned[0]))
     else:
         returned = come_back(partial, 1)
     outs = backward(0, kept0, x0, dx1.astype(BF), returned, [kept1["y0"]])
@@ -1022,8 +1030,7 @@
         [meta] + sets,
         [SM] + [ANY] * 8,
         bring_scratch,
-        flops=4 * all_rows * width * ff,
-        moved=8 * width * ff,
+        us=5,
         name="expert_gradients_sent",
     )
     got = swap_section(sent)
@@ -1035,8 +1042,7 @@
             [meta] + sets + [got],
             [SM] + [ANY] * 8 + [VM],
             bring_scratch,
-            flops=4 * all_rows * width * ff,
-            moved=8 * width * ff,
+            us=6,
             name="expert_gradients_own",
         )
 
@@ -1109,8 +1115,9 @@
             ],
             [meta] + arrived,
             [SM] + [VM] * 4,
-            moved=16 * slab * width,
+            us=2,
             name="finish",
+            vmem=8,
         ))
         smalls[2] = smalls[2].transpose(0, 2, 1)
     return (result_rows[None], *smalls, final_in[None, None], final_out[None, None])

time: 313 us -> 295 us (0.942)
  local copies, waits for them, and re-layouts: 20.4 us -> 10.7 us
  Pallas kernels: 65.7 us -> 59.2 us
  other arithmetic: 10.3 us -> 6.49 us
    unnamed x144 -> x166, local copies, waits for them, and re-layouts: 18.2 us -> 8.51 us
    pallas_call x18, Pallas kernels: 65.7 us -> 59.2 us  [call(): pl.pallas_call(kernel, out_shape=[jax.ShapeDtypeStruct(shape, dtype) for...]
  transfers between devices with their start and end apart: 96 -> 96, of which waited for: 55 -> 52; matrix products, arithmetic and copies ran while one was open for 3% -> 3% of each run, Pallas kernels for 11% -> 11%
where the time goes in v3:
time: 295 us; the launch traced here: 294 us
  waiting for transfers between devices  124 us (42%)
  starting transfers between devices  92.6 us (31%)
  Pallas kernels  59.2 us (20%)
  local copies, waits for them, and re-layouts  10.7 us (4%)
  other arithmetic  6.49 us (2%)
    ppermute x36, waiting for transfers between devices, plane_swap(): return lax.ppermute(v, PLANE, [(i, i ^ mask) for i in range(4)])  60.3 us
    pallas_call x18, Pallas kernels, call(): pl.pallas_call(kernel, out_shape=[jax.ShapeDtypeStruct(shape, dtype) for...  59.2 us
    ppermute x31, waiting for transfers between devices, shift(): return lax.ppermute(v, axis, [(i, (i + by) % n) for i in range(n)])  53.8 us
    ppermute x31, starting transfers between devices, shift(): return lax.ppermute(v, axis, [(i, (i + by) % n) for i in range(n)])  42.4 us
    ppermute x36, starting transfers between devices, plane_swap(): return lax.ppermute(v, PLANE, [(i, i ^ mask) for i in range(4)])  42.2 us
    unnamed x166, local copies, waits for them, and re-layouts  8.51 us
    ppermute x25, waiting for transfers between devices, swap_section(): return lax.ppermute(v, 'section', [(0, 1), (1, 0)])  7.98 us
  transfers between devices with their start and end apart: 96, of which 52 were waited for; matrix products, arithmetic and copies ran while one was open for 3% of the time, Pallas kernels for 11%

profile of v3, /device:TPU:0, one launch (start us, length us, event | category | flops | bytes accessed | tf_op | source)
XLA Modules:
  0.0 294.3 jit_solution(9233800700069923546)
XLA Ops:
  1.9 3.1 %collective-permute-start = (bf16[2,96,768]{2,1,0:T(8,128)(2,1)S(1)}, bf16[2,96,768]{2,1,0:T(8,128)(2,1)S(1)}, u32[]{:S(2)}, u32[]{:S(2)}) collective-permute-start(bf16[2,96,768]{2,1,0:T(8,128)(2,1)S(1)} %fusion.3), channel_id=1, source_target_pairs={{0,2},{2,4},{4,6},{6,0},{1,3},{3,5},{5,7},{7,1},{8,10},{10,12},{12... | collective-permute-start | bytes 884744 | tf_op jit(solution)/shard_map/ppermute | solution.py:678
  6.5 2.2 collective-permute-start.14
  10.1 3.3 %collective-permute-done.3.refs_8_.refs_14_.refs_24_.refs_22_ = bf16[2,96,768]{2,1,0:T(8,128)(2,1)S(1)} collective-permute-done((bf16[2,96,768]{2,1,0:T(8,128)(2,1)S(1)}, bf16[2,96,768]{2,1,0:T(8,128)(2,1)S(1)}, u32[]{:S(2)}, u32[]{:S(2)}) %collective-permute-start.3) | collective-permute-done | bytes 294944 | tf_op jit(solution)/shard_map/ppermute | solution.py:691
  13.5 2.4 collective-permute-start.6
  18.1 2.3 collective-permute-done.6
  30.9 9.1 %collective-permute-done.1.refs_18_.refs_24_.refs_34_.refs_32_ = bf16[2,96,768]{2,1,0:T(8,128)(2,1)S(1)} collective-permute-done((bf16[2,96,768]{2,1,0:T(8,128)(2,1)S(1)}, bf16[2,96,768]{2,1,0:T(8,128)(2,1)S(1)}, u32[]{:S(2)}, u32[]{:S(2)}) %collective-permute-start.1) | collective-permute-done | bytes 294944 | tf_op jit(solution)/shard_map/ppermute | solution.py:678
  44.5 4.4 %collective-permute-done.15.refs_15_.refs_21_.refs_31_.refs_29_ = bf16[2,96,768]{2,1,0:T(8,128)(2,1)S(1)} collective-permute-done((bf16[2,96,768]{2,1,0:T(8,128)(2,1)S(1)}, bf16[2,96,768]{2,1,0:T(8,128)(2,1)S(1)}, u32[]{:S(2)}, u32[]{:S(2)}) %collective-permute-start.15) | collective-permute-done | bytes 294944 | tf_op jit(solution)/shard_map/ppermute | solution.py:691
  54.6 5.8 %collective-permute-done.13.refs_13_.refs_19_.refs_29_.refs_27_ = bf16[2,96,768]{2,1,0:T(8,128)(2,1)S(1)} collective-permute-done((bf16[2,96,768]{2,1,0:T(8,128)(2,1)S(1)}, bf16[2,96,768]{2,1,0:T(8,128)(2,1)S(1)}, u32[]{:S(2)}, u32[]{:S(2)}) %collective-permute-start.13) | collective-permute-done | bytes 294944 | tf_op jit(solution)/shard_map/ppermute | solution.py:691
  62.0 4.5 %collective-permute-done.18.refs_19_.refs_25_.refs_35_.refs_33_ = bf16[2,96,768]{2,1,0:T(8,128)(2,1)S(1)} collective-permute-done((bf16[2,96,768]{2,1,0:T(8,128)(2,1)S(1)}, bf16[2,96,768]{2,1,0:T(8,128)(2,1)S(1)}, u32[]{:S(2)}, u32[]{:S(2)}) %collective-permute-start.18) | collective-permute-done | bytes 294944 | tf_op jit(solution)/shard_map/ppermute | solution.py:691
  69.8 4.3 %collective-permute-done.20.refs_21_.refs_27_.refs_37_.refs_35_ = bf16[1,96,768]{2,1,0:T(8,128)(2,1)S(1)} collective-permute-done((bf16[1,96,768]{2,1,0:T(8,128)(2,1)S(1)}, bf16[1,96,768]{2,1,0:T(8,128)(2,1)S(1)}, u32[]{:S(2)}, u32[]{:S(2)}) %collective-permute-start.20) | collective-permute-done | bytes 147488 | tf_op jit(solution)/shard_map/ppermute | solution.py:691
  77.9 3.0 %collective-permute-done.32.refs_33_.refs_39_.refs_49_.refs_47_ = bf16[2,96,768]{2,1,0:T(8,128)(2,1)} collective-permute-done((bf16[2,96,768]{2,1,0:T(8,128)(2,1)}, bf16[2,96,768]{2,1,0:T(8,128)(2,1)}, u32[]{:S(2)}, u32[]{:S(2)}) %collective-permute-start.32) | collective-permute-done | bytes 294944 | tf_op jit(solution)/shard_map/ppermute | solution.py:687
  81.0 6.1 %attention_forward.2 = (bf16[64,768]{1,0:T(8,128)(2,1)}, bf16[3,64,768]{2,1,0:T(8,128)(2,1)}, f32[6,128,64]{2,1,0:T(8,128)}, bf16[64,768]{1,0:T(8,128)(2,1)}, f3...) custom-call(s32[9]{0:T(128)} %concatenate.10.refs_0_.meta, ...), custom_call_target="tpu_custom_call" | custom-call | flops 6000000000 | bytes 18000000 | tf_op jit(solution)/shard_map/attention_forward/pallas_call | solution.py:662
  88.7 2.2 collective-permute-start.40
  90.9 2.5 collective-permute-done.38
  99.8 2.1 collective-permute-done.42.refs_3_
  101.9 2.0 collective-permute-done.43.refs_4_
  103.9 3.3 %expert_forward.2 = (bf16[1,80,768]{2,1,0:T(8,128)(2,1)S(1)}, bf16[1,80,768]{2,1,0:T(8,128)(2,1)S(1)}, bf16[1,80,768]{2,1,0:T(8,128)(2,1)S(1)}, bf16[1,80,768]{2...) custom-call(s32[9]{0:T(128)S(1)} %copy-done.2, ...), custom_call_target="tpu_custom_call" | custom-call | flops 4000000000 | bytes 12000000 | tf_op jit(solution)/shard_map/expert_forward/pallas_call | solution.py:662
  110.8 1.9 collective-permute-done.46.refs_1_
  113.8 2.4 collective-permute-done.48.refs_3_
  121.4 2.4 collective-permute-done.50
  125.7 6.6 %attention_forward.3 = (bf16[64,768]{1,0:T(8,128)(2,1)}, bf16[3,64,768]{2,1,0:T(8,128)(2,1)}, f32[6,128,64]{2,1,0:T(8,128)}, bf16[64,768]{1,0:T(8,128)(2,1)}, f3...) custom-call(s32[9]{0:T(128)} %concatenate.10.refs_0_.meta, ...), custom_call_target="tpu_custom_call" | custom-call | flops 6000000000 | bytes 18000000 | tf_op jit(solution)/shard_map/attention_forward/pallas_call | solution.py:662
  133.4 2.8 collective-permute-start.54
  136.2 2.6 collective-permute-done.52.refs_1_
  144.4 3.1 %collective-permute-done.55.refs_2_ = bf16[2,80,768]{2,1,0:T(8,128)(2,1)S(1)} collective-permute-done((bf16[2,80,768]{2,1,0:T(8,128)(2,1)S(1)}, bf16[2,80,768]{2,1,0:T(8,128)(2,1)S(1)}, u32[]{:S(2)}, u32[]{:S(2)}) %collective-permute-start.55) | collective-permute-done | bytes 245792 | tf_op jit(solution)/shard_map/ppermute | solution.py:691
  147.6 3.6 %collective-permute-done.57.refs_4_ = bf16[2,80,768]{2,1,0:T(8,128)(2,1)S(1)} collective-permute-done((bf16[2,80,768]{2,1,0:T(8,128)(2,1)S(1)}, bf16[2,80,768]{2,1,0:T(8,128)(2,1)S(1)}, u32[]{:S(2)}, u32[]{:S(2)}) %collective-permute-start.57) | collective-permute-done | bytes 245792 | tf_op jit(solution)/shard_map/ppermute | solution.py:691
  151.2 5.9 %expert_forward.3 = (bf16[2,80,768]{2,1,0:T(8,128)(2,1)S(1)}, bf16[2,80,768]{2,1,0:T(8,128)(2,1)S(1)}, bf16[2,80,768]{2,1,0:T(8,128)(2,1)S(1)}, bf16[2,80,768]{2...) custom-call(s32[9]{0:T(128)S(1)} %copy-done.3, ...), custom_call_target="tpu_custom_call" | custom-call | flops 4000000000 | bytes 12000000 | tf_op jit(solution)/shard_map/expert_forward/pallas_call | solution.py:662
  160.7 2.7 collective-permute-done.58.refs_1_
  163.9 3.6 %collective-permute-done.60.refs_3_ = bf16[2,80,768]{2,1,0:T(8,128)(2,1)S(1)} collective-permute-done((bf16[2,80,768]{2,1,0:T(8,128)(2,1)S(1)}, bf16[2,80,768]{2,1,0:T(8,128)(2,1)S(1)}, u32[]{:S(2)}, u32[]{:S(2)}) %collective-permute-start.60) | collective-permute-done | bytes 245792 | tf_op jit(solution)/shard_map/ppermute | solution.py:691
  168.5 3.0 %collective-permute-start.61 = (bf16[2,24,768]{2,1,0:T(8,128)(2,1)S(1)}, bf16[2,24,768]{2,1,0:T(8,128)(2,1)S(1)}, u32[]{:S(2)}, u32[]{:S(2)}) collective-permute-start(bf16[2,24,768]{2,1,0:T(8,128)(2,1)S(1)} %get-tuple-element.184), channel_id=1, source_target_pairs={{0,6},{2,0},{4,2},{6,4},{1,7},{3,1},{5,3},{7,5},{8,14},{10,8},{12,... | collective-permute-start | bytes 221192 | tf_op jit(solution)/shard_map/ppermute | solution.py:678
  173.5 3.3 %collective-permute-done.62.refs_21_ = bf16[2,24,768]{2,1,0:T(8,128)(2,1)S(1)} collective-permute-done((bf16[2,24,768]{2,1,0:T(8,128)(2,1)S(1)}, bf16[2,24,768]{2,1,0:T(8,128)(2,1)S(1)}, u32[]{:S(2)}, u32[]{:S(2)}) %collective-permute-start.62) | collective-permute-done | bytes 73760 | tf_op jit(solution)/shard_map/ppermute | solution.py:678
  178.5 7.8 %attention_backward.2 = (f32[64,768]{1,0:T(8,128)}, f32[16,768]{1,0:T(8,128)}, bf16[192,768]{1,0:T(8,128)(2,1)}, bf16[192,768]{1,0:T(8,128)(2,1)}, bf16[192,768]...) custom-call(s32[9]{0:T(128)} %concatenate.10.refs_0_.meta, ...), custom_call_target="tpu_custom_call" | custom-call | flops 8000000000 | bytes 24000000 | tf_op jit(solution)/shard_map/attention_backward/pallas_call | solution.py:662
  187.5 2.7 collective-permute-start.66
  190.2 2.1 collective-permute-done.64
  201.9 4.0 %expert_backward.1 = (bf16[1,80,768]{2,1,0:T(8,128)(2,1)S(1)}, bf16[1,80,768]{2,1,0:T(8,128)(2,1)S(1)}, bf16[1,80,768]{2,1,0:T(8,128)(2,1)S(1)}, bf16[1,80,768]{...) custom-call(s32[9]{0:T(128)S(1)} %copy-done.4, bf16[1,80,768]{2,1,0:T(8,128)(2,1)S(1)} %pack.5.refs_1_, ...), custom_call_target="tpu_custom_call" | custom-call | flops 4000000000 | bytes 12000000 | tf_op jit(solution)/shard_map/expert_backward/pallas_call | solution.py:662
  206.0 2.9 collective-permute-done.75.refs_3_.refs_7_
  217.3 2.8 collective-permute-done.72.refs_3_
  221.0 3.3 %collective-permute-start.76 = (bf16[1,24,768]{2,1,0:T(8,128)(2,1)S(1)}, bf16[1,24,768]{2,1,0:T(8,128)(2,1)S(1)}, u32[]{:S(2)}, u32[]{:S(2)}) collective-permute-start(bf16[1,24,768]{2,1,0:T(8,128)(2,1)S(1)} %get-tuple-element.217), channel_id=1, source_target_pairs={{0,6},{2,0},{4,2},{6,4},{1,7},{3,1},{5,3},{7,5},{8,14},{10,8},{12,... | collective-permute-start | bytes 110600 | tf_op jit(solution)/shard_map/ppermute | solution.py:678
  225.7 3.5 %collective-permute-start.83 = (bf16[112,768]{1,0:T(8,128)(2,1)}, bf16[112,768]{1,0:T(8,128)(2,1)S(1)}, u32[]{:S(2)}, u32[]{:S(2)}) collective-permute-start(bf16[112,768]{1,0:T(8,128)(2,1)} %get-tuple-element.229), channel_id=1, source_target_pairs={{0,6},{2,0},{4,2},{6,4},{1,7},{3,1},{5,3},{7,5},{8,14},{10,8},{12,... | collective-permute-start | bytes 516104 | tf_op jit(solution)/shard_map/ppermute | solution.py:678
  231.2 7.1 %attention_backward.3 = (f32[64,768]{1,0:T(8,128)}, f32[16,768]{1,0:T(8,128)}, bf16[64,768]{1,0:T(8,128)(2,1)}, bf16[64,768]{1,0:T(8,128)(2,1)}, bf16[64,768]{1,0:T(8,128)(2,1)}, /*index=5*/bf16[64,768]{1,0:T(8,128)(2,1)}) custom-call(s32[9]{0:T(128)} %concatenate.10.refs_0_.meta, bf16[2,2,4,8,96]{4,3,2,1,0:T(8,128)(2,1)} %pad_maximum_fusion.1.refs_1_, ...), custom_call_target="tpu_custom_call" | custom-call | flops 2000000000 | bytes 6000000 | tf_op jit(solution)/shard_map/attention_backward/pallas_call | solution.py:662
  238.4 6.2 %collective-permute-done.82 = bf16[112,768]{1,0:T(8,128)(2,1)S(1)} collective-permute-done((bf16[112,768]{1,0:T(8,128)(2,1)S(1)}, bf16[112,768]{1,0:T(8,128)(2,1)S(1)}, u32[]{:S(2)}, u32[]{:S(2)}) %collective-permute-start.82) | collective-permute-done | bytes 172064 | tf_op jit(solution)/shard_map/ppermute | solution.py:678
  250.4 5.4 %expert_gradients_sent.1 = bf16[2,768,768]{2,1,0:T(8,128)(2,1)} custom-call(s32[9]{0:T(128)} %concatenate.10.refs_0_.meta, bf16[320,768]{1,0:T(8,128)(2,1)} %copy-done.25, bf16[320,768]{1,0:T(8,128)(2,1)} %copy-done.20, bf16[320,768]{1,0:T(8,128)(2,1)} %copy-done.26, bf16[320,768]{1,0:T(8,128)(2,1)} %copy-done.19, bf16[320,768]{1,0:T(8,128)(2,1)} %copy-done.21, ...), custom_call_target="tpu_custom_call" | custom-call | flops 5000000000 | bytes 15000000 | tf_op jit(solution)/shard_map/expert_gradients_sent/pallas_call | solution.py:662
  258.1 3.4 %collective-permute-done.87 = bf16[4,112,768]{2,1,0:T(8,128)(2,1)S(1)} collective-permute-done((bf16[4,112,768]{2,1,0:T(8,128)(2,1)S(1)}, bf16[4,112,768]{2,1,0:T(8,128)(2,1)S(1)}, u32[]{:S(2)}, u32[]{:S(2)}) %collective-permute-start.87) | collective-permute-done | bytes 688160 | tf_op jit(solution)/shard_map/ppermute | solution.py:687
  261.8 1.9 collective-permute-start.89
  263.6 1.9 collective-permute-start.88
  265.7 2.9 collective-permute-done.90
  268.6 10.7 %collective-permute-done.89 = bf16[112,768]{1,0:T(8,128)(2,1)S(1)} collective-permute-done((bf16[112,768]{1,0:T(8,128)(2,1)S(1)}, bf16[112,768]{1,0:T(8,128)(2,1)S(1)}, u32[]{:S(2)}, u32[]{:S(2)}) %collective-permute-start.89) | collective-permute-done | bytes 172064 | tf_op jit(solution)/shard_map/ppermute | solution.py:678
  281.1 1.9 collective-permute-start.93
  284.7 6.3 %expert_gradients_own.1 = (f32[768,768]{1,0:T(8,128)}, f32[768,768]{1,0:T(8,128)}) custom-call(s32[9]{0:T(128)} %concatenate.10.refs_0_.meta, bf16[320,768]{1,0:T(8,128)(2,1)} %copy-done.25, bf16[320,768]{1,0:T(8,128)(2,1)} %copy-done.20, bf16[320,768]{1,0:T(8,128)(2,1)} %copy-done.26, bf16[320,768]{1,0:T(8,128)(2,1)} %copy-done.19, ...), custom_call_target="tpu_custom_call" | custom-call | flops 6000000000 | bytes 18000000 | tf_op jit(solution)/shard_map/expert_gradients_own/pallas_call | solution.py:662
  (355 shorter events, 109.1 us)
Async XLA Ops:
  1.9 22.2 %collective-permute-start = (bf16[2,96,768]{2,1,0:T(8,128)(2,1)S(1)}, bf16[2,96,768]{2,1,0:T(8,128)(2,1)S(1)}, u32[]{:S(2)}, u32[]{:S(2)}) collective-permute-start(bf16[2,96,768]{2,1,0:T(8,128)(2,1)S(1)} %fusion.3), channel_id=1, source_target_pairs={{0,2},{2,4},{4,6},{6,0},{1,3},{3,5},{5,7},{7,1},{8,10},{10,12},{12... | collective-permute-start | bytes 884744 | tf_op jit(solution)/shard_map/ppermute | solution.py:678
  5.0 8.5 %collective-permute-start.3 = (bf16[2,96,768]{2,1,0:T(8,128)(2,1)S(1)}, bf16[2,96,768]{2,1,0:T(8,128)(2,1)S(1)}, u32[]{:S(2)}, u32[]{:S(2)}) collective-permute-start(bf16[2,96,768]{2,1,0:T(8,128)(2,1)S(1)} %fusion.3), channel_id=1, source_target_pairs={{0,1},{1,0},{8,9},{9,8},{2,3},{3,2},{10,11},{11,10},{4,5},{5,4},{1... | collective-permute-start | bytes 884744 | tf_op jit(solution)/shard_map/ppermute | solution.py:691
  6.5 22.7 %collective-permute-start.14 = (bf16[2,96,768]{2,1,0:T(8,128)(2,1)S(1)}, bf16[2,96,768]{2,1,0:T(8,128)(2,1)S(1)}, u32[]{:S(2)}, u32[]{:S(2)}) collective-permute-start(bf16[2,96,768]{2,1,0:T(8,128)(2,1)S(1)} %fusion.3), channel_id=1, source_target_pairs={{0,6},{2,0},{4,2},{6,4},{1,7},{3,1},{5,3},{7,5},{8,14},{10,8},{12,... | collective-permute-start | bytes 884744 | tf_op jit(solution)/shard_map/ppermute | solution.py:678
  13.5 7.0 %collective-permute-start.6 = (bf16[8,96]{1,0:T(8,128)(2,1)S(1)}, bf16[8,96]{1,0:T(8,128)(2,1)S(1)}, u32[]{:S(2)}, u32[]{:S(2)}) collective-permute-start(bf16[8,96]{1,0:T(8,128)(2,1)S(1)} %fusion.7), channel_id=1, source_target_pairs={{0,6},{2,0},{4,2},{6,4},{1,7},{3,1},{5,3},{7,5},{8,14},{10,8},{12,... | collective-permute-start | bytes 4616 | tf_op jit(solution)/shard_map/ppermute | solution.py:678
  20.4 7.2 %collective-permute-start.2 = (bf16[64,768]{1,0:T(8,128)(2,1)S(1)}, bf16[64,768]{1,0:T(8,128)(2,1)S(1)}, u32[]{:S(2)}, u32[]{:S(2)}) collective-permute-start(bf16[64,768]{1,0:T(8,128)(2,1)S(1)} %dynamic-slice_bitcast_fusion), channel_id=1, source_target_pairs={{0,16},{16,0},{1,17},{17,1},{2,18},{18,2},{3,19},{19,3},{4,20},{20... | collective-permute-start | bytes 294920 | tf_op jit(solution)/shard_map/ppermute | solution.py:687
  24.1 27.8 %collective-permute-start.22 = (bf16[4,96,768]{2,1,0:T(8,128)(2,1)S(1)}, bf16[4,96,768]{2,1,0:T(8,128)(2,1)S(1)}, u32[]{:S(2)}, u32[]{:S(2)}) collective-permute-start(bf16[4,96,768]{2,1,0:T(8,128)(2,1)S(1)} %pad_maximum_fusion.refs_7_.refs_13_.refs_23_.refs_21_), channel_id=1, source_target_pairs={{0,16},{16,0},{1,17},{17,1},{2,18},{18,2},{3,19},{19,3},{4,20},{20... | collective-permute-start | bytes 1769480 | tf_op jit(solution)/shard_map/ppermute | solution.py:687
  25.6 14.4 %collective-permute-start.1 = (bf16[2,96,768]{2,1,0:T(8,128)(2,1)S(1)}, bf16[2,96,768]{2,1,0:T(8,128)(2,1)S(1)}, u32[]{:S(2)}, u32[]{:S(2)}) collective-permute-start(bf16[2,96,768]{2,1,0:T(8,128)(2,1)S(1)} %fusion.3), channel_id=1, source_target_pairs={{0,4},{2,6},{4,0},{6,2},{1,5},{3,7},{5,1},{7,3},{8,12},{10,14},{12... | collective-permute-start | bytes 884744 | tf_op jit(solution)/shard_map/ppermute | solution.py:678
  26.1 15.7 %collective-permute-start.10 = (bf16[2,96,768]{2,1,0:T(8,128)(2,1)S(1)}, bf16[2,96,768]{2,1,0:T(8,128)(2,1)S(1)}, u32[]{:S(2)}, u32[]{:S(2)}) collective-permute-start(bf16[2,96,768]{2,1,0:T(8,128)(2,1)S(1)} %collective-permute-done.3.refs_8_.refs_14_.refs_24_.refs_22_), channel_id=1, source_target_pairs={{0,8},{1,9},{8,0},{9,1},{2,10},{3,11},{10,2},{11,3},{4,12},{5,13},... | collective-permute-start | bytes 884744 | tf_op jit(solution)/shard_map/ppermute | solution.py:691
  27.6 15.6 %collective-permute-start.11 = (bf16[2,96,768]{2,1,0:T(8,128)(2,1)S(1)}, bf16[2,96,768]{2,1,0:T(8,128)(2,1)S(1)}, u32[]{:S(2)}, u32[]{:S(2)}) collective-permute-start(bf16[2,96,768]{2,1,0:T(8,128)(2,1)S(1)} %collective-permute-done.refs_10_.refs_16_.refs_26_.refs_24_), channel_id=1, source_target_pairs={{0,1},{1,0},{8,9},{9,8},{2,3},{3,2},{10,11},{11,10},{4,5},{5,4},{1... | collective-permute-start | bytes 884744 | tf_op jit(solution)/shard_map/ppermute | solution.py:691
  30.4 13.7 %collective-permute-start.12 = (bf16[2,96,768]{2,1,0:T(8,128)(2,1)S(1)}, bf16[2,96,768]{2,1,0:T(8,128)(2,1)S(1)}, u32[]{:S(2)}, u32[]{:S(2)}) collective-permute-start(bf16[2,96,768]{2,1,0:T(8,128)(2,1)S(1)} %collective-permute-done.refs_10_.refs_16_.refs_26_.refs_24_), channel_id=1, source_target_pairs={{0,8},{1,9},{8,0},{9,1},{2,10},{3,11},{10,2},{11,3},{4,12},{5,13},... | collective-permute-start | bytes 884744 | tf_op jit(solution)/shard_map/ppermute | solution.py:691
  40.0 8.9 %collective-permute-start.15 = (bf16[2,96,768]{2,1,0:T(8,128)(2,1)S(1)}, bf16[2,96,768]{2,1,0:T(8,128)(2,1)S(1)}, u32[]{:S(2)}, u32[]{:S(2)}) collective-permute-start(bf16[2,96,768]{2,1,0:T(8,128)(2,1)S(1)} %collective-permute-done.14.refs_14_.refs_20_.refs_30_.refs_28_), channel_id=1, source_target_pairs={{0,1},{1,0},{8,9},{9,8},{2,3},{3,2},{10,11},{11,10},{4,5},{5,4},{1... | collective-permute-start | bytes 884744 | tf_op jit(solution)/shard_map/ppermute | solution.py:691
  41.8 8.7 %collective-permute-start.16 = (bf16[2,96,768]{2,1,0:T(8,128)(2,1)S(1)}, bf16[2,96,768]{2,1,0:T(8,128)(2,1)S(1)}, u32[]{:S(2)}, u32[]{:S(2)}) collective-permute-start(bf16[2,96,768]{2,1,0:T(8,128)(2,1)S(1)} %collective-permute-done.14.refs_14_.refs_20_.refs_30_.refs_28_), channel_id=1, source_target_pairs={{0,8},{1,9},{8,0},{9,1},{2,10},{3,11},{10,2},{11,3},{4,12},{5,13},... | collective-permute-start | bytes 884744 | tf_op jit(solution)/shard_map/ppermute | solution.py:691
  43.3 9.4 %collective-permute-start.23 = (bf16[2,96,768]{2,1,0:T(8,128)(2,1)S(1)}, bf16[2,96,768]{2,1,0:T(8,128)(2,1)}, u32[]{:S(2)}, u32[]{:S(2)}) collective-permute-start(bf16[2,96,768]{2,1,0:T(8,128)(2,1)S(1)} %collective-permute-done.3.refs_8_.refs_14_.refs_24_.refs_22_), channel_id=1, source_target_pairs={{0,16},{16,0},{1,17},{17,1},{2,18},{18,2},{3,19},{19,3},{4,20},{20... | collective-permute-start | bytes 884744 | tf_op jit(solution)/shard_map/ppermute | solution.py:687
  44.1 9.9 %collective-permute-start.25 = (bf16[2,96,768]{2,1,0:T(8,128)(2,1)S(1)}, bf16[2,96,768]{2,1,0:T(8,128)(2,1)S(1)}, u32[]{:S(2)}, u32[]{:S(2)}) collective-permute-start(bf16[2,96,768]{2,1,0:T(8,128)(2,1)S(1)} %collective-permute-done.refs_10_.refs_16_.refs_26_.refs_24_), channel_id=1, source_target_pairs={{0,16},{16,0},{1,17},{17,1},{2,18},{18,2},{3,19},{19,3},{4,20},{20... | collective-permute-start | bytes 884744 | tf_op jit(solution)/shard_map/ppermute | solution.py:687
  50.5 9.9 %collective-permute-start.13 = (bf16[2,96,768]{2,1,0:T(8,128)(2,1)S(1)}, bf16[2,96,768]{2,1,0:T(8,128)(2,1)S(1)}, u32[]{:S(2)}, u32[]{:S(2)}) collective-permute-start(bf16[2,96,768]{2,1,0:T(8,128)(2,1)S(1)} %collective-permute-done.11.refs_11_.refs_17_.refs_27_.refs_25_), channel_id=1, source_target_pairs={{0,8},{1,9},{8,0},{9,1},{2,10},{3,11},{10,2},{11,3},{4,12},{5,13},... | collective-permute-start | bytes 884744 | tf_op jit(solution)/shard_map/ppermute | solution.py:691
  51.9 10.1 %collective-permute-start.17 = (bf16[2,96,768]{2,1,0:T(8,128)(2,1)S(1)}, bf16[2,96,768]{2,1,0:T(8,128)(2,1)}, u32[]{:S(2)}, u32[]{:S(2)}) collective-permute-start(bf16[2,96,768]{2,1,0:T(8,128)(2,1)S(1)} %collective-permute-done.16.refs_16_.refs_22_.refs_32_.refs_30_), channel_id=1, source_target_pairs={{0,1},{1,0},{8,9},{9,8},{2,3},{3,2},{10,11},{11,10},{4,5},{5,4},{1... | collective-permute-start | bytes 884744 | tf_op jit(solution)/shard_map/ppermute | solution.py:691
  52.7 13.8 %collective-permute-start.18 = (bf16[2,96,768]{2,1,0:T(8,128)(2,1)S(1)}, bf16[2,96,768]{2,1,0:T(8,128)(2,1)S(1)}, u32[]{:S(2)}, u32[]{:S(2)}) collective-permute-start(bf16[2,96,768]{2,1,0:T(8,128)(2,1)S(1)} %collective-permute-done.1.refs_18_.refs_24_.refs_34_.refs_32_), channel_id=1, source_target_pairs={{0,1},{1,0},{8,9},{9,8},{2,3},{3,2},{10,11},{11,10},{4,5},{5,4},{1... | collective-permute-start | bytes 884744 | tf_op jit(solution)/shard_map/ppermute | solution.py:691
  54.0 12.5 %collective-permute-start.19 = (bf16[2,96,768]{2,1,0:T(8,128)(2,1)S(1)}, bf16[2,96,768]{2,1,0:T(8,128)(2,1)S(1)}, u32[]{:S(2)}, u32[]{:S(2)}) collective-permute-start(bf16[2,96,768]{2,1,0:T(8,128)(2,1)S(1)} %collective-permute-done.1.refs_18_.refs_24_.refs_34_.refs_32_), channel_id=1, source_target_pairs={{0,8},{1,9},{8,0},{9,1},{2,10},{3,11},{10,2},{11,3},{4,12},{5,13},... | collective-permute-start | bytes 884744 | tf_op jit(solution)/shard_map/ppermute | solution.py:691
  54.6 12.4 %collective-permute-start.24 = (bf16[2,96,768]{2,1,0:T(8,128)(2,1)S(1)}, bf16[2,96,768]{2,1,0:T(8,128)(2,1)S(1)}, u32[]{:S(2)}, u32[]{:S(2)}) collective-permute-start(bf16[2,96,768]{2,1,0:T(8,128)(2,1)S(1)} %collective-permute-done.10.refs_9_.refs_15_.refs_25_.refs_23_), channel_id=1, source_target_pairs={{0,16},{16,0},{1,17},{17,1},{2,18},{18,2},{3,19},{19,3},{4,20},{20... | collective-permute-start | bytes 884744 | tf_op jit(solution)/shard_map/ppermute | solution.py:687
  60.4 7.5 %collective-permute-start.26 = (bf16[2,96,768]{2,1,0:T(8,128)(2,1)S(1)}, bf16[2,96,768]{2,1,0:T(8,128)(2,1)S(1)}, u32[]{:S(2)}, u32[]{:S(2)}) collective-permute-start(bf16[2,96,768]{2,1,0:T(8,128)(2,1)S(1)} %collective-permute-done.11.refs_11_.refs_17_.refs_27_.refs_25_), channel_id=1, source_target_pairs={{0,16},{16,0},{1,17},{17,1},{2,18},{18,2},{3,19},{19,3},{4,20},{20... | collective-permute-start | bytes 884744 | tf_op jit(solution)/shard_map/ppermute | solution.py:687
  62.0 6.5 %collective-permute-start.27 = (bf16[2,96,768]{2,1,0:T(8,128)(2,1)S(1)}, bf16[2,96,768]{2,1,0:T(8,128)(2,1)S(1)}, u32[]{:S(2)}, u32[]{:S(2)}) collective-permute-start(bf16[2,96,768]{2,1,0:T(8,128)(2,1)S(1)} %collective-permute-done.12.refs_12_.refs_18_.refs_28_.refs_26_), channel_id=1, source_target_pairs={{0,16},{16,0},{1,17},{17,1},{2,18},{18,2},{3,19},{19,3},{4,20},{20... | collective-permute-start | bytes 884744 | tf_op jit(solution)/shard_map/ppermute | solution.py:687
  66.5 8.2 %collective-permute-start.31 = (bf16[2,96,768]{2,1,0:T(8,128)(2,1)S(1)}, bf16[2,96,768]{2,1,0:T(8,128)(2,1)S(1)}, u32[]{:S(2)}, u32[]{:S(2)}) collective-permute-start(bf16[2,96,768]{2,1,0:T(8,128)(2,1)S(1)} %collective-permute-done.16.refs_16_.refs_22_.refs_32_.refs_30_), channel_id=1, source_target_pairs={{0,16},{16,0},{1,17},{17,1},{2,18},{18,2},{3,19},{19,3},{4,20},{20... | collective-permute-start | bytes 884744 | tf_op jit(solution)/shard_map/ppermute | solution.py:687
  67.7 7.3 %collective-permute-start.33 = (bf16[2,96,768]{2,1,0:T(8,128)(2,1)S(1)}, bf16[2,96,768]{2,1,0:T(8,128)(2,1)S(1)}, u32[]{:S(2)}, u32[]{:S(2)}) collective-permute-start(bf16[2,96,768]{2,1,0:T(8,128)(2,1)S(1)} %collective-permute-done.1.refs_18_.refs_24_.refs_34_.refs_32_), channel_id=1, source_target_pairs={{0,16},{16,0},{1,17},{17,1},{2,18},{18,2},{3,19},{19,3},{4,20},{20... | collective-permute-start | bytes 884744 | tf_op jit(solution)/shard_map/ppermute | solution.py:687
  74.7 23.7 %collective-permute-start.44 = (bf16[768,768]{1,0:T(8,128)(2,1)S(1)}, bf16[768,768]{1,0:T(8,128)(2,1)}, u32[]{:S(2)}, u32[]{:S(2)}) collective-permute-start(bf16[768,768]{1,0:T(8,128)(2,1)S(1)} %bitcast.89), channel_id=1, source_target_pairs={{0,16},{16,0},{1,17},{17,1},{2,18},{18,2},{3,19},{19,3},{4,20},{20... | collective-permute-start | bytes 3538952 | tf_op jit(solution)/shard_map/ppermute | solution.py:687
  75.0 23.4 %collective-permute-start.45 = (bf16[768,768]{1,0:T(8,128)(2,1)}, bf16[768,768]{1,0:T(8,128)(2,1)}, u32[]{:S(2)}, u32[]{:S(2)}) collective-permute-start(bf16[768,768]{1,0:T(8,128)(2,1)} %bitcast.32.refs_7_), channel_id=1, source_target_pairs={{0,16},{16,0},{1,17},{17,1},{2,18},{18,2},{3,19},{19,3},{4,20},{20... | collective-permute-start | bytes 3538952 | tf_op jit(solution)/shard_map/ppermute | solution.py:687
  109.5 6.7 %collective-permute-start.48 = (bf16[1,80,768]{2,1,0:T(8,128)(2,1)S(1)}, bf16[1,80,768]{2,1,0:T(8,128)(2,1)S(1)}, u32[]{:S(2)}, u32[]{:S(2)}) collective-permute-start(bf16[1,80,768]{2,1,0:T(8,128)(2,1)S(1)} %get-tuple-element.160), channel_id=1, source_target_pairs={{0,9},{1,8},{8,1},{9,0},{2,11},{3,10},{10,3},{11,2},{4,13},{5,12},... | collective-permute-start | bytes 368648 | tf_op jit(solution)/shard_map/ppermute | solution.py:691
  140.8 6.6 %collective-permute-start.55 = (bf16[2,80,768]{2,1,0:T(8,128)(2,1)S(1)}, bf16[2,80,768]{2,1,0:T(8,128)(2,1)S(1)}, u32[]{:S(2)}, u32[]{:S(2)}) collective-permute-start(bf16[2,80,768]{2,1,0:T(8,128)(2,1)S(1)} %pack.4.refs_1_), channel_id=1, source_target_pairs={{0,1},{1,0},{8,9},{9,8},{2,3},{3,2},{10,11},{11,10},{4,5},{5,4},{1... | collective-permute-start | bytes 737288 | tf_op jit(solution)/shard_map/ppermute | solution.py:691
  142.8 8.3 %collective-permute-start.57 = (bf16[2,80,768]{2,1,0:T(8,128)(2,1)S(1)}, bf16[2,80,768]{2,1,0:T(8,128)(2,1)S(1)}, u32[]{:S(2)}, u32[]{:S(2)}) collective-permute-start(bf16[2,80,768]{2,1,0:T(8,128)(2,1)S(1)} %pack.4.refs_1_), channel_id=1, source_target_pairs={{0,9},{1,8},{8,1},{9,0},{2,11},{3,10},{10,3},{11,2},{4,13},{5,12},... | collective-permute-start | bytes 737288 | tf_op jit(solution)/shard_map/ppermute | solution.py:691
  159.2 8.3 %collective-permute-start.60 = (bf16[2,80,768]{2,1,0:T(8,128)(2,1)S(1)}, bf16[2,80,768]{2,1,0:T(8,128)(2,1)S(1)}, u32[]{:S(2)}, u32[]{:S(2)}) collective-permute-start(bf16[2,80,768]{2,1,0:T(8,128)(2,1)S(1)} %get-tuple-element.182), channel_id=1, source_target_pairs={{0,9},{1,8},{8,1},{9,0},{2,11},{3,10},{10,3},{11,2},{4,13},{5,12},... | collective-permute-start | bytes 737288 | tf_op jit(solution)/shard_map/ppermute | solution.py:691
  197.6 8.4 %collective-permute-start.73 = (bf16[192,768]{1,0:T(8,128)(2,1)S(1)}, bf16[192,768]{1,0:T(8,128)(2,1)S(1)}, u32[]{:S(2)}, u32[]{:S(2)}) collective-permute-start(bf16[192,768]{1,0:T(8,128)(2,1)S(1)} %copy-done.76), channel_id=1, source_target_pairs={{0,1},{1,0},{8,9},{9,8},{2,3},{3,2},{10,11},{11,10},{4,5},{5,4},{1... | collective-permute-start | bytes 884744 | tf_op jit(solution)/shard_map/ppermute | solution.py:691
  198.0 7.9 %collective-permute-start.74 = (bf16[192,768]{1,0:T(8,128)(2,1)S(1)}, bf16[192,768]{1,0:T(8,128)(2,1)S(1)}, u32[]{:S(2)}, u32[]{:S(2)}) collective-permute-start(bf16[192,768]{1,0:T(8,128)(2,1)S(1)} %copy-done.75), channel_id=1, source_target_pairs={{0,8},{1,9},{8,0},{9,1},{2,10},{3,11},{10,2},{11,3},{4,12},{5,13},... | collective-permute-start | bytes 884744 | tf_op jit(solution)/shard_map/ppermute | solution.py:691
  199.5 9.4 %collective-permute-start.75 = (bf16[192,768]{1,0:T(8,128)(2,1)S(1)}, bf16[192,768]{1,0:T(8,128)(2,1)S(1)}, u32[]{:S(2)}, u32[]{:S(2)}) collective-permute-start(bf16[192,768]{1,0:T(8,128)(2,1)S(1)} %copy-done.74), channel_id=1, source_target_pairs={{0,9},{1,8},{8,1},{9,0},{2,11},{3,10},{10,3},{11,2},{4,13},{5,12},... | collective-permute-start | bytes 884744 | tf_op jit(solution)/shard_map/ppermute | solution.py:691
  210.5 14.3 %collective-permute-start.80 = (bf16[4,112,768]{2,1,0:T(8,128)(2,1)S(1)}, bf16[4,112,768]{2,1,0:T(8,128)(2,1)S(1)}, u32[]{:S(2)}, u32[]{:S(2)}) collective-permute-start(bf16[4,112,768]{2,1,0:T(8,128)(2,1)S(1)} %get-tuple-element.211), channel_id=1, source_target_pairs={{0,16},{16,0},{1,17},{17,1},{2,18},{18,2},{3,19},{19,3},{4,20},{20... | collective-permute-start | bytes 2064392 | tf_op jit(solution)/shard_map/ppermute | solution.py:687
  212.6 7.5 %collective-permute-start.72 = (bf16[1,80,768]{2,1,0:T(8,128)(2,1)S(1)}, bf16[1,80,768]{2,1,0:T(8,128)(2,1)S(1)}, u32[]{:S(2)}, u32[]{:S(2)}) collective-permute-start(bf16[1,80,768]{2,1,0:T(8,128)(2,1)S(1)} %get-tuple-element.200), channel_id=1, source_target_pairs={{0,9},{1,8},{8,1},{9,0},{2,11},{3,10},{10,3},{11,2},{4,13},{5,12},... | collective-permute-start | bytes 368648 | tf_op jit(solution)/shard_map/ppermute | solution.py:691
  221.0 9.1 %collective-permute-start.76 = (bf16[1,24,768]{2,1,0:T(8,128)(2,1)S(1)}, bf16[1,24,768]{2,1,0:T(8,128)(2,1)S(1)}, u32[]{:S(2)}, u32[]{:S(2)}) collective-permute-start(bf16[1,24,768]{2,1,0:T(8,128)(2,1)S(1)} %get-tuple-element.217), channel_id=1, source_target_pairs={{0,6},{2,0},{4,2},{6,4},{1,7},{3,1},{5,3},{7,5},{8,14},{10,8},{12,... | collective-permute-start | bytes 110600 | tf_op jit(solution)/shard_map/ppermute | solution.py:678
  225.7 12.6 %collective-permute-start.83 = (bf16[112,768]{1,0:T(8,128)(2,1)}, bf16[112,768]{1,0:T(8,128)(2,1)S(1)}, u32[]{:S(2)}, u32[]{:S(2)}) collective-permute-start(bf16[112,768]{1,0:T(8,128)(2,1)} %get-tuple-element.229), channel_id=1, source_target_pairs={{0,6},{2,0},{4,2},{6,4},{1,7},{3,1},{5,3},{7,5},{8,14},{10,8},{12,... | collective-permute-start | bytes 516104 | tf_op jit(solution)/shard_map/ppermute | solution.py:678
  229.2 15.3 %collective-permute-start.82 = (bf16[112,768]{1,0:T(8,128)(2,1)S(1)}, bf16[112,768]{1,0:T(8,128)(2,1)S(1)}, u32[]{:S(2)}, u32[]{:S(2)}) collective-permute-start(bf16[112,768]{1,0:T(8,128)(2,1)S(1)} %get-tuple-element.228), channel_id=1, source_target_pairs={{0,4},{2,6},{4,0},{6,2},{1,5},{3,7},{5,1},{7,3},{8,12},{10,14},{12... | collective-permute-start | bytes 516104 | tf_op jit(solution)/shard_map/ppermute | solution.py:678
  230.1 14.4 %collective-permute-start.81 = (bf16[112,768]{1,0:T(8,128)(2,1)S(1)}, bf16[112,768]{1,0:T(8,128)(2,1)S(1)}, u32[]{:S(2)}, u32[]{:S(2)}) collective-permute-start(bf16[112,768]{1,0:T(8,128)(2,1)S(1)} %get-tuple-element.227), channel_id=1, source_target_pairs={{0,2},{2,4},{4,6},{6,0},{1,3},{3,5},{5,7},{7,1},{8,10},{10,12},{12... | collective-permute-start | bytes 516104 | tf_op jit(solution)/shard_map/ppermute | solution.py:678
  245.8 10.2 %collective-permute-start.85 = (bf16[64,768]{1,0:T(8,128)(2,1)}, bf16[64,768]{1,0:T(8,128)(2,1)S(1)}, u32[]{:S(2)}, u32[]{:S(2)}) collective-permute-start(bf16[64,768]{1,0:T(8,128)(2,1)} %get-tuple-element.232), channel_id=1, source_target_pairs={{0,8},{1,9},{8,0},{9,1},{2,10},{3,11},{10,2},{11,3},{4,12},{5,13},... | collective-permute-start | bytes 294920 | tf_op jit(solution)/shard_map/ppermute | solution.py:691
  247.2 8.8 %collective-permute-start.86 = (bf16[64,768]{1,0:T(8,128)(2,1)}, bf16[64,768]{1,0:T(8,128)(2,1)S(1)}, u32[]{:S(2)}, u32[]{:S(2)}) collective-permute-start(bf16[64,768]{1,0:T(8,128)(2,1)} %get-tuple-element.233), channel_id=1, source_target_pairs={{0,9},{1,8},{8,1},{9,0},{2,11},{3,10},{10,3},{11,2},{4,13},{5,12},... | collective-permute-start | bytes 294920 | tf_op jit(solution)/shard_map/ppermute | solution.py:691
  255.9 28.9 %collective-permute-start.95 = (bf16[2,768,768]{2,1,0:T(8,128)(2,1)}, bf16[2,768,768]{2,1,0:T(8,128)(2,1)}, u32[]{:S(2)}, u32[]{:S(2)}) collective-permute-start(bf16[2,768,768]{2,1,0:T(8,128)(2,1)} %expert_gradients_sent.1), channel_id=1, source_target_pairs={{0,16},{16,0},{1,17},{17,1},{2,18},{18,2},{3,19},{19,3},{4,20},{20... | collective-permute-start | bytes 7077896 | tf_op jit(solution)/shard_map/ppermute | solution.py:687
  261.7 6.9 %collective-permute-start.90 = (bf16[112,768]{1,0:T(8,128)(2,1)S(1)}, bf16[112,768]{1,0:T(8,128)(2,1)S(1)}, u32[]{:S(2)}, u32[]{:S(2)}) collective-permute-start(bf16[112,768]{1,0:T(8,128)(2,1)S(1)} %get-tuple-element.276), channel_id=1, source_target_pairs={{0,6},{2,0},{4,2},{6,4},{1,7},{3,1},{5,3},{7,5},{8,14},{10,8},{12,... | collective-permute-start | bytes 516104 | tf_op jit(solution)/shard_map/ppermute | solution.py:678
  261.8 17.5 %collective-permute-start.89 = (bf16[112,768]{1,0:T(8,128)(2,1)S(1)}, bf16[112,768]{1,0:T(8,128)(2,1)S(1)}, u32[]{:S(2)}, u32[]{:S(2)}) collective-permute-start(bf16[112,768]{1,0:T(8,128)(2,1)S(1)} %get-tuple-element.277), channel_id=1, source_target_pairs={{0,4},{2,6},{4,0},{6,2},{1,5},{3,7},{5,1},{7,3},{8,12},{10,14},{12... | collective-permute-start | bytes 516104 | tf_op jit(solution)/shard_map/ppermute | solution.py:678
  263.6 15.7 %collective-permute-start.88 = (bf16[112,768]{1,0:T(8,128)(2,1)S(1)}, bf16[112,768]{1,0:T(8,128)(2,1)S(1)}, u32[]{:S(2)}, u32[]{:S(2)}) collective-permute-start(bf16[112,768]{1,0:T(8,128)(2,1)S(1)} %get-tuple-element.275), channel_id=1, source_target_pairs={{0,2},{2,4},{4,6},{6,0},{1,3},{3,5},{5,7},{7,1},{8,10},{10,12},{12... | collective-permute-start | bytes 516104 | tf_op jit(solution)/shard_map/ppermute | solution.py:678
  265.6 14.6 %collective-permute-start.79 = (f32[64,768]{1,0:T(8,128)S(1)}, f32[64,768]{1,0:T(8,128)S(1)}, u32[]{:S(2)}, u32[]{:S(2)}) collective-permute-start(f32[64,768]{1,0:T(8,128)S(1)} %broadcast_select_fusion.2), channel_id=1, source_target_pairs={{0,16},{16,0},{1,17},{17,1},{2,18},{18,2},{3,19},{19,3},{4,20},{20... | collective-permute-start | bytes 589832 | tf_op jit(solution)/shard_map/ppermute | solution.py:687
  281.1 10.0 %collective-permute-start.92 = (bf16[112,768]{1,0:T(8,128)(2,1)S(1)}, bf16[112,768]{1,0:T(8,128)(2,1)S(1)}, u32[]{:S(2)}, u32[]{:S(2)}) collective-permute-start(bf16[112,768]{1,0:T(8,128)(2,1)S(1)} %broadcast_select_fusion.1), channel_id=1, source_target_pairs={{0,8},{1,24},{8,0},{9,16},{16,9},{17,25},{24,1},{25,17},{2,10},{3,... | collective-permute-start | bytes 516104 | tf_op jit(solution)/shard_map/ppermute | solution.py:1104
  281.1 10.0 %collective-permute-start.93 = (bf16[112,768]{1,0:T(8,128)(2,1)S(1)}, bf16[112,768]{1,0:T(8,128)(2,1)S(1)}, u32[]{:S(2)}, u32[]{:S(2)}) collective-permute-start(bf16[112,768]{1,0:T(8,128)(2,1)S(1)} %get-tuple-element.272), channel_id=1, source_target_pairs={{0,16},{1,0},{8,24},{9,8},{16,17},{17,1},{24,25},{25,9},{2,18},{3,... | collective-permute-start | bytes 516104 | tf_op jit(solution)/shard_map/ppermute | solution.py:1104
  283.0 9.6 %collective-permute-start.94 = (bf16[112,768]{1,0:T(8,128)(2,1)S(1)}, bf16[112,768]{1,0:T(8,128)(2,1)S(1)}, u32[]{:S(2)}, u32[]{:S(2)}) collective-permute-start(bf16[112,768]{1,0:T(8,128)(2,1)S(1)} %get-tuple-element.272), channel_id=1, source_target_pairs={{0,24},{1,8},{8,16},{9,0},{16,25},{17,9},{24,17},{25,1},{2,26},{3,... | collective-permute-start | bytes 516104 | tf_op jit(solution)/shard_map/ppermute | solution.py:1104
  (131 other events, 1247.5 us)

commit v4 on v3

--- a/solution.py
+++ b/solution.py
@@ -750,7 +750,8 @@
         along = {1: shift(piece, "expert", 1), 3: shift(piece, "expert", 3)}
         over_y0 = plane_swap(piece, 1)
         along[2] = shift(after([piece], along[1])[0], "expert", 2)
-        early = (over_y0,)
+        over = {1: (plane_swap(along[1], 1), plane_swap(along[1], 2))}
+        early = (over[1][0],)
 
     small_rows = up(experts + 3, 8)
     table_row = jnp.pad(rel_table, ((0, 0), (0, slab - table_slab)))
@@ -783,8 +784,9 @@
         for i in (1, 3, 2):
             got = along[i]
             if i == 2:
-                got, x0, g1, *common = after([got, x0, g1] + common)
-            over_y, over_x = plane_swap(got, 1), plane_swap(got, 2)
+                got, x0, g1, meta_, *common = after([got, x0, g1, common[0]] + common[2:])
+                common = [meta_, small_all] + common
+            over_y, over_x = over[i] if i in over else (plane_swap(got, 1), plane_swap(got, 2))
             pieces += [got, over_y, over_x]
             plan += [(i, 0, 0, 0, 2), (i, 1, 0, 0, 2), (i, 0, 1, 0, 2)]
             if i == 1:
@@ -796,11 +798,9 @@
             else:
                 pieces += [plane_swap(over_y[:1], 2), plane_swap(over_x[1:], 1)]
                 plan += [(i, 1, 1, 0, 1), (i, 1, 1, 1, 1)]
-        copied = [swap_section(v) for v in pieces]
+        held_back = after(pieces[:7], pieces[9])
+        copied = [swap_section(v) for v in held_back + pieces[7:]]
         attn_w = [pieces + copied] * 2
-    other_in = swap_section(expert_in[0, 0])
-    other_out = swap_section(expert_out[0, 0])
-    expert_w = [expert_in[0, 0], other_in, expert_out[0, 0], other_out]
 
     n_w = len(attn_w[0])
     n_ret = 1 if big else experts
@@ -962,6 +962,8 @@
         return total.astype(BF)
 
     kept0, blocks = forward(0, [x0])
+    w_in, w_out = after([expert_in[0, 0], expert_out[0, 0]], kept0["probs"])
+    expert_w = [w_in, swap_section(w_in), w_out, swap_section(w_out)]
     joined = dispatch(blocks, 1)
     partial, (rows0, act0, pre0) = expert_forward(0, joined, False)
     returned = come_back(partial, 1)
@@ -1016,7 +1018,7 @@
 
     sets = [rows0, dpre0, act0, grows0, rows1, dpre1, act1, grows1]
     if not big:
-        sets = after(sets, rights0[1])
+        sets = after(sets, dx0)
     bring_scratch = [
         pltpu.VMEM((all_rows, width), BF),
         pltpu.VMEM((all_rows, ff), BF),

time: 295 us -> 282 us (0.956)
  waiting for transfers between devices: 124 us -> 94.1 us
  starting transfers between devices: 92.6 us -> 105 us
  local copies, waits for them, and re-layouts: 10.7 us -> 13.7 us
    ppermute x36, waiting for transfers between devices: 60.3 us -> 38.7 us  [plane_swap(): return lax.ppermute(v, PLANE, [(i, i ^ mask) for i in range(4)])]
    ppermute x31, starting transfers between devices: 42.4 us -> 49.5 us  [shift(): return lax.ppermute(v, axis, [(i, (i + by) % n) for i in range(n)])]
    ppermute x31, waiting for transfers between devices: 53.8 us -> 49.1 us  [shift(): return lax.ppermute(v, axis, [(i, (i + by) % n) for i in range(n)])]
    ppermute x25, waiting for transfers between devices: 7.98 us -> 4.18 us  [swap_section(): return lax.ppermute(v, 'section', [(0, 1), (1, 0)])]
    ppermute x36, starting transfers between devices: 42.2 us -> 45.6 us  [plane_swap(): return lax.ppermute(v, PLANE, [(i, i ^ mask) for i in range(4)])]
    unnamed x166 -> x168, local copies, waits for them, and re-layouts: 8.51 us -> 10.7 us
  transfers between devices with their start and end apart: 96 -> 96, of which waited for: 52 -> 46; matrix products, arithmetic and copies ran while one was open for 3% -> 3% of each run, Pallas kernels for 11% -> 9%
where the time goes in v4:
time: 282 us; the launch traced here: 281 us
  starting transfers between devices  105 us (37%)
  waiting for transfers between devices  94.1 us (33%)
  Pallas kernels  58.8 us (21%)
  local copies, waits for them, and re-layouts  13.7 us (5%)
  other arithmetic  7.57 us (3%)
    pallas_call x18, Pallas kernels, call(): pl.pallas_call(kernel, out_shape=[jax.ShapeDtypeStruct(shape, dtype) for...  58.8 us
    ppermute x31, starting transfers between devices, shift(): return lax.ppermute(v, axis, [(i, (i + by) % n) for i in range(n)])  49.5 us
    ppermute x31, waiting for transfers between devices, shift(): return lax.ppermute(v, axis, [(i, (i + by) % n) for i in range(n)])  49.1 us
    ppermute x36, starting transfers between devices, plane_swap(): return lax.ppermute(v, PLANE, [(i, i ^ mask) for i in range(4)])  45.6 us
    ppermute x36, waiting for transfers between devices, plane_swap(): return lax.ppermute(v, PLANE, [(i, i ^ mask) for i in range(4)])  38.7 us
    unnamed x168, local copies, waits for them, and re-layouts  10.7 us
  transfers between devices with their start and end apart: 96, of which 46 were waited for; matrix products, arithmetic and copies ran while one was open for 3% of the time, Pallas kernels for 9%

profile of v4, /device:TPU:0, one launch (start us, length us, event | category | flops | bytes accessed | tf_op | source)
XLA Modules:
  0.0 280.9 jit_solution(596692427318911212)
XLA Ops:
  1.8 3.1 %collective-permute-start = (bf16[2,96,768]{2,1,0:T(8,128)(2,1)S(1)}, bf16[2,96,768]{2,1,0:T(8,128)(2,1)S(1)}, u32[]{:S(2)}, u32[]{:S(2)}) collective-permute-start(bf16[2,96,768]{2,1,0:T(8,128)(2,1)S(1)} %fusion.3), channel_id=1, source_target_pairs={{0,2},{2,4},{4,6},{6,0},{1,3},{3,5},{5,7},{7,1},{8,10},{10,12},{12... | collective-permute-start | bytes 884744 | tf_op jit(solution)/shard_map/ppermute | solution.py:678
  6.4 2.2 collective-permute-start.14
  11.6 3.2 %collective-permute-done.refs_10_.refs_16_.refs_26_.refs_24_ = bf16[2,96,768]{2,1,0:T(8,128)(2,1)S(1)} collective-permute-done((bf16[2,96,768]{2,1,0:T(8,128)(2,1)S(1)}, bf16[2,96,768]{2,1,0:T(8,128)(2,1)S(1)}, u32[]{:S(2)}, u32[]{:S(2)}) %collective-permute-start) | collective-permute-done | bytes 294944 | tf_op jit(solution)/shard_map/ppermute | solution.py:678
  14.8 1.8 collective-permute-start.4
  17.2 9.1 %collective-permute-start.1 = (bf16[2,96,768]{2,1,0:T(8,128)(2,1)S(1)}, bf16[2,96,768]{2,1,0:T(8,128)(2,1)S(1)}, u32[]{:S(2)}, u32[]{:S(2)}) collective-permute-start(bf16[2,96,768]{2,1,0:T(8,128)(2,1)S(1)} %fusion.3), channel_id=1, source_target_pairs={{0,4},{2,6},{4,0},{6,2},{1,5},{3,7},{5,1},{7,3},{8,12},{10,14},{12... | collective-permute-start | bytes 884744 | tf_op jit(solution)/shard_map/ppermute | solution.py:678
  28.5 2.4 collective-permute-start.6
  38.8 2.6 collective-permute-done.5
  44.6 2.0 collective-permute-start.13
  46.5 2.3 collective-permute-start.17
  48.9 2.6 collective-permute-done.8
  54.1 3.5 %collective-permute-done.13.refs_13_.refs_19_.refs_29_.refs_27_ = bf16[2,96,768]{2,1,0:T(8,128)(2,1)} collective-permute-done((bf16[2,96,768]{2,1,0:T(8,128)(2,1)S(1)}, bf16[2,96,768]{2,1,0:T(8,128)(2,1)}, u32[]{:S(2)}, u32[]{:S(2)}) %collective-permute-start.13) | collective-permute-done | bytes 294944 | tf_op jit(solution)/shard_map/ppermute | solution.py:691
  60.3 2.4 collective-permute-done.20.refs_21_.refs_27_.refs_37_.refs_35_
  70.4 6.1 %attention_forward.2 = (bf16[64,768]{1,0:T(8,128)(2,1)}, bf16[3,64,768]{2,1,0:T(8,128)(2,1)}, f32[6,128,64]{2,1,0:T(8,128)}, bf16[64,768]{1,0:T(8,128)(2,1)}, f3...) custom-call(s32[9]{0:T(128)} %concatenate.10.refs_0_.meta, ...), custom_call_target="tpu_custom_call" | custom-call | flops 6000000000 | bytes 18000000 | tf_op jit(solution)/shard_map/attention_forward/pallas_call | solution.py:662
  78.0 2.9 %collective-permute-start.40 = (bf16[24,768]{1,0:T(8,128)(2,1)}, bf16[24,768]{1,0:T(8,128)(2,1)S(1)}, u32[]{:S(2)}, u32[]{:S(2)}) collective-permute-start(bf16[24,768]{1,0:T(8,128)(2,1)} %get-tuple-element.170), channel_id=1, source_target_pairs={{0,6},{2,0},{4,2},{6,4},{1,7},{3,1},{5,3},{7,5},{8,14},{10,8},{12,... | collective-permute-start | bytes 110600 | tf_op jit(solution)/shard_map/ppermute | solution.py:678
  80.9 2.5 collective-permute-done.38
  88.3 2.7 collective-permute-done.41.refs_2_
  93.1 3.6 %expert_forward.2 = (bf16[1,80,768]{2,1,0:T(8,128)(2,1)S(1)}, bf16[1,80,768]{2,1,0:T(8,128)(2,1)S(1)}, bf16[1,80,768]{2,1,0:T(8,128)(2,1)S(1)}, bf16[1,80,768]{2...) custom-call(s32[9]{0:T(128)S(1)} %copy-done.2, ...), custom_call_target="tpu_custom_call" | custom-call | flops 4000000000 | bytes 12000000 | tf_op jit(solution)/shard_map/expert_forward/pallas_call | solution.py:662
  100.4 2.2 collective-permute-done.46.refs_1_
  105.6 2.8 collective-permute-start.49
  110.0 3.2 %collective-permute-done.50 = bf16[1,24,768]{2,1,0:T(8,128)(2,1)S(1)} collective-permute-done((bf16[1,24,768]{2,1,0:T(8,128)(2,1)S(1)}, bf16[1,24,768]{2,1,0:T(8,128)(2,1)S(1)}, u32[]{:S(2)}, u32[]{:S(2)}) %collective-permute-start.50) | collective-permute-done | bytes 36896 | tf_op jit(solution)/shard_map/ppermute | solution.py:678
  115.1 6.6 %attention_forward.3 = (bf16[64,768]{1,0:T(8,128)(2,1)}, bf16[3,64,768]{2,1,0:T(8,128)(2,1)}, f32[6,128,64]{2,1,0:T(8,128)}, bf16[64,768]{1,0:T(8,128)(2,1)}, f3...) custom-call(s32[9]{0:T(128)} %concatenate.10.refs_0_.meta, ...), custom_call_target="tpu_custom_call" | custom-call | flops 6000000000 | bytes 18000000 | tf_op jit(solution)/shard_map/attention_forward/pallas_call | solution.py:662
  122.6 3.0 %collective-permute-start.54 = (bf16[2,24,768]{2,1,0:T(8,128)(2,1)}, bf16[2,24,768]{2,1,0:T(8,128)(2,1)S(1)}, u32[]{:S(2)}, u32[]{:S(2)}) collective-permute-start(bf16[2,24,768]{2,1,0:T(8,128)(2,1)} %get-tuple-element.194), channel_id=1, source_target_pairs={{0,6},{2,0},{4,2},{6,4},{1,7},{3,1},{5,3},{7,5},{8,14},{10,8},{12,... | collective-permute-start | bytes 221192 | tf_op jit(solution)/shard_map/ppermute | solution.py:678
  125.5 2.6 collective-permute-done.52.refs_1_
  133.7 2.7 collective-permute-done.55.refs_2_
  137.7 2.8 collective-permute-done.57.refs_4_
  140.5 5.2 %expert_forward.3 = (bf16[2,80,768]{2,1,0:T(8,128)(2,1)S(1)}, bf16[2,80,768]{2,1,0:T(8,128)(2,1)S(1)}, bf16[2,80,768]{2,1,0:T(8,128)(2,1)S(1)}, bf16[2,80,768]{2...) custom-call(s32[9]{0:T(128)S(1)} %copy-done.3, ...), custom_call_target="tpu_custom_call" | custom-call | flops 4000000000 | bytes 12000000 | tf_op jit(solution)/shard_map/expert_forward/pallas_call | solution.py:662
  149.3 2.7 collective-permute-done.58.refs_1_
  153.4 2.8 collective-permute-done.60.refs_3_
  157.1 3.1 %collective-permute-start.61 = (bf16[2,24,768]{2,1,0:T(8,128)(2,1)S(1)}, bf16[2,24,768]{2,1,0:T(8,128)(2,1)S(1)}, u32[]{:S(2)}, u32[]{:S(2)}) collective-permute-start(bf16[2,24,768]{2,1,0:T(8,128)(2,1)S(1)} %get-tuple-element.200), channel_id=1, source_target_pairs={{0,6},{2,0},{4,2},{6,4},{1,7},{3,1},{5,3},{7,5},{8,14},{10,8},{12,... | collective-permute-start | bytes 221192 | tf_op jit(solution)/shard_map/ppermute | solution.py:678
  162.2 3.3 %collective-permute-done.62.refs_21_ = bf16[2,24,768]{2,1,0:T(8,128)(2,1)S(1)} collective-permute-done((bf16[2,24,768]{2,1,0:T(8,128)(2,1)S(1)}, bf16[2,24,768]{2,1,0:T(8,128)(2,1)S(1)}, u32[]{:S(2)}, u32[]{:S(2)}) %collective-permute-start.62) | collective-permute-done | bytes 73760 | tf_op jit(solution)/shard_map/ppermute | solution.py:678
  167.2 7.8 %attention_backward.2 = (f32[64,768]{1,0:T(8,128)}, f32[16,768]{1,0:T(8,128)}, bf16[192,768]{1,0:T(8,128)(2,1)}, bf16[192,768]{1,0:T(8,128)(2,1)}, bf16[192,768]...) custom-call(s32[9]{0:T(128)} %concatenate.10.refs_0_.meta, ...), custom_call_target="tpu_custom_call" | custom-call | flops 8000000000 | bytes 24000000 | tf_op jit(solution)/shard_map/attention_backward/pallas_call | solution.py:662
  176.2 2.7 collective-permute-start.66
  178.9 2.1 collective-permute-done.64
  191.8 4.3 %expert_backward.1 = (bf16[1,80,768]{2,1,0:T(8,128)(2,1)S(1)}, bf16[1,80,768]{2,1,0:T(8,128)(2,1)S(1)}, bf16[1,80,768]{2,1,0:T(8,128)(2,1)S(1)}, bf16[1,80,768]{...) custom-call(s32[9]{0:T(128)S(1)} %copy-done.4, bf16[1,80,768]{2,1,0:T(8,128)(2,1)S(1)} %pack.5.refs_1_, ...), custom_call_target="tpu_custom_call" | custom-call | flops 4000000000 | bytes 12000000 | tf_op jit(solution)/shard_map/expert_backward/pallas_call | solution.py:662
  205.2 1.8 collective-permute-done.71.refs_2_
  207.0 2.0 collective-permute-done.72.refs_3_
  209.9 3.3 %collective-permute-start.76 = (bf16[1,24,768]{2,1,0:T(8,128)(2,1)S(1)}, bf16[1,24,768]{2,1,0:T(8,128)(2,1)S(1)}, u32[]{:S(2)}, u32[]{:S(2)}) collective-permute-start(bf16[1,24,768]{2,1,0:T(8,128)(2,1)S(1)} %get-tuple-element.233), channel_id=1, source_target_pairs={{0,6},{2,0},{4,2},{6,4},{1,7},{3,1},{5,3},{7,5},{8,14},{10,8},{12,... | collective-permute-start | bytes 110600 | tf_op jit(solution)/shard_map/ppermute | solution.py:678
  214.0 3.5 %collective-permute-start.83 = (bf16[112,768]{1,0:T(8,128)(2,1)S(1)}, bf16[112,768]{1,0:T(8,128)(2,1)S(1)}, u32[]{:S(2)}, u32[]{:S(2)}) collective-permute-start(bf16[112,768]{1,0:T(8,128)(2,1)S(1)} %get-tuple-element.245), channel_id=1, source_target_pairs={{0,6},{2,0},{4,2},{6,4},{1,7},{3,1},{5,3},{7,5},{8,14},{10,8},{12,... | collective-permute-start | bytes 516104 | tf_op jit(solution)/shard_map/ppermute | solution.py:678
  220.3 7.1 %attention_backward.3 = (f32[64,768]{1,0:T(8,128)}, f32[16,768]{1,0:T(8,128)}, bf16[64,768]{1,0:T(8,128)(2,1)}, bf16[64,768]{1,0:T(8,128)(2,1)}, bf16[64,768]{1,0:T(8,128)(2,1)}, /*index=5*/bf16[64,768]{1,0:T(8,128)(2,1)}) custom-call(s32[9]{0:T(128)} %concatenate.10.refs_0_.meta, bf16[2,2,4,8,96]{4,3,2,1,0:T(8,128)(2,1)} %pad_maximum_fusion.1.refs_1_, ...), custom_call_target="tpu_custom_call" | custom-call | flops 2000000000 | bytes 6000000 | tf_op jit(solution)/shard_map/attention_backward/pallas_call | solution.py:662
  227.5 5.6 %collective-permute-done.82 = bf16[112,768]{1,0:T(8,128)(2,1)S(1)} collective-permute-done((bf16[112,768]{1,0:T(8,128)(2,1)S(1)}, bf16[112,768]{1,0:T(8,128)(2,1)S(1)}, u32[]{:S(2)}, u32[]{:S(2)}) %collective-permute-start.82) | collective-permute-done | bytes 172064 | tf_op jit(solution)/shard_map/ppermute | solution.py:678
  237.3 5.3 %expert_gradients_sent.1 = bf16[2,768,768]{2,1,0:T(8,128)(2,1)} custom-call(s32[9]{0:T(128)} %concatenate.10.refs_0_.meta, bf16[320,768]{1,0:T(8,128)(2,1)} %copy-done.34, bf16[320,768]{1,0:T(8,128)(2,1)} %copy-done.29, bf16[320,768]{1,0:T(8,128)(2,1)} %copy-done.35, bf16[320,768]{1,0:T(8,128)(2,1)} %copy-done.28, bf16[320,768]{1,0:T(8,128)(2,1)} %copy-done.30, ...), custom_call_target="tpu_custom_call" | custom-call | flops 5000000000 | bytes 15000000 | tf_op jit(solution)/shard_map/expert_gradients_sent/pallas_call | solution.py:662
  244.8 3.4 %collective-permute-done.87 = bf16[4,112,768]{2,1,0:T(8,128)(2,1)S(1)} collective-permute-done((bf16[4,112,768]{2,1,0:T(8,128)(2,1)S(1)}, bf16[4,112,768]{2,1,0:T(8,128)(2,1)S(1)}, u32[]{:S(2)}, u32[]{:S(2)}) %collective-permute-start.87) | collective-permute-done | bytes 688160 | tf_op jit(solution)/shard_map/ppermute | solution.py:687
  249.6 1.9 collective-permute-start.88
  251.6 4.3 %collective-permute-done.90 = bf16[112,768]{1,0:T(8,128)(2,1)S(1)} collective-permute-done((bf16[112,768]{1,0:T(8,128)(2,1)S(1)}, bf16[112,768]{1,0:T(8,128)(2,1)S(1)}, u32[]{:S(2)}, u32[]{:S(2)}) %collective-permute-start.90) | collective-permute-done | bytes 172064 | tf_op jit(solution)/shard_map/ppermute | solution.py:678
  256.0 9.3 %collective-permute-done.89 = bf16[112,768]{1,0:T(8,128)(2,1)S(1)} collective-permute-done((bf16[112,768]{1,0:T(8,128)(2,1)S(1)}, bf16[112,768]{1,0:T(8,128)(2,1)S(1)}, u32[]{:S(2)}, u32[]{:S(2)}) %collective-permute-start.89) | collective-permute-done | bytes 172064 | tf_op jit(solution)/shard_map/ppermute | solution.py:678
  268.4 2.0 collective-permute-start.93
  270.7 6.3 %expert_gradients_own.1 = (f32[768,768]{1,0:T(8,128)}, f32[768,768]{1,0:T(8,128)}) custom-call(s32[9]{0:T(128)} %concatenate.10.refs_0_.meta, bf16[320,768]{1,0:T(8,128)(2,1)} %copy-done.34, bf16[320,768]{1,0:T(8,128)(2,1)} %copy-done.29, bf16[320,768]{1,0:T(8,128)(2,1)} %copy-done.35, bf16[320,768]{1,0:T(8,128)(2,1)} %copy-done.28, ...), custom_call_target="tpu_custom_call" | custom-call | flops 6000000000 | bytes 18000000 | tf_op jit(solution)/shard_map/expert_gradients_own/pallas_call | solution.py:662
  277.1 2.2 collective-permute-done.94.refs_3_
  (357 shorter events, 106.4 us)
Async XLA Ops:
  1.8 13.0 %collective-permute-start = (bf16[2,96,768]{2,1,0:T(8,128)(2,1)S(1)}, bf16[2,96,768]{2,1,0:T(8,128)(2,1)S(1)}, u32[]{:S(2)}, u32[]{:S(2)}) collective-permute-start(bf16[2,96,768]{2,1,0:T(8,128)(2,1)S(1)} %fusion.3), channel_id=1, source_target_pairs={{0,2},{2,4},{4,6},{6,0},{1,3},{3,5},{5,7},{7,1},{8,10},{10,12},{12... | collective-permute-start | bytes 884744 | tf_op jit(solution)/shard_map/ppermute | solution.py:678
  4.9 21.4 %collective-permute-start.10 = (bf16[2,96,768]{2,1,0:T(8,128)(2,1)S(1)}, bf16[2,96,768]{2,1,0:T(8,128)(2,1)S(1)}, u32[]{:S(2)}, u32[]{:S(2)}) collective-permute-start(bf16[2,96,768]{2,1,0:T(8,128)(2,1)S(1)} %fusion.3), channel_id=1, source_target_pairs={{0,1},{1,0},{8,9},{9,8},{2,3},{3,2},{10,11},{11,10},{4,5},{5,4},{1... | collective-permute-start | bytes 884744 | tf_op jit(solution)/shard_map/ppermute | solution.py:691
  6.4 25.1 %collective-permute-start.14 = (bf16[2,96,768]{2,1,0:T(8,128)(2,1)S(1)}, bf16[2,96,768]{2,1,0:T(8,128)(2,1)S(1)}, u32[]{:S(2)}, u32[]{:S(2)}) collective-permute-start(bf16[2,96,768]{2,1,0:T(8,128)(2,1)S(1)} %fusion.3), channel_id=1, source_target_pairs={{0,6},{2,0},{4,2},{6,4},{1,7},{3,1},{5,3},{7,5},{8,14},{10,8},{12,... | collective-permute-start | bytes 884744 | tf_op jit(solution)/shard_map/ppermute | solution.py:678
  9.6 18.9 %collective-permute-start.2 = (bf16[64,768]{1,0:T(8,128)(2,1)S(1)}, bf16[64,768]{1,0:T(8,128)(2,1)S(1)}, u32[]{:S(2)}, u32[]{:S(2)}) collective-permute-start(bf16[64,768]{1,0:T(8,128)(2,1)S(1)} %dynamic-slice_bitcast_fusion), channel_id=1, source_target_pairs={{0,16},{16,0},{1,17},{17,1},{2,18},{18,2},{3,19},{19,3},{4,20},{20... | collective-permute-start | bytes 294920 | tf_op jit(solution)/shard_map/ppermute | solution.py:687
  10.2 7.0 %collective-permute-start.3 = (s32[64]{0:T(128)S(1)}, s32[64]{0:T(128)S(1)}, u32[]{:S(2)}, u32[]{:S(2)}) collective-permute-start(s32[64]{0:T(128)S(1)} %fusion.11), channel_id=1, source_target_pairs={{0,16},{16,0},{1,17},{17,1},{2,18},{18,2},{3,19},{19,3},{4,20},{20... | collective-permute-start | bytes 776 | tf_op jit(solution)/shard_map/ppermute | solution.py:687
  14.8 13.6 %collective-permute-start.4 = (bf16[2,96,768]{2,1,0:T(8,128)(2,1)S(1)}, bf16[2,96,768]{2,1,0:T(8,128)(2,1)S(1)}, u32[]{:S(2)}, u32[]{:S(2)}) collective-permute-start(bf16[2,96,768]{2,1,0:T(8,128)(2,1)S(1)} %collective-permute-done.refs_10_.refs_16_.refs_26_.refs_24_), channel_id=1, source_target_pairs={{0,1},{1,0},{8,9},{9,8},{2,3},{3,2},{10,11},{11,10},{4,5},{5,4},{1... | collective-permute-start | bytes 884744 | tf_op jit(solution)/shard_map/ppermute | solution.py:691
  17.2 15.8 %collective-permute-start.1 = (bf16[2,96,768]{2,1,0:T(8,128)(2,1)S(1)}, bf16[2,96,768]{2,1,0:T(8,128)(2,1)S(1)}, u32[]{:S(2)}, u32[]{:S(2)}) collective-permute-start(bf16[2,96,768]{2,1,0:T(8,128)(2,1)S(1)} %fusion.3), channel_id=1, source_target_pairs={{0,4},{2,6},{4,0},{6,2},{1,5},{3,7},{5,1},{7,3},{8,12},{10,14},{12... | collective-permute-start | bytes 884744 | tf_op jit(solution)/shard_map/ppermute | solution.py:678
  26.3 8.2 %collective-permute-start.11 = (bf16[2,96,768]{2,1,0:T(8,128)(2,1)S(1)}, bf16[2,96,768]{2,1,0:T(8,128)(2,1)S(1)}, u32[]{:S(2)}, u32[]{:S(2)}) collective-permute-start(bf16[2,96,768]{2,1,0:T(8,128)(2,1)S(1)} %collective-permute-done.10.refs_8_.refs_14_.refs_24_.refs_22_), channel_id=1, source_target_pairs={{0,8},{1,9},{8,0},{9,1},{2,10},{3,11},{10,2},{11,3},{4,12},{5,13},... | collective-permute-start | bytes 884744 | tf_op jit(solution)/shard_map/ppermute | solution.py:691
  28.4 7.5 %collective-permute-start.7 = (bf16[8,96]{1,0:T(8,128)(2,1)S(1)}, bf16[8,96]{1,0:T(8,128)(2,1)S(1)}, u32[]{:S(2)}, u32[]{:S(2)}) collective-permute-start(bf16[8,96]{1,0:T(8,128)(2,1)S(1)} %fusion.7), channel_id=1, source_target_pairs={{0,6},{2,0},{4,2},{6,4},{1,7},{3,1},{5,3},{7,5},{8,14},{10,8},{12,... | collective-permute-start | bytes 4616 | tf_op jit(solution)/shard_map/ppermute | solution.py:678
  28.5 7.5 %collective-permute-start.6 = (bf16[8,96]{1,0:T(8,128)(2,1)S(1)}, bf16[8,96]{1,0:T(8,128)(2,1)S(1)}, u32[]{:S(2)}, u32[]{:S(2)}) collective-permute-start(bf16[8,96]{1,0:T(8,128)(2,1)S(1)} %fusion.7), channel_id=1, source_target_pairs={{0,4},{2,6},{4,0},{6,2},{1,5},{3,7},{5,1},{7,3},{8,12},{10,14},{12... | collective-permute-start | bytes 4616 | tf_op jit(solution)/shard_map/ppermute | solution.py:678
  31.5 10.4 %collective-permute-start.12 = (bf16[2,96,768]{2,1,0:T(8,128)(2,1)S(1)}, bf16[2,96,768]{2,1,0:T(8,128)(2,1)S(1)}, u32[]{:S(2)}, u32[]{:S(2)}) collective-permute-start(bf16[2,96,768]{2,1,0:T(8,128)(2,1)S(1)} %collective-permute-done.refs_10_.refs_16_.refs_26_.refs_24_), channel_id=1, source_target_pairs={{0,8},{1,9},{8,0},{9,1},{2,10},{3,11},{10,2},{11,3},{4,12},{5,13},... | collective-permute-start | bytes 884744 | tf_op jit(solution)/shard_map/ppermute | solution.py:691
  33.0 10.5 %collective-permute-start.15 = (bf16[2,96,768]{2,1,0:T(8,128)(2,1)S(1)}, bf16[2,96,768]{2,1,0:T(8,128)(2,1)S(1)}, u32[]{:S(2)}, u32[]{:S(2)}) collective-permute-start(bf16[2,96,768]{2,1,0:T(8,128)(2,1)S(1)} %collective-permute-done.14.refs_14_.refs_20_.refs_30_.refs_28_), channel_id=1, source_target_pairs={{0,1},{1,0},{8,9},{9,8},{2,3},{3,2},{10,11},{11,10},{4,5},{5,4},{1... | collective-permute-start | bytes 884744 | tf_op jit(solution)/shard_map/ppermute | solution.py:691
  34.5 10.0 %collective-permute-start.16 = (bf16[2,96,768]{2,1,0:T(8,128)(2,1)S(1)}, bf16[2,96,768]{2,1,0:T(8,128)(2,1)S(1)}, u32[]{:S(2)}, u32[]{:S(2)}) collective-permute-start(bf16[2,96,768]{2,1,0:T(8,128)(2,1)S(1)} %collective-permute-done.14.refs_14_.refs_20_.refs_30_.refs_28_), channel_id=1, source_target_pairs={{0,8},{1,9},{8,0},{9,1},{2,10},{3,11},{10,2},{11,3},{4,12},{5,13},... | collective-permute-start | bytes 884744 | tf_op jit(solution)/shard_map/ppermute | solution.py:691
  36.0 10.6 %collective-permute-start.29 = (bf16[2,96,768]{2,1,0:T(8,128)(2,1)S(1)}, bf16[2,96,768]{2,1,0:T(8,128)(2,1)S(1)}, u32[]{:S(2)}, u32[]{:S(2)}) collective-permute-start(bf16[2,96,768]{2,1,0:T(8,128)(2,1)S(1)} %collective-permute-done.14.refs_14_.refs_20_.refs_30_.refs_28_), channel_id=1, source_target_pairs={{0,16},{16,0},{1,17},{17,1},{2,18},{18,2},{3,19},{19,3},{4,20},{20... | collective-permute-start | bytes 884744 | tf_op jit(solution)/shard_map/ppermute | solution.py:687
  41.4 10.1 %collective-permute-start.18 = (bf16[2,96,768]{2,1,0:T(8,128)(2,1)S(1)}, bf16[2,96,768]{2,1,0:T(8,128)(2,1)S(1)}, u32[]{:S(2)}, u32[]{:S(2)}) collective-permute-start(bf16[2,96,768]{2,1,0:T(8,128)(2,1)S(1)} %collective-permute-done.1.refs_18_.refs_24_.refs_34_.refs_32_), channel_id=1, source_target_pairs={{0,1},{1,0},{8,9},{9,8},{2,3},{3,2},{10,11},{11,10},{4,5},{5,4},{1... | collective-permute-start | bytes 884744 | tf_op jit(solution)/shard_map/ppermute | solution.py:691
  41.9 9.6 %collective-permute-start.8 = (bf16[4,8,96]{2,1,0:T(8,128)(2,1)S(1)}, bf16[4,8,96]{2,1,0:T(8,128)(2,1)S(1)}, u32[]{:S(2)}, u32[]{:S(2)}) collective-permute-start(bf16[4,8,96]{2,1,0:T(8,128)(2,1)S(1)} %get-tuple-element.305), channel_id=1, source_target_pairs={{0,1},{1,0},{2,3},{3,2},{4,5},{5,4},{6,7},{7,6},{8,9},{9,8},{10,11... | collective-permute-start | bytes 18440 | tf_op jit(solution)/shard_map/ppermute | solution.py:678
  43.5 9.9 %collective-permute-start.19 = (bf16[2,96,768]{2,1,0:T(8,128)(2,1)S(1)}, bf16[2,96,768]{2,1,0:T(8,128)(2,1)S(1)}, u32[]{:S(2)}, u32[]{:S(2)}) collective-permute-start(bf16[2,96,768]{2,1,0:T(8,128)(2,1)S(1)} %collective-permute-done.1.refs_18_.refs_24_.refs_34_.refs_32_), channel_id=1, source_target_pairs={{0,8},{1,9},{8,0},{9,1},{2,10},{3,11},{10,2},{11,3},{4,12},{5,13},... | collective-permute-start | bytes 884744 | tf_op jit(solution)/shard_map/ppermute | solution.py:691
  44.6 13.1 %collective-permute-start.13 = (bf16[2,96,768]{2,1,0:T(8,128)(2,1)S(1)}, bf16[2,96,768]{2,1,0:T(8,128)(2,1)}, u32[]{:S(2)}, u32[]{:S(2)}) collective-permute-start(bf16[2,96,768]{2,1,0:T(8,128)(2,1)S(1)} %collective-permute-done.4.refs_11_.refs_17_.refs_27_.refs_25_), channel_id=1, source_target_pairs={{0,8},{1,9},{8,0},{9,1},{2,10},{3,11},{10,2},{11,3},{4,12},{5,13},... | collective-permute-start | bytes 884744 | tf_op jit(solution)/shard_map/ppermute | solution.py:691
  46.5 12.2 %collective-permute-start.17 = (bf16[2,96,768]{2,1,0:T(8,128)(2,1)S(1)}, bf16[2,96,768]{2,1,0:T(8,128)(2,1)}, u32[]{:S(2)}, u32[]{:S(2)}) collective-permute-start(bf16[2,96,768]{2,1,0:T(8,128)(2,1)S(1)} %collective-permute-done.16.refs_16_.refs_22_.refs_32_.refs_30_), channel_id=1, source_target_pairs={{0,1},{1,0},{8,9},{9,8},{2,3},{3,2},{10,11},{11,10},{4,5},{5,4},{1... | collective-permute-start | bytes 884744 | tf_op jit(solution)/shard_map/ppermute | solution.py:691
  51.5 8.8 %collective-permute-start.30 = (bf16[2,96,768]{2,1,0:T(8,128)(2,1)S(1)}, bf16[2,96,768]{2,1,0:T(8,128)(2,1)S(1)}, u32[]{:S(2)}, u32[]{:S(2)}) collective-permute-start(bf16[2,96,768]{2,1,0:T(8,128)(2,1)S(1)} %collective-permute-done.15.refs_15_.refs_21_.refs_31_.refs_29_), channel_id=1, source_target_pairs={{0,16},{16,0},{1,17},{17,1},{2,18},{18,2},{3,19},{19,3},{4,20},{20... | collective-permute-start | bytes 884744 | tf_op jit(solution)/shard_map/ppermute | solution.py:687
  53.5 10.4 %collective-permute-start.31 = (bf16[2,96,768]{2,1,0:T(8,128)(2,1)S(1)}, bf16[2,96,768]{2,1,0:T(8,128)(2,1)S(1)}, u32[]{:S(2)}, u32[]{:S(2)}) collective-permute-start(bf16[2,96,768]{2,1,0:T(8,128)(2,1)S(1)} %collective-permute-done.16.refs_16_.refs_22_.refs_32_.refs_30_), channel_id=1, source_target_pairs={{0,16},{16,0},{1,17},{17,1},{2,18},{18,2},{3,19},{19,3},{4,20},{20... | collective-permute-start | bytes 884744 | tf_op jit(solution)/shard_map/ppermute | solution.py:687
  53.5 10.9 %collective-permute-start.33 = (bf16[2,96,768]{2,1,0:T(8,128)(2,1)S(1)}, bf16[2,96,768]{2,1,0:T(8,128)(2,1)S(1)}, u32[]{:S(2)}, u32[]{:S(2)}) collective-permute-start(bf16[2,96,768]{2,1,0:T(8,128)(2,1)S(1)} %collective-permute-done.1.refs_18_.refs_24_.refs_34_.refs_32_), channel_id=1, source_target_pairs={{0,16},{16,0},{1,17},{17,1},{2,18},{18,2},{3,19},{19,3},{4,20},{20... | collective-permute-start | bytes 884744 | tf_op jit(solution)/shard_map/ppermute | solution.py:687
  76.5 16.6 %collective-permute-start.44 = (bf16[768,768]{1,0:T(8,128)(2,1)S(1)}, bf16[768,768]{1,0:T(8,128)(2,1)S(1)}, u32[]{:S(2)}, u32[]{:S(2)}) collective-permute-start(bf16[768,768]{1,0:T(8,128)(2,1)S(1)} %bitcast.89), channel_id=1, source_target_pairs={{0,16},{16,0},{1,17},{17,1},{2,18},{18,2},{3,19},{19,3},{4,20},{20... | collective-permute-start | bytes 3538952 | tf_op jit(solution)/shard_map/ppermute | solution.py:687
  76.8 16.3 %collective-permute-start.45 = (bf16[768,768]{1,0:T(8,128)(2,1)}, bf16[768,768]{1,0:T(8,128)(2,1)S(1)}, u32[]{:S(2)}, u32[]{:S(2)}) collective-permute-start(bf16[768,768]{1,0:T(8,128)(2,1)} %bitcast.93), channel_id=1, source_target_pairs={{0,16},{16,0},{1,17},{17,1},{2,18},{18,2},{3,19},{19,3},{4,20},{20... | collective-permute-start | bytes 3538952 | tf_op jit(solution)/shard_map/ppermute | solution.py:687
  121.7 6.4 %collective-permute-start.52 = (bf16[2,24,768]{2,1,0:T(8,128)(2,1)}, bf16[2,24,768]{2,1,0:T(8,128)(2,1)S(1)}, u32[]{:S(2)}, u32[]{:S(2)}) collective-permute-start(bf16[2,24,768]{2,1,0:T(8,128)(2,1)} %get-tuple-element.192), channel_id=1, source_target_pairs={{0,2},{2,4},{4,6},{6,0},{1,3},{3,5},{5,7},{7,1},{8,10},{10,12},{12... | collective-permute-start | bytes 221192 | tf_op jit(solution)/shard_map/ppermute | solution.py:678
  121.7 6.4 %collective-permute-start.53 = (bf16[2,24,768]{2,1,0:T(8,128)(2,1)}, bf16[2,24,768]{2,1,0:T(8,128)(2,1)S(1)}, u32[]{:S(2)}, u32[]{:S(2)}) collective-permute-start(bf16[2,24,768]{2,1,0:T(8,128)(2,1)} %get-tuple-element.193), channel_id=1, source_target_pairs={{0,4},{2,6},{4,0},{6,2},{1,5},{3,7},{5,1},{7,3},{8,12},{10,14},{12... | collective-permute-start | bytes 221192 | tf_op jit(solution)/shard_map/ppermute | solution.py:678
  132.2 8.3 %collective-permute-start.57 = (bf16[2,80,768]{2,1,0:T(8,128)(2,1)S(1)}, bf16[2,80,768]{2,1,0:T(8,128)(2,1)S(1)}, u32[]{:S(2)}, u32[]{:S(2)}) collective-permute-start(bf16[2,80,768]{2,1,0:T(8,128)(2,1)S(1)} %pack.4.refs_1_), channel_id=1, source_target_pairs={{0,9},{1,8},{8,1},{9,0},{2,11},{3,10},{10,3},{11,2},{4,13},{5,12},... | collective-permute-start | bytes 737288 | tf_op jit(solution)/shard_map/ppermute | solution.py:691
  147.8 8.3 %collective-permute-start.60 = (bf16[2,80,768]{2,1,0:T(8,128)(2,1)S(1)}, bf16[2,80,768]{2,1,0:T(8,128)(2,1)S(1)}, u32[]{:S(2)}, u32[]{:S(2)}) collective-permute-start(bf16[2,80,768]{2,1,0:T(8,128)(2,1)S(1)} %get-tuple-element.198), channel_id=1, source_target_pairs={{0,9},{1,8},{8,1},{9,0},{2,11},{3,10},{10,3},{11,2},{4,13},{5,12},... | collective-permute-start | bytes 737288 | tf_op jit(solution)/shard_map/ppermute | solution.py:691
  186.2 10.7 %collective-permute-start.73 = (bf16[192,768]{1,0:T(8,128)(2,1)}, bf16[192,768]{1,0:T(8,128)(2,1)S(1)}, u32[]{:S(2)}, u32[]{:S(2)}) collective-permute-start(bf16[192,768]{1,0:T(8,128)(2,1)} %get-tuple-element.218), channel_id=1, source_target_pairs={{0,1},{1,0},{8,9},{9,8},{2,3},{3,2},{10,11},{11,10},{4,5},{5,4},{1... | collective-permute-start | bytes 884744 | tf_op jit(solution)/shard_map/ppermute | solution.py:691
  187.5 9.4 %collective-permute-start.74 = (bf16[192,768]{1,0:T(8,128)(2,1)}, bf16[192,768]{1,0:T(8,128)(2,1)S(1)}, u32[]{:S(2)}, u32[]{:S(2)}) collective-permute-start(bf16[192,768]{1,0:T(8,128)(2,1)} %get-tuple-element.219), channel_id=1, source_target_pairs={{0,8},{1,9},{8,0},{9,1},{2,10},{3,11},{10,2},{11,3},{4,12},{5,13},... | collective-permute-start | bytes 884744 | tf_op jit(solution)/shard_map/ppermute | solution.py:691
  188.2 9.6 %collective-permute-start.75 = (bf16[192,768]{1,0:T(8,128)(2,1)}, bf16[192,768]{1,0:T(8,128)(2,1)S(1)}, u32[]{:S(2)}, u32[]{:S(2)}) collective-permute-start(bf16[192,768]{1,0:T(8,128)(2,1)} %get-tuple-element.220), channel_id=1, source_target_pairs={{0,9},{1,8},{8,1},{9,0},{2,11},{3,10},{10,3},{11,2},{4,13},{5,12},... | collective-permute-start | bytes 884744 | tf_op jit(solution)/shard_map/ppermute | solution.py:691
  199.4 14.3 %collective-permute-start.80 = (bf16[4,112,768]{2,1,0:T(8,128)(2,1)S(1)}, bf16[4,112,768]{2,1,0:T(8,128)(2,1)S(1)}, u32[]{:S(2)}, u32[]{:S(2)}) collective-permute-start(bf16[4,112,768]{2,1,0:T(8,128)(2,1)S(1)} %get-tuple-element.227), channel_id=1, source_target_pairs={{0,16},{16,0},{1,17},{17,1},{2,18},{18,2},{3,19},{19,3},{4,20},{20... | collective-permute-start | bytes 2064392 | tf_op jit(solution)/shard_map/ppermute | solution.py:687
  201.5 7.5 %collective-permute-start.72 = (bf16[1,80,768]{2,1,0:T(8,128)(2,1)S(1)}, bf16[1,80,768]{2,1,0:T(8,128)(2,1)S(1)}, u32[]{:S(2)}, u32[]{:S(2)}) collective-permute-start(bf16[1,80,768]{2,1,0:T(8,128)(2,1)S(1)} %get-tuple-element.216), channel_id=1, source_target_pairs={{0,9},{1,8},{8,1},{9,0},{2,11},{3,10},{10,3},{11,2},{4,13},{5,12},... | collective-permute-start | bytes 368648 | tf_op jit(solution)/shard_map/ppermute | solution.py:691
  209.9 8.5 %collective-permute-start.76 = (bf16[1,24,768]{2,1,0:T(8,128)(2,1)S(1)}, bf16[1,24,768]{2,1,0:T(8,128)(2,1)S(1)}, u32[]{:S(2)}, u32[]{:S(2)}) collective-permute-start(bf16[1,24,768]{2,1,0:T(8,128)(2,1)S(1)} %get-tuple-element.233), channel_id=1, source_target_pairs={{0,6},{2,0},{4,2},{6,4},{1,7},{3,1},{5,3},{7,5},{8,14},{10,8},{12,... | collective-permute-start | bytes 110600 | tf_op jit(solution)/shard_map/ppermute | solution.py:678
  214.0 13.5 %collective-permute-start.83 = (bf16[112,768]{1,0:T(8,128)(2,1)S(1)}, bf16[112,768]{1,0:T(8,128)(2,1)S(1)}, u32[]{:S(2)}, u32[]{:S(2)}) collective-permute-start(bf16[112,768]{1,0:T(8,128)(2,1)S(1)} %get-tuple-element.245), channel_id=1, source_target_pairs={{0,6},{2,0},{4,2},{6,4},{1,7},{3,1},{5,3},{7,5},{8,14},{10,8},{12,... | collective-permute-start | bytes 516104 | tf_op jit(solution)/shard_map/ppermute | solution.py:678
  217.5 15.5 %collective-permute-start.82 = (bf16[112,768]{1,0:T(8,128)(2,1)S(1)}, bf16[112,768]{1,0:T(8,128)(2,1)S(1)}, u32[]{:S(2)}, u32[]{:S(2)}) collective-permute-start(bf16[112,768]{1,0:T(8,128)(2,1)S(1)} %get-tuple-element.244), channel_id=1, source_target_pairs={{0,4},{2,6},{4,0},{6,2},{1,5},{3,7},{5,1},{7,3},{8,12},{10,14},{12... | collective-permute-start | bytes 516104 | tf_op jit(solution)/shard_map/ppermute | solution.py:678
  218.4 14.6 %collective-permute-start.81 = (bf16[112,768]{1,0:T(8,128)(2,1)S(1)}, bf16[112,768]{1,0:T(8,128)(2,1)S(1)}, u32[]{:S(2)}, u32[]{:S(2)}) collective-permute-start(bf16[112,768]{1,0:T(8,128)(2,1)S(1)} %get-tuple-element.243), channel_id=1, source_target_pairs={{0,2},{2,4},{4,6},{6,0},{1,3},{3,5},{5,7},{7,1},{8,10},{10,12},{12... | collective-permute-start | bytes 516104 | tf_op jit(solution)/shard_map/ppermute | solution.py:678
  233.8 8.9 %collective-permute-start.84 = (bf16[64,768]{1,0:T(8,128)(2,1)}, bf16[64,768]{1,0:T(8,128)(2,1)S(1)}, u32[]{:S(2)}, u32[]{:S(2)}) collective-permute-start(bf16[64,768]{1,0:T(8,128)(2,1)} %get-tuple-element.247), channel_id=1, source_target_pairs={{0,1},{1,0},{8,9},{9,8},{2,3},{3,2},{10,11},{11,10},{4,5},{5,4},{1... | collective-permute-start | bytes 294920 | tf_op jit(solution)/shard_map/ppermute | solution.py:691
  235.1 7.6 %collective-permute-start.85 = (bf16[64,768]{1,0:T(8,128)(2,1)}, bf16[64,768]{1,0:T(8,128)(2,1)S(1)}, u32[]{:S(2)}, u32[]{:S(2)}) collective-permute-start(bf16[64,768]{1,0:T(8,128)(2,1)} %get-tuple-element.248), channel_id=1, source_target_pairs={{0,8},{1,9},{8,0},{9,1},{2,10},{3,11},{10,2},{11,3},{4,12},{5,13},... | collective-permute-start | bytes 294920 | tf_op jit(solution)/shard_map/ppermute | solution.py:691
  235.8 6.9 %collective-permute-start.86 = (bf16[64,768]{1,0:T(8,128)(2,1)}, bf16[64,768]{1,0:T(8,128)(2,1)S(1)}, u32[]{:S(2)}, u32[]{:S(2)}) collective-permute-start(bf16[64,768]{1,0:T(8,128)(2,1)} %get-tuple-element.249), channel_id=1, source_target_pairs={{0,9},{1,8},{8,1},{9,0},{2,11},{3,10},{10,3},{11,2},{4,13},{5,12},... | collective-permute-start | bytes 294920 | tf_op jit(solution)/shard_map/ppermute | solution.py:691
  242.6 28.1 %collective-permute-start.95 = (bf16[2,768,768]{2,1,0:T(8,128)(2,1)}, bf16[2,768,768]{2,1,0:T(8,128)(2,1)}, u32[]{:S(2)}, u32[]{:S(2)}) collective-permute-start(bf16[2,768,768]{2,1,0:T(8,128)(2,1)} %expert_gradients_sent.1), channel_id=1, source_target_pairs={{0,16},{16,0},{1,17},{17,1},{2,18},{18,2},{3,19},{19,3},{4,20},{20... | collective-permute-start | bytes 7077896 | tf_op jit(solution)/shard_map/ppermute | solution.py:687
  248.4 7.5 %collective-permute-start.90 = (bf16[112,768]{1,0:T(8,128)(2,1)S(1)}, bf16[112,768]{1,0:T(8,128)(2,1)S(1)}, u32[]{:S(2)}, u32[]{:S(2)}) collective-permute-start(bf16[112,768]{1,0:T(8,128)(2,1)S(1)} %get-tuple-element.292), channel_id=1, source_target_pairs={{0,6},{2,0},{4,2},{6,4},{1,7},{3,1},{5,3},{7,5},{8,14},{10,8},{12,... | collective-permute-start | bytes 516104 | tf_op jit(solution)/shard_map/ppermute | solution.py:678
  248.5 16.7 %collective-permute-start.89 = (bf16[112,768]{1,0:T(8,128)(2,1)S(1)}, bf16[112,768]{1,0:T(8,128)(2,1)S(1)}, u32[]{:S(2)}, u32[]{:S(2)}) collective-permute-start(bf16[112,768]{1,0:T(8,128)(2,1)S(1)} %get-tuple-element.293), channel_id=1, source_target_pairs={{0,4},{2,6},{4,0},{6,2},{1,5},{3,7},{5,1},{7,3},{8,12},{10,14},{12... | collective-permute-start | bytes 516104 | tf_op jit(solution)/shard_map/ppermute | solution.py:678
  249.6 15.7 %collective-permute-start.88 = (bf16[112,768]{1,0:T(8,128)(2,1)S(1)}, bf16[112,768]{1,0:T(8,128)(2,1)S(1)}, u32[]{:S(2)}, u32[]{:S(2)}) collective-permute-start(bf16[112,768]{1,0:T(8,128)(2,1)S(1)} %get-tuple-element.291), channel_id=1, source_target_pairs={{0,2},{2,4},{4,6},{6,0},{1,3},{3,5},{5,7},{7,1},{8,10},{10,12},{12... | collective-permute-start | bytes 516104 | tf_op jit(solution)/shard_map/ppermute | solution.py:678
  251.6 14.6 %collective-permute-start.79 = (f32[64,768]{1,0:T(8,128)S(1)}, f32[64,768]{1,0:T(8,128)S(1)}, u32[]{:S(2)}, u32[]{:S(2)}) collective-permute-start(f32[64,768]{1,0:T(8,128)S(1)} %broadcast_select_fusion.2), channel_id=1, source_target_pairs={{0,16},{16,0},{1,17},{17,1},{2,18},{18,2},{3,19},{19,3},{4,20},{20... | collective-permute-start | bytes 589832 | tf_op jit(solution)/shard_map/ppermute | solution.py:687
  267.0 10.1 %collective-permute-start.92 = (bf16[112,768]{1,0:T(8,128)(2,1)S(1)}, bf16[112,768]{1,0:T(8,128)(2,1)S(1)}, u32[]{:S(2)}, u32[]{:S(2)}) collective-permute-start(bf16[112,768]{1,0:T(8,128)(2,1)S(1)} %broadcast_select_fusion.1), channel_id=1, source_target_pairs={{0,8},{1,24},{8,0},{9,16},{16,9},{17,25},{24,1},{25,17},{2,10},{3,... | collective-permute-start | bytes 516104 | tf_op jit(solution)/shard_map/ppermute | solution.py:1106
  268.4 8.6 %collective-permute-start.93 = (bf16[112,768]{1,0:T(8,128)(2,1)S(1)}, bf16[112,768]{1,0:T(8,128)(2,1)S(1)}, u32[]{:S(2)}, u32[]{:S(2)}) collective-permute-start(bf16[112,768]{1,0:T(8,128)(2,1)S(1)} %get-tuple-element.288), channel_id=1, source_target_pairs={{0,16},{1,0},{8,24},{9,8},{16,17},{17,1},{24,25},{25,9},{2,18},{3,... | collective-permute-start | bytes 516104 | tf_op jit(solution)/shard_map/ppermute | solution.py:1106
  270.5 8.8 %collective-permute-start.94 = (bf16[112,768]{1,0:T(8,128)(2,1)S(1)}, bf16[112,768]{1,0:T(8,128)(2,1)S(1)}, u32[]{:S(2)}, u32[]{:S(2)}) collective-permute-start(bf16[112,768]{1,0:T(8,128)(2,1)S(1)} %get-tuple-element.288), channel_id=1, source_target_pairs={{0,24},{1,8},{8,16},{9,0},{16,25},{17,9},{24,17},{25,1},{2,26},{3,... | collective-permute-start | bytes 516104 | tf_op jit(solution)/shard_map/ppermute | solution.py:1106
  (132 other events, 1094.2 us)

commit v5 on v4

--- a/solution.py
+++ b/solution.py
@@ -719,7 +719,7 @@
     table_slab = rel_table.shape[1]
     cap = max(2, rows // experts + 1)
     cap_pad = up(cap, 8)
-    packed = up(experts * cap, 16)
+    packed = up(experts * cap, 8)
     ff = expert_in.shape[3]
     first = s == 0
 

time: 282 us -> 280 us (level)
    ppermute x31, waiting for transfers between devices: 49.1 us -> 42.8 us  [shift(): return lax.ppermute(v, axis, [(i, (i + by) % n) for i in range(n)])]
    ppermute x36, waiting for transfers between devices: 38.7 us -> 43.9 us  [plane_swap(): return lax.ppermute(v, PLANE, [(i, i ^ mask) for i in range(4)])]
    unnamed x168 -> x166, local copies, waits for them, and re-layouts: 10.7 us -> 10.5 us
  transfers between devices with their start and end apart: 96 -> 96, of which waited for: 46 -> 43; matrix products, arithmetic and copies ran while one was open for 3% -> 3% of each run, Pallas kernels for 9% -> 9%
where the time goes in v5:
time: 280 us; the launch traced here: 279 us
  starting transfers between devices  104 us (37%)
  waiting for transfers between devices  94.2 us (34%)
  Pallas kernels  57.6 us (21%)
  local copies, waits for them, and re-layouts  13.5 us (5%)
  other arithmetic  7.54 us (3%)
    pallas_call x18, Pallas kernels, call(): pl.pallas_call(kernel, out_shape=[jax.ShapeDtypeStruct(shape, dtype) for...  57.6 us
    ppermute x31, starting transfers between devices, shift(): return lax.ppermute(v, axis, [(i, (i + by) % n) for i in range(n)])  52.1 us
    ppermute x36, waiting for transfers between devices, plane_swap(): return lax.ppermute(v, PLANE, [(i, i ^ mask) for i in range(4)])  43.9 us
    ppermute x36, starting transfers between devices, plane_swap(): return lax.ppermute(v, PLANE, [(i, i ^ mask) for i in range(4)])  42.9 us
    ppermute x31, waiting for transfers between devices, shift(): return lax.ppermute(v, axis, [(i, (i + by) % n) for i in range(n)])  42.8 us
    unnamed x166, local copies, waits for them, and re-layouts  10.5 us
  transfers between devices with their start and end apart: 96, of which 43 were waited for; matrix products, arithmetic and copies ran while one was open for 3% of the time, Pallas kernels for 9%

profile of v5, /device:TPU:0, one launch (start us, length us, event | category | flops | bytes accessed | tf_op | source)
XLA Modules:
  0.0 278.8 jit_solution(14637276459461555834)
XLA Ops:
  1.8 3.1 %collective-permute-start = (bf16[2,96,768]{2,1,0:T(8,128)(2,1)S(1)}, bf16[2,96,768]{2,1,0:T(8,128)(2,1)S(1)}, u32[]{:S(2)}, u32[]{:S(2)}) collective-permute-start(bf16[2,96,768]{2,1,0:T(8,128)(2,1)S(1)} %fusion.3), channel_id=1, source_target_pairs={{0,2},{2,4},{4,6},{6,0},{1,3},{3,5},{5,7},{7,1},{8,10},{10,12},{12... | collective-permute-start | bytes 884744 | tf_op jit(solution)/shard_map/ppermute | solution.py:678
  4.9 2.1 collective-permute-start.14
  11.6 3.2 %collective-permute-done.refs_10_.refs_16_.refs_26_.refs_24_ = bf16[2,96,768]{2,1,0:T(8,128)(2,1)S(1)} collective-permute-done((bf16[2,96,768]{2,1,0:T(8,128)(2,1)S(1)}, bf16[2,96,768]{2,1,0:T(8,128)(2,1)S(1)}, u32[]{:S(2)}, u32[]{:S(2)}) %collective-permute-start) | collective-permute-done | bytes 294944 | tf_op jit(solution)/shard_map/ppermute | solution.py:678
  17.2 9.1 %collective-permute-start.1 = (bf16[2,96,768]{2,1,0:T(8,128)(2,1)S(1)}, bf16[2,96,768]{2,1,0:T(8,128)(2,1)S(1)}, u32[]{:S(2)}, u32[]{:S(2)}) collective-permute-start(bf16[2,96,768]{2,1,0:T(8,128)(2,1)S(1)} %fusion.3), channel_id=1, source_target_pairs={{0,4},{2,6},{4,0},{6,2},{1,5},{3,7},{5,1},{7,3},{8,12},{10,14},{12... | collective-permute-start | bytes 884744 | tf_op jit(solution)/shard_map/ppermute | solution.py:678
  28.4 2.5 collective-permute-start.6
  36.1 2.1 collective-permute-start.7
  41.9 2.7 collective-permute-done.11.refs_9_.refs_15_.refs_25_.refs_23_
  46.7 2.0 collective-permute-done.8
  51.2 3.4 %collective-permute-done.19.refs_20_.refs_26_.refs_36_.refs_34_ = bf16[2,96,768]{2,1,0:T(8,128)(2,1)S(1)} collective-permute-done((bf16[2,96,768]{2,1,0:T(8,128)(2,1)S(1)}, bf16[2,96,768]{2,1,0:T(8,128)(2,1)S(1)}, u32[]{:S(2)}, u32[]{:S(2)}) %collective-permute-start.19) | collective-permute-done | bytes 294944 | tf_op jit(solution)/shard_map/ppermute | solution.py:691
  56.1 4.8 %collective-permute-done.13.refs_13_.refs_19_.refs_29_.refs_27_ = bf16[2,96,768]{2,1,0:T(8,128)(2,1)} collective-permute-done((bf16[2,96,768]{2,1,0:T(8,128)(2,1)}, bf16[2,96,768]{2,1,0:T(8,128)(2,1)}, u32[]{:S(2)}, u32[]{:S(2)}) %collective-permute-start.13) | collective-permute-done | bytes 294944 | tf_op jit(solution)/shard_map/ppermute | solution.py:691
  62.6 3.5 %collective-permute-done.21.refs_22_.refs_28_.refs_38_.refs_36_ = bf16[1,96,768]{2,1,0:T(8,128)(2,1)S(1)} collective-permute-done((bf16[1,96,768]{2,1,0:T(8,128)(2,1)S(1)}, bf16[1,96,768]{2,1,0:T(8,128)(2,1)S(1)}, u32[]{:S(2)}, u32[]{:S(2)}) %collective-permute-start.21) | collective-permute-done | bytes 147488 | tf_op jit(solution)/shard_map/ppermute | solution.py:691
  73.1 6.1 %attention_forward.2 = (bf16[64,768]{1,0:T(8,128)(2,1)}, bf16[3,64,768]{2,1,0:T(8,128)(2,1)}, f32[6,128,64]{2,1,0:T(8,128)}, bf16[64,768]{1,0:T(8,128)(2,1)}, f3...) custom-call(s32[9]{0:T(128)} %concatenate.10.refs_0_.meta, ...), custom_call_target="tpu_custom_call" | custom-call | flops 6000000000 | bytes 18000000 | tf_op jit(solution)/shard_map/attention_forward/pallas_call | solution.py:662
  79.7 3.5 %collective-permute-start.39 = (bf16[24,768]{1,0:T(8,128)(2,1)}, bf16[24,768]{1,0:T(8,128)(2,1)S(1)}, u32[]{:S(2)}, u32[]{:S(2)}) collective-permute-start(bf16[24,768]{1,0:T(8,128)(2,1)} %get-tuple-element.169), channel_id=1, source_target_pairs={{0,4},{2,6},{4,0},{6,2},{1,5},{3,7},{5,1},{7,3},{8,12},{10,14},{12... | collective-permute-start | bytes 110600 | tf_op jit(solution)/shard_map/ppermute | solution.py:678
  83.6 2.5 collective-permute-done.38
  89.5 2.5 collective-permute-start.43
  92.0 2.4 collective-permute-done.41.refs_2_
  94.4 1.8 collective-permute-done.43.refs_4_
  96.3 3.2 %expert_forward.2 = (bf16[1,72,768]{2,1,0:T(8,128)(2,1)S(1)}, bf16[1,72,768]{2,1,0:T(8,128)(2,1)S(1)}, bf16[1,72,768]{2,1,0:T(8,128)(2,1)S(1)}, bf16[1,72,768]{2...) custom-call(s32[9]{0:T(128)S(1)} %copy-done.2, ...), custom_call_target="tpu_custom_call" | custom-call | flops 4000000000 | bytes 12000000 | tf_op jit(solution)/shard_map/expert_forward/pallas_call | solution.py:662
  103.1 2.3 collective-permute-done.46.refs_1_
  105.4 1.8 collective-permute-done.48.refs_3_
  108.1 2.2 collective-permute-start.49
  112.1 3.1 %collective-permute-done.50 = bf16[1,24,768]{2,1,0:T(8,128)(2,1)S(1)} collective-permute-done((bf16[1,24,768]{2,1,0:T(8,128)(2,1)S(1)}, bf16[1,24,768]{2,1,0:T(8,128)(2,1)S(1)}, u32[]{:S(2)}, u32[]{:S(2)}) %collective-permute-start.50) | collective-permute-done | bytes 36896 | tf_op jit(solution)/shard_map/ppermute | solution.py:678
  116.8 6.6 %attention_forward.3 = (bf16[64,768]{1,0:T(8,128)(2,1)}, bf16[3,64,768]{2,1,0:T(8,128)(2,1)}, f32[6,128,64]{2,1,0:T(8,128)}, bf16[64,768]{1,0:T(8,128)(2,1)}, f3...) custom-call(s32[9]{0:T(128)} %concatenate.10.refs_0_.meta, ...), custom_call_target="tpu_custom_call" | custom-call | flops 6000000000 | bytes 18000000 | tf_op jit(solution)/shard_map/attention_forward/pallas_call | solution.py:662
  124.6 2.8 %collective-permute-start.54 = (bf16[2,24,768]{2,1,0:T(8,128)(2,1)}, bf16[2,24,768]{2,1,0:T(8,128)(2,1)S(1)}, u32[]{:S(2)}, u32[]{:S(2)}) collective-permute-start(bf16[2,24,768]{2,1,0:T(8,128)(2,1)} %get-tuple-element.194), channel_id=1, source_target_pairs={{0,6},{2,0},{4,2},{6,4},{1,7},{3,1},{5,3},{7,5},{8,14},{10,8},{12,... | collective-permute-start | bytes 221192 | tf_op jit(solution)/shard_map/ppermute | solution.py:678
  127.4 2.5 collective-permute-done.52.refs_1_
  135.5 2.4 collective-permute-done.55.refs_2_
  139.2 2.6 collective-permute-done.57.refs_4_
  141.8 4.7 %expert_forward.3 = (bf16[2,72,768]{2,1,0:T(8,128)(2,1)S(1)}, bf16[2,72,768]{2,1,0:T(8,128)(2,1)S(1)}, bf16[2,72,768]{2,1,0:T(8,128)(2,1)S(1)}, bf16[2,72,768]{2...) custom-call(s32[9]{0:T(128)S(1)} %copy-done.3, ...), custom_call_target="tpu_custom_call" | custom-call | flops 4000000000 | bytes 12000000 | tf_op jit(solution)/shard_map/expert_forward/pallas_call | solution.py:662
  150.1 2.4 collective-permute-done.58.refs_1_
  153.8 2.6 collective-permute-done.60.refs_3_
  157.4 3.2 %collective-permute-start.61 = (bf16[2,24,768]{2,1,0:T(8,128)(2,1)S(1)}, bf16[2,24,768]{2,1,0:T(8,128)(2,1)S(1)}, u32[]{:S(2)}, u32[]{:S(2)}) collective-permute-start(bf16[2,24,768]{2,1,0:T(8,128)(2,1)S(1)} %get-tuple-element.200), channel_id=1, source_target_pairs={{0,6},{2,0},{4,2},{6,4},{1,7},{3,1},{5,3},{7,5},{8,14},{10,8},{12,... | collective-permute-start | bytes 221192 | tf_op jit(solution)/shard_map/ppermute | solution.py:678
  162.5 3.3 %collective-permute-done.62.refs_21_ = bf16[2,24,768]{2,1,0:T(8,128)(2,1)S(1)} collective-permute-done((bf16[2,24,768]{2,1,0:T(8,128)(2,1)S(1)}, bf16[2,24,768]{2,1,0:T(8,128)(2,1)S(1)}, u32[]{:S(2)}, u32[]{:S(2)}) %collective-permute-start.62) | collective-permute-done | bytes 73760 | tf_op jit(solution)/shard_map/ppermute | solution.py:678
  167.5 7.8 %attention_backward.2 = (f32[64,768]{1,0:T(8,128)}, f32[16,768]{1,0:T(8,128)}, bf16[192,768]{1,0:T(8,128)(2,1)}, bf16[192,768]{1,0:T(8,128)(2,1)}, bf16[192,768]...) custom-call(s32[9]{0:T(128)} %concatenate.10.refs_0_.meta, ...), custom_call_target="tpu_custom_call" | custom-call | flops 8000000000 | bytes 24000000 | tf_op jit(solution)/shard_map/attention_backward/pallas_call | solution.py:662
  176.6 2.7 collective-permute-start.66
  179.3 2.0 collective-permute-done.64
  191.7 4.0 %expert_backward.1 = (bf16[1,72,768]{2,1,0:T(8,128)(2,1)S(1)}, bf16[1,72,768]{2,1,0:T(8,128)(2,1)S(1)}, bf16[1,72,768]{2,1,0:T(8,128)(2,1)S(1)}, bf16[1,72,768]{...) custom-call(s32[9]{0:T(128)S(1)} %copy-done.4, bf16[1,72,768]{2,1,0:T(8,128)(2,1)S(1)} %pack.5.refs_1_, ...), custom_call_target="tpu_custom_call" | custom-call | flops 4000000000 | bytes 12000000 | tf_op jit(solution)/shard_map/expert_backward/pallas_call | solution.py:662
  206.9 1.9 collective-permute-done.72.refs_3_
  209.6 3.4 %collective-permute-start.76 = (bf16[1,24,768]{2,1,0:T(8,128)(2,1)S(1)}, bf16[1,24,768]{2,1,0:T(8,128)(2,1)S(1)}, u32[]{:S(2)}, u32[]{:S(2)}) collective-permute-start(bf16[1,24,768]{2,1,0:T(8,128)(2,1)S(1)} %get-tuple-element.233), channel_id=1, source_target_pairs={{0,6},{2,0},{4,2},{6,4},{1,7},{3,1},{5,3},{7,5},{8,14},{10,8},{12,... | collective-permute-start | bytes 110600 | tf_op jit(solution)/shard_map/ppermute | solution.py:678
  213.8 3.0 %collective-permute-start.81 = (bf16[112,768]{1,0:T(8,128)(2,1)S(1)}, bf16[112,768]{1,0:T(8,128)(2,1)S(1)}, u32[]{:S(2)}, u32[]{:S(2)}) collective-permute-start(bf16[112,768]{1,0:T(8,128)(2,1)S(1)} %get-tuple-element.243), channel_id=1, source_target_pairs={{0,2},{2,4},{4,6},{6,0},{1,3},{3,5},{5,7},{7,1},{8,10},{10,12},{12... | collective-permute-start | bytes 516104 | tf_op jit(solution)/shard_map/ppermute | solution.py:678
  219.2 5.2 %collective-permute-done.77 = bf16[1,24,768]{2,1,0:T(8,128)(2,1)S(1)} collective-permute-done((bf16[1,24,768]{2,1,0:T(8,128)(2,1)S(1)}, bf16[1,24,768]{2,1,0:T(8,128)(2,1)S(1)}, u32[]{:S(2)}, u32[]{:S(2)}) %collective-permute-start.77) | collective-permute-done | bytes 36896 | tf_op jit(solution)/shard_map/ppermute | solution.py:678
  225.0 7.1 %attention_backward.3 = (f32[64,768]{1,0:T(8,128)}, f32[16,768]{1,0:T(8,128)}, bf16[64,768]{1,0:T(8,128)(2,1)}, bf16[64,768]{1,0:T(8,128)(2,1)}, bf16[64,768]{1,0:T(8,128)(2,1)}, /*index=5*/bf16[64,768]{1,0:T(8,128)(2,1)}) custom-call(s32[9]{0:T(128)} %concatenate.10.refs_0_.meta, bf16[2,2,4,8,96]{4,3,2,1,0:T(8,128)(2,1)} %pad_maximum_fusion.1.refs_1_, ...), custom_call_target="tpu_custom_call" | custom-call | flops 2000000000 | bytes 6000000 | tf_op jit(solution)/shard_map/attention_backward/pallas_call | solution.py:662
  236.5 5.3 %expert_gradients_sent.1 = bf16[2,768,768]{2,1,0:T(8,128)(2,1)} custom-call(s32[9]{0:T(128)} %concatenate.10.refs_0_.meta, bf16[288,768]{1,0:T(8,128)(2,1)} %copy-done.34, bf16[288,768]{1,0:T(8,128)(2,1)} %copy-done.29, bf16[288,768]{1,0:T(8,128)(2,1)} %copy-done.35, bf16[288,768]{1,0:T(8,128)(2,1)} %copy-done.28, bf16[288,768]{1,0:T(8,128)(2,1)} %copy-done.30, ...), custom_call_target="tpu_custom_call" | custom-call | flops 5000000000 | bytes 15000000 | tf_op jit(solution)/shard_map/expert_gradients_sent/pallas_call | solution.py:662
  244.0 3.4 %collective-permute-done.87 = bf16[4,112,768]{2,1,0:T(8,128)(2,1)S(1)} collective-permute-done((bf16[4,112,768]{2,1,0:T(8,128)(2,1)S(1)}, bf16[4,112,768]{2,1,0:T(8,128)(2,1)S(1)}, u32[]{:S(2)}, u32[]{:S(2)}) %collective-permute-start.87) | collective-permute-done | bytes 688160 | tf_op jit(solution)/shard_map/ppermute | solution.py:687
  248.5 2.0 collective-permute-start.89
  251.6 5.2 %collective-permute-done.88 = bf16[112,768]{1,0:T(8,128)(2,1)S(1)} collective-permute-done((bf16[112,768]{1,0:T(8,128)(2,1)S(1)}, bf16[112,768]{1,0:T(8,128)(2,1)S(1)}, u32[]{:S(2)}, u32[]{:S(2)}) %collective-permute-start.88) | collective-permute-done | bytes 172064 | tf_op jit(solution)/shard_map/ppermute | solution.py:678
  256.8 6.6 %collective-permute-done.89 = bf16[112,768]{1,0:T(8,128)(2,1)S(1)} collective-permute-done((bf16[112,768]{1,0:T(8,128)(2,1)S(1)}, bf16[112,768]{1,0:T(8,128)(2,1)S(1)}, u32[]{:S(2)}, u32[]{:S(2)}) %collective-permute-start.89) | collective-permute-done | bytes 172064 | tf_op jit(solution)/shard_map/ppermute | solution.py:678
  268.6 6.3 %expert_gradients_own.1 = (f32[768,768]{1,0:T(8,128)}, f32[768,768]{1,0:T(8,128)}) custom-call(s32[9]{0:T(128)} %concatenate.10.refs_0_.meta, bf16[288,768]{1,0:T(8,128)(2,1)} %copy-done.34, bf16[288,768]{1,0:T(8,128)(2,1)} %copy-done.29, bf16[288,768]{1,0:T(8,128)(2,1)} %copy-done.35, bf16[288,768]{1,0:T(8,128)(2,1)} %copy-done.28, ...), custom_call_target="tpu_custom_call" | custom-call | flops 6000000000 | bytes 18000000 | tf_op jit(solution)/shard_map/expert_gradients_own/pallas_call | solution.py:662
  275.0 2.2 collective-permute-done.94.refs_3_
  (355 shorter events, 105.9 us)
Async XLA Ops:
  1.8 13.0 %collective-permute-start = (bf16[2,96,768]{2,1,0:T(8,128)(2,1)S(1)}, bf16[2,96,768]{2,1,0:T(8,128)(2,1)S(1)}, u32[]{:S(2)}, u32[]{:S(2)}) collective-permute-start(bf16[2,96,768]{2,1,0:T(8,128)(2,1)S(1)} %fusion.3), channel_id=1, source_target_pairs={{0,2},{2,4},{4,6},{6,0},{1,3},{3,5},{5,7},{7,1},{8,10},{10,12},{12... | collective-permute-start | bytes 884744 | tf_op jit(solution)/shard_map/ppermute | solution.py:678
  4.9 21.4 %collective-permute-start.14 = (bf16[2,96,768]{2,1,0:T(8,128)(2,1)S(1)}, bf16[2,96,768]{2,1,0:T(8,128)(2,1)S(1)}, u32[]{:S(2)}, u32[]{:S(2)}) collective-permute-start(bf16[2,96,768]{2,1,0:T(8,128)(2,1)S(1)} %fusion.3), channel_id=1, source_target_pairs={{0,6},{2,0},{4,2},{6,4},{1,7},{3,1},{5,3},{7,5},{8,14},{10,8},{12,... | collective-permute-start | bytes 884744 | tf_op jit(solution)/shard_map/ppermute | solution.py:678
  7.0 24.6 %collective-permute-start.10 = (bf16[2,96,768]{2,1,0:T(8,128)(2,1)S(1)}, bf16[2,96,768]{2,1,0:T(8,128)(2,1)S(1)}, u32[]{:S(2)}, u32[]{:S(2)}) collective-permute-start(bf16[2,96,768]{2,1,0:T(8,128)(2,1)S(1)} %fusion.3), channel_id=1, source_target_pairs={{0,1},{1,0},{8,9},{9,8},{2,3},{3,2},{10,11},{11,10},{4,5},{5,4},{1... | collective-permute-start | bytes 884744 | tf_op jit(solution)/shard_map/ppermute | solution.py:691
  9.3 7.9 %collective-permute-start.3 = (s32[64]{0:T(128)S(1)}, s32[64]{0:T(128)S(1)}, u32[]{:S(2)}, u32[]{:S(2)}) collective-permute-start(s32[64]{0:T(128)S(1)} %fusion.11), channel_id=1, source_target_pairs={{0,16},{16,0},{1,17},{17,1},{2,18},{18,2},{3,19},{19,3},{4,20},{20... | collective-permute-start | bytes 776 | tf_op jit(solution)/shard_map/ppermute | solution.py:687
  10.2 18.2 %collective-permute-start.2 = (bf16[64,768]{1,0:T(8,128)(2,1)S(1)}, bf16[64,768]{1,0:T(8,128)(2,1)S(1)}, u32[]{:S(2)}, u32[]{:S(2)}) collective-permute-start(bf16[64,768]{1,0:T(8,128)(2,1)S(1)} %dynamic-slice_bitcast_fusion), channel_id=1, source_target_pairs={{0,16},{16,0},{1,17},{17,1},{2,18},{18,2},{3,19},{19,3},{4,20},{20... | collective-permute-start | bytes 294920 | tf_op jit(solution)/shard_map/ppermute | solution.py:687
  14.8 13.6 %collective-permute-start.4 = (bf16[2,96,768]{2,1,0:T(8,128)(2,1)S(1)}, bf16[2,96,768]{2,1,0:T(8,128)(2,1)}, u32[]{:S(2)}, u32[]{:S(2)}) collective-permute-start(bf16[2,96,768]{2,1,0:T(8,128)(2,1)S(1)} %collective-permute-done.refs_10_.refs_16_.refs_26_.refs_24_), channel_id=1, source_target_pairs={{0,1},{1,0},{8,9},{9,8},{2,3},{3,2},{10,11},{11,10},{4,5},{5,4},{1... | collective-permute-start | bytes 884744 | tf_op jit(solution)/shard_map/ppermute | solution.py:691
  17.2 15.8 %collective-permute-start.1 = (bf16[2,96,768]{2,1,0:T(8,128)(2,1)S(1)}, bf16[2,96,768]{2,1,0:T(8,128)(2,1)S(1)}, u32[]{:S(2)}, u32[]{:S(2)}) collective-permute-start(bf16[2,96,768]{2,1,0:T(8,128)(2,1)S(1)} %fusion.3), channel_id=1, source_target_pairs={{0,4},{2,6},{4,0},{6,2},{1,5},{3,7},{5,1},{7,3},{8,12},{10,14},{12... | collective-permute-start | bytes 884744 | tf_op jit(solution)/shard_map/ppermute | solution.py:678
  26.3 8.3 %collective-permute-start.16 = (bf16[2,96,768]{2,1,0:T(8,128)(2,1)S(1)}, bf16[2,96,768]{2,1,0:T(8,128)(2,1)S(1)}, u32[]{:S(2)}, u32[]{:S(2)}) collective-permute-start(bf16[2,96,768]{2,1,0:T(8,128)(2,1)S(1)} %collective-permute-done.14.refs_14_.refs_20_.refs_30_.refs_28_), channel_id=1, source_target_pairs={{0,8},{1,9},{8,0},{9,1},{2,10},{3,11},{10,2},{11,3},{4,12},{5,13},... | collective-permute-start | bytes 884744 | tf_op jit(solution)/shard_map/ppermute | solution.py:691
  28.4 7.6 %collective-permute-start.6 = (bf16[8,96]{1,0:T(8,128)(2,1)S(1)}, bf16[8,96]{1,0:T(8,128)(2,1)S(1)}, u32[]{:S(2)}, u32[]{:S(2)}) collective-permute-start(bf16[8,96]{1,0:T(8,128)(2,1)S(1)} %fusion.7), channel_id=1, source_target_pairs={{0,4},{2,6},{4,0},{6,2},{1,5},{3,7},{5,1},{7,3},{8,12},{10,14},{12... | collective-permute-start | bytes 4616 | tf_op jit(solution)/shard_map/ppermute | solution.py:678
  31.6 8.7 %collective-permute-start.12 = (bf16[2,96,768]{2,1,0:T(8,128)(2,1)S(1)}, bf16[2,96,768]{2,1,0:T(8,128)(2,1)}, u32[]{:S(2)}, u32[]{:S(2)}) collective-permute-start(bf16[2,96,768]{2,1,0:T(8,128)(2,1)S(1)} %collective-permute-done.refs_10_.refs_16_.refs_26_.refs_24_), channel_id=1, source_target_pairs={{0,8},{1,9},{8,0},{9,1},{2,10},{3,11},{10,2},{11,3},{4,12},{5,13},... | collective-permute-start | bytes 884744 | tf_op jit(solution)/shard_map/ppermute | solution.py:691
  33.0 13.0 %collective-permute-start.15 = (bf16[2,96,768]{2,1,0:T(8,128)(2,1)S(1)}, bf16[2,96,768]{2,1,0:T(8,128)(2,1)S(1)}, u32[]{:S(2)}, u32[]{:S(2)}) collective-permute-start(bf16[2,96,768]{2,1,0:T(8,128)(2,1)S(1)} %collective-permute-done.14.refs_14_.refs_20_.refs_30_.refs_28_), channel_id=1, source_target_pairs={{0,1},{1,0},{8,9},{9,8},{2,3},{3,2},{10,11},{11,10},{4,5},{5,4},{1... | collective-permute-start | bytes 884744 | tf_op jit(solution)/shard_map/ppermute | solution.py:691
  34.6 11.5 %collective-permute-start.29 = (bf16[2,96,768]{2,1,0:T(8,128)(2,1)S(1)}, bf16[2,96,768]{2,1,0:T(8,128)(2,1)S(1)}, u32[]{:S(2)}, u32[]{:S(2)}) collective-permute-start(bf16[2,96,768]{2,1,0:T(8,128)(2,1)S(1)} %collective-permute-done.14.refs_14_.refs_20_.refs_30_.refs_28_), channel_id=1, source_target_pairs={{0,16},{16,0},{1,17},{17,1},{2,18},{18,2},{3,19},{19,3},{4,20},{20... | collective-permute-start | bytes 884744 | tf_op jit(solution)/shard_map/ppermute | solution.py:687
  34.6 10.0 %collective-permute-start.11 = (bf16[2,96,768]{2,1,0:T(8,128)(2,1)S(1)}, bf16[2,96,768]{2,1,0:T(8,128)(2,1)S(1)}, u32[]{:S(2)}, u32[]{:S(2)}) collective-permute-start(bf16[2,96,768]{2,1,0:T(8,128)(2,1)S(1)} %collective-permute-done.10.refs_8_.refs_14_.refs_24_.refs_22_), channel_id=1, source_target_pairs={{0,8},{1,9},{8,0},{9,1},{2,10},{3,11},{10,2},{11,3},{4,12},{5,13},... | collective-permute-start | bytes 884744 | tf_op jit(solution)/shard_map/ppermute | solution.py:691
  39.8 9.9 %collective-permute-start.18 = (bf16[2,96,768]{2,1,0:T(8,128)(2,1)S(1)}, bf16[2,96,768]{2,1,0:T(8,128)(2,1)S(1)}, u32[]{:S(2)}, u32[]{:S(2)}) collective-permute-start(bf16[2,96,768]{2,1,0:T(8,128)(2,1)S(1)} %collective-permute-done.1.refs_18_.refs_24_.refs_34_.refs_32_), channel_id=1, source_target_pairs={{0,1},{1,0},{8,9},{9,8},{2,3},{3,2},{10,11},{11,10},{4,5},{5,4},{1... | collective-permute-start | bytes 884744 | tf_op jit(solution)/shard_map/ppermute | solution.py:691
  40.3 8.4 %collective-permute-start.8 = (bf16[4,8,96]{2,1,0:T(8,128)(2,1)S(1)}, bf16[4,8,96]{2,1,0:T(8,128)(2,1)S(1)}, u32[]{:S(2)}, u32[]{:S(2)}) collective-permute-start(bf16[4,8,96]{2,1,0:T(8,128)(2,1)S(1)} %get-tuple-element.305), channel_id=1, source_target_pairs={{0,1},{1,0},{2,3},{3,2},{4,5},{5,4},{6,7},{7,6},{8,9},{9,8},{10,11... | collective-permute-start | bytes 18440 | tf_op jit(solution)/shard_map/ppermute | solution.py:678
  44.6 9.9 %collective-permute-start.19 = (bf16[2,96,768]{2,1,0:T(8,128)(2,1)S(1)}, bf16[2,96,768]{2,1,0:T(8,128)(2,1)S(1)}, u32[]{:S(2)}, u32[]{:S(2)}) collective-permute-start(bf16[2,96,768]{2,1,0:T(8,128)(2,1)S(1)} %collective-permute-done.1.refs_18_.refs_24_.refs_34_.refs_32_), channel_id=1, source_target_pairs={{0,8},{1,9},{8,0},{9,1},{2,10},{3,11},{10,2},{11,3},{4,12},{5,13},... | collective-permute-start | bytes 884744 | tf_op jit(solution)/shard_map/ppermute | solution.py:691
  46.1 8.5 %collective-permute-start.33 = (bf16[2,96,768]{2,1,0:T(8,128)(2,1)S(1)}, bf16[2,96,768]{2,1,0:T(8,128)(2,1)S(1)}, u32[]{:S(2)}, u32[]{:S(2)}) collective-permute-start(bf16[2,96,768]{2,1,0:T(8,128)(2,1)S(1)} %collective-permute-done.1.refs_18_.refs_24_.refs_34_.refs_32_), channel_id=1, source_target_pairs={{0,16},{16,0},{1,17},{17,1},{2,18},{18,2},{3,19},{19,3},{4,20},{20... | collective-permute-start | bytes 884744 | tf_op jit(solution)/shard_map/ppermute | solution.py:687
  46.1 14.8 %collective-permute-start.13 = (bf16[2,96,768]{2,1,0:T(8,128)(2,1)}, bf16[2,96,768]{2,1,0:T(8,128)(2,1)}, u32[]{:S(2)}, u32[]{:S(2)}) collective-permute-start(bf16[2,96,768]{2,1,0:T(8,128)(2,1)} %collective-permute-done.4.refs_11_.refs_17_.refs_27_.refs_25_), channel_id=1, source_target_pairs={{0,8},{1,9},{8,0},{9,1},{2,10},{3,11},{10,2},{11,3},{4,12},{5,13},... | collective-permute-start | bytes 884744 | tf_op jit(solution)/shard_map/ppermute | solution.py:691
  48.8 12.2 %collective-permute-start.17 = (bf16[2,96,768]{2,1,0:T(8,128)(2,1)S(1)}, bf16[2,96,768]{2,1,0:T(8,128)(2,1)}, u32[]{:S(2)}, u32[]{:S(2)}) collective-permute-start(bf16[2,96,768]{2,1,0:T(8,128)(2,1)S(1)} %collective-permute-done.16.refs_16_.refs_22_.refs_32_.refs_30_), channel_id=1, source_target_pairs={{0,1},{1,0},{8,9},{9,8},{2,3},{3,2},{10,11},{11,10},{4,5},{5,4},{1... | collective-permute-start | bytes 884744 | tf_op jit(solution)/shard_map/ppermute | solution.py:691
  51.0 15.3 %collective-permute-start.31 = (bf16[2,96,768]{2,1,0:T(8,128)(2,1)S(1)}, bf16[2,96,768]{2,1,0:T(8,128)(2,1)S(1)}, u32[]{:S(2)}, u32[]{:S(2)}) collective-permute-start(bf16[2,96,768]{2,1,0:T(8,128)(2,1)S(1)} %collective-permute-done.16.refs_16_.refs_22_.refs_32_.refs_30_), channel_id=1, source_target_pairs={{0,16},{16,0},{1,17},{17,1},{2,18},{18,2},{3,19},{19,3},{4,20},{20... | collective-permute-start | bytes 884744 | tf_op jit(solution)/shard_map/ppermute | solution.py:687
  54.5 12.3 %collective-permute-start.30 = (bf16[2,96,768]{2,1,0:T(8,128)(2,1)S(1)}, bf16[2,96,768]{2,1,0:T(8,128)(2,1)S(1)}, u32[]{:S(2)}, u32[]{:S(2)}) collective-permute-start(bf16[2,96,768]{2,1,0:T(8,128)(2,1)S(1)} %collective-permute-done.15.refs_15_.refs_21_.refs_31_.refs_29_), channel_id=1, source_target_pairs={{0,16},{16,0},{1,17},{17,1},{2,18},{18,2},{3,19},{19,3},{4,20},{20... | collective-permute-start | bytes 884744 | tf_op jit(solution)/shard_map/ppermute | solution.py:687
  54.6 8.0 %collective-permute-start.20 = (bf16[1,96,768]{2,1,0:T(8,128)(2,1)S(1)}, bf16[1,96,768]{2,1,0:T(8,128)(2,1)S(1)}, u32[]{:S(2)}, u32[]{:S(2)}) collective-permute-start(bf16[1,96,768]{2,1,0:T(8,128)(2,1)S(1)} %slice.68), channel_id=1, source_target_pairs={{0,8},{1,9},{8,0},{9,1},{2,10},{3,11},{10,2},{11,3},{4,12},{5,13},... | collective-permute-start | bytes 442376 | tf_op jit(solution)/shard_map/ppermute | solution.py:691
  79.2 17.1 %collective-permute-start.44 = (bf16[768,768]{1,0:T(8,128)(2,1)S(1)}, bf16[768,768]{1,0:T(8,128)(2,1)S(1)}, u32[]{:S(2)}, u32[]{:S(2)}) collective-permute-start(bf16[768,768]{1,0:T(8,128)(2,1)S(1)} %bitcast.89), channel_id=1, source_target_pairs={{0,16},{16,0},{1,17},{17,1},{2,18},{18,2},{3,19},{19,3},{4,20},{20... | collective-permute-start | bytes 3538952 | tf_op jit(solution)/shard_map/ppermute | solution.py:687
  79.3 16.9 %collective-permute-start.45 = (bf16[768,768]{1,0:T(8,128)(2,1)}, bf16[768,768]{1,0:T(8,128)(2,1)S(1)}, u32[]{:S(2)}, u32[]{:S(2)}) collective-permute-start(bf16[768,768]{1,0:T(8,128)(2,1)} %bitcast.93), channel_id=1, source_target_pairs={{0,16},{16,0},{1,17},{17,1},{2,18},{18,2},{3,19},{19,3},{4,20},{20... | collective-permute-start | bytes 3538952 | tf_op jit(solution)/shard_map/ppermute | solution.py:687
  133.9 7.9 %collective-permute-start.57 = (bf16[2,72,768]{2,1,0:T(8,128)(2,1)S(1)}, bf16[2,72,768]{2,1,0:T(8,128)(2,1)S(1)}, u32[]{:S(2)}, u32[]{:S(2)}) collective-permute-start(bf16[2,72,768]{2,1,0:T(8,128)(2,1)S(1)} %pack.4.refs_1_), channel_id=1, source_target_pairs={{0,9},{1,8},{8,1},{9,0},{2,11},{3,10},{10,3},{11,2},{4,13},{5,12},... | collective-permute-start | bytes 663560 | tf_op jit(solution)/shard_map/ppermute | solution.py:691
  148.5 7.9 %collective-permute-start.60 = (bf16[2,72,768]{2,1,0:T(8,128)(2,1)S(1)}, bf16[2,72,768]{2,1,0:T(8,128)(2,1)S(1)}, u32[]{:S(2)}, u32[]{:S(2)}) collective-permute-start(bf16[2,72,768]{2,1,0:T(8,128)(2,1)S(1)} %get-tuple-element.198), channel_id=1, source_target_pairs={{0,9},{1,8},{8,1},{9,0},{2,11},{3,10},{10,3},{11,2},{4,13},{5,12},... | collective-permute-start | bytes 663560 | tf_op jit(solution)/shard_map/ppermute | solution.py:691
  186.5 10.0 %collective-permute-start.73 = (bf16[192,768]{1,0:T(8,128)(2,1)}, bf16[192,768]{1,0:T(8,128)(2,1)S(1)}, u32[]{:S(2)}, u32[]{:S(2)}) collective-permute-start(bf16[192,768]{1,0:T(8,128)(2,1)} %get-tuple-element.218), channel_id=1, source_target_pairs={{0,1},{1,0},{8,9},{9,8},{2,3},{3,2},{10,11},{11,10},{4,5},{5,4},{1... | collective-permute-start | bytes 884744 | tf_op jit(solution)/shard_map/ppermute | solution.py:691
  187.7 8.8 %collective-permute-start.74 = (bf16[192,768]{1,0:T(8,128)(2,1)}, bf16[192,768]{1,0:T(8,128)(2,1)S(1)}, u32[]{:S(2)}, u32[]{:S(2)}) collective-permute-start(bf16[192,768]{1,0:T(8,128)(2,1)} %get-tuple-element.219), channel_id=1, source_target_pairs={{0,8},{1,9},{8,0},{9,1},{2,10},{3,11},{10,2},{11,3},{4,12},{5,13},... | collective-permute-start | bytes 884744 | tf_op jit(solution)/shard_map/ppermute | solution.py:691
  188.4 9.7 %collective-permute-start.75 = (bf16[192,768]{1,0:T(8,128)(2,1)}, bf16[192,768]{1,0:T(8,128)(2,1)S(1)}, u32[]{:S(2)}, u32[]{:S(2)}) collective-permute-start(bf16[192,768]{1,0:T(8,128)(2,1)} %get-tuple-element.220), channel_id=1, source_target_pairs={{0,9},{1,8},{8,1},{9,0},{2,11},{3,10},{10,3},{11,2},{4,13},{5,12},... | collective-permute-start | bytes 884744 | tf_op jit(solution)/shard_map/ppermute | solution.py:691
  199.7 13.9 %collective-permute-start.80 = (bf16[4,112,768]{2,1,0:T(8,128)(2,1)S(1)}, bf16[4,112,768]{2,1,0:T(8,128)(2,1)S(1)}, u32[]{:S(2)}, u32[]{:S(2)}) collective-permute-start(bf16[4,112,768]{2,1,0:T(8,128)(2,1)S(1)} %get-tuple-element.227), channel_id=1, source_target_pairs={{0,16},{16,0},{1,17},{17,1},{2,18},{18,2},{3,19},{19,3},{4,20},{20... | collective-permute-start | bytes 2064392 | tf_op jit(solution)/shard_map/ppermute | solution.py:687
  201.7 7.1 %collective-permute-start.72 = (bf16[1,72,768]{2,1,0:T(8,128)(2,1)S(1)}, bf16[1,72,768]{2,1,0:T(8,128)(2,1)S(1)}, u32[]{:S(2)}, u32[]{:S(2)}) collective-permute-start(bf16[1,72,768]{2,1,0:T(8,128)(2,1)S(1)} %get-tuple-element.216), channel_id=1, source_target_pairs={{0,9},{1,8},{8,1},{9,0},{2,11},{3,10},{10,3},{11,2},{4,13},{5,12},... | collective-permute-start | bytes 331784 | tf_op jit(solution)/shard_map/ppermute | solution.py:691
  209.6 8.2 %collective-permute-start.76 = (bf16[1,24,768]{2,1,0:T(8,128)(2,1)S(1)}, bf16[1,24,768]{2,1,0:T(8,128)(2,1)S(1)}, u32[]{:S(2)}, u32[]{:S(2)}) collective-permute-start(bf16[1,24,768]{2,1,0:T(8,128)(2,1)S(1)} %get-tuple-element.233), channel_id=1, source_target_pairs={{0,6},{2,0},{4,2},{6,4},{1,7},{3,1},{5,3},{7,5},{8,14},{10,8},{12,... | collective-permute-start | bytes 110600 | tf_op jit(solution)/shard_map/ppermute | solution.py:678
  213.0 11.4 %collective-permute-start.77 = (bf16[1,24,768]{2,1,0:T(8,128)(2,1)S(1)}, bf16[1,24,768]{2,1,0:T(8,128)(2,1)S(1)}, u32[]{:S(2)}, u32[]{:S(2)}) collective-permute-start(bf16[1,24,768]{2,1,0:T(8,128)(2,1)S(1)} %get-tuple-element.234), channel_id=1, source_target_pairs={{0,4},{2,6},{4,0},{6,2},{1,5},{3,7},{5,1},{7,3},{8,12},{10,14},{12... | collective-permute-start | bytes 110600 | tf_op jit(solution)/shard_map/ppermute | solution.py:678
  213.1 11.3 %collective-permute-start.78 = (bf16[1,24,768]{2,1,0:T(8,128)(2,1)S(1)}, bf16[1,24,768]{2,1,0:T(8,128)(2,1)S(1)}, u32[]{:S(2)}, u32[]{:S(2)}) collective-permute-start(bf16[1,24,768]{2,1,0:T(8,128)(2,1)S(1)} %get-tuple-element.235), channel_id=1, source_target_pairs={{0,2},{2,4},{4,6},{6,0},{1,3},{3,5},{5,7},{7,1},{8,10},{10,12},{12... | collective-permute-start | bytes 110600 | tf_op jit(solution)/shard_map/ppermute | solution.py:678
  213.8 18.4 %collective-permute-start.81 = (bf16[112,768]{1,0:T(8,128)(2,1)S(1)}, bf16[112,768]{1,0:T(8,128)(2,1)S(1)}, u32[]{:S(2)}, u32[]{:S(2)}) collective-permute-start(bf16[112,768]{1,0:T(8,128)(2,1)S(1)} %get-tuple-element.243), channel_id=1, source_target_pairs={{0,2},{2,4},{4,6},{6,0},{1,3},{3,5},{5,7},{7,1},{8,10},{10,12},{12... | collective-permute-start | bytes 516104 | tf_op jit(solution)/shard_map/ppermute | solution.py:678
  216.8 15.4 %collective-permute-start.82 = (bf16[112,768]{1,0:T(8,128)(2,1)S(1)}, bf16[112,768]{1,0:T(8,128)(2,1)S(1)}, u32[]{:S(2)}, u32[]{:S(2)}) collective-permute-start(bf16[112,768]{1,0:T(8,128)(2,1)S(1)} %get-tuple-element.244), channel_id=1, source_target_pairs={{0,4},{2,6},{4,0},{6,2},{1,5},{3,7},{5,1},{7,3},{8,12},{10,14},{12... | collective-permute-start | bytes 516104 | tf_op jit(solution)/shard_map/ppermute | solution.py:678
  217.8 14.4 %collective-permute-start.83 = (bf16[112,768]{1,0:T(8,128)(2,1)S(1)}, bf16[112,768]{1,0:T(8,128)(2,1)S(1)}, u32[]{:S(2)}, u32[]{:S(2)}) collective-permute-start(bf16[112,768]{1,0:T(8,128)(2,1)S(1)} %get-tuple-element.245), channel_id=1, source_target_pairs={{0,6},{2,0},{4,2},{6,4},{1,7},{3,1},{5,3},{7,5},{8,14},{10,8},{12,... | collective-permute-start | bytes 516104 | tf_op jit(solution)/shard_map/ppermute | solution.py:678
  233.0 8.9 %collective-permute-start.84 = (bf16[64,768]{1,0:T(8,128)(2,1)}, bf16[64,768]{1,0:T(8,128)(2,1)S(1)}, u32[]{:S(2)}, u32[]{:S(2)}) collective-permute-start(bf16[64,768]{1,0:T(8,128)(2,1)} %get-tuple-element.247), channel_id=1, source_target_pairs={{0,1},{1,0},{8,9},{9,8},{2,3},{3,2},{10,11},{11,10},{4,5},{5,4},{1... | collective-permute-start | bytes 294920 | tf_op jit(solution)/shard_map/ppermute | solution.py:691
  234.1 7.8 %collective-permute-start.85 = (bf16[64,768]{1,0:T(8,128)(2,1)}, bf16[64,768]{1,0:T(8,128)(2,1)S(1)}, u32[]{:S(2)}, u32[]{:S(2)}) collective-permute-start(bf16[64,768]{1,0:T(8,128)(2,1)} %get-tuple-element.248), channel_id=1, source_target_pairs={{0,8},{1,9},{8,0},{9,1},{2,10},{3,11},{10,2},{11,3},{4,12},{5,13},... | collective-permute-start | bytes 294920 | tf_op jit(solution)/shard_map/ppermute | solution.py:691
  235.0 7.0 %collective-permute-start.86 = (bf16[64,768]{1,0:T(8,128)(2,1)}, bf16[64,768]{1,0:T(8,128)(2,1)S(1)}, u32[]{:S(2)}, u32[]{:S(2)}) collective-permute-start(bf16[64,768]{1,0:T(8,128)(2,1)} %get-tuple-element.249), channel_id=1, source_target_pairs={{0,9},{1,8},{8,1},{9,0},{2,11},{3,10},{10,3},{11,2},{4,13},{5,12},... | collective-permute-start | bytes 294920 | tf_op jit(solution)/shard_map/ppermute | solution.py:691
  241.8 26.8 %collective-permute-start.95 = (bf16[2,768,768]{2,1,0:T(8,128)(2,1)}, bf16[2,768,768]{2,1,0:T(8,128)(2,1)}, u32[]{:S(2)}, u32[]{:S(2)}) collective-permute-start(bf16[2,768,768]{2,1,0:T(8,128)(2,1)} %expert_gradients_sent.1), channel_id=1, source_target_pairs={{0,16},{16,0},{1,17},{17,1},{2,18},{18,2},{3,19},{19,3},{4,20},{20... | collective-permute-start | bytes 7077896 | tf_op jit(solution)/shard_map/ppermute | solution.py:687
  247.6 9.2 %collective-permute-start.88 = (bf16[112,768]{1,0:T(8,128)(2,1)S(1)}, bf16[112,768]{1,0:T(8,128)(2,1)S(1)}, u32[]{:S(2)}, u32[]{:S(2)}) collective-permute-start(bf16[112,768]{1,0:T(8,128)(2,1)S(1)} %get-tuple-element.291), channel_id=1, source_target_pairs={{0,2},{2,4},{4,6},{6,0},{1,3},{3,5},{5,7},{7,1},{8,10},{10,12},{12... | collective-permute-start | bytes 516104 | tf_op jit(solution)/shard_map/ppermute | solution.py:678
  248.5 14.9 %collective-permute-start.89 = (bf16[112,768]{1,0:T(8,128)(2,1)S(1)}, bf16[112,768]{1,0:T(8,128)(2,1)S(1)}, u32[]{:S(2)}, u32[]{:S(2)}) collective-permute-start(bf16[112,768]{1,0:T(8,128)(2,1)S(1)} %get-tuple-element.293), channel_id=1, source_target_pairs={{0,4},{2,6},{4,0},{6,2},{1,5},{3,7},{5,1},{7,3},{8,12},{10,14},{12... | collective-permute-start | bytes 516104 | tf_op jit(solution)/shard_map/ppermute | solution.py:678
  250.5 12.9 %collective-permute-start.90 = (bf16[112,768]{1,0:T(8,128)(2,1)S(1)}, bf16[112,768]{1,0:T(8,128)(2,1)S(1)}, u32[]{:S(2)}, u32[]{:S(2)}) collective-permute-start(bf16[112,768]{1,0:T(8,128)(2,1)S(1)} %get-tuple-element.292), channel_id=1, source_target_pairs={{0,6},{2,0},{4,2},{6,4},{1,7},{3,1},{5,3},{7,5},{8,14},{10,8},{12,... | collective-permute-start | bytes 516104 | tf_op jit(solution)/shard_map/ppermute | solution.py:678
  251.5 12.8 %collective-permute-start.79 = (f32[64,768]{1,0:T(8,128)S(1)}, f32[64,768]{1,0:T(8,128)S(1)}, u32[]{:S(2)}, u32[]{:S(2)}) collective-permute-start(f32[64,768]{1,0:T(8,128)S(1)} %broadcast_select_fusion.2), channel_id=1, source_target_pairs={{0,16},{16,0},{1,17},{17,1},{2,18},{18,2},{3,19},{19,3},{4,20},{20... | collective-permute-start | bytes 589832 | tf_op jit(solution)/shard_map/ppermute | solution.py:687
  265.2 9.8 %collective-permute-start.92 = (bf16[112,768]{1,0:T(8,128)(2,1)S(1)}, bf16[112,768]{1,0:T(8,128)(2,1)S(1)}, u32[]{:S(2)}, u32[]{:S(2)}) collective-permute-start(bf16[112,768]{1,0:T(8,128)(2,1)S(1)} %broadcast_select_fusion.1), channel_id=1, source_target_pairs={{0,8},{1,24},{8,0},{9,16},{16,9},{17,25},{24,1},{25,17},{2,10},{3,... | collective-permute-start | bytes 516104 | tf_op jit(solution)/shard_map/ppermute | solution.py:1106
  266.5 8.5 %collective-permute-start.93 = (bf16[112,768]{1,0:T(8,128)(2,1)S(1)}, bf16[112,768]{1,0:T(8,128)(2,1)S(1)}, u32[]{:S(2)}, u32[]{:S(2)}) collective-permute-start(bf16[112,768]{1,0:T(8,128)(2,1)S(1)} %get-tuple-element.288), channel_id=1, source_target_pairs={{0,16},{1,0},{8,24},{9,8},{16,17},{17,1},{24,25},{25,9},{2,18},{3,... | collective-permute-start | bytes 516104 | tf_op jit(solution)/shard_map/ppermute | solution.py:1106
  268.2 8.9 %collective-permute-start.94 = (bf16[112,768]{1,0:T(8,128)(2,1)S(1)}, bf16[112,768]{1,0:T(8,128)(2,1)S(1)}, u32[]{:S(2)}, u32[]{:S(2)}) collective-permute-start(bf16[112,768]{1,0:T(8,128)(2,1)S(1)} %get-tuple-element.288), channel_id=1, source_target_pairs={{0,24},{1,8},{8,16},{9,0},{16,25},{17,9},{24,17},{25,1},{2,26},{3,... | collective-permute-start | bytes 516104 | tf_op jit(solution)/shard_map/ppermute | solution.py:1106
  (131 other events, 1088.6 us)

commit v6 on v4

--- a/solution.py
+++ b/solution.py
@@ -1093,6 +1093,8 @@
         )
         final_in, final_out = own_experts(sets, got)
     else:
+        final_in, final_out = own_experts(after(sets, *parts0), got)
+        moved0 = after(moved0, final_in)
         blocks = [add_up(moved0), add_up(moved1)]
         arrived = []
         trade = ("section", "rep", "half")
@@ -1104,8 +1106,6 @@
                     si, xi, yi = i // 4, (i // 2) % 2, i % 2
                     pairs.append((i, (yi ^ a) * 4 + (xi ^ b) * 2 + si))
                 arrived.append(lax.ppermute(message, trade, pairs))
-        final_in, final_out = own_experts(after(sets, arrived[0]), got)
-        arrived = after(arrived, final_in)
         smalls = list(call(
             functools.partial(finish_kernel, experts, slab, table_slab),
             [

time: 282 us -> 293 us (1.039)
  waiting for transfers between devices: 94.1 us -> 101 us
    ppermute x4, waiting for transfers between devices: 2.18 us -> 7.62 us  [local(): arrived.append(lax.ppermute(message, trade, pairs))]
    unnamed x168 -> x176, local copies, waits for them, and re-layouts: 10.7 us -> 9.14 us
  transfers between devices with their start and end apart: 96 -> 96, of which waited for: 46 -> 52; matrix products, arithmetic and copies ran while one was open for 3% -> 5% of each run, Pallas kernels for 9% -> 9%
where the time goes in v6:
time: 293 us; the launch traced here: 292 us
  starting transfers between devices  106 us (36%)
  waiting for transfers between devices  101 us (34%)
  Pallas kernels  58.9 us (20%)
  local copies, waits for them, and re-layouts  13.7 us (5%)
  other arithmetic  9.75 us (3%)
    pallas_call x18, Pallas kernels, call(): pl.pallas_call(kernel, out_shape=[jax.ShapeDtypeStruct(shape, dtype) for...  58.9 us
    ppermute x31, waiting for transfers between devices, shift(): return lax.ppermute(v, axis, [(i, (i + by) % n) for i in range(n)])  51.2 us
    ppermute x31, starting transfers between devices, shift(): return lax.ppermute(v, axis, [(i, (i + by) % n) for i in range(n)])  50.4 us
    ppermute x36, starting transfers between devices, plane_swap(): return lax.ppermute(v, PLANE, [(i, i ^ mask) for i in range(4)])  45.6 us
    ppermute x36, waiting for transfers between devices, plane_swap(): return lax.ppermute(v, PLANE, [(i, i ^ mask) for i in range(4)])  40.1 us
    unnamed x176, local copies, waits for them, and re-layouts  9.14 us
    ppermute x4, waiting for transfers between devices, local(): arrived.append(lax.ppermute(message, trade, pairs))  7.62 us
  transfers between devices with their start and end apart: 96, of which 52 were waited for; matrix products, arithmetic and copies ran while one was open for 5% of the time, Pallas kernels for 9%

profile of v6, /device:TPU:0, one launch (start us, length us, event | category | flops | bytes accessed | tf_op | source)
XLA Modules:
  0.0 291.6 jit_solution(6458521871176524676)
XLA Ops:
  1.8 3.1 %collective-permute-start = (bf16[2,96,768]{2,1,0:T(8,128)(2,1)S(1)}, bf16[2,96,768]{2,1,0:T(8,128)(2,1)S(1)}, u32[]{:S(2)}, u32[]{:S(2)}) collective-permute-start(bf16[2,96,768]{2,1,0:T(8,128)(2,1)S(1)} %fusion), channel_id=1, source_target_pairs={{0,2},{2,4},{4,6},{6,0},{1,3},{3,5},{5,7},{7,1},{8,10},{10,12},{12... | collective-permute-start | bytes 884744 | tf_op jit(solution)/shard_map/ppermute | solution.py:678
  6.4 2.2 collective-permute-start.14
  11.6 3.2 %collective-permute-done.refs_10_.refs_16_.refs_26_.refs_24_ = bf16[2,96,768]{2,1,0:T(8,128)(2,1)S(1)} collective-permute-done((bf16[2,96,768]{2,1,0:T(8,128)(2,1)S(1)}, bf16[2,96,768]{2,1,0:T(8,128)(2,1)S(1)}, u32[]{:S(2)}, u32[]{:S(2)}) %collective-permute-start) | collective-permute-done | bytes 294944 | tf_op jit(solution)/shard_map/ppermute | solution.py:678
  14.8 1.8 collective-permute-start.4
  17.2 9.1 %collective-permute-start.1 = (bf16[2,96,768]{2,1,0:T(8,128)(2,1)S(1)}, bf16[2,96,768]{2,1,0:T(8,128)(2,1)S(1)}, u32[]{:S(2)}, u32[]{:S(2)}) collective-permute-start(bf16[2,96,768]{2,1,0:T(8,128)(2,1)S(1)} %fusion), channel_id=1, source_target_pairs={{0,4},{2,6},{4,0},{6,2},{1,5},{3,7},{5,1},{7,3},{8,12},{10,14},{12... | collective-permute-start | bytes 884744 | tf_op jit(solution)/shard_map/ppermute | solution.py:678
  28.6 2.4 collective-permute-start.6
  38.8 2.7 collective-permute-done.5
  44.6 2.0 collective-permute-start.13
  46.5 2.4 collective-permute-start.17
  49.0 2.5 collective-permute-done.8
  54.1 3.5 %collective-permute-done.13.refs_13_.refs_19_.refs_29_.refs_27_ = bf16[2,96,768]{2,1,0:T(8,128)(2,1)} collective-permute-done((bf16[2,96,768]{2,1,0:T(8,128)(2,1)S(1)}, bf16[2,96,768]{2,1,0:T(8,128)(2,1)}, u32[]{:S(2)}, u32[]{:S(2)}) %collective-permute-start.13) | collective-permute-done | bytes 294944 | tf_op jit(solution)/shard_map/ppermute | solution.py:691
  60.3 2.4 collective-permute-done.20.refs_21_.refs_27_.refs_37_.refs_35_
  70.4 6.1 %attention_forward.2 = (bf16[64,768]{1,0:T(8,128)(2,1)}, bf16[3,64,768]{2,1,0:T(8,128)(2,1)}, f32[6,128,64]{2,1,0:T(8,128)}, bf16[64,768]{1,0:T(8,128)(2,1)}, f3...) custom-call(s32[9]{0:T(128)} %concatenate.10.refs_0_.meta, ...), custom_call_target="tpu_custom_call" | custom-call | flops 6000000000 | bytes 18000000 | tf_op jit(solution)/shard_map/attention_forward/pallas_call | solution.py:662
  78.0 2.9 collective-permute-start.40
  80.9 2.5 collective-permute-done.38
  88.3 2.7 collective-permute-done.41.refs_2_
  93.1 3.6 %expert_forward.2 = (bf16[1,80,768]{2,1,0:T(8,128)(2,1)S(1)}, bf16[1,80,768]{2,1,0:T(8,128)(2,1)S(1)}, bf16[1,80,768]{2,1,0:T(8,128)(2,1)S(1)}, bf16[1,80,768]{2...) custom-call(s32[9]{0:T(128)S(1)} %copy-done.2, ...), custom_call_target="tpu_custom_call" | custom-call | flops 4000000000 | bytes 12000000 | tf_op jit(solution)/shard_map/expert_forward/pallas_call | solution.py:662
  100.3 2.2 collective-permute-done.46.refs_1_
  105.6 2.8 collective-permute-start.49
  110.0 3.2 %collective-permute-done.50 = bf16[1,24,768]{2,1,0:T(8,128)(2,1)S(1)} collective-permute-done((bf16[1,24,768]{2,1,0:T(8,128)(2,1)S(1)}, bf16[1,24,768]{2,1,0:T(8,128)(2,1)S(1)}, u32[]{:S(2)}, u32[]{:S(2)}) %collective-permute-start.50) | collective-permute-done | bytes 36896 | tf_op jit(solution)/shard_map/ppermute | solution.py:678
  115.1 6.6 %attention_forward.3 = (bf16[64,768]{1,0:T(8,128)(2,1)}, bf16[3,64,768]{2,1,0:T(8,128)(2,1)}, f32[6,128,64]{2,1,0:T(8,128)}, bf16[64,768]{1,0:T(8,128)(2,1)}, f3...) custom-call(s32[9]{0:T(128)} %concatenate.10.refs_0_.meta, ...), custom_call_target="tpu_custom_call" | custom-call | flops 6000000000 | bytes 18000000 | tf_op jit(solution)/shard_map/attention_forward/pallas_call | solution.py:662
  122.6 2.9 %collective-permute-start.54 = (bf16[2,24,768]{2,1,0:T(8,128)(2,1)}, bf16[2,24,768]{2,1,0:T(8,128)(2,1)S(1)}, u32[]{:S(2)}, u32[]{:S(2)}) collective-permute-start(bf16[2,24,768]{2,1,0:T(8,128)(2,1)} %get-tuple-element.194), channel_id=1, source_target_pairs={{0,6},{2,0},{4,2},{6,4},{1,7},{3,1},{5,3},{7,5},{8,14},{10,8},{12,... | collective-permute-start | bytes 221192 | tf_op jit(solution)/shard_map/ppermute | solution.py:678
  125.5 2.6 collective-permute-done.52.refs_1_
  133.7 2.7 collective-permute-done.55.refs_2_
  137.7 2.8 collective-permute-done.57.refs_4_
  140.5 5.2 %expert_forward.3 = (bf16[2,80,768]{2,1,0:T(8,128)(2,1)S(1)}, bf16[2,80,768]{2,1,0:T(8,128)(2,1)S(1)}, bf16[2,80,768]{2,1,0:T(8,128)(2,1)S(1)}, bf16[2,80,768]{2...) custom-call(s32[9]{0:T(128)S(1)} %copy-done.3, ...), custom_call_target="tpu_custom_call" | custom-call | flops 4000000000 | bytes 12000000 | tf_op jit(solution)/shard_map/expert_forward/pallas_call | solution.py:662
  149.3 2.7 collective-permute-done.58.refs_1_
  153.3 2.8 collective-permute-done.60.refs_3_
  157.1 3.1 %collective-permute-start.61 = (bf16[2,24,768]{2,1,0:T(8,128)(2,1)S(1)}, bf16[2,24,768]{2,1,0:T(8,128)(2,1)S(1)}, u32[]{:S(2)}, u32[]{:S(2)}) collective-permute-start(bf16[2,24,768]{2,1,0:T(8,128)(2,1)S(1)} %get-tuple-element.200), channel_id=1, source_target_pairs={{0,6},{2,0},{4,2},{6,4},{1,7},{3,1},{5,3},{7,5},{8,14},{10,8},{12,... | collective-permute-start | bytes 221192 | tf_op jit(solution)/shard_map/ppermute | solution.py:678
  162.1 3.3 %collective-permute-done.62.refs_21_ = bf16[2,24,768]{2,1,0:T(8,128)(2,1)S(1)} collective-permute-done((bf16[2,24,768]{2,1,0:T(8,128)(2,1)S(1)}, bf16[2,24,768]{2,1,0:T(8,128)(2,1)S(1)}, u32[]{:S(2)}, u32[]{:S(2)}) %collective-permute-start.62) | collective-permute-done | bytes 73760 | tf_op jit(solution)/shard_map/ppermute | solution.py:678
  167.2 7.8 %attention_backward.2 = (f32[64,768]{1,0:T(8,128)}, f32[16,768]{1,0:T(8,128)}, bf16[192,768]{1,0:T(8,128)(2,1)}, bf16[192,768]{1,0:T(8,128)(2,1)}, bf16[192,768]...) custom-call(s32[9]{0:T(128)} %concatenate.10.refs_0_.meta, ...), custom_call_target="tpu_custom_call" | custom-call | flops 8000000000 | bytes 24000000 | tf_op jit(solution)/shard_map/attention_backward/pallas_call | solution.py:662
  176.2 2.7 collective-permute-start.66
  178.9 2.1 collective-permute-done.64
  192.1 4.3 %expert_backward.1 = (bf16[1,80,768]{2,1,0:T(8,128)(2,1)S(1)}, bf16[1,80,768]{2,1,0:T(8,128)(2,1)S(1)}, bf16[1,80,768]{2,1,0:T(8,128)(2,1)S(1)}, bf16[1,80,768]{...) custom-call(s32[9]{0:T(128)S(1)} %copy-done.4, bf16[1,80,768]{2,1,0:T(8,128)(2,1)S(1)} %pack.5.refs_1_, ...), custom_call_target="tpu_custom_call" | custom-call | flops 4000000000 | bytes 12000000 | tf_op jit(solution)/shard_map/expert_backward/pallas_call | solution.py:662
  205.3 3.2 %collective-permute-start.76 = (bf16[1,24,768]{2,1,0:T(8,128)(2,1)S(1)}, bf16[1,24,768]{2,1,0:T(8,128)(2,1)S(1)}, u32[]{:S(2)}, u32[]{:S(2)}) collective-permute-start(bf16[1,24,768]{2,1,0:T(8,128)(2,1)S(1)} %get-tuple-element.233), channel_id=1, source_target_pairs={{0,6},{2,0},{4,2},{6,4},{1,7},{3,1},{5,3},{7,5},{8,14},{10,8},{12,... | collective-permute-start | bytes 110600 | tf_op jit(solution)/shard_map/ppermute | solution.py:678
  210.2 3.2 %collective-permute-done.77 = bf16[1,24,768]{2,1,0:T(8,128)(2,1)S(1)} collective-permute-done((bf16[1,24,768]{2,1,0:T(8,128)(2,1)S(1)}, bf16[1,24,768]{2,1,0:T(8,128)(2,1)S(1)}, u32[]{:S(2)}, u32[]{:S(2)}) %collective-permute-start.77) | collective-permute-done | bytes 36896 | tf_op jit(solution)/shard_map/ppermute | solution.py:678
  214.9 7.1 %attention_backward.3 = (f32[64,768]{1,0:T(8,128)}, f32[16,768]{1,0:T(8,128)}, bf16[64,768]{1,0:T(8,128)(2,1)}, bf16[64,768]{1,0:T(8,128)(2,1)}, bf16[64,768]{1,0:T(8,128)(2,1)}, /*index=5*/bf16[64,768]{1,0:T(8,128)(2,1)}) custom-call(s32[9]{0:T(128)} %concatenate.10.refs_0_.meta, bf16[2,2,4,8,96]{4,3,2,1,0:T(8,128)(2,1)} %pad_maximum_fusion.1.refs_1_, ...), custom_call_target="tpu_custom_call" | custom-call | flops 2000000000 | bytes 6000000 | tf_op jit(solution)/shard_map/attention_backward/pallas_call | solution.py:662
  222.0 5.3 %expert_gradients_sent.1 = bf16[2,768,768]{2,1,0:T(8,128)(2,1)} custom-call(s32[9]{0:T(128)} %concatenate.10.refs_0_.meta, bf16[320,768]{1,0:T(8,128)(2,1)} %copy-done.34, bf16[320,768]{1,0:T(8,128)(2,1)} %copy-done.29, bf16[320,768]{1,0:T(8,128)(2,1)} %copy-done.35, bf16[320,768]{1,0:T(8,128)(2,1)} %copy-done.28, bf16[320,768]{1,0:T(8,128)(2,1)} %copy-done.30, ...), custom_call_target="tpu_custom_call" | custom-call | flops 5000000000 | bytes 15000000 | tf_op jit(solution)/shard_map/expert_gradients_sent/pallas_call | solution.py:662
  230.8 2.0 collective-permute-start.81
  232.8 4.8 %collective-permute-done.83 = bf16[112,768]{1,0:T(8,128)(2,1)S(1)} collective-permute-done((bf16[112,768]{1,0:T(8,128)(2,1)S(1)}, bf16[112,768]{1,0:T(8,128)(2,1)S(1)}, u32[]{:S(2)}, u32[]{:S(2)}) %collective-permute-start.83) | collective-permute-done | bytes 172064 | tf_op jit(solution)/shard_map/ppermute | solution.py:678
  237.6 9.2 %collective-permute-done.82 = bf16[112,768]{1,0:T(8,128)(2,1)S(1)} collective-permute-done((bf16[112,768]{1,0:T(8,128)(2,1)S(1)}, bf16[112,768]{1,0:T(8,128)(2,1)S(1)}, u32[]{:S(2)}, u32[]{:S(2)}) %collective-permute-start.82) | collective-permute-done | bytes 172064 | tf_op jit(solution)/shard_map/ppermute | solution.py:678
  251.4 2.3 collective-permute-done.85.refs_2_
  260.0 2.0 collective-permute-start.89
  262.0 2.9 %collective-permute-start.90 = (bf16[112,768]{1,0:T(8,128)(2,1)}, bf16[112,768]{1,0:T(8,128)(2,1)}, u32[]{:S(2)}, u32[]{:S(2)}) collective-permute-start(bf16[112,768]{1,0:T(8,128)(2,1)} %get-tuple-element.291), channel_id=1, source_target_pairs={{0,6},{2,0},{4,2},{6,4},{1,7},{3,1},{5,3},{7,5},{8,14},{10,8},{12,... | collective-permute-start | bytes 516104 | tf_op jit(solution)/shard_map/ppermute | solution.py:678
  265.0 6.4 %expert_gradients_own.1 = (f32[768,768]{1,0:T(8,128)}, f32[768,768]{1,0:T(8,128)}) custom-call(s32[9]{0:T(128)} %concatenate.10.refs_0_.meta, bf16[320,768]{1,0:T(8,128)(2,1)} %copy-done.34, bf16[320,768]{1,0:T(8,128)(2,1)} %copy-done.29, bf16[320,768]{1,0:T(8,128)(2,1)} %copy-done.35, bf16[320,768]{1,0:T(8,128)(2,1)} %copy-done.28, ...), custom_call_target="tpu_custom_call" | custom-call | flops 6000000000 | bytes 18000000 | tf_op jit(solution)/shard_map/expert_gradients_own/pallas_call | solution.py:662
  271.3 4.2 %collective-permute-done.89 = bf16[112,768]{1,0:T(8,128)(2,1)S(1)} collective-permute-done((bf16[112,768]{1,0:T(8,128)(2,1)}, bf16[112,768]{1,0:T(8,128)(2,1)S(1)}, u32[]{:S(2)}, u32[]{:S(2)}) %collective-permute-start.89) | collective-permute-done | bytes 172064 | tf_op jit(solution)/shard_map/ppermute | solution.py:678
  283.5 2.9 collective-permute-done.94.refs_2_
  286.4 3.5 %collective-permute-done.95.refs_3_ = bf16[112,768]{1,0:T(8,128)(2,1)S(1)} collective-permute-done((bf16[112,768]{1,0:T(8,128)(2,1)S(1)}, bf16[112,768]{1,0:T(8,128)(2,1)S(1)}, u32[]{:S(2)}, u32[]{:S(2)}) %collective-permute-start.95) | collective-permute-done | bytes 172064 | tf_op jit(solution)/shard_map/ppermute | solution.py:1108
  (365 shorter events, 116.0 us)
Async XLA Ops:
  1.8 13.0 %collective-permute-start = (bf16[2,96,768]{2,1,0:T(8,128)(2,1)S(1)}, bf16[2,96,768]{2,1,0:T(8,128)(2,1)S(1)}, u32[]{:S(2)}, u32[]{:S(2)}) collective-permute-start(bf16[2,96,768]{2,1,0:T(8,128)(2,1)S(1)} %fusion), channel_id=1, source_target_pairs={{0,2},{2,4},{4,6},{6,0},{1,3},{3,5},{5,7},{7,1},{8,10},{10,12},{12... | collective-permute-start | bytes 884744 | tf_op jit(solution)/shard_map/ppermute | solution.py:678
  4.9 21.4 %collective-permute-start.10 = (bf16[2,96,768]{2,1,0:T(8,128)(2,1)S(1)}, bf16[2,96,768]{2,1,0:T(8,128)(2,1)S(1)}, u32[]{:S(2)}, u32[]{:S(2)}) collective-permute-start(bf16[2,96,768]{2,1,0:T(8,128)(2,1)S(1)} %fusion), channel_id=1, source_target_pairs={{0,1},{1,0},{8,9},{9,8},{2,3},{3,2},{10,11},{11,10},{4,5},{5,4},{1... | collective-permute-start | bytes 884744 | tf_op jit(solution)/shard_map/ppermute | solution.py:691
  6.4 25.1 %collective-permute-start.14 = (bf16[2,96,768]{2,1,0:T(8,128)(2,1)S(1)}, bf16[2,96,768]{2,1,0:T(8,128)(2,1)S(1)}, u32[]{:S(2)}, u32[]{:S(2)}) collective-permute-start(bf16[2,96,768]{2,1,0:T(8,128)(2,1)S(1)} %fusion), channel_id=1, source_target_pairs={{0,6},{2,0},{4,2},{6,4},{1,7},{3,1},{5,3},{7,5},{8,14},{10,8},{12,... | collective-permute-start | bytes 884744 | tf_op jit(solution)/shard_map/ppermute | solution.py:678
  9.6 19.0 %collective-permute-start.2 = (bf16[64,768]{1,0:T(8,128)(2,1)S(1)}, bf16[64,768]{1,0:T(8,128)(2,1)S(1)}, u32[]{:S(2)}, u32[]{:S(2)}) collective-permute-start(bf16[64,768]{1,0:T(8,128)(2,1)S(1)} %dynamic-slice_bitcast_fusion), channel_id=1, source_target_pairs={{0,16},{16,0},{1,17},{17,1},{2,18},{18,2},{3,19},{19,3},{4,20},{20... | collective-permute-start | bytes 294920 | tf_op jit(solution)/shard_map/ppermute | solution.py:687
  10.2 7.0 %collective-permute-start.3 = (s32[64]{0:T(128)S(1)}, s32[64]{0:T(128)S(1)}, u32[]{:S(2)}, u32[]{:S(2)}) collective-permute-start(s32[64]{0:T(128)S(1)} %fusion.8), channel_id=1, source_target_pairs={{0,16},{16,0},{1,17},{17,1},{2,18},{18,2},{3,19},{19,3},{4,20},{20... | collective-permute-start | bytes 776 | tf_op jit(solution)/shard_map/ppermute | solution.py:687
  14.8 13.7 %collective-permute-start.4 = (bf16[2,96,768]{2,1,0:T(8,128)(2,1)S(1)}, bf16[2,96,768]{2,1,0:T(8,128)(2,1)S(1)}, u32[]{:S(2)}, u32[]{:S(2)}) collective-permute-start(bf16[2,96,768]{2,1,0:T(8,128)(2,1)S(1)} %collective-permute-done.refs_10_.refs_16_.refs_26_.refs_24_), channel_id=1, source_target_pairs={{0,1},{1,0},{8,9},{9,8},{2,3},{3,2},{10,11},{11,10},{4,5},{5,4},{1... | collective-permute-start | bytes 884744 | tf_op jit(solution)/shard_map/ppermute | solution.py:691
  17.2 15.8 %collective-permute-start.1 = (bf16[2,96,768]{2,1,0:T(8,128)(2,1)S(1)}, bf16[2,96,768]{2,1,0:T(8,128)(2,1)S(1)}, u32[]{:S(2)}, u32[]{:S(2)}) collective-permute-start(bf16[2,96,768]{2,1,0:T(8,128)(2,1)S(1)} %fusion), channel_id=1, source_target_pairs={{0,4},{2,6},{4,0},{6,2},{1,5},{3,7},{5,1},{7,3},{8,12},{10,14},{12... | collective-permute-start | bytes 884744 | tf_op jit(solution)/shard_map/ppermute | solution.py:678
  26.3 8.2 %collective-permute-start.11 = (bf16[2,96,768]{2,1,0:T(8,128)(2,1)S(1)}, bf16[2,96,768]{2,1,0:T(8,128)(2,1)S(1)}, u32[]{:S(2)}, u32[]{:S(2)}) collective-permute-start(bf16[2,96,768]{2,1,0:T(8,128)(2,1)S(1)} %collective-permute-done.10.refs_8_.refs_14_.refs_24_.refs_22_), channel_id=1, source_target_pairs={{0,8},{1,9},{8,0},{9,1},{2,10},{3,11},{10,2},{11,3},{4,12},{5,13},... | collective-permute-start | bytes 884744 | tf_op jit(solution)/shard_map/ppermute | solution.py:691
  28.5 7.5 %collective-permute-start.7 = (bf16[8,96]{1,0:T(8,128)(2,1)S(1)}, bf16[8,96]{1,0:T(8,128)(2,1)S(1)}, u32[]{:S(2)}, u32[]{:S(2)}) collective-permute-start(bf16[8,96]{1,0:T(8,128)(2,1)S(1)} %fusion.4), channel_id=1, source_target_pairs={{0,6},{2,0},{4,2},{6,4},{1,7},{3,1},{5,3},{7,5},{8,14},{10,8},{12,... | collective-permute-start | bytes 4616 | tf_op jit(solution)/shard_map/ppermute | solution.py:678
  28.6 7.4 %collective-permute-start.6 = (bf16[8,96]{1,0:T(8,128)(2,1)S(1)}, bf16[8,96]{1,0:T(8,128)(2,1)S(1)}, u32[]{:S(2)}, u32[]{:S(2)}) collective-permute-start(bf16[8,96]{1,0:T(8,128)(2,1)S(1)} %fusion.4), channel_id=1, source_target_pairs={{0,4},{2,6},{4,0},{6,2},{1,5},{3,7},{5,1},{7,3},{8,12},{10,14},{12... | collective-permute-start | bytes 4616 | tf_op jit(solution)/shard_map/ppermute | solution.py:678
  31.5 10.4 %collective-permute-start.12 = (bf16[2,96,768]{2,1,0:T(8,128)(2,1)S(1)}, bf16[2,96,768]{2,1,0:T(8,128)(2,1)S(1)}, u32[]{:S(2)}, u32[]{:S(2)}) collective-permute-start(bf16[2,96,768]{2,1,0:T(8,128)(2,1)S(1)} %collective-permute-done.refs_10_.refs_16_.refs_26_.refs_24_), channel_id=1, source_target_pairs={{0,8},{1,9},{8,0},{9,1},{2,10},{3,11},{10,2},{11,3},{4,12},{5,13},... | collective-permute-start | bytes 884744 | tf_op jit(solution)/shard_map/ppermute | solution.py:691
  33.0 10.5 %collective-permute-start.15 = (bf16[2,96,768]{2,1,0:T(8,128)(2,1)S(1)}, bf16[2,96,768]{2,1,0:T(8,128)(2,1)S(1)}, u32[]{:S(2)}, u32[]{:S(2)}) collective-permute-start(bf16[2,96,768]{2,1,0:T(8,128)(2,1)S(1)} %collective-permute-done.14.refs_14_.refs_20_.refs_30_.refs_28_), channel_id=1, source_target_pairs={{0,1},{1,0},{8,9},{9,8},{2,3},{3,2},{10,11},{11,10},{4,5},{5,4},{1... | collective-permute-start | bytes 884744 | tf_op jit(solution)/shard_map/ppermute | solution.py:691
  34.5 10.0 %collective-permute-start.16 = (bf16[2,96,768]{2,1,0:T(8,128)(2,1)S(1)}, bf16[2,96,768]{2,1,0:T(8,128)(2,1)S(1)}, u32[]{:S(2)}, u32[]{:S(2)}) collective-permute-start(bf16[2,96,768]{2,1,0:T(8,128)(2,1)S(1)} %collective-permute-done.14.refs_14_.refs_20_.refs_30_.refs_28_), channel_id=1, source_target_pairs={{0,8},{1,9},{8,0},{9,1},{2,10},{3,11},{10,2},{11,3},{4,12},{5,13},... | collective-permute-start | bytes 884744 | tf_op jit(solution)/shard_map/ppermute | solution.py:691
  36.0 10.6 %collective-permute-start.29 = (bf16[2,96,768]{2,1,0:T(8,128)(2,1)S(1)}, bf16[2,96,768]{2,1,0:T(8,128)(2,1)S(1)}, u32[]{:S(2)}, u32[]{:S(2)}) collective-permute-start(bf16[2,96,768]{2,1,0:T(8,128)(2,1)S(1)} %collective-permute-done.14.refs_14_.refs_20_.refs_30_.refs_28_), channel_id=1, source_target_pairs={{0,16},{16,0},{1,17},{17,1},{2,18},{18,2},{3,19},{19,3},{4,20},{20... | collective-permute-start | bytes 884744 | tf_op jit(solution)/shard_map/ppermute | solution.py:687
  41.4 10.1 %collective-permute-start.18 = (bf16[2,96,768]{2,1,0:T(8,128)(2,1)S(1)}, bf16[2,96,768]{2,1,0:T(8,128)(2,1)S(1)}, u32[]{:S(2)}, u32[]{:S(2)}) collective-permute-start(bf16[2,96,768]{2,1,0:T(8,128)(2,1)S(1)} %collective-permute-done.1.refs_18_.refs_24_.refs_34_.refs_32_), channel_id=1, source_target_pairs={{0,1},{1,0},{8,9},{9,8},{2,3},{3,2},{10,11},{11,10},{4,5},{5,4},{1... | collective-permute-start | bytes 884744 | tf_op jit(solution)/shard_map/ppermute | solution.py:691
  41.9 9.6 %collective-permute-start.8 = (bf16[4,8,96]{2,1,0:T(8,128)(2,1)S(1)}, bf16[4,8,96]{2,1,0:T(8,128)(2,1)S(1)}, u32[]{:S(2)}, u32[]{:S(2)}) collective-permute-start(bf16[4,8,96]{2,1,0:T(8,128)(2,1)S(1)} %get-tuple-element.306), channel_id=1, source_target_pairs={{0,1},{1,0},{2,3},{3,2},{4,5},{5,4},{6,7},{7,6},{8,9},{9,8},{10,11... | collective-permute-start | bytes 18440 | tf_op jit(solution)/shard_map/ppermute | solution.py:678
  43.5 9.9 %collective-permute-start.19 = (bf16[2,96,768]{2,1,0:T(8,128)(2,1)S(1)}, bf16[2,96,768]{2,1,0:T(8,128)(2,1)S(1)}, u32[]{:S(2)}, u32[]{:S(2)}) collective-permute-start(bf16[2,96,768]{2,1,0:T(8,128)(2,1)S(1)} %collective-permute-done.1.refs_18_.refs_24_.refs_34_.refs_32_), channel_id=1, source_target_pairs={{0,8},{1,9},{8,0},{9,1},{2,10},{3,11},{10,2},{11,3},{4,12},{5,13},... | collective-permute-start | bytes 884744 | tf_op jit(solution)/shard_map/ppermute | solution.py:691
  44.6 13.1 %collective-permute-start.13 = (bf16[2,96,768]{2,1,0:T(8,128)(2,1)S(1)}, bf16[2,96,768]{2,1,0:T(8,128)(2,1)}, u32[]{:S(2)}, u32[]{:S(2)}) collective-permute-start(bf16[2,96,768]{2,1,0:T(8,128)(2,1)S(1)} %collective-permute-done.4.refs_11_.refs_17_.refs_27_.refs_25_), channel_id=1, source_target_pairs={{0,8},{1,9},{8,0},{9,1},{2,10},{3,11},{10,2},{11,3},{4,12},{5,13},... | collective-permute-start | bytes 884744 | tf_op jit(solution)/shard_map/ppermute | solution.py:691
  46.5 12.2 %collective-permute-start.17 = (bf16[2,96,768]{2,1,0:T(8,128)(2,1)S(1)}, bf16[2,96,768]{2,1,0:T(8,128)(2,1)}, u32[]{:S(2)}, u32[]{:S(2)}) collective-permute-start(bf16[2,96,768]{2,1,0:T(8,128)(2,1)S(1)} %collective-permute-done.16.refs_16_.refs_22_.refs_32_.refs_30_), channel_id=1, source_target_pairs={{0,1},{1,0},{8,9},{9,8},{2,3},{3,2},{10,11},{11,10},{4,5},{5,4},{1... | collective-permute-start | bytes 884744 | tf_op jit(solution)/shard_map/ppermute | solution.py:691
  51.5 8.8 %collective-permute-start.30 = (bf16[2,96,768]{2,1,0:T(8,128)(2,1)S(1)}, bf16[2,96,768]{2,1,0:T(8,128)(2,1)S(1)}, u32[]{:S(2)}, u32[]{:S(2)}) collective-permute-start(bf16[2,96,768]{2,1,0:T(8,128)(2,1)S(1)} %collective-permute-done.15.refs_15_.refs_21_.refs_31_.refs_29_), channel_id=1, source_target_pairs={{0,16},{16,0},{1,17},{17,1},{2,18},{18,2},{3,19},{19,3},{4,20},{20... | collective-permute-start | bytes 884744 | tf_op jit(solution)/shard_map/ppermute | solution.py:687
  53.5 10.4 %collective-permute-start.31 = (bf16[2,96,768]{2,1,0:T(8,128)(2,1)S(1)}, bf16[2,96,768]{2,1,0:T(8,128)(2,1)S(1)}, u32[]{:S(2)}, u32[]{:S(2)}) collective-permute-start(bf16[2,96,768]{2,1,0:T(8,128)(2,1)S(1)} %collective-permute-done.16.refs_16_.refs_22_.refs_32_.refs_30_), channel_id=1, source_target_pairs={{0,16},{16,0},{1,17},{17,1},{2,18},{18,2},{3,19},{19,3},{4,20},{20... | collective-permute-start | bytes 884744 | tf_op jit(solution)/shard_map/ppermute | solution.py:687
  53.5 10.9 %collective-permute-start.33 = (bf16[2,96,768]{2,1,0:T(8,128)(2,1)S(1)}, bf16[2,96,768]{2,1,0:T(8,128)(2,1)S(1)}, u32[]{:S(2)}, u32[]{:S(2)}) collective-permute-start(bf16[2,96,768]{2,1,0:T(8,128)(2,1)S(1)} %collective-permute-done.1.refs_18_.refs_24_.refs_34_.refs_32_), channel_id=1, source_target_pairs={{0,16},{16,0},{1,17},{17,1},{2,18},{18,2},{3,19},{19,3},{4,20},{20... | collective-permute-start | bytes 884744 | tf_op jit(solution)/shard_map/ppermute | solution.py:687
  76.5 16.6 %collective-permute-start.44 = (bf16[768,768]{1,0:T(8,128)(2,1)S(1)}, bf16[768,768]{1,0:T(8,128)(2,1)S(1)}, u32[]{:S(2)}, u32[]{:S(2)}) collective-permute-start(bf16[768,768]{1,0:T(8,128)(2,1)S(1)} %bitcast.85), channel_id=1, source_target_pairs={{0,16},{16,0},{1,17},{17,1},{2,18},{18,2},{3,19},{19,3},{4,20},{20... | collective-permute-start | bytes 3538952 | tf_op jit(solution)/shard_map/ppermute | solution.py:687
  76.8 16.3 %collective-permute-start.45 = (bf16[768,768]{1,0:T(8,128)(2,1)}, bf16[768,768]{1,0:T(8,128)(2,1)S(1)}, u32[]{:S(2)}, u32[]{:S(2)}) collective-permute-start(bf16[768,768]{1,0:T(8,128)(2,1)} %bitcast.89), channel_id=1, source_target_pairs={{0,16},{16,0},{1,17},{17,1},{2,18},{18,2},{3,19},{19,3},{4,20},{20... | collective-permute-start | bytes 3538952 | tf_op jit(solution)/shard_map/ppermute | solution.py:687
  77.0 6.3 %collective-permute-start.38 = (bf16[24,768]{1,0:T(8,128)(2,1)}, bf16[24,768]{1,0:T(8,128)(2,1)S(1)}, u32[]{:S(2)}, u32[]{:S(2)}) collective-permute-start(bf16[24,768]{1,0:T(8,128)(2,1)} %get-tuple-element.168), channel_id=1, source_target_pairs={{0,2},{2,4},{4,6},{6,0},{1,3},{3,5},{5,7},{7,1},{8,10},{10,12},{12... | collective-permute-start | bytes 110600 | tf_op jit(solution)/shard_map/ppermute | solution.py:678
  77.1 6.3 %collective-permute-start.39 = (bf16[24,768]{1,0:T(8,128)(2,1)}, bf16[24,768]{1,0:T(8,128)(2,1)S(1)}, u32[]{:S(2)}, u32[]{:S(2)}) collective-permute-start(bf16[24,768]{1,0:T(8,128)(2,1)} %get-tuple-element.169), channel_id=1, source_target_pairs={{0,4},{2,6},{4,0},{6,2},{1,5},{3,7},{5,1},{7,3},{8,12},{10,14},{12... | collective-permute-start | bytes 110600 | tf_op jit(solution)/shard_map/ppermute | solution.py:678
  121.6 6.4 %collective-permute-start.52 = (bf16[2,24,768]{2,1,0:T(8,128)(2,1)}, bf16[2,24,768]{2,1,0:T(8,128)(2,1)S(1)}, u32[]{:S(2)}, u32[]{:S(2)}) collective-permute-start(bf16[2,24,768]{2,1,0:T(8,128)(2,1)} %get-tuple-element.192), channel_id=1, source_target_pairs={{0,2},{2,4},{4,6},{6,0},{1,3},{3,5},{5,7},{7,1},{8,10},{10,12},{12... | collective-permute-start | bytes 221192 | tf_op jit(solution)/shard_map/ppermute | solution.py:678
  121.7 6.4 %collective-permute-start.53 = (bf16[2,24,768]{2,1,0:T(8,128)(2,1)}, bf16[2,24,768]{2,1,0:T(8,128)(2,1)S(1)}, u32[]{:S(2)}, u32[]{:S(2)}) collective-permute-start(bf16[2,24,768]{2,1,0:T(8,128)(2,1)} %get-tuple-element.193), channel_id=1, source_target_pairs={{0,4},{2,6},{4,0},{6,2},{1,5},{3,7},{5,1},{7,3},{8,12},{10,14},{12... | collective-permute-start | bytes 221192 | tf_op jit(solution)/shard_map/ppermute | solution.py:678
  122.6 6.3 %collective-permute-start.54 = (bf16[2,24,768]{2,1,0:T(8,128)(2,1)}, bf16[2,24,768]{2,1,0:T(8,128)(2,1)S(1)}, u32[]{:S(2)}, u32[]{:S(2)}) collective-permute-start(bf16[2,24,768]{2,1,0:T(8,128)(2,1)} %get-tuple-element.194), channel_id=1, source_target_pairs={{0,6},{2,0},{4,2},{6,4},{1,7},{3,1},{5,3},{7,5},{8,14},{10,8},{12,... | collective-permute-start | bytes 221192 | tf_op jit(solution)/shard_map/ppermute | solution.py:678
  130.1 6.3 %collective-permute-start.55 = (bf16[2,80,768]{2,1,0:T(8,128)(2,1)S(1)}, bf16[2,80,768]{2,1,0:T(8,128)(2,1)S(1)}, u32[]{:S(2)}, u32[]{:S(2)}) collective-permute-start(bf16[2,80,768]{2,1,0:T(8,128)(2,1)S(1)} %pack.4.refs_1_), channel_id=1, source_target_pairs={{0,1},{1,0},{8,9},{9,8},{2,3},{3,2},{10,11},{11,10},{4,5},{5,4},{1... | collective-permute-start | bytes 737288 | tf_op jit(solution)/shard_map/ppermute | solution.py:691
  132.2 8.3 %collective-permute-start.57 = (bf16[2,80,768]{2,1,0:T(8,128)(2,1)S(1)}, bf16[2,80,768]{2,1,0:T(8,128)(2,1)S(1)}, u32[]{:S(2)}, u32[]{:S(2)}) collective-permute-start(bf16[2,80,768]{2,1,0:T(8,128)(2,1)S(1)} %pack.4.refs_1_), channel_id=1, source_target_pairs={{0,9},{1,8},{8,1},{9,0},{2,11},{3,10},{10,3},{11,2},{4,13},{5,12},... | collective-permute-start | bytes 737288 | tf_op jit(solution)/shard_map/ppermute | solution.py:691
  145.8 6.3 %collective-permute-start.58 = (bf16[2,80,768]{2,1,0:T(8,128)(2,1)S(1)}, bf16[2,80,768]{2,1,0:T(8,128)(2,1)S(1)}, u32[]{:S(2)}, u32[]{:S(2)}) collective-permute-start(bf16[2,80,768]{2,1,0:T(8,128)(2,1)S(1)} %get-tuple-element.196), channel_id=1, source_target_pairs={{0,1},{1,0},{8,9},{9,8},{2,3},{3,2},{10,11},{11,10},{4,5},{5,4},{1... | collective-permute-start | bytes 737288 | tf_op jit(solution)/shard_map/ppermute | solution.py:691
  147.8 8.3 %collective-permute-start.60 = (bf16[2,80,768]{2,1,0:T(8,128)(2,1)S(1)}, bf16[2,80,768]{2,1,0:T(8,128)(2,1)S(1)}, u32[]{:S(2)}, u32[]{:S(2)}) collective-permute-start(bf16[2,80,768]{2,1,0:T(8,128)(2,1)S(1)} %get-tuple-element.198), channel_id=1, source_target_pairs={{0,9},{1,8},{8,1},{9,0},{2,11},{3,10},{10,3},{11,2},{4,13},{5,12},... | collective-permute-start | bytes 737288 | tf_op jit(solution)/shard_map/ppermute | solution.py:691
  184.0 6.3 %collective-permute-start.68 = (bf16[1,80,768]{2,1,0:T(8,128)(2,1)S(1)}, bf16[1,80,768]{2,1,0:T(8,128)(2,1)S(1)}, u32[]{:S(2)}, u32[]{:S(2)}) collective-permute-start(bf16[1,80,768]{2,1,0:T(8,128)(2,1)S(1)} %pack.5.refs_1_), channel_id=1, source_target_pairs={{0,8},{1,9},{8,0},{9,1},{2,10},{3,11},{10,2},{11,3},{4,12},{5,13},... | collective-permute-start | bytes 368648 | tf_op jit(solution)/shard_map/ppermute | solution.py:691
  186.2 12.5 %collective-permute-start.73 = (bf16[192,768]{1,0:T(8,128)(2,1)}, bf16[192,768]{1,0:T(8,128)(2,1)S(1)}, u32[]{:S(2)}, u32[]{:S(2)}) collective-permute-start(bf16[192,768]{1,0:T(8,128)(2,1)} %get-tuple-element.218), channel_id=1, source_target_pairs={{0,1},{1,0},{8,9},{9,8},{2,3},{3,2},{10,11},{11,10},{4,5},{5,4},{1... | collective-permute-start | bytes 884744 | tf_op jit(solution)/shard_map/ppermute | solution.py:691
  187.5 12.6 %collective-permute-start.74 = (bf16[192,768]{1,0:T(8,128)(2,1)}, bf16[192,768]{1,0:T(8,128)(2,1)S(1)}, u32[]{:S(2)}, u32[]{:S(2)}) collective-permute-start(bf16[192,768]{1,0:T(8,128)(2,1)} %get-tuple-element.219), channel_id=1, source_target_pairs={{0,8},{1,9},{8,0},{9,1},{2,10},{3,11},{10,2},{11,3},{4,12},{5,13},... | collective-permute-start | bytes 884744 | tf_op jit(solution)/shard_map/ppermute | solution.py:691
  188.9 11.1 %collective-permute-start.75 = (bf16[192,768]{1,0:T(8,128)(2,1)}, bf16[192,768]{1,0:T(8,128)(2,1)S(1)}, u32[]{:S(2)}, u32[]{:S(2)}) collective-permute-start(bf16[192,768]{1,0:T(8,128)(2,1)} %get-tuple-element.220), channel_id=1, source_target_pairs={{0,9},{1,8},{8,1},{9,0},{2,11},{3,10},{10,3},{11,2},{4,13},{5,12},... | collective-permute-start | bytes 884744 | tf_op jit(solution)/shard_map/ppermute | solution.py:691
  209.1 18.4 %collective-permute-start.80 = (bf16[4,112,768]{2,1,0:T(8,128)(2,1)S(1)}, bf16[4,112,768]{2,1,0:T(8,128)(2,1)}, u32[]{:S(2)}, u32[]{:S(2)}) collective-permute-start(bf16[4,112,768]{2,1,0:T(8,128)(2,1)S(1)} %get-tuple-element.227), channel_id=1, source_target_pairs={{0,16},{16,0},{1,17},{17,1},{2,18},{18,2},{3,19},{19,3},{4,20},{20... | collective-permute-start | bytes 2064392 | tf_op jit(solution)/shard_map/ppermute | solution.py:687
  227.4 37.6 %collective-permute-start.91 = (bf16[2,768,768]{2,1,0:T(8,128)(2,1)}, bf16[2,768,768]{2,1,0:T(8,128)(2,1)}, u32[]{:S(2)}, u32[]{:S(2)}) collective-permute-start(bf16[2,768,768]{2,1,0:T(8,128)(2,1)} %expert_gradients_sent.1), channel_id=1, source_target_pairs={{0,16},{16,0},{1,17},{17,1},{2,18},{18,2},{3,19},{19,3},{4,20},{20... | collective-permute-start | bytes 7077896 | tf_op jit(solution)/shard_map/ppermute | solution.py:687
  229.6 7.9 %collective-permute-start.83 = (bf16[112,768]{1,0:T(8,128)(2,1)S(1)}, bf16[112,768]{1,0:T(8,128)(2,1)S(1)}, u32[]{:S(2)}, u32[]{:S(2)}) collective-permute-start(bf16[112,768]{1,0:T(8,128)(2,1)S(1)} %get-tuple-element.245), channel_id=1, source_target_pairs={{0,6},{2,0},{4,2},{6,4},{1,7},{3,1},{5,3},{7,5},{8,14},{10,8},{12,... | collective-permute-start | bytes 516104 | tf_op jit(solution)/shard_map/ppermute | solution.py:678
  230.3 16.4 %collective-permute-start.82 = (bf16[112,768]{1,0:T(8,128)(2,1)S(1)}, bf16[112,768]{1,0:T(8,128)(2,1)S(1)}, u32[]{:S(2)}, u32[]{:S(2)}) collective-permute-start(bf16[112,768]{1,0:T(8,128)(2,1)S(1)} %get-tuple-element.244), channel_id=1, source_target_pairs={{0,4},{2,6},{4,0},{6,2},{1,5},{3,7},{5,1},{7,3},{8,12},{10,14},{12... | collective-permute-start | bytes 516104 | tf_op jit(solution)/shard_map/ppermute | solution.py:678
  230.8 15.9 %collective-permute-start.81 = (bf16[112,768]{1,0:T(8,128)(2,1)S(1)}, bf16[112,768]{1,0:T(8,128)(2,1)S(1)}, u32[]{:S(2)}, u32[]{:S(2)}) collective-permute-start(bf16[112,768]{1,0:T(8,128)(2,1)S(1)} %get-tuple-element.243), channel_id=1, source_target_pairs={{0,2},{2,4},{4,6},{6,0},{1,3},{3,5},{5,7},{7,1},{8,10},{10,12},{12... | collective-permute-start | bytes 516104 | tf_op jit(solution)/shard_map/ppermute | solution.py:678
  256.5 25.0 %collective-permute-start.79 = (f32[64,768]{1,0:T(8,128)S(1)}, f32[64,768]{1,0:T(8,128)S(1)}, u32[]{:S(2)}, u32[]{:S(2)}) collective-permute-start(f32[64,768]{1,0:T(8,128)S(1)} %broadcast_select_fusion.2), channel_id=1, source_target_pairs={{0,16},{16,0},{1,17},{17,1},{2,18},{18,2},{3,19},{19,3},{4,20},{20... | collective-permute-start | bytes 589832 | tf_op jit(solution)/shard_map/ppermute | solution.py:687
  259.6 11.8 %collective-permute-start.88 = (bf16[112,768]{1,0:T(8,128)(2,1)}, bf16[112,768]{1,0:T(8,128)(2,1)S(1)}, u32[]{:S(2)}, u32[]{:S(2)}) collective-permute-start(bf16[112,768]{1,0:T(8,128)(2,1)} %get-tuple-element.293), channel_id=1, source_target_pairs={{0,2},{2,4},{4,6},{6,0},{1,3},{3,5},{5,7},{7,1},{8,10},{10,12},{12... | collective-permute-start | bytes 516104 | tf_op jit(solution)/shard_map/ppermute | solution.py:678
  260.0 15.5 %collective-permute-start.89 = (bf16[112,768]{1,0:T(8,128)(2,1)}, bf16[112,768]{1,0:T(8,128)(2,1)S(1)}, u32[]{:S(2)}, u32[]{:S(2)}) collective-permute-start(bf16[112,768]{1,0:T(8,128)(2,1)} %get-tuple-element.292), channel_id=1, source_target_pairs={{0,4},{2,6},{4,0},{6,2},{1,5},{3,7},{5,1},{7,3},{8,12},{10,14},{12... | collective-permute-start | bytes 516104 | tf_op jit(solution)/shard_map/ppermute | solution.py:678
  262.0 13.5 %collective-permute-start.90 = (bf16[112,768]{1,0:T(8,128)(2,1)}, bf16[112,768]{1,0:T(8,128)(2,1)}, u32[]{:S(2)}, u32[]{:S(2)}) collective-permute-start(bf16[112,768]{1,0:T(8,128)(2,1)} %get-tuple-element.291), channel_id=1, source_target_pairs={{0,6},{2,0},{4,2},{6,4},{1,7},{3,1},{5,3},{7,5},{8,14},{10,8},{12,... | collective-permute-start | bytes 516104 | tf_op jit(solution)/shard_map/ppermute | solution.py:678
  279.2 7.2 %collective-permute-start.94 = (bf16[112,768]{1,0:T(8,128)(2,1)S(1)}, bf16[112,768]{1,0:T(8,128)(2,1)S(1)}, u32[]{:S(2)}, u32[]{:S(2)}) collective-permute-start(bf16[112,768]{1,0:T(8,128)(2,1)S(1)} %get-tuple-element.288), channel_id=1, source_target_pairs={{0,16},{1,0},{8,24},{9,8},{16,17},{17,1},{24,25},{25,9},{2,18},{3,... | collective-permute-start | bytes 516104 | tf_op jit(solution)/shard_map/ppermute | solution.py:1108
  280.4 9.5 %collective-permute-start.95 = (bf16[112,768]{1,0:T(8,128)(2,1)S(1)}, bf16[112,768]{1,0:T(8,128)(2,1)S(1)}, u32[]{:S(2)}, u32[]{:S(2)}) collective-permute-start(bf16[112,768]{1,0:T(8,128)(2,1)S(1)} %get-tuple-element.288), channel_id=1, source_target_pairs={{0,24},{1,8},{8,16},{9,0},{16,25},{17,9},{24,17},{25,1},{2,26},{3,... | collective-permute-start | bytes 516104 | tf_op jit(solution)/shard_map/ppermute | solution.py:1108
  (136 other events, 1263.8 us)
